TPU v7x, 128 devices: a whole 4x4x4 slice. The times are simulated.
128 devices in a mesh: gx: 16 (over x, z), gy: 8 (over y, core).
Axes of the slice: x: 4, y: 4, z: 4, core: 2. Of those that a mesh axis runs over, the one named last changes fastest.
Arguments:
- start: float32 [6144, 64], P(('gx', 'gy')), may hold values from -6 to 6
- shifts: float32 [4], replicated, may hold values from 0.2 to 0.8
- diag_blocks: float32 [6144, 64, 64], P(('gx', 'gy'))
- off_blocks: float32 [6144, 6, 64, 64], P(('gx', 'gy')), may hold values from -0.24 to 0.24
- jacobi_inv: float32 [6144, 64, 64], P(('gx', 'gy'))
- prolong: float32 [6144, 64, 8], P(('gx', 'gy')), may hold values from -0.75 to 0.75
- coarse_inv: float32 [3072, 8, 8], P(('gx', 'gy')), may hold values from -1 to 1
- cols: int32 [6144, 6], P(('gx', 'gy')), may hold values from 0 to 111
- send_rows: int32 [128, 4, 16], P(('gx', 'gy')), may hold values from 0 to 47
- owner: int32 [6144, 1], P(('gx', 'gy')), may hold values from 0 to 127; in each aligned block of 48 rows (0 to 47, 48 to 95, ...) at most 2 rows name the same one
- agg_slot: int32 [6144], P(('gx', 'gy')), may hold values from 0 to 23
Outputs:
- basis_q: float32 [5, 6144, 64], P(None, ('gx', 'gy'))
- r_factor: float32 [5, 5], replicated
Inputs may be any that keep to these rules, and one draw needn't show every extreme that they name: In the rows of one device (aligned blocks of 48 rows) no owner id appears more than 2 times, and some id appears exactly 2 times.
All inputs are finite; a program needn't handle non-finite values.
Results may differ from a plain program's by a relative error of at most 0.0003.
Values sent between devices are 32-bit elements; how exact they have to be, the bound alone decides.
No kernel may reach another device: no remote copies, remote signals or barrier semaphores. Data moves between devices by JAX's collectives and lax.ppermute only.
A program may use at most 128 MiB of HBM per device.

v0:
```python
import jax
import jax.numpy as jnp
from jax import lax
from jax.sharding import PartitionSpec as P

highest = lax.Precision.HIGHEST
jacobi_weight = 2.0 / 3.0


def extended_2(block, sides, width):
    for axis, dim in sides:
        count = lax.axis_size(axis)
        forward = [(i, i + 1) for i in range(count - 1)]
        forward.append((count - 1, 0))
        backward = [(target, source) for source, target in forward]
        low = lax.ppermute(
            lax.slice_in_dim(block, block.shape[dim] - width, None, axis=dim), axis, forward
        )
        high = lax.ppermute(lax.slice_in_dim(block, 0, width, axis=dim), axis, backward)
        block = jnp.concatenate([low, block, high], axis=dim)
    return block


def apply_operator(vector, diag_blocks, off_blocks, cols, send_lists):
    block_width = vector.shape[1]
    picked = vector[send_lists]
    pair_x = jnp.stack([picked[1], picked[0]]).reshape(2, -1)
    edges_x = extended_2(pair_x, (("gx", 0),), 1)
    pair_y = jnp.stack([picked[3], picked[2]]).reshape(2, -1)
    edges_y = extended_2(pair_y, (("gy", 0),), 1)
    halo_blocks = jnp.concatenate([edges_x[0], edges_x[3], edges_y[0], edges_y[3]]).reshape(
        -1, block_width
    )
    extended = jnp.concatenate([vector, halo_blocks], axis=0)
    nearby = extended[cols]
    own_term = jnp.einsum("rij,rj->ri", diag_blocks, vector, precision=highest)
    rest_term = jnp.einsum("rkij,rkj->ri", off_blocks, nearby, precision=highest)
    return own_term + rest_term


def coarse_correct(vector, prolong, coarse_inv, owner, agg_slot):
    count_x = lax.axis_size("gx")
    count_y = lax.axis_size("gy")
    devices = count_x * count_y
    row_count = vector.shape[0]
    coarse_width = prolong.shape[2]
    agg_count = coarse_inv.shape[0]
    capacity = max(2, 2 * row_count // devices)
    owner_ids = owner[:, 0]
    members = (owner_ids[:, None] == jnp.arange(devices, dtype=jnp.int32)[None, :]).astype(
        jnp.int32
    )
    slot_rank = jnp.sum(jnp.cumsum(members, axis=0) * members, axis=1) - 1
    target = owner_ids * capacity + slot_rank
    selected = target[None, :] == jnp.arange(devices * capacity, dtype=jnp.int32)[:, None]
    picker = selected.astype(jnp.float32)
    partial_value = jnp.einsum("rbc,rb->rc", prolong, vector, precision=highest)
    outgoing = jnp.dot(picker, partial_value, precision=highest)
    filled = jnp.any(selected, axis=1)
    labels = jnp.where(
        filled, jnp.sum(jnp.where(selected, agg_slot[None, :], 0), axis=1), agg_count
    )
    got_values, got_labels = (
        lax.all_to_all(
            outgoing.reshape(devices, capacity, coarse_width),
            ("gx", "gy"),
            split_axis=0,
            concat_axis=0,
            tiled=True,
        ),
        lax.all_to_all(
            labels.reshape(devices, capacity), ("gx", "gy"), split_axis=0, concat_axis=0, tiled=True
        ),
    )
    incoming = got_values.reshape(-1, coarse_width)
    matches = (
        got_labels.reshape(-1)[:, None] == jnp.arange(agg_count, dtype=jnp.int32)[None, :]
    ).astype(jnp.float32)
    coarse = jnp.dot(matches.T, incoming, precision=highest)
    answer = jnp.einsum("acd,ad->ac", coarse_inv, coarse, precision=highest)
    everything = lax.all_gather(answer, ("gx", "gy"), axis=0, tiled=True)
    row_values = everything[owner_ids * agg_count + agg_slot]
    return jnp.einsum("rbc,rc->rb", prolong, row_values, precision=highest)


def per_device(
    start,
    shifts,
    diag_blocks,
    off_blocks,
    jacobi_inv,
    prolong,
    coarse_inv,
    cols,
    send_rows,
    owner,
    agg_slot,
):
    send_lists = send_rows[0]

    def operator(vector):
        return apply_operator(vector, diag_blocks, off_blocks, cols, send_lists)

    def smooth(vector):
        return jacobi_weight * jnp.einsum("rij,rj->ri", jacobi_inv, vector, precision=highest)

    basis = [start]
    for section in range(shifts.shape[0]):
        latest = basis[-1]
        first = smooth(latest)
        second = first + coarse_correct(
            latest - operator(first), prolong, coarse_inv, owner, agg_slot
        )
        basis.append(
            operator(second + smooth(latest - operator(second))) - shifts[section] * latest
        )
    stacked = jnp.stack(basis)
    flat = stacked.reshape(stacked.shape[0], -1)
    total = flat.shape[1] * lax.axis_size("gx") * lax.axis_size("gy")
    local_gram = jnp.dot(flat, flat.T, precision=highest)
    grams = lax.all_gather(local_gram[None], ("gx", "gy"), axis=0, tiled=True)
    gram = jnp.sum(grams, axis=0) / total
    lower = jnp.linalg.cholesky(gram)
    solved = jax.scipy.linalg.solve_triangular(lower, flat, lower=True)
    return (solved.reshape(stacked.shape), lower.T)


def solution(mesh):
    in_specs = (
        P(("gx", "gy"), None),
        P(),
        P(("gx", "gy"), None, None),
        P(("gx", "gy"), None, None, None),
        P(("gx", "gy"), None, None),
        P(("gx", "gy"), None, None),
        P(("gx", "gy"), None, None),
        P(("gx", "gy"), None),
        P(("gx", "gy"), None, None),
        P(("gx", "gy"), None),
        P(("gx", "gy")),
    )
    out_specs = (P(None, ("gx", "gy"), None), P())
    return jax.shard_map(
        per_device, mesh=mesh, in_specs=in_specs, out_specs=out_specs, check_vma=False
    )
```

profile of v0, /device:TPU:1, one launch (start us, length us, event | category | flops | bytes accessed | tf_op | source)
XLA Modules:
  0.0 658.9 jit_solution(2497899111571072685)
XLA Ops:
  17.7 6.3 all-to-all-start
  31.4 10.0 %fusion.46 = f32[48,1,64,1]{2,1,3,0:T(1,128)S(1)} fusion(f32[48,6,64,1]{2,3,1,0:T(1,128)S(1)} %bitcast.369, f32[48,6,64,64]{3,2,1,0:T(8,128)} %param.14), kind=kOutput, calls=%fused_computation.176 | convolution fusion | flops 14155776 | bytes 4804608 | tf_op jit(solution)/shard_map/rkij,rkj->ri/dot_general | solution.py:37
  42.9 9.8 %all-to-all-start.1 = ((f32[128,2,8]{2,1,0:T(2,128)}), f32[128,2,8]{2,1,0:T(2,128)S(1)}, u32[]{:S(2)}, u32[]{:S(2)}) async-start(f32[128,2,8]{2,1,0:T(2,128)} %bitcast.23), calls=%async_computation.1 | async-start | bytes 262144 | tf_op jit(solution)/shard_map/all_to_all | solution.py:64
  54.1 8.4 %all-to-all-done.1 = f32[128,2,8]{2,1,0:T(2,128)S(1)} async-done(((f32[128,2,8]{2,1,0:T(2,128)}), f32[128,2,8]{2,1,0:T(2,128)S(1)}, u32[]{:S(2)}, u32[]{:S(2)}) %all-to-all-start.1) | async-done | bytes 8224 | tf_op jit(solution)/shard_map/all_to_all | solution.py:64
  62.9 33.5 %all-gather.1 = f32[128,24,8]{1,2,0:T(8,128)S(1)} all-gather(f32[1,24,8]{1,2,0:T(8,128)S(1)} %bitcast.444), channel_id=1, replica_groups=mesh['gx'=16,'gy'=8] {'gx','gy'}, dimensions={0}, use_global_device_ids=true | all-gather | bytes 99072 | tf_op jit(solution)/shard_map/all_gather | solution.py:81
  114.2 10.1 %fusion.50 = f32[48,1,64,1]{2,1,3,0:T(1,128)S(1)} fusion(f32[48,6,64,1]{2,3,1,0:T(1,128)} %bitcast.370, f32[48,6,64,64]{3,2,1,0:T(8,128)} %param.14), kind=kOutput, calls=%fused_computation.180 | convolution fusion | flops 14155776 | bytes 4804608 | tf_op jit(solution)/shard_map/rkij,rkj->ri/dot_general | solution.py:37
  142.6 10.0 %fusion.53 = f32[48,1,64,1]{2,1,3,0:T(1,128)S(1)} fusion(f32[48,6,64,1]{2,3,1,0:T(1,128)} %bitcast.371, f32[48,6,64,64]{3,2,1,0:T(8,128)} %param.14), kind=kOutput, calls=%fused_computation.183 | convolution fusion | flops 14155776 | bytes 4804608 | tf_op jit(solution)/shard_map/rkij,rkj->ri/dot_general | solution.py:37
  174.6 10.0 %fusion.56 = f32[48,1,64,1]{2,1,3,0:T(1,128)S(1)} fusion(f32[48,6,64,1]{2,3,1,0:T(1,128)} %bitcast.372, f32[48,6,64,64]{3,2,1,0:T(8,128)} %param.14), kind=kOutput, calls=%fused_computation.186 | convolution fusion | flops 14155776 | bytes 4804608 | tf_op jit(solution)/shard_map/rkij,rkj->ri/dot_general | solution.py:37
  185.5 15.9 %all_to_all.29 = f32[128,2,8]{2,1,0:T(2,128)S(1)} all-to-all(f32[128,2,8]{2,1,0:T(2,128)S(1)} %bitcast.382), channel_id=1, replica_groups=mesh['gx'=16,'gy'=8] {'gx','gy'}, dimensions={0} | all-to-all | bytes 16384 | tf_op jit(solution)/shard_map/all_to_all | solution.py:64
  201.7 36.3 %all-gather.2 = f32[128,24,8]{1,2,0:T(8,128)} all-gather(f32[1,24,8]{1,2,0:T(8,128)S(1)} %bitcast.445), channel_id=1, replica_groups=mesh['gx'=16,'gy'=8] {'gx','gy'}, dimensions={0}, use_global_device_ids=true | all-gather | bytes 99072 | tf_op jit(solution)/shard_map/all_gather | solution.py:81
  258.9 10.0 %fusion.60 = f32[48,1,64,1]{2,1,3,0:T(1,128)S(1)} fusion(f32[48,6,64,1]{2,3,1,0:T(1,128)} %bitcast.373, f32[48,6,64,64]{3,2,1,0:T(8,128)} %param.14), kind=kOutput, calls=%fused_computation.190 | convolution fusion | flops 14155776 | bytes 4804608 | tf_op jit(solution)/shard_map/rkij,rkj->ri/dot_general | solution.py:37
  288.3 10.0 %fusion.63 = f32[48,1,64,1]{2,1,3,0:T(1,128)S(1)} fusion(f32[48,6,64,1]{2,3,1,0:T(1,128)} %bitcast.374, f32[48,6,64,64]{3,2,1,0:T(8,128)} %param.14), kind=kOutput, calls=%fused_computation.193 | convolution fusion | flops 14155776 | bytes 4804608 | tf_op jit(solution)/shard_map/rkij,rkj->ri/dot_general | solution.py:37
  329.2 10.0 %fusion.66 = f32[48,1,64,1]{2,1,3,0:T(1,128)S(1)} fusion(f32[48,6,64,1]{2,3,1,0:T(1,128)} %bitcast.375, f32[48,6,64,64]{3,2,1,0:T(8,128)} %param.14), kind=kOutput, calls=%fused_computation.196 | convolution fusion | flops 14155776 | bytes 4804608 | tf_op jit(solution)/shard_map/rkij,rkj->ri/dot_general | solution.py:37
  340.0 15.9 %all_to_all.30 = f32[128,2,8]{2,1,0:T(2,128)S(1)} all-to-all(f32[128,2,8]{2,1,0:T(2,128)S(1)} %bitcast.384), channel_id=1, replica_groups=mesh['gx'=16,'gy'=8] {'gx','gy'}, dimensions={0} | all-to-all | bytes 16384 | tf_op jit(solution)/shard_map/all_to_all | solution.py:64
  356.3 36.3 %all-gather.3 = f32[128,24,8]{1,2,0:T(8,128)} all-gather(f32[1,24,8]{1,2,0:T(8,128)S(1)} %bitcast.446), channel_id=1, replica_groups=mesh['gx'=16,'gy'=8] {'gx','gy'}, dimensions={0}, use_global_device_ids=true | all-gather | bytes 99072 | tf_op jit(solution)/shard_map/all_gather | solution.py:81
  419.6 10.0 %fusion.70 = f32[48,1,64,1]{2,1,3,0:T(1,128)S(1)} fusion(f32[48,6,64,1]{2,3,1,0:T(1,128)} %bitcast.376, f32[48,6,64,64]{3,2,1,0:T(8,128)} %param.14), kind=kOutput, calls=%fused_computation.200 | convolution fusion | flops 14155776 | bytes 4804608 | tf_op jit(solution)/shard_map/rkij,rkj->ri/dot_general | solution.py:37
  450.7 10.0 %fusion.73 = f32[48,1,64,1]{2,1,3,0:T(1,128)S(1)} fusion(f32[48,6,64,1]{2,3,1,0:T(1,128)} %bitcast.377, f32[48,6,64,64]{3,2,1,0:T(8,128)} %param.14), kind=kOutput, calls=%fused_computation.203 | convolution fusion | flops 14155776 | bytes 4804608 | tf_op jit(solution)/shard_map/rkij,rkj->ri/dot_general | solution.py:37
  494.2 10.0 %fusion.76 = f32[48,1,64,1]{2,1,3,0:T(1,128)S(1)} fusion(f32[48,6,64,1]{2,3,1,0:T(1,128)} %bitcast.378, f32[48,6,64,64]{3,2,1,0:T(8,128)} %param.14), kind=kOutput, calls=%fused_computation.206 | convolution fusion | flops 14155776 | bytes 4804608 | tf_op jit(solution)/shard_map/rkij,rkj->ri/dot_general | solution.py:37
  505.7 7.4 %all-to-all-start.4 = ((f32[128,2,8]{2,1,0:T(2,128)}), f32[128,2,8]{2,1,0:T(2,128)}, u32[]{:S(2)}, u32[]{:S(2)}) async-start(f32[128,2,8]{2,1,0:T(2,128)} %bitcast.381), calls=%async_computation.4 | async-start | bytes 262144 | tf_op jit(solution)/shard_map/all_to_all | solution.py:64
  514.6 8.3 %all-to-all-done.4 = f32[128,2,8]{2,1,0:T(2,128)} async-done(((f32[128,2,8]{2,1,0:T(2,128)}), f32[128,2,8]{2,1,0:T(2,128)}, u32[]{:S(2)}, u32[]{:S(2)}) %all-to-all-start.4) | async-done | bytes 8224 | tf_op jit(solution)/shard_map/all_to_all | solution.py:64
  524.2 36.4 %all-gather.4 = f32[128,24,8]{1,2,0:T(8,128)} all-gather(f32[1,24,8]{1,2,0:T(8,128)S(1)} %bitcast.447), channel_id=1, replica_groups=mesh['gx'=16,'gy'=8] {'gx','gy'}, dimensions={0}, use_global_device_ids=true | all-gather | bytes 99072 | tf_op jit(solution)/shard_map/all_gather | solution.py:81
  579.9 10.0 %fusion.80 = f32[48,1,64,1]{2,1,3,0:T(1,128)S(1)} fusion(f32[48,6,64,1]{2,3,1,0:T(1,128)} %bitcast.379, f32[48,6,64,64]{3,2,1,0:T(8,128)} %param.14), kind=kOutput, calls=%fused_computation.210 | convolution fusion | flops 14155776 | bytes 4804608 | tf_op jit(solution)/shard_map/rkij,rkj->ri/dot_general | solution.py:37
  607.5 10.0 %fusion.83 = f32[48,1,64,1]{2,1,3,0:T(1,128)S(1)} fusion(f32[48,6,64,1]{2,3,1,0:T(1,128)S(1)} %bitcast.368, f32[48,6,64,64]{3,2,1,0:T(8,128)} %param.14), kind=kOutput, calls=%fused_computation.213 | convolution fusion | flops 14155776 | bytes 4804608 | tf_op jit(solution)/shard_map/rkij,rkj->ri/dot_general | solution.py:37
  618.9 35.1 %all-gather.5 = f32[128,5,5]{2,1,0:T(8,128)S(1)} all-gather(f32[1,5,5]{2,1,0:T(8,128)S(1)} %convolution_bitcast_fusion), channel_id=2, replica_groups=mesh['gx'=16,'gy'=8] {'gx','gy'}, dimensions={0}, use_global_device_ids=true | all-gather | bytes 12900 | tf_op jit(solution)/shard_map/all_gather | solution.py:121
  (483 shorter events, 287.0 us)
Async XLA Ops:
  7.1 20.1 %collective-permute-start = (f32[1,1024]{1,0:T(1,128)S(1)}, f32[1,1024]{1,0:T(1,128)S(1)}, u32[]{:S(2)}, u32[]{:S(2)}) collective-permute-start(f32[1,1024]{1,0:T(1,128)S(1)} %slice.361), channel_id=1, source_target_pairs={{0,8},{8,16},{16,24},{24,32},{32,40},{40,48},{48,56},{56,64},{64,7... | collective-permute-start | bytes 12296 | tf_op jit(solution)/shard_map/ppermute | solution.py:16
  9.7 18.6 %collective-permute-start.1 = (f32[1,1024]{1,0:T(1,128)S(1)}, f32[1,1024]{1,0:T(1,128)S(1)}, u32[]{:S(2)}, u32[]{:S(2)}) collective-permute-start(f32[1,1024]{1,0:T(1,128)S(1)} %slice.363), channel_id=1, source_target_pairs={{8,0},{16,8},{24,16},{32,24},{40,32},{48,40},{56,48},{64,56},{72,6... | collective-permute-start | bytes 12296 | tf_op jit(solution)/shard_map/ppermute | solution.py:19
  14.1 14.9 %collective-permute-start.2 = (f32[1,1024]{1,0:T(1,128)S(1)}, f32[1,1024]{1,0:T(1,128)S(1)}, u32[]{:S(2)}, u32[]{:S(2)}) collective-permute-start(f32[1,1024]{1,0:T(1,128)S(1)} %slice.365), channel_id=1, source_target_pairs={{0,1},{1,2},{2,3},{3,4},{4,5},{5,6},{6,7},{7,0},{8,9},{9,10},{10,1... | collective-permute-start | bytes 12296 | tf_op jit(solution)/shard_map/ppermute | solution.py:16
  16.3 13.3 %collective-permute-start.3 = (f32[1,1024]{1,0:T(1,128)S(1)}, f32[1,1024]{1,0:T(1,128)S(1)}, u32[]{:S(2)}, u32[]{:S(2)}) collective-permute-start(f32[1,1024]{1,0:T(1,128)S(1)} %slice.367), channel_id=1, source_target_pairs={{1,0},{2,1},{3,2},{4,3},{5,4},{6,5},{7,6},{0,7},{9,8},{10,9},{11,1... | collective-permute-start | bytes 12296 | tf_op jit(solution)/shard_map/ppermute | solution.py:19
  17.7 25.2 %all-to-all-start = ((s32[128,1,2]{2,1,0:T(1,128)}), s32[128,1,2]{2,1,0:T(1,128)S(1)}, u32[]{:S(2)}, u32[]{:S(2)}) async-start(s32[128,1,2]{2,1,0:T(1,128)} %bitcast.10), calls=%async_computation | async-start | bytes 131072 | tf_op jit(solution)/shard_map/all_to_all | solution.py:71
  42.9 19.7 %all-to-all-start.1 = ((f32[128,2,8]{2,1,0:T(2,128)}), f32[128,2,8]{2,1,0:T(2,128)S(1)}, u32[]{:S(2)}, u32[]{:S(2)}) async-start(f32[128,2,8]{2,1,0:T(2,128)} %bitcast.23), calls=%async_computation.1 | async-start | bytes 262144 | tf_op jit(solution)/shard_map/all_to_all | solution.py:64
  127.6 10.8 %collective-permute-start.8 = (f32[1,1024]{1,0:T(1,128)S(1)}, f32[1,1024]{1,0:T(1,128)S(1)}, u32[]{:S(2)}, u32[]{:S(2)}) collective-permute-start(f32[1,1024]{1,0:T(1,128)S(1)} %slice.377), channel_id=1, source_target_pairs={{0,8},{8,16},{16,24},{24,32},{32,40},{40,48},{48,56},{56,64},{64,7... | collective-permute-start | bytes 12296 | tf_op jit(solution)/shard_map/ppermute | solution.py:16
  127.7 11.4 %collective-permute-start.9 = (f32[1,1024]{1,0:T(1,128)S(1)}, f32[1,1024]{1,0:T(1,128)S(1)}, u32[]{:S(2)}, u32[]{:S(2)}) collective-permute-start(f32[1,1024]{1,0:T(1,128)S(1)} %slice.379), channel_id=1, source_target_pairs={{8,0},{16,8},{24,16},{32,24},{40,32},{48,40},{56,48},{64,56},{72,6... | collective-permute-start | bytes 12296 | tf_op jit(solution)/shard_map/ppermute | solution.py:19
  157.8 11.3 %collective-permute-start.12 = (f32[1,1024]{1,0:T(1,128)S(1)}, f32[1,1024]{1,0:T(1,128)}, u32[]{:S(2)}, u32[]{:S(2)}) collective-permute-start(f32[1,1024]{1,0:T(1,128)S(1)} %slice.386), channel_id=1, source_target_pairs={{0,8},{8,16},{16,24},{24,32},{32,40},{40,48},{48,56},{56,64},{64,7... | collective-permute-start | bytes 12296 | tf_op jit(solution)/shard_map/ppermute | solution.py:16
  157.9 12.6 %collective-permute-start.13 = (f32[1,1024]{1,0:T(1,128)S(1)}, f32[1,1024]{1,0:T(1,128)}, u32[]{:S(2)}, u32[]{:S(2)}) collective-permute-start(f32[1,1024]{1,0:T(1,128)S(1)} %slice.388), channel_id=1, source_target_pairs={{8,0},{16,8},{24,16},{32,24},{40,32},{48,40},{56,48},{64,56},{72,6... | collective-permute-start | bytes 12296 | tf_op jit(solution)/shard_map/ppermute | solution.py:19
  273.5 10.6 %collective-permute-start.20 = (f32[1,1024]{1,0:T(1,128)S(1)}, f32[1,1024]{1,0:T(1,128)S(1)}, u32[]{:S(2)}, u32[]{:S(2)}) collective-permute-start(f32[1,1024]{1,0:T(1,128)S(1)} %slice.402), channel_id=1, source_target_pairs={{0,8},{8,16},{16,24},{24,32},{32,40},{40,48},{48,56},{56,64},{64,7... | collective-permute-start | bytes 12296 | tf_op jit(solution)/shard_map/ppermute | solution.py:16
  273.6 11.2 %collective-permute-start.21 = (f32[1,1024]{1,0:T(1,128)S(1)}, f32[1,1024]{1,0:T(1,128)S(1)}, u32[]{:S(2)}, u32[]{:S(2)}) collective-permute-start(f32[1,1024]{1,0:T(1,128)S(1)} %slice.404), channel_id=1, source_target_pairs={{8,0},{16,8},{24,16},{32,24},{40,32},{48,40},{56,48},{64,56},{72,6... | collective-permute-start | bytes 12296 | tf_op jit(solution)/shard_map/ppermute | solution.py:19
  305.4 13.0 %collective-permute-start.24 = (f32[1,1024]{1,0:T(1,128)}, f32[1,1024]{1,0:T(1,128)}, u32[]{:S(2)}, u32[]{:S(2)}) collective-permute-start(f32[1,1024]{1,0:T(1,128)} %slice.411), channel_id=1, source_target_pairs={{0,8},{8,16},{16,24},{24,32},{32,40},{40,48},{48,56},{56,64},{64,7... | collective-permute-start | bytes 12296 | tf_op jit(solution)/shard_map/ppermute | solution.py:16
  306.1 13.7 %collective-permute-start.25 = (f32[1,1024]{1,0:T(1,128)}, f32[1,1024]{1,0:T(1,128)}, u32[]{:S(2)}, u32[]{:S(2)}) collective-permute-start(f32[1,1024]{1,0:T(1,128)} %slice.413), channel_id=1, source_target_pairs={{8,0},{16,8},{24,16},{32,24},{40,32},{48,40},{56,48},{64,56},{72,6... | collective-permute-start | bytes 12296 | tf_op jit(solution)/shard_map/ppermute | solution.py:19
  400.6 9.7 %collective-permute-start.29 = (f32[1,1024]{1,0:T(1,128)S(1)}, f32[1,1024]{1,0:T(1,128)}, u32[]{:S(2)}, u32[]{:S(2)}) collective-permute-start(f32[1,1024]{1,0:T(1,128)S(1)} %slice.421), channel_id=1, source_target_pairs={{8,0},{16,8},{24,16},{32,24},{40,32},{48,40},{56,48},{64,56},{72,6... | collective-permute-start | bytes 12296 | tf_op jit(solution)/shard_map/ppermute | solution.py:19
  434.3 10.9 %collective-permute-start.32 = (f32[1,1024]{1,0:T(1,128)S(1)}, f32[1,1024]{1,0:T(1,128)}, u32[]{:S(2)}, u32[]{:S(2)}) collective-permute-start(f32[1,1024]{1,0:T(1,128)S(1)} %slice.427), channel_id=1, source_target_pairs={{0,8},{8,16},{16,24},{24,32},{32,40},{40,48},{48,56},{56,64},{64,7... | collective-permute-start | bytes 12296 | tf_op jit(solution)/shard_map/ppermute | solution.py:16
  434.3 12.2 %collective-permute-start.33 = (f32[1,1024]{1,0:T(1,128)S(1)}, f32[1,1024]{1,0:T(1,128)}, u32[]{:S(2)}, u32[]{:S(2)}) collective-permute-start(f32[1,1024]{1,0:T(1,128)S(1)} %slice.429), channel_id=1, source_target_pairs={{8,0},{16,8},{24,16},{32,24},{40,32},{48,40},{56,48},{64,56},{72,6... | collective-permute-start | bytes 12296 | tf_op jit(solution)/shard_map/ppermute | solution.py:19
  467.8 15.7 %collective-permute-start.36 = (f32[1,1024]{1,0:T(1,128)}, f32[1,1024]{1,0:T(1,128)}, u32[]{:S(2)}, u32[]{:S(2)}) collective-permute-start(f32[1,1024]{1,0:T(1,128)} %slice.436), channel_id=1, source_target_pairs={{0,8},{8,16},{16,24},{24,32},{32,40},{40,48},{48,56},{56,64},{64,7... | collective-permute-start | bytes 12296 | tf_op jit(solution)/shard_map/ppermute | solution.py:16
  469.2 15.7 %collective-permute-start.37 = (f32[1,1024]{1,0:T(1,128)}, f32[1,1024]{1,0:T(1,128)}, u32[]{:S(2)}, u32[]{:S(2)}) collective-permute-start(f32[1,1024]{1,0:T(1,128)} %slice.438), channel_id=1, source_target_pairs={{8,0},{16,8},{24,16},{32,24},{40,32},{48,40},{56,48},{64,56},{72,6... | collective-permute-start | bytes 12296 | tf_op jit(solution)/shard_map/ppermute | solution.py:19
  475.5 10.7 %collective-permute-start.38 = (f32[1,1024]{1,0:T(1,128)}, f32[1,1024]{1,0:T(1,128)}, u32[]{:S(2)}, u32[]{:S(2)}) collective-permute-start(f32[1,1024]{1,0:T(1,128)} %slice.440), channel_id=1, source_target_pairs={{0,1},{1,2},{2,3},{3,4},{4,5},{5,6},{6,7},{7,0},{8,9},{9,10},{10,1... | collective-permute-start | bytes 12296 | tf_op jit(solution)/shard_map/ppermute | solution.py:16
  478.6 10.2 %collective-permute-start.39 = (f32[1,1024]{1,0:T(1,128)}, f32[1,1024]{1,0:T(1,128)}, u32[]{:S(2)}, u32[]{:S(2)}) collective-permute-start(f32[1,1024]{1,0:T(1,128)} %slice.442), channel_id=1, source_target_pairs={{1,0},{2,1},{3,2},{4,3},{5,4},{6,5},{7,6},{0,7},{9,8},{10,9},{11,1... | collective-permute-start | bytes 12296 | tf_op jit(solution)/shard_map/ppermute | solution.py:19
  505.7 17.2 %all-to-all-start.4 = ((f32[128,2,8]{2,1,0:T(2,128)}), f32[128,2,8]{2,1,0:T(2,128)}, u32[]{:S(2)}, u32[]{:S(2)}) async-start(f32[128,2,8]{2,1,0:T(2,128)} %bitcast.381), calls=%async_computation.4 | async-start | bytes 262144 | tf_op jit(solution)/shard_map/all_to_all | solution.py:64
  593.2 10.7 %collective-permute-start.44 = (f32[1,1024]{1,0:T(1,128)S(1)}, f32[1,1024]{1,0:T(1,128)S(1)}, u32[]{:S(2)}, u32[]{:S(2)}) collective-permute-start(f32[1,1024]{1,0:T(1,128)S(1)} %slice.452), channel_id=1, source_target_pairs={{0,8},{8,16},{16,24},{24,32},{32,40},{40,48},{48,56},{56,64},{64,7... | collective-permute-start | bytes 12296 | tf_op jit(solution)/shard_map/ppermute | solution.py:16
  593.3 11.2 %collective-permute-start.45 = (f32[1,1024]{1,0:T(1,128)S(1)}, f32[1,1024]{1,0:T(1,128)S(1)}, u32[]{:S(2)}, u32[]{:S(2)}) collective-permute-start(f32[1,1024]{1,0:T(1,128)S(1)} %slice.454), channel_id=1, source_target_pairs={{8,0},{16,8},{24,16},{32,24},{40,32},{48,40},{56,48},{64,56},{72,6... | collective-permute-start | bytes 12296 | tf_op jit(solution)/shard_map/ppermute | solution.py:19
  (49 other events, 706.4 us)
where the time goes:
time: 669 us; the launch traced here: 659 us
  blocking collectives  210 us (31%)
  matrix products  182 us (27%)
  starting transfers between devices  115 us (17%)
  local copies, waits for them, and re-layouts  84.3 us (13%)
  other arithmetic  48.8 us (7%)
  waiting for transfers between devices  16.9 us (3%)
    all_gather x4, blocking collectives, coarse_correct(): everything = lax.all_gather(answer, ('gx', 'gy'), axis=0, tiled=True)  143 us
    dot_general x12, matrix products, apply_operator(): jnp.einsum('rkij,rkj->ri', off_blocks, nearby, precision=highest)  120 us
    ppermute x24, starting transfers between devices, extended_2(): lax.ppermute(lax.slice_in_dim(block, 0, width, axis=dim), axis, backward)  65.3 us
    all_gather x1, blocking collectives, per_device(): grams = lax.all_gather(local_gram[None], ('gx', 'gy'), axis=0, tiled=True)  35.1 us
    all_to_all x2, blocking collectives, coarse_correct(): lax.all_to_all(outgoing.reshape(devices, capacity, coarse_width), ('gx',...  31.8 us
    dot_general x12, matrix products, apply_operator(): own_term = jnp.einsum('rij,rj->ri', diag_blocks, vector, precision=highest)  31.2 us
    ppermute x24, starting transfers between devices, extended_2(): lax.ppermute(lax.slice_in_dim(block, block.shape[dim] - width, None, axis...  26.3 us
    dot_general x8, matrix products, smooth(): jnp.einsum('rij,rj->ri', jacobi_inv, vector, precision=highest)  21.8 us
  transfers between devices with their start and end apart: 51, of which 2 were waited for; matrix products, arithmetic and copies ran while one was open for 14% of the time, Pallas kernels for 0%

commit v1 on v0

v1 whole, which is shorter than its diff:
```python
import functools

import jax
import jax.numpy as jnp
from jax import lax
from jax.experimental import pallas as pl
from jax.experimental.pallas import tpu as pltpu
from jax.sharding import PartitionSpec as P

F32 = jnp.float32
BF16 = jnp.bfloat16
ROWS = 48
BS = 64
CW = 8
HALO = 16
EXT = ROWS + 4 * HALO
KOFF = 6
WIDTH = 7 * 128
jacobi_weight = 2.0 / 3.0
PAIRS = [(j, l) for j in range(5) for l in range(j, 5)]

VM = pl.BlockSpec(memory_space=pltpu.VMEM)
SM = pl.BlockSpec(memory_space=pltpu.SMEM)
ANY = pl.BlockSpec(memory_space=pl.ANY)
LAST = (((1,), (1,)), ((), ()))


def low_lanes(x):
    return lax.broadcasted_iota(jnp.int32, x.shape, 1) < BS


def swap(x):
    return pltpu.roll(x, BS, 1)


def twice(x):
    return jnp.concatenate([x, x], axis=1)


def pack(x):
    high = x.astype(BF16).astype(F32)
    return jnp.where(low_lanes(x), high, (x - high).astype(BF16).astype(F32))


def lhs_parts(packed):
    low = low_lanes(packed)
    turned = swap(packed)
    return jnp.where(low, packed, turned), jnp.where(low, turned, 0.0)


def row_blocks(top, bottom, w_ref):
    out = []
    for g in range(ROWS // 8):
        lhs = jnp.concatenate([top[8 * g : 8 * g + 8], bottom[8 * g : 8 * g + 8]], axis=0).astype(BF16)
        r = lax.dot_general(lhs, w_ref[512 * g : 512 * g + 512, :], LAST, preferred_element_type=F32)
        s = r[:8] + r[8:]
        own = lax.broadcasted_iota(jnp.int32, s.shape, 0) == lax.broadcasted_iota(jnp.int32, s.shape, 1) // BS
        s = jnp.where(own, s, 0.0)
        t = (s[:, 0:128] + s[:, 128:256]) + (s[:, 256:384] + s[:, 384:512])
        out.append(t + swap(t))
    return jnp.concatenate(out, axis=0)


def smooth(x, wj_ref):
    top, bottom = lhs_parts(pack(x))
    return row_blocks(top, bottom, wj_ref)


def operate(packed, w_ref, gather_ref):
    e = jnp.concatenate([packed, jnp.zeros((128 - EXT, 128), F32)], axis=0)
    s = swap(e)
    low = low_lanes(e)
    zero = jnp.zeros_like(e)
    rhs = jnp.concatenate(
        [
            jnp.concatenate([jnp.where(low, e, zero), jnp.where(low, s, zero)], axis=1),
            jnp.concatenate([jnp.where(low, zero, s), jnp.where(low, zero, e)], axis=1),
        ],
        axis=0,
    ).astype(BF16)
    x = jnp.dot(gather_ref[...], rhs, preferred_element_type=F32)
    high = [x[ROWS * p : ROWS * p + ROWS, 0:128] for p in range(3)]
    rest = [x[ROWS * p : ROWS * p + ROWS, 128:256] for p in range(3)]
    top, bottom = lhs_parts(packed[:ROWS])
    none = [jnp.zeros((ROWS, 128), F32)] * 3
    return row_blocks(
        jnp.concatenate(high + high + [top], axis=1), jnp.concatenate(rest + none + [bottom], axis=1), w_ref
    )


def send_lists(packed, pick_ref, outs):
    picked = jnp.dot(pick_ref[...], packed.astype(BF16), preferred_element_type=F32)
    for s, out in enumerate(outs):
        out[...] = picked[HALO * s : HALO * s + HALO]


def first_kernel(start, jac, pt, ids, listed, v, wj, ptd, pick, z, ze, s0, s1, s2, s3):
    v[...] = twice(start[...])
    for g in range(ROWS // 8):
        wj[512 * g : 512 * g + 512, :] = pack(twice(jac[512 * g : 512 * g + 512, :] * jacobi_weight)).astype(BF16)
    for c in range(CW):
        ptd[c] = twice(pt[c])
    chosen = (listed[...] == lax.broadcasted_iota(jnp.int32, (4 * HALO, ROWS), 1)).astype(F32)
    pick[...] = chosen.astype(BF16)
    z[...] = smooth(v[...], wj)
    ze[...] = pack(z[...])
    low = lax.broadcasted_iota(jnp.int32, (ROWS, 128), 1) < BS
    parts = [jnp.where(low, ptd[r], ptd[r + 4]) for r in range(4)] + [ids[...]]
    parts = [jnp.dot(chosen, x, precision=lax.Precision.HIGHEST, preferred_element_type=F32) for x in parts]
    parts = [jnp.dot(pick[...], ze[...].astype(BF16), preferred_element_type=F32)] + parts
    for s, out in enumerate((s0, s1, s2, s3)):
        for k, x in enumerate(parts):
            out[k] = x[HALO * s : HALO * s + HALO]


def operator_kernel(off, diag, cols, w, gather, buf, dbuf, sems, dsems):
    def copies(g):
        slot = g % 2
        return (
            pltpu.make_async_copy(off.at[pl.ds(8 * g, 8)], buf.at[slot], sems.at[slot]),
            pltpu.make_async_copy(diag.at[pl.ds(8 * g, 8)], dbuf.at[slot], dsems.at[slot]),
        )

    for c in copies(0):
        c.start()
    lane = lax.broadcasted_iota(jnp.int32, (ROWS, 256), 1)
    for p in range(3):
        hit = (lane == cols[:, 2 * p : 2 * p + 1]) | (lane == cols[:, 2 * p + 1 : 2 * p + 2] + 128)
        gather[ROWS * p : ROWS * p + ROWS, :] = hit.astype(F32).astype(BF16)
    for g in range(ROWS // 8):
        if g + 1 < ROWS // 8:
            for c in copies(g + 1):
                c.start()
        for c in copies(g):
            c.wait()
        slot = g % 2

        def row(i, carry):
            at = pl.ds(pl.multiple_of((8 * g + i) * BS, BS), BS)
            for p in range(3):
                x = jnp.concatenate([buf[slot, i, 2 * p], buf[slot, i, 2 * p + 1]], axis=1)
                high = x.astype(BF16)
                w[at, 128 * p : 128 * p + 128] = high
                w[at, 384 + 128 * p : 512 + 128 * p] = (x - high.astype(F32)).astype(BF16)
            w[at, 768:896] = pack(twice(dbuf[slot, i])).astype(BF16)
            return carry

        lax.fori_loop(0, 8, row, 0)


def restrict_kernel(v, ze, h0, h1, h2, h3, w_op, gather, ptd, w, p):
    ext = jnp.concatenate([ze[...], h0[...], h1[...], h2[...], h3[...]], axis=0)
    r = v[...] - operate(ext, w_op, gather)
    w[...] = r
    ones = jnp.ones((16, 128), BF16)
    pad = jnp.zeros((16, 128), F32)
    for k in range(4):
        x = jnp.concatenate([pack(ptd[k] * r), pad, pack(ptd[k + 4] * r), pad], axis=0).astype(BF16)
        p[k : k + 1, :] = lax.dot_general(ones, x, LAST, preferred_element_type=F32)[0:1]


def coarse_kernel(x0, ids, ptd, g0, g1, g2, g3, mask, pte, xp):
    idc = jnp.concatenate(
        [ids[...], g0[5], g1[5], g2[5], g3[5], jnp.full((128 - EXT, 128), -1.0, F32)], axis=0
    )
    low = low_lanes(idc)
    low8 = lax.broadcasted_iota(jnp.int32, (1, 128), 1) < BS
    for q in range(64):
        line = jnp.where(low8, x0[2 * q, 4:5, :], x0[2 * q + 1, 4:5, :])
        mask[:, 128 * q : 128 * q + 128] = (idc == line).astype(F32).astype(BF16)
        xp[q] = jnp.concatenate([x0[2 * q, 0:4, :], x0[2 * q + 1, 0:4, :]], axis=0)
    device = jnp.floor((idc + 0.5) * (1.0 / 24.0))
    slot = idc - 24.0 * device
    upper = slot >= 11.5
    place = device * 16.0 + jnp.where(upper, slot - 12.0, slot)
    total = jnp.zeros((128, 128), F32)
    for b in range(8):
        src = x0[16 * b : 16 * b + 16, 8:24, :].reshape(256, 128)
        high = src.astype(BF16)
        mid = (src - high.astype(F32)).astype(BF16)
        rest = (src - high.astype(F32) - mid.astype(F32)).astype(BF16)
        lane = lax.broadcasted_iota(jnp.int32, (128, 256), 1).astype(F32) + 256.0 * b
        hit = (twice(place) == lane).astype(F32).astype(BF16)
        got = jnp.dot(hit, jnp.concatenate([high, mid, rest], axis=1), preferred_element_type=F32)
        total = total + (got[:, 0:128] + got[:, 128:256] + got[:, 256:384])
    inverse = jnp.where(upper, swap(total), total)[:EXT]
    wide = []
    for c in range(CW):
        around = [g[1 + c % 4] for g in (g0, g1, g2, g3)]
        around = jnp.concatenate(around, axis=0)
        lowh = low_lanes(around)
        turned = swap(around)
        around = jnp.where(lowh, around, turned) if c < 4 else jnp.where(lowh, turned, around)
        wide.append(jnp.concatenate([ptd[c], around], axis=0))
    for d in range(CW):
        acc = wide[0] * inverse[:, d : d + 1]
        for c in range(1, CW):
            acc = acc + wide[c] * inverse[:, c * CW + d : c * CW + d + 1]
        pte[d] = acc


def correct_kernel(x, mask, pte, z, w, w_op, gather, wj, pick, ye, s0, s1, s2, s3, parts):
    sub = lax.broadcasted_iota(jnp.int32, (8, 128), 0) < 4
    lane = lax.broadcasted_iota(jnp.int32, (8, 128), 1) < BS
    keep = sub == lane
    for q in range(64):
        t = x[q]
        t = jnp.where(keep, t, pltpu.roll(swap(t), 4, 0))
        high = t.astype(BF16).astype(F32)
        parts[:, 128 * q : 128 * q + 128] = jnp.concatenate([high, t - high], axis=0).astype(BF16)
    got = lax.dot_general(mask[...], parts[...], LAST, preferred_element_type=F32)
    coarse = got[:EXT, 0:8] + got[:EXT, 8:16]
    u = pte[0] * coarse[:, 0:1]
    for d in range(1, CW):
        u = u + pte[d] * coarse[:, d : d + 1]
    r = w[...] - operate(pack(u), w_op, gather)
    y = z[...] + u[:ROWS] + smooth(r, wj)
    ye[...] = pack(y)
    send_lists(ye[...], pick, (s0, s1, s2, s3))


def advance(k, shifts, v, ye, h0, h1, h2, h3, w_op, gather):
    ext = jnp.concatenate([ye[...], h0[...], h1[...], h2[...], h3[...]], axis=0)
    return operate(ext, w_op, gather) - shifts[k] * v[...]


def advance_kernel(k, shifts, v, ye, h0, h1, h2, h3, w_op, gather, wj, pick, vn, z, ze, s0, s1, s2, s3):
    vn[...] = advance(k, shifts, v, ye, h0, h1, h2, h3, w_op, gather)
    z[...] = smooth(vn[...], wj)
    ze[...] = pack(z[...])
    send_lists(ze[...], pick, (s0, s1, s2, s3))


def last_kernel(shifts, ye, h0, h1, h2, h3, w_op, gather, v0, v1, v2, v3, v4, gram):
    v4[...] = advance(3, shifts, v3, ye, h0, h1, h2, h3, w_op, gather)
    basis = [v[...] for v in (v0, v1, v2, v3, v4)]
    rows = []
    for j, l in PAIRS:
        rows.append(jnp.sum(basis[j] * basis[l], axis=0, keepdims=True))
    rows.append(jnp.zeros((128 - len(rows), 128), F32))
    rows = jnp.concatenate(rows, axis=0)
    sums = lax.dot_general(
        jnp.ones((8, 128), F32), rows, LAST, precision=lax.Precision.HIGHEST, preferred_element_type=F32
    )
    gram[...] = sums[0:1]


def orthogonal_kernel(total, grams, v0, v1, v2, v3, v4, q_out, r_out):
    sums = jnp.sum(grams[...], axis=0, keepdims=True) * (1.0 / (2.0 * total))
    g = {pair: sums[:, n : n + 1] for n, pair in enumerate(PAIRS)}
    lower = {}
    for j in range(5):
        d = g[(j, j)]
        for k in range(j):
            d = d - lower[(j, k)] * lower[(j, k)]
        lower[(j, j)] = jnp.sqrt(d)
        for i in range(j + 1, 5):
            t = g[(j, i)]
            for k in range(j):
                t = t - lower[(i, k)] * lower[(j, k)]
            lower[(i, j)] = t / lower[(j, j)]
    at_row = lax.broadcasted_iota(jnp.int32, (8, 128), 0)
    at_col = lax.broadcasted_iota(jnp.int32, (8, 128), 1)
    r = jnp.zeros((8, 128), F32)
    for (i, j), value in lower.items():
        r = jnp.where((at_row == j) & (at_col == i), value, r)
    r_out[...] = r[0:5, 0:5]
    solved = []
    for i, v in enumerate((v0, v1, v2, v3, v4)):
        t = v[...]
        for k in range(i):
            t = t - lower[(i, k)] * solved[k]
        t = t / lower[(i, i)]
        solved.append(t)
        q_out[i] = t[:, 0:BS]


def shape(*dims, dtype=F32):
    return jax.ShapeDtypeStruct(dims, dtype)


def kept(*dims, dtype=F32):
    return pltpu.VMEM(dims, dtype)


def call(kernel, outs, *args, specs=None, scratch=(), flops=2_000_000, name=None):
    return pl.pallas_call(
        kernel,
        out_shape=outs,
        in_specs=specs or [VM] * len(args),
        out_specs=jax.tree.map(lambda _: VM, outs),
        scratch_shapes=list(scratch),
        compiler_params=pltpu.CompilerParams(vmem_limit_bytes=24 << 20),
        cost_estimate=pl.CostEstimate(flops=flops, bytes_accessed=100_000, transcendentals=0),
        name=name,
    )(*args)


def swap_pairs(count, phase):
    if phase == 0:
        return [(i, i ^ 1) for i in range(count)]
    return [(i, (i - 1) % count if i % 2 == 0 else (i + 1) % count) for i in range(count)]


def exchange(sends):
    nx, ny = lax.axis_size("gx"), lax.axis_size("gy")
    b = lax.ppermute(sends[1], "gx", swap_pairs(nx, 1))
    d = lax.ppermute(sends[3], "gy", swap_pairs(ny, 1))
    a = lax.ppermute(sends[0], "gx", swap_pairs(nx, 0))
    c = lax.ppermute(sends[2], "gy", swap_pairs(ny, 0))
    return a, b, c, d


def everywhere(x):
    count = lax.axis_size("gx") * lax.axis_size("gy")
    y = jnp.broadcast_to(x[None], (count,) + x.shape)
    return lax.all_to_all(y, ("gx", "gy"), split_axis=0, concat_axis=0, tiled=True)


def per_device(start, shifts, diag_blocks, off_blocks, jacobi_inv, prolong, coarse_inv, cols, send_rows, owner, agg_slot):
    odd_x = lax.axis_index("gx") % 2
    odd_y = lax.axis_index("gy") % 2
    lists = send_rows[0]
    lists = jnp.concatenate(
        [jnp.where(odd_x == 1, lists[1::-1], lists[0:2]), jnp.where(odd_y == 1, lists[3:1:-1], lists[2:4])]
    ).reshape(4 * HALO, 1)
    beyond = cols - ROWS
    turn = jnp.where(beyond < 2 * HALO, 1 - odd_x, 1 - odd_y) * HALO
    cols = jnp.where(beyond >= 0, ROWS + (beyond ^ turn), cols)
    ids = (owner[:, 0] * coarse_inv.shape[0] + agg_slot).astype(F32)
    id_col = jnp.broadcast_to(ids[:, None], (ROWS, 128))
    id_pad = jnp.concatenate([ids, jnp.full((BS - ROWS,), -1.0, F32)])
    inv = coarse_inv.reshape(24, BS)
    extra = jnp.concatenate(
        [
            jnp.concatenate([id_pad, id_pad])[None],
            jnp.zeros((3, 128), F32),
            jnp.concatenate([inv[:12], inv[12:]], axis=1),
            jnp.zeros((4, 128), F32),
        ]
    )
    pt = jnp.transpose(prolong, (2, 0, 1))

    halo = [shape(HALO, 128)] * 4
    v, wj, ptd, pick, z, ze, *sends = call(
        first_kernel,
        [
            shape(ROWS, 128),
            kept(ROWS * BS, 128, dtype=BF16),
            shape(CW, ROWS, 128),
            shape(4 * HALO, ROWS, dtype=BF16),
            shape(ROWS, 128),
            shape(ROWS, 128),
        ]
        + [shape(6, HALO, 128)] * 4,
        start,
        jacobi_inv.reshape(ROWS * BS, BS),
        pt,
        id_col,
        lists,
        name="first",
    )
    got = exchange(sends)
    w_op, gather = call(
        operator_kernel,
        [kept(ROWS * BS, WIDTH, dtype=BF16), shape(3 * ROWS, 256, dtype=BF16)],
        off_blocks,
        diag_blocks,
        cols,
        specs=[ANY, ANY, VM],
        scratch=[
            pltpu.VMEM((2, 8, KOFF, BS, BS), F32),
            pltpu.VMEM((2, 8, BS, BS), F32),
            pltpu.SemaphoreType.DMA((2,)),
            pltpu.SemaphoreType.DMA((2,)),
        ],
        flops=2_000_000_000,
        name="operator",
    )
    around = [g[0] for g in got]
    basis = [v]
    mask = pte = None
    for k in range(4):
        w, p = call(
            restrict_kernel, [shape(ROWS, 128), shape(4, 128)], v, ze, *around, w_op, gather, ptd, name="restrict"
        )
        if k == 0:
            both = everywhere(jnp.concatenate([p, extra]))
            mask, pte, x = call(
                coarse_kernel,
                [kept(128, 64 * 128, dtype=BF16), shape(CW, EXT, 128), shape(64, 8, 128)],
                both,
                id_col,
                ptd,
                *got,
                name="coarse",
            )
        else:
            x = everywhere(p).reshape(64, 8, 128)
        ye, *sends = call(
            correct_kernel,
            [shape(ROWS, 128)] + halo,
            x,
            mask,
            pte,
            z,
            w,
            w_op,
            gather,
            wj,
            pick,
            scratch=[pltpu.VMEM((16, 64 * 128), BF16)],
            name="correct",
        )
        around = exchange(sends)
        if k < 3:
            v, z, ze, *sends = call(
                functools.partial(advance_kernel, k),
                [shape(ROWS, 128)] * 3 + halo,
                shifts,
                v,
                ye,
                *around,
                w_op,
                gather,
                wj,
                pick,
                specs=[SM] + [VM] * 10,
                name="advance",
            )
            basis.append(v)
            around = exchange(sends)
    v, gram = call(
        last_kernel,
        [shape(ROWS, 128), shape(1, 128)],
        shifts,
        ye,
        *around,
        w_op,
        gather,
        *basis,
        specs=[SM] + [VM] * 11,
        name="last",
    )
    basis.append(v)
    grams = everywhere(gram).reshape(128, 128)
    total = float(ROWS * BS * 128)
    return tuple(
        call(
            functools.partial(orthogonal_kernel, total),
            [shape(5, ROWS, BS), shape(5, 5)],
            grams,
            *basis,
            name="orthogonal",
        )
    )


def solution(mesh):
    rows = ("gx", "gy")
    in_specs = (
        P(rows, None),
        P(),
        P(rows, None, None),
        P(rows, None, None, None),
        P(rows, None, None),
        P(rows, None, None),
        P(rows, None, None),
        P(rows, None),
        P(rows, None, None),
        P(rows, None),
        P(rows),
    )
    return jax.shard_map(
        per_device, mesh=mesh, in_specs=in_specs, out_specs=(P(None, rows, None), P()), check_vma=False
    )
```

time: 669 us -> 210 us (0.31); the launches traced: 659 us -> 210 us
  matrix products: 182 us -> 0 us
  blocking collectives: 210 us -> 91.8 us
  starting transfers between devices: 115 us -> 38.4 us
  local copies, waits for them, and re-layouts: 84.3 us -> 8.89 us
  other arithmetic: 48.8 us -> 1.64 us
  Pallas kernels: 0 us -> 45.9 us
    dot_general x49 -> x0, matrix products: 182 us -> none  [the longest x12 120 us: apply_operator(): jnp.einsum('rkij,rkj->ri', off_blocks, nearby, precision=highest)]
    all_gather x5 -> x0, blocking collectives: 178 us -> none  [the longest x4 143 us: coarse_correct(): everything = lax.all_gather(answer, ('gx', 'gy'), axis=0, tiled=True)]
    all_to_all x2 -> x5, blocking collectives: 31.8 us -> 91.8 us  [everywhere(): lax.all_to_all(y, ('gx', 'gy'), split_axis=0, concat_axis=0, tiled=True)]
    ppermute x48 -> x32, starting transfers between devices: 91.5 us -> 38.4 us  [the longest x8 23 us: exchange(): b = lax.ppermute(sends[1], 'gx', swap_pairs(nx, 1))]
    pallas_call x0 -> x16, Pallas kernels: none -> 45.9 us  [call(): pl.pallas_call(kernel, out_shape=outs, in_specs=specs or [VM] * len(args)...]
    ppermute x48 -> x0, other arithmetic: 40.7 us -> none  [the longest x24 20.6 us: extended_2(): lax.ppermute(lax.slice_in_dim(block, 0, width, axis=dim), axis, backward)]
    gather x28 -> x0, local copies, waits for them, and re-layouts: 37.7 us -> none  [the longest x12 18 us: apply_operator(): nearby = extended[cols]]
    all_to_all x3 -> x0, starting transfers between devices: 23.5 us -> none  [the longest x2 17.1 us: coarse_correct(): lax.all_to_all(outgoing.reshape(devices, capacity, coarse_width), ('gx',...]
  transfers between devices with their start and end apart: 51 -> 32, of which waited for: 2 -> 14; matrix products, arithmetic and copies ran while one was open for 14% -> 0% of each run, Pallas kernels for 0% -> 3%
where the time goes in v1:
time: 210 us
  blocking collectives  91.8 us (44%)
  Pallas kernels  45.9 us (22%)
  starting transfers between devices  38.4 us (18%)
  waiting for transfers between devices  22.4 us (11%)
  local copies, waits for them, and re-layouts  8.89 us (4%)
    all_to_all x5, blocking collectives, everywhere(): lax.all_to_all(y, ('gx', 'gy'), split_axis=0, concat_axis=0, tiled=True)  91.8 us
    pallas_call x16, Pallas kernels, call(): pl.pallas_call(kernel, out_shape=outs, in_specs=specs or [VM] * len(args)...  45.9 us
    ppermute x8, starting transfers between devices, exchange(): b = lax.ppermute(sends[1], 'gx', swap_pairs(nx, 1))  23 us
    ppermute x8, waiting for transfers between devices, exchange(): b = lax.ppermute(sends[1], 'gx', swap_pairs(nx, 1))  13.4 us
    ppermute x8, waiting for transfers between devices, exchange(): d = lax.ppermute(sends[3], 'gy', swap_pairs(ny, 1))  8.71 us
    ppermute x8, starting transfers between devices, exchange(): c = lax.ppermute(sends[2], 'gy', swap_pairs(ny, 0))  8.53 us
    unnamed x20, local copies, waits for them, and re-layouts  7.22 us
  transfers between devices with their start and end apart: 32, of which 14 were waited for; matrix products, arithmetic and copies ran while one was open for 0% of the time, Pallas kernels for 3%

profile of v1, /device:TPU:1, one launch (start us, length us, event | category | flops | bytes accessed | tf_op | source)
XLA Modules:
  0.0 210.0 jit_solution(1736613371088179616)
XLA Ops:
  7.3 2.5 %collective-permute-start = (f32[6,16,128]{2,1,0:T(8,128)S(1)}, f32[6,16,128]{2,1,0:T(8,128)S(1)}, u32[]{:S(2)}, u32[]{:S(2)}) collective-permute-start(f32[6,16,128]{2,1,0:T(8,128)S(1)} %get-tuple-element.70), channel_id=1, source_target_pairs={{0,8},{8,0},{16,24},{24,16},{32,40},{40,32},{48,56},{56,48},{64,72... | collective-permute-start | bytes 147464 | tf_op jit(solution)/shard_map/ppermute | solution.py:309
  9.8 4.4 %collective-permute-start.1 = (f32[6,16,128]{2,1,0:T(8,128)S(1)}, f32[6,16,128]{2,1,0:T(8,128)S(1)}, u32[]{:S(2)}, u32[]{:S(2)}) collective-permute-start(f32[6,16,128]{2,1,0:T(8,128)S(1)} %get-tuple-element.71), channel_id=1, source_target_pairs={{0,120},{8,16},{16,8},{24,32},{32,24},{40,48},{48,40},{56,64},{64,... | collective-permute-start | bytes 147464 | tf_op jit(solution)/shard_map/ppermute | solution.py:307
  17.1 3.7 %copy-done.2 = f32[48,6,64,64]{3,2,1,0:T(8,128)S(1)} copy-done((f32[48,6,64,64]{3,2,1,0:T(8,128)S(1)}, f32[48,6,64,64]{3,2,1,0:T(8,128)}, u32[]{:S(2)}) %copy-start.2) | copy-done | bytes 4718616
  20.8 5.9 %operator.1 = (bf16[3072,896]{1,0:T(8,128)(2,1)S(1)}, bf16[144,256]{1,0:T(8,128)(2,1)S(1)}) custom-call(f32[48,6,64,64]{3,2,1,0:T(8,128)S(1)} %copy-done.2, f32[48,64,64]{2,1,0:T(8,128)S(1)} %copy-done.3, s32[48,6]{1,0:T(8,128)S(1)} %add_select_fusion.cols), custom_call_target="tpu_custom_call" | custom-call | flops 2000000000 | bytes 100000 | tf_op jit(solution)/shard_map/operator/pallas_call | solution.py:287
  29.3 29.8 %all_to_all.25.x0 = f32[128,24,128]{2,1,0:T(8,128)S(1)} all-to-all(f32[128,24,128]{2,1,0:T(8,128)S(1)} %broadcast_in_dim.61), channel_id=1, replica_groups=mesh['gx'=16,'gy'=8] {'gx','gy'}, dimensions={0} | all-to-all | bytes 3145728 | tf_op jit(solution)/shard_map/all_to_all | solution.py:317
  61.3 4.3 %correct.4 = (f32[48,128]{1,0:T(8,128)S(1)}, f32[16,128]{1,0:T(8,128)S(1)}, f32[16,128]{1,0:T(8,128)S(1)}, f32[16,128]{1,0:T(8,128)S(1)}, f32[16,128]{1,0:T(8,128)S(1)}) custom-call(f32[64,8,128]{2,1,0:T(8,128)S(1)} %get-tuple-element.78.x, bf16[128,8192]{1,0:T(8,128)(2,1)S(1)} %get-tuple-element.79.mask, f32[8,112,128]{2,1,0:T(8,128)S(1)} %get-tuple-element.80.pte, ...), custom_call_target="tpu_custom_call" | custom-call | flops 2000000 | bytes 100000 | tf_op jit(solution)/shard_map/correct/pallas_call | solution.py:287
  68.8 2.9 %collective-permute-done.5.h1 = f32[16,128]{1,0:T(8,128)S(1)} collective-permute-done((f32[16,128]{1,0:T(8,128)S(1)}, f32[16,128]{1,0:T(8,128)S(1)}, u32[]{:S(2)}, u32[]{:S(2)}) %collective-permute-start.5) | collective-permute-done | bytes 8224 | tf_op jit(solution)/shard_map/ppermute | solution.py:307
  71.7 2.7 %advance.3 = (f32[48,128]{1,0:T(8,128)S(1)}, f32[48,128]{1,0:T(8,128)S(1)}, f32[48,128]{1,0:T(8,128)S(1)}, f32[16,128]{1,0:T(8,128)S(1)}, f32[16,128]{1,0:T(8,12...) custom-call(f32[4]{0:T(128)S(1)} %copy-done.6, f32[48,128]{1,0:T(8,128)S(1)} %get-tuple-element.68.v.v0, ...), custom_call_target="tpu_custom_call" | custom-call | flops 2000000 | bytes 100000 | tf_op jit(solution)/shard_map/advance/pallas_call | solution.py:287
  74.6 4.1 %collective-permute-start.9 = (f32[16,128]{1,0:T(8,128)S(1)}, f32[16,128]{1,0:T(8,128)S(1)}, u32[]{:S(2)}, u32[]{:S(2)}) collective-permute-start(f32[16,128]{1,0:T(8,128)S(1)} %get-tuple-element.93), channel_id=1, source_target_pairs={{0,120},{8,16},{16,8},{24,32},{32,24},{40,48},{48,40},{56,64},{64,... | collective-permute-start | bytes 24584 | tf_op jit(solution)/shard_map/ppermute | solution.py:307
  80.8 2.5 %collective-permute-done.11.h3 = f32[16,128]{1,0:T(8,128)S(1)} collective-permute-done((f32[16,128]{1,0:T(8,128)S(1)}, f32[16,128]{1,0:T(8,128)S(1)}, u32[]{:S(2)}, u32[]{:S(2)}) %collective-permute-start.11) | collective-permute-done | bytes 8224 | tf_op jit(solution)/shard_map/ppermute | solution.py:308
  85.3 15.2 %all_to_all.26 = f32[128,4,128]{2,1,0:T(4,128)S(1)} all-to-all(f32[128,4,128]{2,1,0:T(4,128)S(1)} %broadcast_in_dim.62), channel_id=1, replica_groups=mesh['gx'=16,'gy'=8] {'gx','gy'}, dimensions={0} | all-to-all | bytes 524288 | tf_op jit(solution)/shard_map/all_to_all | solution.py:317
  100.5 4.3 %correct.5 = (f32[48,128]{1,0:T(8,128)S(1)}, f32[16,128]{1,0:T(8,128)S(1)}, f32[16,128]{1,0:T(8,128)S(1)}, f32[16,128]{1,0:T(8,128)S(1)}, f32[16,128]{1,0:T(8,128)S(1)}) custom-call(f32[64,8,128]{2,1,0:T(8,128)S(1)} %bitcast.37, bf16[128,8192]{1,0:T(8,128)(2,1)S(1)} %get-tuple-element.79.mask, f32[8,112,128]{2,1,0:T(8,128)S(1)} %get-tuple-element.80.pte, ...), custom_call_target="tpu_custom_call" | custom-call | flops 2000000 | bytes 100000 | tf_op jit(solution)/shard_map/correct/pallas_call | solution.py:287
  108.5 2.5 %collective-permute-done.13.h1 = f32[16,128]{1,0:T(8,128)S(1)} collective-permute-done((f32[16,128]{1,0:T(8,128)S(1)}, f32[16,128]{1,0:T(8,128)S(1)}, u32[]{:S(2)}, u32[]{:S(2)}) %collective-permute-start.13) | collective-permute-done | bytes 8224 | tf_op jit(solution)/shard_map/ppermute | solution.py:307
  111.6 2.7 %advance.4 = (f32[48,128]{1,0:T(8,128)S(1)}, f32[48,128]{1,0:T(8,128)S(1)}, f32[48,128]{1,0:T(8,128)S(1)}, f32[16,128]{1,0:T(8,128)S(1)}, f32[16,128]{1,0:T(8,12...) custom-call(f32[4]{0:T(128)S(1)} %copy-done.6, f32[48,128]{1,0:T(8,128)S(1)} %get-tuple-element.90.v.v1, ...), custom_call_target="tpu_custom_call" | custom-call | flops 2000000 | bytes 100000 | tf_op jit(solution)/shard_map/advance/pallas_call | solution.py:287
  114.3 3.4 %collective-permute-start.17 = (f32[16,128]{1,0:T(8,128)S(1)}, f32[16,128]{1,0:T(8,128)S(1)}, u32[]{:S(2)}, u32[]{:S(2)}) collective-permute-start(f32[16,128]{1,0:T(8,128)S(1)} %get-tuple-element.107), channel_id=1, source_target_pairs={{0,120},{8,16},{16,8},{24,32},{32,24},{40,48},{48,40},{56,64},{64,... | collective-permute-start | bytes 24584 | tf_op jit(solution)/shard_map/ppermute | solution.py:307
  124.3 15.8 %all_to_all.27 = f32[128,4,128]{2,1,0:T(4,128)S(1)} all-to-all(f32[128,4,128]{2,1,0:T(4,128)S(1)} %broadcast_in_dim.63), channel_id=1, replica_groups=mesh['gx'=16,'gy'=8] {'gx','gy'}, dimensions={0} | all-to-all | bytes 524288 | tf_op jit(solution)/shard_map/all_to_all | solution.py:317
  140.1 4.3 %correct.6 = (f32[48,128]{1,0:T(8,128)S(1)}, f32[16,128]{1,0:T(8,128)S(1)}, f32[16,128]{1,0:T(8,128)S(1)}, f32[16,128]{1,0:T(8,128)S(1)}, f32[16,128]{1,0:T(8,128)S(1)}) custom-call(f32[64,8,128]{2,1,0:T(8,128)S(1)} %bitcast.38, bf16[128,8192]{1,0:T(8,128)(2,1)S(1)} %get-tuple-element.79.mask, f32[8,112,128]{2,1,0:T(8,128)S(1)} %get-tuple-element.80.pte, ...), custom_call_target="tpu_custom_call" | custom-call | flops 2000000 | bytes 100000 | tf_op jit(solution)/shard_map/correct/pallas_call | solution.py:287
  148.1 2.5 %collective-permute-done.21.h1 = f32[16,128]{1,0:T(8,128)S(1)} collective-permute-done((f32[16,128]{1,0:T(8,128)S(1)}, f32[16,128]{1,0:T(8,128)S(1)}, u32[]{:S(2)}, u32[]{:S(2)}) %collective-permute-start.21) | collective-permute-done | bytes 8224 | tf_op jit(solution)/shard_map/ppermute | solution.py:307
  151.2 2.7 %advance.5 = (f32[48,128]{1,0:T(8,128)S(1)}, f32[48,128]{1,0:T(8,128)S(1)}, f32[48,128]{1,0:T(8,128)S(1)}, f32[16,128]{1,0:T(8,128)S(1)}, f32[16,128]{1,0:T(8,12...) custom-call(f32[4]{0:T(128)S(1)} %copy-done.6, f32[48,128]{1,0:T(8,128)S(1)} %get-tuple-element.104.v.v2, ...), custom_call_target="tpu_custom_call" | custom-call | flops 2000000 | bytes 100000 | tf_op jit(solution)/shard_map/advance/pallas_call | solution.py:287
  153.9 3.4 %collective-permute-start.25 = (f32[16,128]{1,0:T(8,128)S(1)}, f32[16,128]{1,0:T(8,128)S(1)}, u32[]{:S(2)}, u32[]{:S(2)}) collective-permute-start(f32[16,128]{1,0:T(8,128)S(1)} %get-tuple-element.121), channel_id=1, source_target_pairs={{0,120},{8,16},{16,8},{24,32},{32,24},{40,48},{48,40},{56,64},{64,... | collective-permute-start | bytes 24584 | tf_op jit(solution)/shard_map/ppermute | solution.py:307
  164.0 15.8 %all_to_all.28 = f32[128,4,128]{2,1,0:T(4,128)S(1)} all-to-all(f32[128,4,128]{2,1,0:T(4,128)S(1)} %broadcast_in_dim.64), channel_id=1, replica_groups=mesh['gx'=16,'gy'=8] {'gx','gy'}, dimensions={0} | all-to-all | bytes 524288 | tf_op jit(solution)/shard_map/all_to_all | solution.py:317
  179.7 4.3 %correct.7 = (f32[48,128]{1,0:T(8,128)S(1)}, f32[16,128]{1,0:T(8,128)S(1)}, f32[16,128]{1,0:T(8,128)S(1)}, f32[16,128]{1,0:T(8,128)S(1)}, f32[16,128]{1,0:T(8,128)S(1)}) custom-call(f32[64,8,128]{2,1,0:T(8,128)S(1)} %bitcast.36, bf16[128,8192]{1,0:T(8,128)(2,1)S(1)} %get-tuple-element.79.mask, f32[8,112,128]{2,1,0:T(8,128)S(1)} %get-tuple-element.80.pte, ...), custom_call_target="tpu_custom_call" | custom-call | flops 2000000 | bytes 100000 | tf_op jit(solution)/shard_map/correct/pallas_call | solution.py:287
  187.7 2.5 %collective-permute-done.29.h1 = f32[16,128]{1,0:T(8,128)S(1)} collective-permute-done((f32[16,128]{1,0:T(8,128)S(1)}, f32[16,128]{1,0:T(8,128)S(1)}, u32[]{:S(2)}, u32[]{:S(2)}) %collective-permute-start.29) | collective-permute-done | bytes 8224 | tf_op jit(solution)/shard_map/ppermute | solution.py:307
  193.3 15.3 %all_to_all.29 = f32[128,1,128]{2,1,0:T(1,128)S(1)} all-to-all(f32[128,1,128]{2,1,0:T(1,128)S(1)} %broadcast_in_dim.66), channel_id=1, replica_groups=mesh['gx'=16,'gy'=8] {'gx','gy'}, dimensions={0} | all-to-all | bytes 131072 | tf_op jit(solution)/shard_map/all_to_all | solution.py:317
  (108 shorter events, 51.8 us)
Async XLA Ops:
  7.3 19.5 %collective-permute-start = (f32[6,16,128]{2,1,0:T(8,128)S(1)}, f32[6,16,128]{2,1,0:T(8,128)S(1)}, u32[]{:S(2)}, u32[]{:S(2)}) collective-permute-start(f32[6,16,128]{2,1,0:T(8,128)S(1)} %get-tuple-element.70), channel_id=1, source_target_pairs={{0,8},{8,0},{16,24},{24,16},{32,40},{40,32},{48,56},{56,48},{64,72... | collective-permute-start | bytes 147464 | tf_op jit(solution)/shard_map/ppermute | solution.py:309
  9.8 17.0 %collective-permute-start.1 = (f32[6,16,128]{2,1,0:T(8,128)S(1)}, f32[6,16,128]{2,1,0:T(8,128)S(1)}, u32[]{:S(2)}, u32[]{:S(2)}) collective-permute-start(f32[6,16,128]{2,1,0:T(8,128)S(1)} %get-tuple-element.71), channel_id=1, source_target_pairs={{0,120},{8,16},{16,8},{24,32},{32,24},{40,48},{48,40},{56,64},{64,... | collective-permute-start | bytes 147464 | tf_op jit(solution)/shard_map/ppermute | solution.py:307
  14.2 12.6 %collective-permute-start.2 = (f32[6,16,128]{2,1,0:T(8,128)S(1)}, f32[6,16,128]{2,1,0:T(8,128)S(1)}, u32[]{:S(2)}, u32[]{:S(2)}) collective-permute-start(f32[6,16,128]{2,1,0:T(8,128)S(1)} %get-tuple-element.72), channel_id=1, source_target_pairs={{0,1},{1,0},{2,3},{3,2},{4,5},{5,4},{6,7},{7,6},{8,9},{9,8},{10,11... | collective-permute-start | bytes 147464 | tf_op jit(solution)/shard_map/ppermute | solution.py:310
  15.4 11.4 %collective-permute-start.3 = (f32[6,16,128]{2,1,0:T(8,128)S(1)}, f32[6,16,128]{2,1,0:T(8,128)S(1)}, u32[]{:S(2)}, u32[]{:S(2)}) collective-permute-start(f32[6,16,128]{2,1,0:T(8,128)S(1)} %get-tuple-element.73), channel_id=1, source_target_pairs={{0,7},{1,2},{2,1},{3,4},{4,3},{5,6},{6,5},{7,0},{8,15},{9,10},{10,... | collective-permute-start | bytes 147464 | tf_op jit(solution)/shard_map/ppermute | solution.py:308
  65.9 5.8 %collective-permute-start.5 = (f32[16,128]{1,0:T(8,128)S(1)}, f32[16,128]{1,0:T(8,128)S(1)}, u32[]{:S(2)}, u32[]{:S(2)}) collective-permute-start(f32[16,128]{1,0:T(8,128)S(1)} %get-tuple-element.87), channel_id=1, source_target_pairs={{0,120},{8,16},{16,8},{24,32},{32,24},{40,48},{48,40},{56,64},{64,... | collective-permute-start | bytes 24584 | tf_op jit(solution)/shard_map/ppermute | solution.py:307
  67.0 4.7 %collective-permute-start.6 = (f32[16,128]{1,0:T(8,128)S(1)}, f32[16,128]{1,0:T(8,128)S(1)}, u32[]{:S(2)}, u32[]{:S(2)}) collective-permute-start(f32[16,128]{1,0:T(8,128)S(1)} %get-tuple-element.88), channel_id=1, source_target_pairs={{0,1},{1,0},{2,3},{3,2},{4,5},{5,4},{6,7},{7,6},{8,9},{9,8},{10,11... | collective-permute-start | bytes 24584 | tf_op jit(solution)/shard_map/ppermute | solution.py:310
  67.9 3.8 %collective-permute-start.7 = (f32[16,128]{1,0:T(8,128)S(1)}, f32[16,128]{1,0:T(8,128)S(1)}, u32[]{:S(2)}, u32[]{:S(2)}) collective-permute-start(f32[16,128]{1,0:T(8,128)S(1)} %get-tuple-element.89), channel_id=1, source_target_pairs={{0,7},{1,2},{2,1},{3,4},{4,3},{5,6},{6,5},{7,0},{8,15},{9,10},{10,... | collective-permute-start | bytes 24584 | tf_op jit(solution)/shard_map/ppermute | solution.py:308
  74.5 5.5 %collective-permute-start.8 = (f32[16,128]{1,0:T(8,128)S(1)}, f32[16,128]{1,0:T(8,128)S(1)}, u32[]{:S(2)}, u32[]{:S(2)}) collective-permute-start(f32[16,128]{1,0:T(8,128)S(1)} %get-tuple-element.92), channel_id=1, source_target_pairs={{0,8},{8,0},{16,24},{24,16},{32,40},{40,32},{48,56},{56,48},{64,72... | collective-permute-start | bytes 24584 | tf_op jit(solution)/shard_map/ppermute | solution.py:309
  74.6 5.8 %collective-permute-start.9 = (f32[16,128]{1,0:T(8,128)S(1)}, f32[16,128]{1,0:T(8,128)S(1)}, u32[]{:S(2)}, u32[]{:S(2)}) collective-permute-start(f32[16,128]{1,0:T(8,128)S(1)} %get-tuple-element.93), channel_id=1, source_target_pairs={{0,120},{8,16},{16,8},{24,32},{32,24},{40,48},{48,40},{56,64},{64,... | collective-permute-start | bytes 24584 | tf_op jit(solution)/shard_map/ppermute | solution.py:307
  79.9 3.4 %collective-permute-start.11 = (f32[16,128]{1,0:T(8,128)S(1)}, f32[16,128]{1,0:T(8,128)S(1)}, u32[]{:S(2)}, u32[]{:S(2)}) collective-permute-start(f32[16,128]{1,0:T(8,128)S(1)} %get-tuple-element.95), channel_id=1, source_target_pairs={{0,7},{1,2},{2,1},{3,4},{4,3},{5,6},{6,5},{7,0},{8,15},{9,10},{10,... | collective-permute-start | bytes 24584 | tf_op jit(solution)/shard_map/ppermute | solution.py:308
  104.8 3.7 %collective-permute-start.12 = (f32[16,128]{1,0:T(8,128)S(1)}, f32[16,128]{1,0:T(8,128)S(1)}, u32[]{:S(2)}, u32[]{:S(2)}) collective-permute-start(f32[16,128]{1,0:T(8,128)S(1)} %get-tuple-element.100), channel_id=1, source_target_pairs={{0,8},{8,0},{16,24},{24,16},{32,40},{40,32},{48,56},{56,48},{64,72... | collective-permute-start | bytes 24584 | tf_op jit(solution)/shard_map/ppermute | solution.py:309
  105.1 5.8 %collective-permute-start.13 = (f32[16,128]{1,0:T(8,128)S(1)}, f32[16,128]{1,0:T(8,128)S(1)}, u32[]{:S(2)}, u32[]{:S(2)}) collective-permute-start(f32[16,128]{1,0:T(8,128)S(1)} %get-tuple-element.101), channel_id=1, source_target_pairs={{0,120},{8,16},{16,8},{24,32},{32,24},{40,48},{48,40},{56,64},{64,... | collective-permute-start | bytes 24584 | tf_op jit(solution)/shard_map/ppermute | solution.py:307
  107.3 3.7 %collective-permute-start.14 = (f32[16,128]{1,0:T(8,128)S(1)}, f32[16,128]{1,0:T(8,128)S(1)}, u32[]{:S(2)}, u32[]{:S(2)}) collective-permute-start(f32[16,128]{1,0:T(8,128)S(1)} %get-tuple-element.102), channel_id=1, source_target_pairs={{0,1},{1,0},{2,3},{3,2},{4,5},{5,4},{6,7},{7,6},{8,9},{9,8},{10,11... | collective-permute-start | bytes 24584 | tf_op jit(solution)/shard_map/ppermute | solution.py:310
  114.3 4.7 %collective-permute-start.16 = (f32[16,128]{1,0:T(8,128)S(1)}, f32[16,128]{1,0:T(8,128)S(1)}, u32[]{:S(2)}, u32[]{:S(2)}) collective-permute-start(f32[16,128]{1,0:T(8,128)S(1)} %get-tuple-element.106), channel_id=1, source_target_pairs={{0,8},{8,0},{16,24},{24,16},{32,40},{40,32},{48,56},{56,48},{64,72... | collective-permute-start | bytes 24584 | tf_op jit(solution)/shard_map/ppermute | solution.py:309
  114.3 5.9 %collective-permute-start.17 = (f32[16,128]{1,0:T(8,128)S(1)}, f32[16,128]{1,0:T(8,128)S(1)}, u32[]{:S(2)}, u32[]{:S(2)}) collective-permute-start(f32[16,128]{1,0:T(8,128)S(1)} %get-tuple-element.107), channel_id=1, source_target_pairs={{0,120},{8,16},{16,8},{24,32},{32,24},{40,48},{48,40},{56,64},{64,... | collective-permute-start | bytes 24584 | tf_op jit(solution)/shard_map/ppermute | solution.py:307
  144.4 3.7 %collective-permute-start.20 = (f32[16,128]{1,0:T(8,128)S(1)}, f32[16,128]{1,0:T(8,128)S(1)}, u32[]{:S(2)}, u32[]{:S(2)}) collective-permute-start(f32[16,128]{1,0:T(8,128)S(1)} %get-tuple-element.114), channel_id=1, source_target_pairs={{0,8},{8,0},{16,24},{24,16},{32,40},{40,32},{48,56},{56,48},{64,72... | collective-permute-start | bytes 24584 | tf_op jit(solution)/shard_map/ppermute | solution.py:309
  144.7 5.8 %collective-permute-start.21 = (f32[16,128]{1,0:T(8,128)S(1)}, f32[16,128]{1,0:T(8,128)S(1)}, u32[]{:S(2)}, u32[]{:S(2)}) collective-permute-start(f32[16,128]{1,0:T(8,128)S(1)} %get-tuple-element.115), channel_id=1, source_target_pairs={{0,120},{8,16},{16,8},{24,32},{32,24},{40,48},{48,40},{56,64},{64,... | collective-permute-start | bytes 24584 | tf_op jit(solution)/shard_map/ppermute | solution.py:307
  146.9 3.7 %collective-permute-start.22 = (f32[16,128]{1,0:T(8,128)S(1)}, f32[16,128]{1,0:T(8,128)S(1)}, u32[]{:S(2)}, u32[]{:S(2)}) collective-permute-start(f32[16,128]{1,0:T(8,128)S(1)} %get-tuple-element.116), channel_id=1, source_target_pairs={{0,1},{1,0},{2,3},{3,2},{4,5},{5,4},{6,7},{7,6},{8,9},{9,8},{10,11... | collective-permute-start | bytes 24584 | tf_op jit(solution)/shard_map/ppermute | solution.py:310
  147.8 3.4 %collective-permute-start.23 = (f32[16,128]{1,0:T(8,128)S(1)}, f32[16,128]{1,0:T(8,128)S(1)}, u32[]{:S(2)}, u32[]{:S(2)}) collective-permute-start(f32[16,128]{1,0:T(8,128)S(1)} %get-tuple-element.117), channel_id=1, source_target_pairs={{0,7},{1,2},{2,1},{3,4},{4,3},{5,6},{6,5},{7,0},{8,15},{9,10},{10,... | collective-permute-start | bytes 24584 | tf_op jit(solution)/shard_map/ppermute | solution.py:308
  153.9 4.7 %collective-permute-start.24 = (f32[16,128]{1,0:T(8,128)S(1)}, f32[16,128]{1,0:T(8,128)S(1)}, u32[]{:S(2)}, u32[]{:S(2)}) collective-permute-start(f32[16,128]{1,0:T(8,128)S(1)} %get-tuple-element.120), channel_id=1, source_target_pairs={{0,8},{8,0},{16,24},{24,16},{32,40},{40,32},{48,56},{56,48},{64,72... | collective-permute-start | bytes 24584 | tf_op jit(solution)/shard_map/ppermute | solution.py:309
  153.9 5.9 %collective-permute-start.25 = (f32[16,128]{1,0:T(8,128)S(1)}, f32[16,128]{1,0:T(8,128)S(1)}, u32[]{:S(2)}, u32[]{:S(2)}) collective-permute-start(f32[16,128]{1,0:T(8,128)S(1)} %get-tuple-element.121), channel_id=1, source_target_pairs={{0,120},{8,16},{16,8},{24,32},{32,24},{40,48},{48,40},{56,64},{64,... | collective-permute-start | bytes 24584 | tf_op jit(solution)/shard_map/ppermute | solution.py:307
  184.0 3.7 %collective-permute-start.28 = (f32[16,128]{1,0:T(8,128)S(1)}, f32[16,128]{1,0:T(8,128)S(1)}, u32[]{:S(2)}, u32[]{:S(2)}) collective-permute-start(f32[16,128]{1,0:T(8,128)S(1)} %get-tuple-element.128), channel_id=1, source_target_pairs={{0,8},{8,0},{16,24},{24,16},{32,40},{40,32},{48,56},{56,48},{64,72... | collective-permute-start | bytes 24584 | tf_op jit(solution)/shard_map/ppermute | solution.py:309
  184.3 5.8 %collective-permute-start.29 = (f32[16,128]{1,0:T(8,128)S(1)}, f32[16,128]{1,0:T(8,128)S(1)}, u32[]{:S(2)}, u32[]{:S(2)}) collective-permute-start(f32[16,128]{1,0:T(8,128)S(1)} %get-tuple-element.129), channel_id=1, source_target_pairs={{0,120},{8,16},{16,8},{24,32},{32,24},{40,48},{48,40},{56,64},{64,... | collective-permute-start | bytes 24584 | tf_op jit(solution)/shard_map/ppermute | solution.py:307
  186.5 3.7 %collective-permute-start.30 = (f32[16,128]{1,0:T(8,128)S(1)}, f32[16,128]{1,0:T(8,128)S(1)}, u32[]{:S(2)}, u32[]{:S(2)}) collective-permute-start(f32[16,128]{1,0:T(8,128)S(1)} %get-tuple-element.130), channel_id=1, source_target_pairs={{0,1},{1,0},{2,3},{3,2},{4,5},{5,4},{6,7},{7,6},{8,9},{9,8},{10,11... | collective-permute-start | bytes 24584 | tf_op jit(solution)/shard_map/ppermute | solution.py:310
  (17 other events, 111.7 us)

commit v2 on v1

--- a/solution.py
+++ b/solution.py
@@ -20,8 +20,7 @@
 PAIRS = [(j, l) for j in range(5) for l in range(j, 5)]
 
 VM = pl.BlockSpec(memory_space=pltpu.VMEM)
-SM = pl.BlockSpec(memory_space=pltpu.SMEM)
-ANY = pl.BlockSpec(memory_space=pl.ANY)
+HBM = pl.BlockSpec(memory_space=pltpu.HBM)
 LAST = (((1,), (1,)), ((), ()))
 
 
@@ -52,7 +51,7 @@
     out = []
     for g in range(ROWS // 8):
         lhs = jnp.concatenate([top[8 * g : 8 * g + 8], bottom[8 * g : 8 * g + 8]], axis=0).astype(BF16)
-        r = lax.dot_general(lhs, w_ref[512 * g : 512 * g + 512, :], LAST, preferred_element_type=F32)
+        r = jnp.dot(lhs, w_ref[:, 512 * g : 512 * g + 512], preferred_element_type=F32)
         s = r[:8] + r[8:]
         own = lax.broadcasted_iota(jnp.int32, s.shape, 0) == lax.broadcasted_iota(jnp.int32, s.shape, 1) // BS
         s = jnp.where(own, s, 0.0)
@@ -94,12 +93,18 @@
         out[...] = picked[HALO * s : HALO * s + HALO]
 
 
+def pair_rows(x):
+    t = twice(x).T
+    high = t.astype(BF16).astype(F32)
+    return jnp.where(lax.broadcasted_iota(jnp.int32, t.shape, 0) < BS, high, t - high).astype(BF16)
+
+
 def first_kernel(start, jac, pt, ids, listed, v, wj, ptd, pick, z, ze, s0, s1, s2, s3):
     v[...] = twice(start[...])
-    for g in range(ROWS // 8):
-        wj[512 * g : 512 * g + 512, :] = pack(twice(jac[512 * g : 512 * g + 512, :] * jacobi_weight)).astype(BF16)
+    for n in range(ROWS // 2):
+        wj[:, 128 * n : 128 * n + 128] = pair_rows(jac[128 * n : 128 * n + 128, :] * jacobi_weight)
     for c in range(CW):
-        ptd[c] = twice(pt[c])
+        ptd[c] = twice(pt[:, c, :])
     chosen = (listed[...] == lax.broadcasted_iota(jnp.int32, (4 * HALO, ROWS), 1)).astype(F32)
     pick[...] = chosen.astype(BF16)
     z[...] = smooth(v[...], wj)
@@ -135,20 +140,25 @@
             c.wait()
         slot = g % 2
 
-        def row(i, carry):
-            at = pl.ds(pl.multiple_of((8 * g + i) * BS, BS), BS)
+        for n in range(4):
+            at = slice(128 * (4 * g + n), 128 * (4 * g + n) + 128)
+            i, j = 2 * n, 2 * n + 1
             for p in range(3):
-                x = jnp.concatenate([buf[slot, i, 2 * p], buf[slot, i, 2 * p + 1]], axis=1)
+                x = jnp.concatenate(
+                    [
+                        jnp.concatenate([buf[slot, i, 2 * p], buf[slot, i, 2 * p + 1]], axis=1),
+                        jnp.concatenate([buf[slot, j, 2 * p], buf[slot, j, 2 * p + 1]], axis=1),
+                    ],
+                    axis=0,
+                ).T
                 high = x.astype(BF16)
-                w[at, 128 * p : 128 * p + 128] = high
-                w[at, 384 + 128 * p : 512 + 128 * p] = (x - high.astype(F32)).astype(BF16)
-            w[at, 768:896] = pack(twice(dbuf[slot, i])).astype(BF16)
-            return carry
-
-        lax.fori_loop(0, 8, row, 0)
-
-
-def restrict_kernel(v, ze, h0, h1, h2, h3, w_op, gather, ptd, w, p):
+                w[128 * p : 128 * p + 128, at] = high
+                w[384 + 128 * p : 512 + 128 * p, at] = (x - high.astype(F32)).astype(BF16)
+            w[768:896, at] = pair_rows(jnp.concatenate([dbuf[slot, i], dbuf[slot, j]], axis=0))
+
+
+def restrict_kernel(v, ze, h0, h1, h2, h3, w_op, gather, ptd, *rest):
+    *extra, w, p = rest
     ext = jnp.concatenate([ze[...], h0[...], h1[...], h2[...], h3[...]], axis=0)
     r = v[...] - operate(ext, w_op, gather)
     w[...] = r
@@ -156,26 +166,31 @@
     pad = jnp.zeros((16, 128), F32)
     for k in range(4):
         x = jnp.concatenate([pack(ptd[k] * r), pad, pack(ptd[k + 4] * r), pad], axis=0).astype(BF16)
-        p[k : k + 1, :] = lax.dot_general(ones, x, LAST, preferred_element_type=F32)[0:1]
+        line = lax.dot_general(ones, x, LAST, preferred_element_type=F32)[0:1]
+        p[k : k + 1, :] = line + extra[0][k : k + 1, :] if extra else line
+    if extra:
+        p[4:16, :] = extra[0][4:16, :]
 
 
 def coarse_kernel(x0, ids, ptd, g0, g1, g2, g3, mask, pte, xp):
     idc = jnp.concatenate(
         [ids[...], g0[5], g1[5], g2[5], g3[5], jnp.full((128 - EXT, 128), -1.0, F32)], axis=0
     )
-    low = low_lanes(idc)
-    low8 = lax.broadcasted_iota(jnp.int32, (1, 128), 1) < BS
+    wanted = idc.T[0:1]
+    given = [x0[:, r, :].T[ROWS:BS] for r in range(3)] + [jnp.full((BS - ROWS, 128), -1.0, F32)]
+    given = jnp.concatenate(given + given, axis=0)
+    upper_rows = lax.broadcasted_iota(jnp.int32, (128, 1), 0) < BS
     for q in range(64):
-        line = jnp.where(low8, x0[2 * q, 4:5, :], x0[2 * q + 1, 4:5, :])
-        mask[:, 128 * q : 128 * q + 128] = (idc == line).astype(F32).astype(BF16)
+        line = jnp.where(upper_rows, given[:, 2 * q : 2 * q + 1], given[:, 2 * q + 1 : 2 * q + 2])
+        mask[128 * q : 128 * q + 128, :] = (line == wanted).astype(F32).astype(BF16)
         xp[q] = jnp.concatenate([x0[2 * q, 0:4, :], x0[2 * q + 1, 0:4, :]], axis=0)
     device = jnp.floor((idc + 0.5) * (1.0 / 24.0))
     slot = idc - 24.0 * device
     upper = slot >= 11.5
-    place = device * 16.0 + jnp.where(upper, slot - 12.0, slot)
+    place = device * 16.0 + 4.0 + jnp.where(upper, slot - 12.0, slot)
     total = jnp.zeros((128, 128), F32)
     for b in range(8):
-        src = x0[16 * b : 16 * b + 16, 8:24, :].reshape(256, 128)
+        src = x0[16 * b : 16 * b + 16].reshape(256, 128)
         high = src.astype(BF16)
         mid = (src - high.astype(F32)).astype(BF16)
         rest = (src - high.astype(F32) - mid.astype(F32)).astype(BF16)
@@ -208,8 +223,8 @@
         t = jnp.where(keep, t, pltpu.roll(swap(t), 4, 0))
         high = t.astype(BF16).astype(F32)
         parts[:, 128 * q : 128 * q + 128] = jnp.concatenate([high, t - high], axis=0).astype(BF16)
-    got = lax.dot_general(mask[...], parts[...], LAST, preferred_element_type=F32)
-    coarse = got[:EXT, 0:8] + got[:EXT, 8:16]
+    got = jnp.dot(parts[...], mask[...], preferred_element_type=F32)
+    coarse = jnp.concatenate([got[0:8] + got[8:16], jnp.zeros((120, 128), F32)], axis=0).T[:EXT]
     u = pte[0] * coarse[:, 0:1]
     for d in range(1, CW):
         u = u + pte[d] * coarse[:, d : d + 1]
@@ -221,7 +236,7 @@
 
 def advance(k, shifts, v, ye, h0, h1, h2, h3, w_op, gather):
     ext = jnp.concatenate([ye[...], h0[...], h1[...], h2[...], h3[...]], axis=0)
-    return operate(ext, w_op, gather) - shifts[k] * v[...]
+    return operate(ext, w_op, gather) - shifts[k : k + 1, :] * v[...]
 
 
 def advance_kernel(k, shifts, v, ye, h0, h1, h2, h3, w_op, gather, wj, pick, vn, z, ze, s0, s1, s2, s3):
@@ -329,24 +344,18 @@
     cols = jnp.where(beyond >= 0, ROWS + (beyond ^ turn), cols)
     ids = (owner[:, 0] * coarse_inv.shape[0] + agg_slot).astype(F32)
     id_col = jnp.broadcast_to(ids[:, None], (ROWS, 128))
-    id_pad = jnp.concatenate([ids, jnp.full((BS - ROWS,), -1.0, F32)])
     inv = coarse_inv.reshape(24, BS)
-    extra = jnp.concatenate(
-        [
-            jnp.concatenate([id_pad, id_pad])[None],
-            jnp.zeros((3, 128), F32),
-            jnp.concatenate([inv[:12], inv[12:]], axis=1),
-            jnp.zeros((4, 128), F32),
-        ]
-    )
-    pt = jnp.transpose(prolong, (2, 0, 1))
+    spare = jnp.pad(ids.reshape(3, BS - ROWS), ((0, 1), (ROWS, BS)))
+    extra = jnp.concatenate([spare, jnp.concatenate([inv[:12], inv[12:]], axis=1)])
+    slopes = jnp.broadcast_to(shifts[:, None], (4, 128))
+    pt = jnp.transpose(prolong, (0, 2, 1))
 
     halo = [shape(HALO, 128)] * 4
     v, wj, ptd, pick, z, ze, *sends = call(
         first_kernel,
         [
             shape(ROWS, 128),
-            kept(ROWS * BS, 128, dtype=BF16),
+            kept(128, ROWS * BS, dtype=BF16),
             shape(CW, ROWS, 128),
             shape(4 * HALO, ROWS, dtype=BF16),
             shape(ROWS, 128),
@@ -363,11 +372,11 @@
     got = exchange(sends)
     w_op, gather = call(
         operator_kernel,
-        [kept(ROWS * BS, WIDTH, dtype=BF16), shape(3 * ROWS, 256, dtype=BF16)],
-        off_blocks,
-        diag_blocks,
+        [kept(WIDTH, ROWS * BS, dtype=BF16), shape(3 * ROWS, 256, dtype=BF16)],
+        pltpu.with_memory_space_constraint(off_blocks, pltpu.HBM),
+        pltpu.with_memory_space_constraint(diag_blocks, pltpu.HBM),
         cols,
-        specs=[ANY, ANY, VM],
+        specs=[HBM, HBM, VM],
         scratch=[
             pltpu.VMEM((2, 8, KOFF, BS, BS), F32),
             pltpu.VMEM((2, 8, BS, BS), F32),
@@ -382,21 +391,29 @@
     mask = pte = None
     for k in range(4):
         w, p = call(
-            restrict_kernel, [shape(ROWS, 128), shape(4, 128)], v, ze, *around, w_op, gather, ptd, name="restrict"
+            restrict_kernel,
+            [shape(ROWS, 128), shape(4 if k else 16, 128)],
+            v,
+            ze,
+            *around,
+            w_op,
+            gather,
+            ptd,
+            *([] if k else [extra]),
+            name="restrict",
         )
+        x = everywhere(p)
         if k == 0:
-            both = everywhere(jnp.concatenate([p, extra]))
             mask, pte, x = call(
                 coarse_kernel,
-                [kept(128, 64 * 128, dtype=BF16), shape(CW, EXT, 128), shape(64, 8, 128)],
-                both,
+                [kept(64 * 128, 128, dtype=BF16), shape(CW, EXT, 128), shape(64, 8, 128)],
+                x,
                 id_col,
                 ptd,
                 *got,
                 name="coarse",
             )
-        else:
-            x = everywhere(p).reshape(64, 8, 128)
+        x = x.reshape(64, 8, 128)
         ye, *sends = call(
             correct_kernel,
             [shape(ROWS, 128)] + halo,
@@ -417,7 +434,7 @@
             v, z, ze, *sends = call(
                 functools.partial(advance_kernel, k),
                 [shape(ROWS, 128)] * 3 + halo,
-                shifts,
+                slopes,
                 v,
                 ye,
                 *around,
@@ -425,7 +442,6 @@
                 gather,
                 wj,
                 pick,
-                specs=[SM] + [VM] * 10,
                 name="advance",
             )
             basis.append(v)
@@ -433,13 +449,12 @@
     v, gram = call(
         last_kernel,
         [shape(ROWS, 128), shape(1, 128)],
-        shifts,
+        slopes,
         ye,
         *around,
         w_op,
         gather,
         *basis,
-        specs=[SM] + [VM] * 11,
         name="last",
     )
     basis.append(v)

time: 210 us -> 191 us (0.910)
  Pallas kernels: 45.9 us -> 32.7 us
  blocking collectives: 91.8 us -> 87.7 us
  local copies, waits for them, and re-layouts: 8.89 us -> 6.4 us
    pallas_call x16, Pallas kernels: 45.9 us -> 32.7 us  [call(): pl.pallas_call(kernel, out_shape=outs, in_specs=specs or [VM] * len(args)...]
    all_to_all x5, blocking collectives: 91.8 us -> 87.7 us  [everywhere(): lax.all_to_all(y, ('gx', 'gy'), split_axis=0, concat_axis=0, tiled=True)]
    unnamed x20 -> x9, local copies, waits for them, and re-layouts: 7.22 us -> 3.85 us
    ppermute x8, starting transfers between devices: 4.08 us -> 1.62 us  [exchange(): a = lax.ppermute(sends[0], 'gx', swap_pairs(nx, 0))]
  transfers between devices with their start and end apart: 32 -> 32, of which waited for: 14 -> 13; matrix products, arithmetic and copies ran while one was open for 0% -> 1% of each run, Pallas kernels for 3% -> 4%
where the time goes in v2:
time: 191 us
  blocking collectives  87.7 us (46%)
  starting transfers between devices  38.9 us (20%)
  Pallas kernels  32.7 us (17%)
  waiting for transfers between devices  22.4 us (12%)
  local copies, waits for them, and re-layouts  6.4 us (3%)
    all_to_all x5, blocking collectives, everywhere(): lax.all_to_all(y, ('gx', 'gy'), split_axis=0, concat_axis=0, tiled=True)  87.7 us
    pallas_call x16, Pallas kernels, call(): pl.pallas_call(kernel, out_shape=outs, in_specs=specs or [VM] * len(args)...  32.7 us
    ppermute x8, starting transfers between devices, exchange(): b = lax.ppermute(sends[1], 'gx', swap_pairs(nx, 1))  23.1 us
    ppermute x8, waiting for transfers between devices, exchange(): b = lax.ppermute(sends[1], 'gx', swap_pairs(nx, 1))  15.3 us
    ppermute x8, starting transfers between devices, exchange(): c = lax.ppermute(sends[2], 'gy', swap_pairs(ny, 0))  9.67 us
    ppermute x8, waiting for transfers between devices, exchange(): d = lax.ppermute(sends[3], 'gy', swap_pairs(ny, 1))  7.15 us
    ppermute x8, starting transfers between devices, exchange(): d = lax.ppermute(sends[3], 'gy', swap_pairs(ny, 1))  4.58 us
    unnamed x9, local copies, waits for them, and re-layouts  3.85 us
  transfers between devices with their start and end apart: 32, of which 13 were waited for; matrix products, arithmetic and copies ran while one was open for 1% of the time, Pallas kernels for 4%

profile of v2, /device:TPU:1, one launch (start us, length us, event | category | flops | bytes accessed | tf_op | source)
XLA Modules:
  0.0 190.5 jit_solution(719716735503638843)
XLA Ops:
  7.5 2.8 %collective-permute-start.3 = (f32[6,16,128]{2,1,0:T(8,128)S(1)}, f32[6,16,128]{2,1,0:T(8,128)S(1)}, u32[]{:S(2)}, u32[]{:S(2)}) collective-permute-start(f32[6,16,128]{2,1,0:T(8,128)S(1)} %get-tuple-element.73), channel_id=1, source_target_pairs={{0,7},{1,2},{2,1},{3,4},{4,3},{5,6},{6,5},{7,0},{8,15},{9,10},{10,... | collective-permute-start | bytes 147464 | tf_op jit(solution)/shard_map/ppermute | solution.py:323
  11.6 6.0 %collective-permute-start.1 = (f32[6,16,128]{2,1,0:T(8,128)S(1)}, f32[6,16,128]{2,1,0:T(8,128)S(1)}, u32[]{:S(2)}, u32[]{:S(2)}) collective-permute-start(f32[6,16,128]{2,1,0:T(8,128)S(1)} %get-tuple-element.71), channel_id=1, source_target_pairs={{0,120},{8,16},{16,8},{24,32},{32,24},{40,48},{48,40},{56,64},{64,... | collective-permute-start | bytes 147464 | tf_op jit(solution)/shard_map/ppermute | solution.py:322
  19.5 6.9 %operator.1 = (bf16[896,3072]{1,0:T(8,128)(2,1)S(1)}, bf16[144,256]{1,0:T(8,128)(2,1)S(1)}) custom-call(f32[48,6,64,64]{3,2,1,0:T(8,128)} %off.1, f32[48,64,64]{2,1,0:T(8,128)} %diag.1, s32[48,6]{1,0:T(8,128)S(1)} %add_select_fusion.cols), custom_call_target="tpu_custom_call" | custom-call | flops 2000000000 | bytes 100000 | tf_op jit(solution)/shard_map/operator/pallas_call | solution.py:302
  28.0 23.9 %all_to_all.25.x0 = f32[128,16,128]{2,1,0:T(8,128)S(1)} all-to-all(f32[128,16,128]{2,1,0:T(8,128)S(1)} %broadcast_in_dim.28), channel_id=1, replica_groups=mesh['gx'=16,'gy'=8] {'gx','gy'}, dimensions={0} | all-to-all | bytes 2097152 | tf_op jit(solution)/shard_map/all_to_all | solution.py:332
  51.8 2.8 %coarse.1 = (bf16[8192,128]{1,0:T(8,128)(2,1)S(1)}, f32[8,112,128]{2,1,0:T(8,128)S(1)}, f32[64,8,128]{2,1,0:T(8,128)S(1)}) custom-call(f32[128,16,128]{2,1,0:T(8,128)S(1)} %all_to_all.25.x0, f32[48,128]{1,0:T(8,128)S(1)} %broadcast_in_dim.25.ids, f32[8,48,128]{2,1,0:T(8,128)S(1)} %get-tuple-element.76.ptd, f32[6,16,128]{2,1,0:T(8,128)S(1)} %collective-permute-done.g0, ...), custom_call_target="tpu_custom_call" | custom-call | flops 2000000 | bytes 100000 | tf_op jit(solution)/shard_map/coarse/pallas_call | solution.py:302
  54.7 2.3 %correct.4 = (f32[48,128]{1,0:T(8,128)S(1)}, f32[16,128]{1,0:T(8,128)S(1)}, f32[16,128]{1,0:T(8,128)S(1)}, f32[16,128]{1,0:T(8,128)S(1)}, f32[16,128]{1,0:T(8,128)S(1)}) custom-call(f32[64,8,128]{2,1,0:T(8,128)S(1)} %get-tuple-element.78.x, bf16[8192,128]{1,0:T(8,128)(2,1)S(1)} %get-tuple-element.79.mask, f32[8,112,128]{2,1,0:T(8,128)S(1)} %get-tuple-element.80.pte, ...), custom_call_target="tpu_custom_call" | custom-call | flops 2000000 | bytes 100000 | tf_op jit(solution)/shard_map/correct/pallas_call | solution.py:302
  60.5 2.9 %collective-permute-done.5.h1 = f32[16,128]{1,0:T(8,128)S(1)} collective-permute-done((f32[16,128]{1,0:T(8,128)S(1)}, f32[16,128]{1,0:T(8,128)S(1)}, u32[]{:S(2)}, u32[]{:S(2)}) %collective-permute-start.5) | collective-permute-done | bytes 8224 | tf_op jit(solution)/shard_map/ppermute | solution.py:322
  65.0 2.7 %collective-permute-start.10 = (f32[16,128]{1,0:T(8,128)S(1)}, f32[16,128]{1,0:T(8,128)S(1)}, u32[]{:S(2)}, u32[]{:S(2)}) collective-permute-start(f32[16,128]{1,0:T(8,128)S(1)} %get-tuple-element.94), channel_id=1, source_target_pairs={{0,1},{1,0},{2,3},{3,2},{4,5},{5,4},{6,7},{7,6},{8,9},{9,8},{10,11... | collective-permute-start | bytes 24584 | tf_op jit(solution)/shard_map/ppermute | solution.py:325
  67.7 2.4 %collective-permute-start.9 = (f32[16,128]{1,0:T(8,128)S(1)}, f32[16,128]{1,0:T(8,128)S(1)}, u32[]{:S(2)}, u32[]{:S(2)}) collective-permute-start(f32[16,128]{1,0:T(8,128)S(1)} %get-tuple-element.93), channel_id=1, source_target_pairs={{0,120},{8,16},{16,8},{24,32},{32,24},{40,48},{48,40},{56,64},{64,... | collective-permute-start | bytes 24584 | tf_op jit(solution)/shard_map/ppermute | solution.py:322
  71.0 2.5 %collective-permute-done.9.h1 = f32[16,128]{1,0:T(8,128)S(1)} collective-permute-done((f32[16,128]{1,0:T(8,128)S(1)}, f32[16,128]{1,0:T(8,128)S(1)}, u32[]{:S(2)}, u32[]{:S(2)}) %collective-permute-start.9) | collective-permute-done | bytes 8224 | tf_op jit(solution)/shard_map/ppermute | solution.py:322
  74.9 16.9 %all_to_all.26 = f32[128,4,128]{2,1,0:T(4,128)S(1)} all-to-all(f32[128,4,128]{2,1,0:T(4,128)S(1)} %broadcast_in_dim.29), channel_id=1, replica_groups=mesh['gx'=16,'gy'=8] {'gx','gy'}, dimensions={0} | all-to-all | bytes 524288 | tf_op jit(solution)/shard_map/all_to_all | solution.py:332
  91.8 2.3 %correct.5 = (f32[48,128]{1,0:T(8,128)S(1)}, f32[16,128]{1,0:T(8,128)S(1)}, f32[16,128]{1,0:T(8,128)S(1)}, f32[16,128]{1,0:T(8,128)S(1)}, f32[16,128]{1,0:T(8,128)S(1)}) custom-call(f32[64,8,128]{2,1,0:T(8,128)S(1)} %bitcast.33, bf16[8192,128]{1,0:T(8,128)(2,1)S(1)} %get-tuple-element.79.mask, f32[8,112,128]{2,1,0:T(8,128)S(1)} %get-tuple-element.80.pte, ...), custom_call_target="tpu_custom_call" | custom-call | flops 2000000 | bytes 100000 | tf_op jit(solution)/shard_map/correct/pallas_call | solution.py:302
  94.5 2.2 %collective-permute-start.13 = (f32[16,128]{1,0:T(8,128)S(1)}, f32[16,128]{1,0:T(8,128)S(1)}, u32[]{:S(2)}, u32[]{:S(2)}) collective-permute-start(f32[16,128]{1,0:T(8,128)S(1)} %get-tuple-element.101), channel_id=1, source_target_pairs={{0,120},{8,16},{16,8},{24,32},{32,24},{40,48},{48,40},{56,64},{64,... | collective-permute-start | bytes 24584 | tf_op jit(solution)/shard_map/ppermute | solution.py:322
  97.8 2.5 %collective-permute-done.13.h1 = f32[16,128]{1,0:T(8,128)S(1)} collective-permute-done((f32[16,128]{1,0:T(8,128)S(1)}, f32[16,128]{1,0:T(8,128)S(1)}, u32[]{:S(2)}, u32[]{:S(2)}) %collective-permute-start.13) | collective-permute-done | bytes 8224 | tf_op jit(solution)/shard_map/ppermute | solution.py:322
  102.5 3.4 %collective-permute-start.17 = (f32[16,128]{1,0:T(8,128)S(1)}, f32[16,128]{1,0:T(8,128)S(1)}, u32[]{:S(2)}, u32[]{:S(2)}) collective-permute-start(f32[16,128]{1,0:T(8,128)S(1)} %get-tuple-element.107), channel_id=1, source_target_pairs={{0,120},{8,16},{16,8},{24,32},{32,24},{40,48},{48,40},{56,64},{64,... | collective-permute-start | bytes 24584 | tf_op jit(solution)/shard_map/ppermute | solution.py:322
  111.8 15.8 %all_to_all.27 = f32[128,4,128]{2,1,0:T(4,128)S(1)} all-to-all(f32[128,4,128]{2,1,0:T(4,128)S(1)} %broadcast_in_dim.30), channel_id=1, replica_groups=mesh['gx'=16,'gy'=8] {'gx','gy'}, dimensions={0} | all-to-all | bytes 524288 | tf_op jit(solution)/shard_map/all_to_all | solution.py:332
  127.6 2.3 %correct.6 = (f32[48,128]{1,0:T(8,128)S(1)}, f32[16,128]{1,0:T(8,128)S(1)}, f32[16,128]{1,0:T(8,128)S(1)}, f32[16,128]{1,0:T(8,128)S(1)}, f32[16,128]{1,0:T(8,128)S(1)}) custom-call(f32[64,8,128]{2,1,0:T(8,128)S(1)} %bitcast.34, bf16[8192,128]{1,0:T(8,128)(2,1)S(1)} %get-tuple-element.79.mask, f32[8,112,128]{2,1,0:T(8,128)S(1)} %get-tuple-element.80.pte, ...), custom_call_target="tpu_custom_call" | custom-call | flops 2000000 | bytes 100000 | tf_op jit(solution)/shard_map/correct/pallas_call | solution.py:302
  130.2 2.2 %collective-permute-start.21 = (f32[16,128]{1,0:T(8,128)S(1)}, f32[16,128]{1,0:T(8,128)S(1)}, u32[]{:S(2)}, u32[]{:S(2)}) collective-permute-start(f32[16,128]{1,0:T(8,128)S(1)} %get-tuple-element.115), channel_id=1, source_target_pairs={{0,120},{8,16},{16,8},{24,32},{32,24},{40,48},{48,40},{56,64},{64,... | collective-permute-start | bytes 24584 | tf_op jit(solution)/shard_map/ppermute | solution.py:322
  133.6 2.5 %collective-permute-done.21.h1 = f32[16,128]{1,0:T(8,128)S(1)} collective-permute-done((f32[16,128]{1,0:T(8,128)S(1)}, f32[16,128]{1,0:T(8,128)S(1)}, u32[]{:S(2)}, u32[]{:S(2)}) %collective-permute-start.21) | collective-permute-done | bytes 8224 | tf_op jit(solution)/shard_map/ppermute | solution.py:322
  138.2 3.4 %collective-permute-start.25 = (f32[16,128]{1,0:T(8,128)S(1)}, f32[16,128]{1,0:T(8,128)S(1)}, u32[]{:S(2)}, u32[]{:S(2)}) collective-permute-start(f32[16,128]{1,0:T(8,128)S(1)} %get-tuple-element.121), channel_id=1, source_target_pairs={{0,120},{8,16},{16,8},{24,32},{32,24},{40,48},{48,40},{56,64},{64,... | collective-permute-start | bytes 24584 | tf_op jit(solution)/shard_map/ppermute | solution.py:322
  147.6 15.8 %all_to_all.28 = f32[128,4,128]{2,1,0:T(4,128)S(1)} all-to-all(f32[128,4,128]{2,1,0:T(4,128)S(1)} %broadcast_in_dim.31), channel_id=1, replica_groups=mesh['gx'=16,'gy'=8] {'gx','gy'}, dimensions={0} | all-to-all | bytes 524288 | tf_op jit(solution)/shard_map/all_to_all | solution.py:332
  163.4 2.3 %correct.7 = (f32[48,128]{1,0:T(8,128)S(1)}, f32[16,128]{1,0:T(8,128)S(1)}, f32[16,128]{1,0:T(8,128)S(1)}, f32[16,128]{1,0:T(8,128)S(1)}, f32[16,128]{1,0:T(8,128)S(1)}) custom-call(f32[64,8,128]{2,1,0:T(8,128)S(1)} %bitcast.32, bf16[8192,128]{1,0:T(8,128)(2,1)S(1)} %get-tuple-element.79.mask, f32[8,112,128]{2,1,0:T(8,128)S(1)} %get-tuple-element.80.pte, ...), custom_call_target="tpu_custom_call" | custom-call | flops 2000000 | bytes 100000 | tf_op jit(solution)/shard_map/correct/pallas_call | solution.py:302
  169.4 2.5 %collective-permute-done.29.h1 = f32[16,128]{1,0:T(8,128)S(1)} collective-permute-done((f32[16,128]{1,0:T(8,128)S(1)}, f32[16,128]{1,0:T(8,128)S(1)}, u32[]{:S(2)}, u32[]{:S(2)}) %collective-permute-start.29) | collective-permute-done | bytes 8224 | tf_op jit(solution)/shard_map/ppermute | solution.py:322
  173.8 15.3 %all_to_all.29 = f32[128,1,128]{2,1,0:T(1,128)S(1)} all-to-all(f32[128,1,128]{2,1,0:T(1,128)S(1)} %broadcast_in_dim.61), channel_id=1, replica_groups=mesh['gx'=16,'gy'=8] {'gx','gy'}, dimensions={0} | all-to-all | bytes 131072 | tf_op jit(solution)/shard_map/all_to_all | solution.py:332
  (94 shorter events, 45.4 us)
Async XLA Ops:
  7.5 19.0 %collective-permute-start.3 = (f32[6,16,128]{2,1,0:T(8,128)S(1)}, f32[6,16,128]{2,1,0:T(8,128)S(1)}, u32[]{:S(2)}, u32[]{:S(2)}) collective-permute-start(f32[6,16,128]{2,1,0:T(8,128)S(1)} %get-tuple-element.73), channel_id=1, source_target_pairs={{0,7},{1,2},{2,1},{3,4},{4,3},{5,6},{6,5},{7,0},{8,15},{9,10},{10,... | collective-permute-start | bytes 147464 | tf_op jit(solution)/shard_map/ppermute | solution.py:323
  10.3 16.2 %collective-permute-start.2 = (f32[6,16,128]{2,1,0:T(8,128)S(1)}, f32[6,16,128]{2,1,0:T(8,128)S(1)}, u32[]{:S(2)}, u32[]{:S(2)}) collective-permute-start(f32[6,16,128]{2,1,0:T(8,128)S(1)} %get-tuple-element.72), channel_id=1, source_target_pairs={{0,1},{1,0},{2,3},{3,2},{4,5},{5,4},{6,7},{7,6},{8,9},{9,8},{10,11... | collective-permute-start | bytes 147464 | tf_op jit(solution)/shard_map/ppermute | solution.py:325
  11.6 14.9 %collective-permute-start.1 = (f32[6,16,128]{2,1,0:T(8,128)S(1)}, f32[6,16,128]{2,1,0:T(8,128)S(1)}, u32[]{:S(2)}, u32[]{:S(2)}) collective-permute-start(f32[6,16,128]{2,1,0:T(8,128)S(1)} %get-tuple-element.71), channel_id=1, source_target_pairs={{0,120},{8,16},{16,8},{24,32},{32,24},{40,48},{48,40},{56,64},{64,... | collective-permute-start | bytes 147464 | tf_op jit(solution)/shard_map/ppermute | solution.py:322
  17.5 9.0 %collective-permute-start = (f32[6,16,128]{2,1,0:T(8,128)S(1)}, f32[6,16,128]{2,1,0:T(8,128)S(1)}, u32[]{:S(2)}, u32[]{:S(2)}) collective-permute-start(f32[6,16,128]{2,1,0:T(8,128)S(1)} %get-tuple-element.70), channel_id=1, source_target_pairs={{0,8},{8,0},{16,24},{24,16},{32,40},{40,32},{48,56},{56,48},{64,72... | collective-permute-start | bytes 147464 | tf_op jit(solution)/shard_map/ppermute | solution.py:324
  57.0 3.5 %collective-permute-start.4 = (f32[16,128]{1,0:T(8,128)S(1)}, f32[16,128]{1,0:T(8,128)S(1)}, u32[]{:S(2)}, u32[]{:S(2)}) collective-permute-start(f32[16,128]{1,0:T(8,128)S(1)} %get-tuple-element.86), channel_id=1, source_target_pairs={{0,8},{8,0},{16,24},{24,16},{32,40},{40,32},{48,56},{56,48},{64,72... | collective-permute-start | bytes 24584 | tf_op jit(solution)/shard_map/ppermute | solution.py:324
  57.6 5.8 %collective-permute-start.5 = (f32[16,128]{1,0:T(8,128)S(1)}, f32[16,128]{1,0:T(8,128)S(1)}, u32[]{:S(2)}, u32[]{:S(2)}) collective-permute-start(f32[16,128]{1,0:T(8,128)S(1)} %get-tuple-element.87), channel_id=1, source_target_pairs={{0,120},{8,16},{16,8},{24,32},{32,24},{40,48},{48,40},{56,64},{64,... | collective-permute-start | bytes 24584 | tf_op jit(solution)/shard_map/ppermute | solution.py:322
  59.0 4.4 %collective-permute-start.6 = (f32[16,128]{1,0:T(8,128)S(1)}, f32[16,128]{1,0:T(8,128)S(1)}, u32[]{:S(2)}, u32[]{:S(2)}) collective-permute-start(f32[16,128]{1,0:T(8,128)S(1)} %get-tuple-element.88), channel_id=1, source_target_pairs={{0,1},{1,0},{2,3},{3,2},{4,5},{5,4},{6,7},{7,6},{8,9},{9,8},{10,11... | collective-permute-start | bytes 24584 | tf_op jit(solution)/shard_map/ppermute | solution.py:325
  59.4 4.0 %collective-permute-start.7 = (f32[16,128]{1,0:T(8,128)S(1)}, f32[16,128]{1,0:T(8,128)S(1)}, u32[]{:S(2)}, u32[]{:S(2)}) collective-permute-start(f32[16,128]{1,0:T(8,128)S(1)} %get-tuple-element.89), channel_id=1, source_target_pairs={{0,7},{1,2},{2,1},{3,4},{4,3},{5,6},{6,5},{7,0},{8,15},{9,10},{10,... | collective-permute-start | bytes 24584 | tf_op jit(solution)/shard_map/ppermute | solution.py:323
  65.0 5.1 %collective-permute-start.10 = (f32[16,128]{1,0:T(8,128)S(1)}, f32[16,128]{1,0:T(8,128)S(1)}, u32[]{:S(2)}, u32[]{:S(2)}) collective-permute-start(f32[16,128]{1,0:T(8,128)S(1)} %get-tuple-element.94), channel_id=1, source_target_pairs={{0,1},{1,0},{2,3},{3,2},{4,5},{5,4},{6,7},{7,6},{8,9},{9,8},{10,11... | collective-permute-start | bytes 24584 | tf_op jit(solution)/shard_map/ppermute | solution.py:325
  67.7 3.4 %collective-permute-start.11 = (f32[16,128]{1,0:T(8,128)S(1)}, f32[16,128]{1,0:T(8,128)S(1)}, u32[]{:S(2)}, u32[]{:S(2)}) collective-permute-start(f32[16,128]{1,0:T(8,128)S(1)} %get-tuple-element.95), channel_id=1, source_target_pairs={{0,7},{1,2},{2,1},{3,4},{4,3},{5,6},{6,5},{7,0},{8,15},{9,10},{10,... | collective-permute-start | bytes 24584 | tf_op jit(solution)/shard_map/ppermute | solution.py:323
  67.7 5.8 %collective-permute-start.9 = (f32[16,128]{1,0:T(8,128)S(1)}, f32[16,128]{1,0:T(8,128)S(1)}, u32[]{:S(2)}, u32[]{:S(2)}) collective-permute-start(f32[16,128]{1,0:T(8,128)S(1)} %get-tuple-element.93), channel_id=1, source_target_pairs={{0,120},{8,16},{16,8},{24,32},{32,24},{40,48},{48,40},{56,64},{64,... | collective-permute-start | bytes 24584 | tf_op jit(solution)/shard_map/ppermute | solution.py:322
  94.1 3.7 %collective-permute-start.12 = (f32[16,128]{1,0:T(8,128)S(1)}, f32[16,128]{1,0:T(8,128)S(1)}, u32[]{:S(2)}, u32[]{:S(2)}) collective-permute-start(f32[16,128]{1,0:T(8,128)S(1)} %get-tuple-element.100), channel_id=1, source_target_pairs={{0,8},{8,0},{16,24},{24,16},{32,40},{40,32},{48,56},{56,48},{64,72... | collective-permute-start | bytes 24584 | tf_op jit(solution)/shard_map/ppermute | solution.py:324
  94.5 5.8 %collective-permute-start.13 = (f32[16,128]{1,0:T(8,128)S(1)}, f32[16,128]{1,0:T(8,128)S(1)}, u32[]{:S(2)}, u32[]{:S(2)}) collective-permute-start(f32[16,128]{1,0:T(8,128)S(1)} %get-tuple-element.101), channel_id=1, source_target_pairs={{0,120},{8,16},{16,8},{24,32},{32,24},{40,48},{48,40},{56,64},{64,... | collective-permute-start | bytes 24584 | tf_op jit(solution)/shard_map/ppermute | solution.py:322
  96.6 3.7 %collective-permute-start.14 = (f32[16,128]{1,0:T(8,128)S(1)}, f32[16,128]{1,0:T(8,128)S(1)}, u32[]{:S(2)}, u32[]{:S(2)}) collective-permute-start(f32[16,128]{1,0:T(8,128)S(1)} %get-tuple-element.102), channel_id=1, source_target_pairs={{0,1},{1,0},{2,3},{3,2},{4,5},{5,4},{6,7},{7,6},{8,9},{9,8},{10,11... | collective-permute-start | bytes 24584 | tf_op jit(solution)/shard_map/ppermute | solution.py:325
  102.5 4.6 %collective-permute-start.16 = (f32[16,128]{1,0:T(8,128)S(1)}, f32[16,128]{1,0:T(8,128)S(1)}, u32[]{:S(2)}, u32[]{:S(2)}) collective-permute-start(f32[16,128]{1,0:T(8,128)S(1)} %get-tuple-element.106), channel_id=1, source_target_pairs={{0,8},{8,0},{16,24},{24,16},{32,40},{40,32},{48,56},{56,48},{64,72... | collective-permute-start | bytes 24584 | tf_op jit(solution)/shard_map/ppermute | solution.py:324
  102.5 5.9 %collective-permute-start.17 = (f32[16,128]{1,0:T(8,128)S(1)}, f32[16,128]{1,0:T(8,128)S(1)}, u32[]{:S(2)}, u32[]{:S(2)}) collective-permute-start(f32[16,128]{1,0:T(8,128)S(1)} %get-tuple-element.107), channel_id=1, source_target_pairs={{0,120},{8,16},{16,8},{24,32},{32,24},{40,48},{48,40},{56,64},{64,... | collective-permute-start | bytes 24584 | tf_op jit(solution)/shard_map/ppermute | solution.py:322
  129.9 3.7 %collective-permute-start.20 = (f32[16,128]{1,0:T(8,128)S(1)}, f32[16,128]{1,0:T(8,128)S(1)}, u32[]{:S(2)}, u32[]{:S(2)}) collective-permute-start(f32[16,128]{1,0:T(8,128)S(1)} %get-tuple-element.114), channel_id=1, source_target_pairs={{0,8},{8,0},{16,24},{24,16},{32,40},{40,32},{48,56},{56,48},{64,72... | collective-permute-start | bytes 24584 | tf_op jit(solution)/shard_map/ppermute | solution.py:324
  130.2 5.8 %collective-permute-start.21 = (f32[16,128]{1,0:T(8,128)S(1)}, f32[16,128]{1,0:T(8,128)S(1)}, u32[]{:S(2)}, u32[]{:S(2)}) collective-permute-start(f32[16,128]{1,0:T(8,128)S(1)} %get-tuple-element.115), channel_id=1, source_target_pairs={{0,120},{8,16},{16,8},{24,32},{32,24},{40,48},{48,40},{56,64},{64,... | collective-permute-start | bytes 24584 | tf_op jit(solution)/shard_map/ppermute | solution.py:322
  132.4 3.7 %collective-permute-start.22 = (f32[16,128]{1,0:T(8,128)S(1)}, f32[16,128]{1,0:T(8,128)S(1)}, u32[]{:S(2)}, u32[]{:S(2)}) collective-permute-start(f32[16,128]{1,0:T(8,128)S(1)} %get-tuple-element.116), channel_id=1, source_target_pairs={{0,1},{1,0},{2,3},{3,2},{4,5},{5,4},{6,7},{7,6},{8,9},{9,8},{10,11... | collective-permute-start | bytes 24584 | tf_op jit(solution)/shard_map/ppermute | solution.py:325
  138.2 4.6 %collective-permute-start.24 = (f32[16,128]{1,0:T(8,128)S(1)}, f32[16,128]{1,0:T(8,128)S(1)}, u32[]{:S(2)}, u32[]{:S(2)}) collective-permute-start(f32[16,128]{1,0:T(8,128)S(1)} %get-tuple-element.120), channel_id=1, source_target_pairs={{0,8},{8,0},{16,24},{24,16},{32,40},{40,32},{48,56},{56,48},{64,72... | collective-permute-start | bytes 24584 | tf_op jit(solution)/shard_map/ppermute | solution.py:324
  138.2 5.9 %collective-permute-start.25 = (f32[16,128]{1,0:T(8,128)S(1)}, f32[16,128]{1,0:T(8,128)S(1)}, u32[]{:S(2)}, u32[]{:S(2)}) collective-permute-start(f32[16,128]{1,0:T(8,128)S(1)} %get-tuple-element.121), channel_id=1, source_target_pairs={{0,120},{8,16},{16,8},{24,32},{32,24},{40,48},{48,40},{56,64},{64,... | collective-permute-start | bytes 24584 | tf_op jit(solution)/shard_map/ppermute | solution.py:322
  165.7 3.7 %collective-permute-start.28 = (f32[16,128]{1,0:T(8,128)S(1)}, f32[16,128]{1,0:T(8,128)S(1)}, u32[]{:S(2)}, u32[]{:S(2)}) collective-permute-start(f32[16,128]{1,0:T(8,128)S(1)} %get-tuple-element.128), channel_id=1, source_target_pairs={{0,8},{8,0},{16,24},{24,16},{32,40},{40,32},{48,56},{56,48},{64,72... | collective-permute-start | bytes 24584 | tf_op jit(solution)/shard_map/ppermute | solution.py:324
  166.0 5.8 %collective-permute-start.29 = (f32[16,128]{1,0:T(8,128)S(1)}, f32[16,128]{1,0:T(8,128)S(1)}, u32[]{:S(2)}, u32[]{:S(2)}) collective-permute-start(f32[16,128]{1,0:T(8,128)S(1)} %get-tuple-element.129), channel_id=1, source_target_pairs={{0,120},{8,16},{16,8},{24,32},{32,24},{40,48},{48,40},{56,64},{64,... | collective-permute-start | bytes 24584 | tf_op jit(solution)/shard_map/ppermute | solution.py:322
  168.2 3.7 %collective-permute-start.30 = (f32[16,128]{1,0:T(8,128)S(1)}, f32[16,128]{1,0:T(8,128)S(1)}, u32[]{:S(2)}, u32[]{:S(2)}) collective-permute-start(f32[16,128]{1,0:T(8,128)S(1)} %get-tuple-element.130), channel_id=1, source_target_pairs={{0,1},{1,0},{2,3},{3,2},{4,5},{5,4},{6,7},{7,6},{8,9},{9,8},{10,11... | collective-permute-start | bytes 24584 | tf_op jit(solution)/shard_map/ppermute | solution.py:325
  (12 other events, 37.0 us)

commit v3 on v2

--- a/solution.py
+++ b/solution.py
@@ -51,7 +51,8 @@
     out = []
     for g in range(ROWS // 8):
         lhs = jnp.concatenate([top[8 * g : 8 * g + 8], bottom[8 * g : 8 * g + 8]], axis=0).astype(BF16)
-        r = jnp.dot(lhs, w_ref[:, 512 * g : 512 * g + 512], preferred_element_type=F32)
+        ref, n = (w_ref[g // 3], g % 3) if isinstance(w_ref, tuple) else (w_ref, g)
+        r = jnp.dot(lhs, ref[:, 512 * n : 512 * n + 512], preferred_element_type=F32)
         s = r[:8] + r[8:]
         own = lax.broadcasted_iota(jnp.int32, s.shape, 0) == lax.broadcasted_iota(jnp.int32, s.shape, 1) // BS
         s = jnp.where(own, s, 0.0)
@@ -99,16 +100,44 @@
     return jnp.where(lax.broadcasted_iota(jnp.int32, t.shape, 0) < BS, high, t - high).astype(BF16)
 
 
-def first_kernel(start, jac, pt, ids, listed, v, wj, ptd, pick, z, ze, s0, s1, s2, s3):
+def column(line):
+    line = jnp.concatenate([line, jnp.zeros((1, 128 - line.shape[1]), F32)], axis=1)
+    return jnp.broadcast_to(line, (128, 128)).T
+
+
+def first_kernel(*refs):
+    sources, off, rest = refs[:8], refs[8], refs[9:]
+    v, wj, ptd, pick, z, ze, ids, extra, slopes, s0, s1, s2, s3, near = rest[:14]
+    here, sems, far = rest[14:22], rest[22], rest[23]
+    copies = [pltpu.make_async_copy(x, y, sems.at[n]) for n, (x, y) in enumerate(zip(sources, here))]
+    for c in copies:
+        c.start()
+    ahead = pltpu.make_async_copy(off.at[pl.ds(0, ROWS // 2)], near, far)
+    ahead.start()
+    for c in copies:
+        c.wait()
+    start, jac, pt, inverse, listed, owner, slot, shifts = here
     v[...] = twice(start[...])
     for n in range(ROWS // 2):
         wj[:, 128 * n : 128 * n + 128] = pair_rows(jac[128 * n : 128 * n + 128, :] * jacobi_weight)
+    z[...] = smooth(v[...], wj)
+    ze[...] = pack(z[...])
+    odd_x = lax.axis_index("gx") % 2 == 1
+    odd_y = lax.axis_index("gy") % 2 == 1
+    lists = listed[...].astype(F32)
+    order = [
+        jnp.where(odd_x, lists[1:2], lists[0:1]),
+        jnp.where(odd_x, lists[0:1], lists[1:2]),
+        jnp.where(odd_y, lists[3:4], lists[2:3]),
+        jnp.where(odd_y, lists[2:3], lists[3:4]),
+    ]
+    chosen = jnp.concatenate([column(x)[0:HALO, 0:ROWS] for x in order], axis=0)
+    chosen = (chosen == lax.broadcasted_iota(jnp.int32, (4 * HALO, ROWS), 1).astype(F32)).astype(F32)
+    pick[...] = chosen.astype(BF16)
+    number = (owner[...] * 24 + slot[...]).astype(F32)
+    ids[...] = column(number)[0:ROWS]
     for c in range(CW):
         ptd[c] = twice(pt[:, c, :])
-    chosen = (listed[...] == lax.broadcasted_iota(jnp.int32, (4 * HALO, ROWS), 1)).astype(F32)
-    pick[...] = chosen.astype(BF16)
-    z[...] = smooth(v[...], wj)
-    ze[...] = pack(z[...])
     low = lax.broadcasted_iota(jnp.int32, (ROWS, 128), 1) < BS
     parts = [jnp.where(low, ptd[r], ptd[r + 4]) for r in range(4)] + [ids[...]]
     parts = [jnp.dot(chosen, x, precision=lax.Precision.HIGHEST, preferred_element_type=F32) for x in parts]
@@ -116,51 +145,73 @@
     for s, out in enumerate((s0, s1, s2, s3)):
         for k, x in enumerate(parts):
             out[k] = x[HALO * s : HALO * s + HALO]
-
-
-def operator_kernel(off, diag, cols, w, gather, buf, dbuf, sems, dsems):
-    def copies(g):
-        slot = g % 2
-        return (
-            pltpu.make_async_copy(off.at[pl.ds(8 * g, 8)], buf.at[slot], sems.at[slot]),
-            pltpu.make_async_copy(diag.at[pl.ds(8 * g, 8)], dbuf.at[slot], dsems.at[slot]),
-        )
-
-    for c in copies(0):
+    wide = jnp.concatenate([inverse[...], jnp.zeros((BS, 104), F32)], axis=1)
+    wide = jnp.concatenate([wide, jnp.zeros((BS, 128), F32)], axis=0).T[0:24]
+    extra[4:16, :] = wide[0:12] + swap(wide[12:24])
+    number = jnp.concatenate([number, jnp.zeros((1, 128 - ROWS), F32)], axis=1)
+    lane = lax.broadcasted_iota(jnp.int32, (1, 128), 1)
+    spare = (lane >= ROWS) & (lane < BS)
+    for r in range(3):
+        extra[r : r + 1, :] = jnp.where(spare, pltpu.roll(jnp.broadcast_to(number, (8, 128)), ROWS - 16 * r, 1)[0:1], 0.0)
+    extra[3:4, :] = jnp.zeros((1, 128), F32)
+    for k in range(4):
+        slopes[k : k + 1, :] = jnp.broadcast_to(shifts[:, k : k + 1], (1, 128))
+    ahead.wait()
+
+
+def pack_rows(buf, dbuf, n, g, w):
+    at = slice(BS * n, BS * n + 128)
+    for p in range(3):
+        x = jnp.concatenate(
+            [
+                jnp.concatenate([buf[n, 2 * p], buf[n, 2 * p + 1]], axis=1),
+                jnp.concatenate([buf[n + 1, 2 * p], buf[n + 1, 2 * p + 1]], axis=1),
+            ],
+            axis=0,
+        ).T
+        high = x.astype(BF16)
+        w[128 * p : 128 * p + 128, at] = high
+        w[384 + 128 * p : 512 + 128 * p, at] = (x - high.astype(F32)).astype(BF16)
+    w[768:896, at] = pair_rows(jnp.concatenate([dbuf[g + n], dbuf[g + n + 1]], axis=0))
+
+
+def operator_kernel(off, diag, cols, near, wa, wb, gather, buf, dbuf, cbuf, sems):
+    half = ROWS // 2
+    named = pltpu.make_async_copy(cols, cbuf, sems.at[0])
+    named.start()
+    middle = pltpu.make_async_copy(diag, dbuf, sems.at[1])
+    middle.start()
+    later = [
+        pltpu.make_async_copy(off.at[pl.ds(half + 8 * g, 8)], buf.at[pl.ds(8 * g, 8)], sems.at[2 + g]) for g in range(3)
+    ]
+    for c in later:
         c.start()
-    lane = lax.broadcasted_iota(jnp.int32, (ROWS, 256), 1)
+    named.wait()
+    turn_x = (1 - lax.axis_index("gx") % 2) * HALO
+    turn_y = (1 - lax.axis_index("gy") % 2) * HALO
+    number = cbuf[...]
+    beyond = number - ROWS
+    turned = ROWS + (beyond ^ jnp.where(beyond < 2 * HALO, turn_x, turn_y))
+    number = jnp.where(beyond >= 0, turned, number).astype(F32)
+    number = jnp.concatenate([number, jnp.zeros((KOFF, 128 - ROWS), F32)], axis=1)
+    number = jnp.concatenate([number, jnp.zeros((128 - KOFF, 128), F32)], axis=0).T[0:ROWS]
+    lane = lax.broadcasted_iota(jnp.int32, (ROWS, 256), 1).astype(F32)
     for p in range(3):
-        hit = (lane == cols[:, 2 * p : 2 * p + 1]) | (lane == cols[:, 2 * p + 1 : 2 * p + 2] + 128)
+        hit = (lane == number[:, 2 * p : 2 * p + 1]) | (lane == number[:, 2 * p + 1 : 2 * p + 2] + 128.0)
         gather[ROWS * p : ROWS * p + ROWS, :] = hit.astype(F32).astype(BF16)
-    for g in range(ROWS // 8):
-        if g + 1 < ROWS // 8:
-            for c in copies(g + 1):
-                c.start()
-        for c in copies(g):
-            c.wait()
-        slot = g % 2
-
-        for n in range(4):
-            at = slice(128 * (4 * g + n), 128 * (4 * g + n) + 128)
-            i, j = 2 * n, 2 * n + 1
-            for p in range(3):
-                x = jnp.concatenate(
-                    [
-                        jnp.concatenate([buf[slot, i, 2 * p], buf[slot, i, 2 * p + 1]], axis=1),
-                        jnp.concatenate([buf[slot, j, 2 * p], buf[slot, j, 2 * p + 1]], axis=1),
-                    ],
-                    axis=0,
-                ).T
-                high = x.astype(BF16)
-                w[128 * p : 128 * p + 128, at] = high
-                w[384 + 128 * p : 512 + 128 * p, at] = (x - high.astype(F32)).astype(BF16)
-            w[768:896, at] = pair_rows(jnp.concatenate([dbuf[slot, i], dbuf[slot, j]], axis=0))
-
-
-def restrict_kernel(v, ze, h0, h1, h2, h3, w_op, gather, ptd, *rest):
+    middle.wait()
+    for n in range(0, half, 2):
+        pack_rows(near, dbuf, n, 0, wa)
+    for g in range(3):
+        later[g].wait()
+        for n in range(8 * g, 8 * g + 8, 2):
+            pack_rows(buf, dbuf, n, half, wb)
+
+
+def restrict_kernel(v, ze, h0, h1, h2, h3, wa, wb, gather, ptd, *rest):
     *extra, w, p = rest
     ext = jnp.concatenate([ze[...], h0[...], h1[...], h2[...], h3[...]], axis=0)
-    r = v[...] - operate(ext, w_op, gather)
+    r = v[...] - operate(ext, (wa, wb), gather)
     w[...] = r
     ones = jnp.ones((16, 128), BF16)
     pad = jnp.zeros((16, 128), F32)
@@ -179,9 +230,8 @@
     wanted = idc.T[0:1]
     given = [x0[:, r, :].T[ROWS:BS] for r in range(3)] + [jnp.full((BS - ROWS, 128), -1.0, F32)]
     given = jnp.concatenate(given + given, axis=0)
-    upper_rows = lax.broadcasted_iota(jnp.int32, (128, 1), 0) < BS
     for q in range(64):
-        line = jnp.where(upper_rows, given[:, 2 * q : 2 * q + 1], given[:, 2 * q + 1 : 2 * q + 2])
+        line = jnp.concatenate([given[0:BS, 2 * q : 2 * q + 1], given[BS:128, 2 * q + 1 : 2 * q + 2]], axis=0)
         mask[128 * q : 128 * q + 128, :] = (line == wanted).astype(F32).astype(BF16)
         xp[q] = jnp.concatenate([x0[2 * q, 0:4, :], x0[2 * q + 1, 0:4, :]], axis=0)
     device = jnp.floor((idc + 0.5) * (1.0 / 24.0))
@@ -214,7 +264,7 @@
         pte[d] = acc
 
 
-def correct_kernel(x, mask, pte, z, w, w_op, gather, wj, pick, ye, s0, s1, s2, s3, parts):
+def correct_kernel(x, mask, pte, z, w, wa, wb, gather, wj, pick, ye, s0, s1, s2, s3, parts):
     sub = lax.broadcasted_iota(jnp.int32, (8, 128), 0) < 4
     lane = lax.broadcasted_iota(jnp.int32, (8, 128), 1) < BS
     keep = sub == lane
@@ -228,7 +278,7 @@
     u = pte[0] * coarse[:, 0:1]
     for d in range(1, CW):
         u = u + pte[d] * coarse[:, d : d + 1]
-    r = w[...] - operate(pack(u), w_op, gather)
+    r = w[...] - operate(pack(u), (wa, wb), gather)
     y = z[...] + u[:ROWS] + smooth(r, wj)
     ye[...] = pack(y)
     send_lists(ye[...], pick, (s0, s1, s2, s3))
@@ -239,15 +289,15 @@
     return operate(ext, w_op, gather) - shifts[k : k + 1, :] * v[...]
 
 
-def advance_kernel(k, shifts, v, ye, h0, h1, h2, h3, w_op, gather, wj, pick, vn, z, ze, s0, s1, s2, s3):
-    vn[...] = advance(k, shifts, v, ye, h0, h1, h2, h3, w_op, gather)
+def advance_kernel(k, shifts, v, ye, h0, h1, h2, h3, wa, wb, gather, wj, pick, vn, z, ze, s0, s1, s2, s3):
+    vn[...] = advance(k, shifts, v, ye, h0, h1, h2, h3, (wa, wb), gather)
     z[...] = smooth(vn[...], wj)
     ze[...] = pack(z[...])
     send_lists(ze[...], pick, (s0, s1, s2, s3))
 
 
-def last_kernel(shifts, ye, h0, h1, h2, h3, w_op, gather, v0, v1, v2, v3, v4, gram):
-    v4[...] = advance(3, shifts, v3, ye, h0, h1, h2, h3, w_op, gather)
+def last_kernel(shifts, ye, h0, h1, h2, h3, wa, wb, gather, v0, v1, v2, v3, v4, gram):
+    v4[...] = advance(3, shifts, v3, ye, h0, h1, h2, h3, (wa, wb), gather)
     basis = [v[...] for v in (v0, v1, v2, v3, v4)]
     rows = []
     for j, l in PAIRS:
@@ -333,25 +383,19 @@
 
 
 def per_device(start, shifts, diag_blocks, off_blocks, jacobi_inv, prolong, coarse_inv, cols, send_rows, owner, agg_slot):
-    odd_x = lax.axis_index("gx") % 2
-    odd_y = lax.axis_index("gy") % 2
-    lists = send_rows[0]
-    lists = jnp.concatenate(
-        [jnp.where(odd_x == 1, lists[1::-1], lists[0:2]), jnp.where(odd_y == 1, lists[3:1:-1], lists[2:4])]
-    ).reshape(4 * HALO, 1)
-    beyond = cols - ROWS
-    turn = jnp.where(beyond < 2 * HALO, 1 - odd_x, 1 - odd_y) * HALO
-    cols = jnp.where(beyond >= 0, ROWS + (beyond ^ turn), cols)
-    ids = (owner[:, 0] * coarse_inv.shape[0] + agg_slot).astype(F32)
-    id_col = jnp.broadcast_to(ids[:, None], (ROWS, 128))
-    inv = coarse_inv.reshape(24, BS)
-    spare = jnp.pad(ids.reshape(3, BS - ROWS), ((0, 1), (ROWS, BS)))
-    extra = jnp.concatenate([spare, jnp.concatenate([inv[:12], inv[12:]], axis=1)])
-    slopes = jnp.broadcast_to(shifts[:, None], (4, 128))
-    pt = jnp.transpose(prolong, (0, 2, 1))
-
     halo = [shape(HALO, 128)] * 4
-    v, wj, ptd, pick, z, ze, *sends = call(
+    matrices = [pltpu.with_memory_space_constraint(x, pltpu.HBM) for x in (off_blocks, diag_blocks, jnp.transpose(cols))]
+    sources = [
+        start,
+        jacobi_inv.reshape(ROWS * BS, BS),
+        jnp.transpose(prolong, (0, 2, 1)),
+        jnp.transpose(coarse_inv, (1, 2, 0)).reshape(BS, 24),
+        send_rows[0],
+        owner.reshape(1, ROWS),
+        agg_slot.reshape(1, ROWS),
+        shifts.reshape(1, 4),
+    ]
+    v, wj, ptd, pick, z, ze, id_col, extra, slopes, *sends, near = call(
         first_kernel,
         [
             shape(ROWS, 128),
@@ -360,28 +404,32 @@
             shape(4 * HALO, ROWS, dtype=BF16),
             shape(ROWS, 128),
             shape(ROWS, 128),
+            shape(ROWS, 128),
+            shape(16, 128),
+            shape(4, 128),
         ]
-        + [shape(6, HALO, 128)] * 4,
-        start,
-        jacobi_inv.reshape(ROWS * BS, BS),
-        pt,
-        id_col,
-        lists,
+        + [shape(6, HALO, 128)] * 4
+        + [kept(ROWS // 2, KOFF, BS, BS)],
+        *[pltpu.with_memory_space_constraint(x, pltpu.HBM) for x in sources],
+        matrices[0],
+        specs=[HBM] * (len(sources) + 1),
+        scratch=[pltpu.VMEM(x.shape, x.dtype) for x in sources]
+        + [pltpu.SemaphoreType.DMA((len(sources),)), pltpu.SemaphoreType.DMA],
         name="first",
     )
     got = exchange(sends)
-    w_op, gather = call(
+    half = kept(WIDTH, ROWS * BS // 2, dtype=BF16)
+    *w_op, gather = call(
         operator_kernel,
-        [kept(WIDTH, ROWS * BS, dtype=BF16), shape(3 * ROWS, 256, dtype=BF16)],
-        pltpu.with_memory_space_constraint(off_blocks, pltpu.HBM),
-        pltpu.with_memory_space_constraint(diag_blocks, pltpu.HBM),
-        cols,
-        specs=[HBM, HBM, VM],
+        [half, half, shape(3 * ROWS, 256, dtype=BF16)],
+        *matrices,
+        near,
+        specs=[HBM] * 3 + [VM],
         scratch=[
-            pltpu.VMEM((2, 8, KOFF, BS, BS), F32),
-            pltpu.VMEM((2, 8, BS, BS), F32),
-            pltpu.SemaphoreType.DMA((2,)),
-            pltpu.SemaphoreType.DMA((2,)),
+            pltpu.VMEM((ROWS // 2, KOFF, BS, BS), F32),
+            pltpu.VMEM((ROWS, BS, BS), F32),
+            pltpu.VMEM((KOFF, ROWS), jnp.int32),
+            pltpu.SemaphoreType.DMA((5,)),
         ],
         flops=2_000_000_000,
         name="operator",
@@ -396,7 +444,7 @@
             v,
             ze,
             *around,
-            w_op,
+            *w_op,
             gather,
             ptd,
             *([] if k else [extra]),
@@ -422,7 +470,7 @@
             pte,
             z,
             w,
-            w_op,
+            *w_op,
             gather,
             wj,
             pick,
@@ -438,7 +486,7 @@
                 v,
                 ye,
                 *around,
-                w_op,
+                *w_op,
                 gather,
                 wj,
                 pick,
@@ -452,7 +500,7 @@
         slopes,
         ye,
         *around,
-        w_op,
+        *w_op,
         gather,
         *basis,
         name="last",

time: 191 us -> 183 us (0.958)
  local copies, waits for them, and re-layouts: 6.4 us -> 0.37 us
    unnamed x9 -> x0, local copies, waits for them, and re-layouts: 3.85 us -> none
  transfers between devices with their start and end apart: 32 -> 32, of which waited for: 13 -> 13; matrix products, arithmetic and copies ran while one was open for 1% -> 0% of each run, Pallas kernels for 4% -> 3%
where the time goes in v3:
time: 183 us
  blocking collectives  87.7 us (48%)
  starting transfers between devices  38.8 us (21%)
  Pallas kernels  32.5 us (18%)
  waiting for transfers between devices  22.4 us (12%)
    all_to_all x5, blocking collectives, everywhere(): lax.all_to_all(y, ('gx', 'gy'), split_axis=0, concat_axis=0, tiled=True)  87.7 us
    pallas_call x16, Pallas kernels, call(): pl.pallas_call(kernel, out_shape=outs, in_specs=specs or [VM] * len(args)...  32.5 us
    ppermute x8, starting transfers between devices, exchange(): b = lax.ppermute(sends[1], 'gx', swap_pairs(nx, 1))  23.1 us
    ppermute x8, waiting for transfers between devices, exchange(): b = lax.ppermute(sends[1], 'gx', swap_pairs(nx, 1))  15.3 us
    ppermute x8, starting transfers between devices, exchange(): c = lax.ppermute(sends[2], 'gy', swap_pairs(ny, 0))  9.67 us
    ppermute x8, waiting for transfers between devices, exchange(): d = lax.ppermute(sends[3], 'gy', swap_pairs(ny, 1))  7.15 us
    ppermute x8, starting transfers between devices, exchange(): d = lax.ppermute(sends[3], 'gy', swap_pairs(ny, 1))  4.58 us
  transfers between devices with their start and end apart: 32, of which 13 were waited for; matrix products, arithmetic and copies ran while one was open for 0% of the time, Pallas kernels for 3%

profile of v3, /device:TPU:1, one launch (start us, length us, event | category | flops | bytes accessed | tf_op | source)
XLA Modules:
  0.0 182.6 jit_solution(15242782653271730954)
XLA Ops:
  0.6 3.1 %first.1 = (f32[48,128]{1,0:T(8,128)S(1)}, bf16[128,3072]{1,0:T(8,128)(2,1)S(1)}, f32[8,48,128]{2,1,0:T(8,128)S(1)}, bf16[64,48]{1,0:T(8,128)(2,1)S(1)}, f32[48,...) custom-call(f32[48,64]{1,0:T(8,128)} %refs_0_.1, ...), custom_call_target="tpu_custom_call" | custom-call | flops 2000000 | bytes 100000 | tf_op jit(solution)/shard_map/first/pallas_call | solution.py:352
  3.7 2.8 %collective-permute-start.3 = (f32[6,16,128]{2,1,0:T(8,128)S(1)}, f32[6,16,128]{2,1,0:T(8,128)S(1)}, u32[]{:S(2)}, u32[]{:S(2)}) collective-permute-start(f32[6,16,128]{2,1,0:T(8,128)S(1)} %get-tuple-element.79), channel_id=1, source_target_pairs={{0,7},{1,2},{2,1},{3,4},{4,3},{5,6},{6,5},{7,0},{8,15},{9,10},{10,... | collective-permute-start | bytes 147464 | tf_op jit(solution)/shard_map/ppermute | solution.py:373
  7.7 6.0 %collective-permute-start.1 = (f32[6,16,128]{2,1,0:T(8,128)S(1)}, f32[6,16,128]{2,1,0:T(8,128)S(1)}, u32[]{:S(2)}, u32[]{:S(2)}) collective-permute-start(f32[6,16,128]{2,1,0:T(8,128)S(1)} %get-tuple-element.77), channel_id=1, source_target_pairs={{0,120},{8,16},{16,8},{24,32},{32,24},{40,48},{48,40},{56,64},{64,... | collective-permute-start | bytes 147464 | tf_op jit(solution)/shard_map/ppermute | solution.py:372
  13.7 5.1 %operator.1 = (bf16[896,1536]{1,0:T(8,128)(2,1)S(1)}, bf16[896,1536]{1,0:T(8,128)(2,1)S(1)}, bf16[144,256]{1,0:T(8,128)(2,1)S(1)}) custom-call(f32[48,6,64,64]{3,2,1,0:T(8,128)} %off.1, f32[48,64,64]{2,1,0:T(8,128)} %diag.1, s32[6,48]{1,0:T(8,128)} %bitcast.31, f32[24,6,64,64]{3,2,1,0:T(8,128)S(1)} %get-tuple-element.80.near), custom_call_target="tpu_custom_call" | custom-call | flops 2000000000 | bytes 100000 | tf_op jit(solution)/shard_map/operator/pallas_call | solution.py:352
  20.3 23.9 %all_to_all.25.x0 = f32[128,16,128]{2,1,0:T(8,128)S(1)} all-to-all(f32[128,16,128]{2,1,0:T(8,128)S(1)} %broadcast_in_dim.12), channel_id=1, replica_groups=mesh['gx'=16,'gy'=8] {'gx','gy'}, dimensions={0} | all-to-all | bytes 2097152 | tf_op jit(solution)/shard_map/all_to_all | solution.py:382
  44.2 2.8 %coarse.1 = (bf16[8192,128]{1,0:T(8,128)(2,1)S(1)}, f32[8,112,128]{2,1,0:T(8,128)S(1)}, f32[64,8,128]{2,1,0:T(8,128)S(1)}) custom-call(f32[128,16,128]{2,1,0:T(8,128)S(1)} %all_to_all.25.x0, f32[48,128]{1,0:T(8,128)S(1)} %get-tuple-element.87.ids, f32[8,48,128]{2,1,0:T(8,128)S(1)} %get-tuple-element.84.ptd, f32[6,16,128]{2,1,0:T(8,128)S(1)} %collective-permute-done.g0, ...), custom_call_target="tpu_custom_call" | custom-call | flops 2000000 | bytes 100000 | tf_op jit(solution)/shard_map/coarse/pallas_call | solution.py:352
  46.9 2.3 %correct.4 = (f32[48,128]{1,0:T(8,128)S(1)}, f32[16,128]{1,0:T(8,128)S(1)}, f32[16,128]{1,0:T(8,128)S(1)}, f32[16,128]{1,0:T(8,128)S(1)}, f32[16,128]{1,0:T(8,128)S(1)}) custom-call(f32[64,8,128]{2,1,0:T(8,128)S(1)} %get-tuple-element.88.x, bf16[8192,128]{1,0:T(8,128)(2,1)S(1)} %get-tuple-element.89.mask, f32[8,112,128]{2,1,0:T(8,128)S(1)} %get-tuple-element.90.pte, ...), custom_call_target="tpu_custom_call" | custom-call | flops 2000000 | bytes 100000 | tf_op jit(solution)/shard_map/correct/pallas_call | solution.py:352
  52.6 2.9 %collective-permute-done.5.h1 = f32[16,128]{1,0:T(8,128)S(1)} collective-permute-done((f32[16,128]{1,0:T(8,128)S(1)}, f32[16,128]{1,0:T(8,128)S(1)}, u32[]{:S(2)}, u32[]{:S(2)}) %collective-permute-start.5) | collective-permute-done | bytes 8224 | tf_op jit(solution)/shard_map/ppermute | solution.py:372
  57.0 2.7 %collective-permute-start.10 = (f32[16,128]{1,0:T(8,128)S(1)}, f32[16,128]{1,0:T(8,128)S(1)}, u32[]{:S(2)}, u32[]{:S(2)}) collective-permute-start(f32[16,128]{1,0:T(8,128)S(1)} %get-tuple-element.104), channel_id=1, source_target_pairs={{0,1},{1,0},{2,3},{3,2},{4,5},{5,4},{6,7},{7,6},{8,9},{9,8},{10,11... | collective-permute-start | bytes 24584 | tf_op jit(solution)/shard_map/ppermute | solution.py:375
  59.7 2.4 %collective-permute-start.9 = (f32[16,128]{1,0:T(8,128)S(1)}, f32[16,128]{1,0:T(8,128)S(1)}, u32[]{:S(2)}, u32[]{:S(2)}) collective-permute-start(f32[16,128]{1,0:T(8,128)S(1)} %get-tuple-element.103), channel_id=1, source_target_pairs={{0,120},{8,16},{16,8},{24,32},{32,24},{40,48},{48,40},{56,64},{64,... | collective-permute-start | bytes 24584 | tf_op jit(solution)/shard_map/ppermute | solution.py:372
  63.1 2.5 %collective-permute-done.9.h1 = f32[16,128]{1,0:T(8,128)S(1)} collective-permute-done((f32[16,128]{1,0:T(8,128)S(1)}, f32[16,128]{1,0:T(8,128)S(1)}, u32[]{:S(2)}, u32[]{:S(2)}) %collective-permute-start.9) | collective-permute-done | bytes 8224 | tf_op jit(solution)/shard_map/ppermute | solution.py:372
  66.9 16.9 %all_to_all.26 = f32[128,4,128]{2,1,0:T(4,128)S(1)} all-to-all(f32[128,4,128]{2,1,0:T(4,128)S(1)} %broadcast_in_dim.13), channel_id=1, replica_groups=mesh['gx'=16,'gy'=8] {'gx','gy'}, dimensions={0} | all-to-all | bytes 524288 | tf_op jit(solution)/shard_map/all_to_all | solution.py:382
  83.8 2.3 %correct.5 = (f32[48,128]{1,0:T(8,128)S(1)}, f32[16,128]{1,0:T(8,128)S(1)}, f32[16,128]{1,0:T(8,128)S(1)}, f32[16,128]{1,0:T(8,128)S(1)}, f32[16,128]{1,0:T(8,128)S(1)}) custom-call(f32[64,8,128]{2,1,0:T(8,128)S(1)} %bitcast.24, bf16[8192,128]{1,0:T(8,128)(2,1)S(1)} %get-tuple-element.89.mask, f32[8,112,128]{2,1,0:T(8,128)S(1)} %get-tuple-element.90.pte, ...), custom_call_target="tpu_custom_call" | custom-call | flops 2000000 | bytes 100000 | tf_op jit(solution)/shard_map/correct/pallas_call | solution.py:352
  86.5 2.2 %collective-permute-start.13 = (f32[16,128]{1,0:T(8,128)S(1)}, f32[16,128]{1,0:T(8,128)S(1)}, u32[]{:S(2)}, u32[]{:S(2)}) collective-permute-start(f32[16,128]{1,0:T(8,128)S(1)} %get-tuple-element.111), channel_id=1, source_target_pairs={{0,120},{8,16},{16,8},{24,32},{32,24},{40,48},{48,40},{56,64},{64,... | collective-permute-start | bytes 24584 | tf_op jit(solution)/shard_map/ppermute | solution.py:372
  89.8 2.5 %collective-permute-done.13.h1 = f32[16,128]{1,0:T(8,128)S(1)} collective-permute-done((f32[16,128]{1,0:T(8,128)S(1)}, f32[16,128]{1,0:T(8,128)S(1)}, u32[]{:S(2)}, u32[]{:S(2)}) %collective-permute-start.13) | collective-permute-done | bytes 8224 | tf_op jit(solution)/shard_map/ppermute | solution.py:372
  94.5 3.4 %collective-permute-start.17 = (f32[16,128]{1,0:T(8,128)S(1)}, f32[16,128]{1,0:T(8,128)S(1)}, u32[]{:S(2)}, u32[]{:S(2)}) collective-permute-start(f32[16,128]{1,0:T(8,128)S(1)} %get-tuple-element.117), channel_id=1, source_target_pairs={{0,120},{8,16},{16,8},{24,32},{32,24},{40,48},{48,40},{56,64},{64,... | collective-permute-start | bytes 24584 | tf_op jit(solution)/shard_map/ppermute | solution.py:372
  103.8 15.8 %all_to_all.27 = f32[128,4,128]{2,1,0:T(4,128)S(1)} all-to-all(f32[128,4,128]{2,1,0:T(4,128)S(1)} %broadcast_in_dim.14), channel_id=1, replica_groups=mesh['gx'=16,'gy'=8] {'gx','gy'}, dimensions={0} | all-to-all | bytes 524288 | tf_op jit(solution)/shard_map/all_to_all | solution.py:382
  119.6 2.3 %correct.6 = (f32[48,128]{1,0:T(8,128)S(1)}, f32[16,128]{1,0:T(8,128)S(1)}, f32[16,128]{1,0:T(8,128)S(1)}, f32[16,128]{1,0:T(8,128)S(1)}, f32[16,128]{1,0:T(8,128)S(1)}) custom-call(f32[64,8,128]{2,1,0:T(8,128)S(1)} %bitcast.25, bf16[8192,128]{1,0:T(8,128)(2,1)S(1)} %get-tuple-element.89.mask, f32[8,112,128]{2,1,0:T(8,128)S(1)} %get-tuple-element.90.pte, ...), custom_call_target="tpu_custom_call" | custom-call | flops 2000000 | bytes 100000 | tf_op jit(solution)/shard_map/correct/pallas_call | solution.py:352
  125.6 2.5 %collective-permute-done.21.h1 = f32[16,128]{1,0:T(8,128)S(1)} collective-permute-done((f32[16,128]{1,0:T(8,128)S(1)}, f32[16,128]{1,0:T(8,128)S(1)}, u32[]{:S(2)}, u32[]{:S(2)}) %collective-permute-start.21) | collective-permute-done | bytes 8224 | tf_op jit(solution)/shard_map/ppermute | solution.py:372
  130.3 3.4 %collective-permute-start.25 = (f32[16,128]{1,0:T(8,128)S(1)}, f32[16,128]{1,0:T(8,128)S(1)}, u32[]{:S(2)}, u32[]{:S(2)}) collective-permute-start(f32[16,128]{1,0:T(8,128)S(1)} %get-tuple-element.131), channel_id=1, source_target_pairs={{0,120},{8,16},{16,8},{24,32},{32,24},{40,48},{48,40},{56,64},{64,... | collective-permute-start | bytes 24584 | tf_op jit(solution)/shard_map/ppermute | solution.py:372
  139.6 15.8 %all_to_all.28 = f32[128,4,128]{2,1,0:T(4,128)S(1)} all-to-all(f32[128,4,128]{2,1,0:T(4,128)S(1)} %broadcast_in_dim.15), channel_id=1, replica_groups=mesh['gx'=16,'gy'=8] {'gx','gy'}, dimensions={0} | all-to-all | bytes 524288 | tf_op jit(solution)/shard_map/all_to_all | solution.py:382
  155.4 2.3 %correct.7 = (f32[48,128]{1,0:T(8,128)S(1)}, f32[16,128]{1,0:T(8,128)S(1)}, f32[16,128]{1,0:T(8,128)S(1)}, f32[16,128]{1,0:T(8,128)S(1)}, f32[16,128]{1,0:T(8,128)S(1)}) custom-call(f32[64,8,128]{2,1,0:T(8,128)S(1)} %bitcast.23, bf16[8192,128]{1,0:T(8,128)(2,1)S(1)} %get-tuple-element.89.mask, f32[8,112,128]{2,1,0:T(8,128)S(1)} %get-tuple-element.90.pte, ...), custom_call_target="tpu_custom_call" | custom-call | flops 2000000 | bytes 100000 | tf_op jit(solution)/shard_map/correct/pallas_call | solution.py:352
  161.4 2.5 %collective-permute-done.29.h1 = f32[16,128]{1,0:T(8,128)S(1)} collective-permute-done((f32[16,128]{1,0:T(8,128)S(1)}, f32[16,128]{1,0:T(8,128)S(1)}, u32[]{:S(2)}, u32[]{:S(2)}) %collective-permute-start.29) | collective-permute-done | bytes 8224 | tf_op jit(solution)/shard_map/ppermute | solution.py:372
  165.8 15.3 %all_to_all.29 = f32[128,1,128]{2,1,0:T(1,128)S(1)} all-to-all(f32[128,1,128]{2,1,0:T(1,128)S(1)} %broadcast_in_dim.17), channel_id=1, replica_groups=mesh['gx'=16,'gy'=8] {'gx','gy'}, dimensions={0} | all-to-all | bytes 131072 | tf_op jit(solution)/shard_map/all_to_all | solution.py:382
  (70 shorter events, 38.4 us)
Async XLA Ops:
  3.7 15.1 %collective-permute-start.3 = (f32[6,16,128]{2,1,0:T(8,128)S(1)}, f32[6,16,128]{2,1,0:T(8,128)S(1)}, u32[]{:S(2)}, u32[]{:S(2)}) collective-permute-start(f32[6,16,128]{2,1,0:T(8,128)S(1)} %get-tuple-element.79), channel_id=1, source_target_pairs={{0,7},{1,2},{2,1},{3,4},{4,3},{5,6},{6,5},{7,0},{8,15},{9,10},{10,... | collective-permute-start | bytes 147464 | tf_op jit(solution)/shard_map/ppermute | solution.py:373
  6.5 12.3 %collective-permute-start.2 = (f32[6,16,128]{2,1,0:T(8,128)S(1)}, f32[6,16,128]{2,1,0:T(8,128)S(1)}, u32[]{:S(2)}, u32[]{:S(2)}) collective-permute-start(f32[6,16,128]{2,1,0:T(8,128)S(1)} %get-tuple-element.78), channel_id=1, source_target_pairs={{0,1},{1,0},{2,3},{3,2},{4,5},{5,4},{6,7},{7,6},{8,9},{9,8},{10,11... | collective-permute-start | bytes 147464 | tf_op jit(solution)/shard_map/ppermute | solution.py:375
  7.7 11.1 %collective-permute-start.1 = (f32[6,16,128]{2,1,0:T(8,128)S(1)}, f32[6,16,128]{2,1,0:T(8,128)S(1)}, u32[]{:S(2)}, u32[]{:S(2)}) collective-permute-start(f32[6,16,128]{2,1,0:T(8,128)S(1)} %get-tuple-element.77), channel_id=1, source_target_pairs={{0,120},{8,16},{16,8},{24,32},{32,24},{40,48},{48,40},{56,64},{64,... | collective-permute-start | bytes 147464 | tf_op jit(solution)/shard_map/ppermute | solution.py:372
  13.7 5.2 %collective-permute-start = (f32[6,16,128]{2,1,0:T(8,128)S(1)}, f32[6,16,128]{2,1,0:T(8,128)S(1)}, u32[]{:S(2)}, u32[]{:S(2)}) collective-permute-start(f32[6,16,128]{2,1,0:T(8,128)S(1)} %get-tuple-element.76), channel_id=1, source_target_pairs={{0,8},{8,0},{16,24},{24,16},{32,40},{40,32},{48,56},{56,48},{64,72... | collective-permute-start | bytes 147464 | tf_op jit(solution)/shard_map/ppermute | solution.py:374
  49.7 5.8 %collective-permute-start.5 = (f32[16,128]{1,0:T(8,128)S(1)}, f32[16,128]{1,0:T(8,128)S(1)}, u32[]{:S(2)}, u32[]{:S(2)}) collective-permute-start(f32[16,128]{1,0:T(8,128)S(1)} %get-tuple-element.97), channel_id=1, source_target_pairs={{0,120},{8,16},{16,8},{24,32},{32,24},{40,48},{48,40},{56,64},{64,... | collective-permute-start | bytes 24584 | tf_op jit(solution)/shard_map/ppermute | solution.py:372
  51.1 4.4 %collective-permute-start.6 = (f32[16,128]{1,0:T(8,128)S(1)}, f32[16,128]{1,0:T(8,128)S(1)}, u32[]{:S(2)}, u32[]{:S(2)}) collective-permute-start(f32[16,128]{1,0:T(8,128)S(1)} %get-tuple-element.98), channel_id=1, source_target_pairs={{0,1},{1,0},{2,3},{3,2},{4,5},{5,4},{6,7},{7,6},{8,9},{9,8},{10,11... | collective-permute-start | bytes 24584 | tf_op jit(solution)/shard_map/ppermute | solution.py:375
  51.5 4.0 %collective-permute-start.7 = (f32[16,128]{1,0:T(8,128)S(1)}, f32[16,128]{1,0:T(8,128)S(1)}, u32[]{:S(2)}, u32[]{:S(2)}) collective-permute-start(f32[16,128]{1,0:T(8,128)S(1)} %get-tuple-element.99), channel_id=1, source_target_pairs={{0,7},{1,2},{2,1},{3,4},{4,3},{5,6},{6,5},{7,0},{8,15},{9,10},{10,... | collective-permute-start | bytes 24584 | tf_op jit(solution)/shard_map/ppermute | solution.py:373
  57.0 5.1 %collective-permute-start.10 = (f32[16,128]{1,0:T(8,128)S(1)}, f32[16,128]{1,0:T(8,128)S(1)}, u32[]{:S(2)}, u32[]{:S(2)}) collective-permute-start(f32[16,128]{1,0:T(8,128)S(1)} %get-tuple-element.104), channel_id=1, source_target_pairs={{0,1},{1,0},{2,3},{3,2},{4,5},{5,4},{6,7},{7,6},{8,9},{9,8},{10,11... | collective-permute-start | bytes 24584 | tf_op jit(solution)/shard_map/ppermute | solution.py:375
  59.7 3.4 %collective-permute-start.11 = (f32[16,128]{1,0:T(8,128)S(1)}, f32[16,128]{1,0:T(8,128)S(1)}, u32[]{:S(2)}, u32[]{:S(2)}) collective-permute-start(f32[16,128]{1,0:T(8,128)S(1)} %get-tuple-element.105), channel_id=1, source_target_pairs={{0,7},{1,2},{2,1},{3,4},{4,3},{5,6},{6,5},{7,0},{8,15},{9,10},{10,... | collective-permute-start | bytes 24584 | tf_op jit(solution)/shard_map/ppermute | solution.py:373
  59.7 5.8 %collective-permute-start.9 = (f32[16,128]{1,0:T(8,128)S(1)}, f32[16,128]{1,0:T(8,128)S(1)}, u32[]{:S(2)}, u32[]{:S(2)}) collective-permute-start(f32[16,128]{1,0:T(8,128)S(1)} %get-tuple-element.103), channel_id=1, source_target_pairs={{0,120},{8,16},{16,8},{24,32},{32,24},{40,48},{48,40},{56,64},{64,... | collective-permute-start | bytes 24584 | tf_op jit(solution)/shard_map/ppermute | solution.py:372
  86.1 3.7 %collective-permute-start.12 = (f32[16,128]{1,0:T(8,128)S(1)}, f32[16,128]{1,0:T(8,128)S(1)}, u32[]{:S(2)}, u32[]{:S(2)}) collective-permute-start(f32[16,128]{1,0:T(8,128)S(1)} %get-tuple-element.110), channel_id=1, source_target_pairs={{0,8},{8,0},{16,24},{24,16},{32,40},{40,32},{48,56},{56,48},{64,72... | collective-permute-start | bytes 24584 | tf_op jit(solution)/shard_map/ppermute | solution.py:374
  86.5 5.8 %collective-permute-start.13 = (f32[16,128]{1,0:T(8,128)S(1)}, f32[16,128]{1,0:T(8,128)S(1)}, u32[]{:S(2)}, u32[]{:S(2)}) collective-permute-start(f32[16,128]{1,0:T(8,128)S(1)} %get-tuple-element.111), channel_id=1, source_target_pairs={{0,120},{8,16},{16,8},{24,32},{32,24},{40,48},{48,40},{56,64},{64,... | collective-permute-start | bytes 24584 | tf_op jit(solution)/shard_map/ppermute | solution.py:372
  88.7 3.7 %collective-permute-start.14 = (f32[16,128]{1,0:T(8,128)S(1)}, f32[16,128]{1,0:T(8,128)S(1)}, u32[]{:S(2)}, u32[]{:S(2)}) collective-permute-start(f32[16,128]{1,0:T(8,128)S(1)} %get-tuple-element.112), channel_id=1, source_target_pairs={{0,1},{1,0},{2,3},{3,2},{4,5},{5,4},{6,7},{7,6},{8,9},{9,8},{10,11... | collective-permute-start | bytes 24584 | tf_op jit(solution)/shard_map/ppermute | solution.py:375
  94.5 4.6 %collective-permute-start.16 = (f32[16,128]{1,0:T(8,128)S(1)}, f32[16,128]{1,0:T(8,128)S(1)}, u32[]{:S(2)}, u32[]{:S(2)}) collective-permute-start(f32[16,128]{1,0:T(8,128)S(1)} %get-tuple-element.116), channel_id=1, source_target_pairs={{0,8},{8,0},{16,24},{24,16},{32,40},{40,32},{48,56},{56,48},{64,72... | collective-permute-start | bytes 24584 | tf_op jit(solution)/shard_map/ppermute | solution.py:374
  94.5 5.9 %collective-permute-start.17 = (f32[16,128]{1,0:T(8,128)S(1)}, f32[16,128]{1,0:T(8,128)S(1)}, u32[]{:S(2)}, u32[]{:S(2)}) collective-permute-start(f32[16,128]{1,0:T(8,128)S(1)} %get-tuple-element.117), channel_id=1, source_target_pairs={{0,120},{8,16},{16,8},{24,32},{32,24},{40,48},{48,40},{56,64},{64,... | collective-permute-start | bytes 24584 | tf_op jit(solution)/shard_map/ppermute | solution.py:372
  121.9 3.7 %collective-permute-start.20 = (f32[16,128]{1,0:T(8,128)S(1)}, f32[16,128]{1,0:T(8,128)S(1)}, u32[]{:S(2)}, u32[]{:S(2)}) collective-permute-start(f32[16,128]{1,0:T(8,128)S(1)} %get-tuple-element.124), channel_id=1, source_target_pairs={{0,8},{8,0},{16,24},{24,16},{32,40},{40,32},{48,56},{56,48},{64,72... | collective-permute-start | bytes 24584 | tf_op jit(solution)/shard_map/ppermute | solution.py:374
  122.3 5.8 %collective-permute-start.21 = (f32[16,128]{1,0:T(8,128)S(1)}, f32[16,128]{1,0:T(8,128)S(1)}, u32[]{:S(2)}, u32[]{:S(2)}) collective-permute-start(f32[16,128]{1,0:T(8,128)S(1)} %get-tuple-element.125), channel_id=1, source_target_pairs={{0,120},{8,16},{16,8},{24,32},{32,24},{40,48},{48,40},{56,64},{64,... | collective-permute-start | bytes 24584 | tf_op jit(solution)/shard_map/ppermute | solution.py:372
  124.4 3.7 %collective-permute-start.22 = (f32[16,128]{1,0:T(8,128)S(1)}, f32[16,128]{1,0:T(8,128)S(1)}, u32[]{:S(2)}, u32[]{:S(2)}) collective-permute-start(f32[16,128]{1,0:T(8,128)S(1)} %get-tuple-element.126), channel_id=1, source_target_pairs={{0,1},{1,0},{2,3},{3,2},{4,5},{5,4},{6,7},{7,6},{8,9},{9,8},{10,11... | collective-permute-start | bytes 24584 | tf_op jit(solution)/shard_map/ppermute | solution.py:375
  125.4 3.4 %collective-permute-start.23 = (f32[16,128]{1,0:T(8,128)S(1)}, f32[16,128]{1,0:T(8,128)S(1)}, u32[]{:S(2)}, u32[]{:S(2)}) collective-permute-start(f32[16,128]{1,0:T(8,128)S(1)} %get-tuple-element.127), channel_id=1, source_target_pairs={{0,7},{1,2},{2,1},{3,4},{4,3},{5,6},{6,5},{7,0},{8,15},{9,10},{10,... | collective-permute-start | bytes 24584 | tf_op jit(solution)/shard_map/ppermute | solution.py:373
  130.3 4.6 %collective-permute-start.24 = (f32[16,128]{1,0:T(8,128)S(1)}, f32[16,128]{1,0:T(8,128)S(1)}, u32[]{:S(2)}, u32[]{:S(2)}) collective-permute-start(f32[16,128]{1,0:T(8,128)S(1)} %get-tuple-element.130), channel_id=1, source_target_pairs={{0,8},{8,0},{16,24},{24,16},{32,40},{40,32},{48,56},{56,48},{64,72... | collective-permute-start | bytes 24584 | tf_op jit(solution)/shard_map/ppermute | solution.py:374
  130.3 5.9 %collective-permute-start.25 = (f32[16,128]{1,0:T(8,128)S(1)}, f32[16,128]{1,0:T(8,128)S(1)}, u32[]{:S(2)}, u32[]{:S(2)}) collective-permute-start(f32[16,128]{1,0:T(8,128)S(1)} %get-tuple-element.131), channel_id=1, source_target_pairs={{0,120},{8,16},{16,8},{24,32},{32,24},{40,48},{48,40},{56,64},{64,... | collective-permute-start | bytes 24584 | tf_op jit(solution)/shard_map/ppermute | solution.py:372
  157.7 3.7 %collective-permute-start.28 = (f32[16,128]{1,0:T(8,128)S(1)}, f32[16,128]{1,0:T(8,128)S(1)}, u32[]{:S(2)}, u32[]{:S(2)}) collective-permute-start(f32[16,128]{1,0:T(8,128)S(1)} %get-tuple-element.138), channel_id=1, source_target_pairs={{0,8},{8,0},{16,24},{24,16},{32,40},{40,32},{48,56},{56,48},{64,72... | collective-permute-start | bytes 24584 | tf_op jit(solution)/shard_map/ppermute | solution.py:374
  158.1 5.8 %collective-permute-start.29 = (f32[16,128]{1,0:T(8,128)S(1)}, f32[16,128]{1,0:T(8,128)S(1)}, u32[]{:S(2)}, u32[]{:S(2)}) collective-permute-start(f32[16,128]{1,0:T(8,128)S(1)} %get-tuple-element.139), channel_id=1, source_target_pairs={{0,120},{8,16},{16,8},{24,32},{32,24},{40,48},{48,40},{56,64},{64,... | collective-permute-start | bytes 24584 | tf_op jit(solution)/shard_map/ppermute | solution.py:372
  160.2 3.7 %collective-permute-start.30 = (f32[16,128]{1,0:T(8,128)S(1)}, f32[16,128]{1,0:T(8,128)S(1)}, u32[]{:S(2)}, u32[]{:S(2)}) collective-permute-start(f32[16,128]{1,0:T(8,128)S(1)} %get-tuple-element.140), channel_id=1, source_target_pairs={{0,1},{1,0},{2,3},{3,2},{4,5},{5,4},{6,7},{7,6},{8,9},{9,8},{10,11... | collective-permute-start | bytes 24584 | tf_op jit(solution)/shard_map/ppermute | solution.py:375
  (8 other events, 25.2 us)

commit v4 on v3

--- a/solution.py
+++ b/solution.py
@@ -15,9 +15,10 @@
 HALO = 16
 EXT = ROWS + 4 * HALO
 KOFF = 6
+EARLY = 16
 WIDTH = 7 * 128
 jacobi_weight = 2.0 / 3.0
-PAIRS = [(j, l) for j in range(5) for l in range(j, 5)]
+PAIRS = [(j, l) for l in range(5) for j in range(l + 1)]
 
 VM = pl.BlockSpec(memory_space=pltpu.VMEM)
 HBM = pl.BlockSpec(memory_space=pltpu.HBM)
@@ -112,7 +113,7 @@
     copies = [pltpu.make_async_copy(x, y, sems.at[n]) for n, (x, y) in enumerate(zip(sources, here))]
     for c in copies:
         c.start()
-    ahead = pltpu.make_async_copy(off.at[pl.ds(0, ROWS // 2)], near, far)
+    ahead = pltpu.make_async_copy(off.at[pl.ds(0, EARLY)], near, far)
     ahead.start()
     for c in copies:
         c.wait()
@@ -122,14 +123,14 @@
         wj[:, 128 * n : 128 * n + 128] = pair_rows(jac[128 * n : 128 * n + 128, :] * jacobi_weight)
     z[...] = smooth(v[...], wj)
     ze[...] = pack(z[...])
-    odd_x = lax.axis_index("gx") % 2 == 1
-    odd_y = lax.axis_index("gy") % 2 == 1
+    even_x = lax.axis_index("gx") % 2 == 0
+    even_y = lax.axis_index("gy") % 2 == 0
     lists = listed[...].astype(F32)
     order = [
-        jnp.where(odd_x, lists[1:2], lists[0:1]),
-        jnp.where(odd_x, lists[0:1], lists[1:2]),
-        jnp.where(odd_y, lists[3:4], lists[2:3]),
-        jnp.where(odd_y, lists[2:3], lists[3:4]),
+        jnp.where(even_x, lists[1:2], lists[0:1]),
+        jnp.where(even_x, lists[0:1], lists[1:2]),
+        jnp.where(even_y, lists[3:4], lists[2:3]),
+        jnp.where(even_y, lists[2:3], lists[3:4]),
     ]
     chosen = jnp.concatenate([column(x)[0:HALO, 0:ROWS] for x in order], axis=0)
     chosen = (chosen == lax.broadcasted_iota(jnp.int32, (4 * HALO, ROWS), 1).astype(F32)).astype(F32)
@@ -159,8 +160,9 @@
     ahead.wait()
 
 
-def pack_rows(buf, dbuf, n, g, w):
-    at = slice(BS * n, BS * n + 128)
+def pack_rows(buf, n, dbuf, row, w):
+    at = BS * (row % (ROWS // 2))
+    at = slice(at, at + 128)
     for p in range(3):
         x = jnp.concatenate(
             [
@@ -172,23 +174,24 @@
         high = x.astype(BF16)
         w[128 * p : 128 * p + 128, at] = high
         w[384 + 128 * p : 512 + 128 * p, at] = (x - high.astype(F32)).astype(BF16)
-    w[768:896, at] = pair_rows(jnp.concatenate([dbuf[g + n], dbuf[g + n + 1]], axis=0))
+    w[768:896, at] = pair_rows(jnp.concatenate([dbuf[row], dbuf[row + 1]], axis=0))
 
 
 def operator_kernel(off, diag, cols, near, wa, wb, gather, buf, dbuf, cbuf, sems):
-    half = ROWS // 2
+    steps = (ROWS - EARLY) // 8
     named = pltpu.make_async_copy(cols, cbuf, sems.at[0])
     named.start()
     middle = pltpu.make_async_copy(diag, dbuf, sems.at[1])
     middle.start()
     later = [
-        pltpu.make_async_copy(off.at[pl.ds(half + 8 * g, 8)], buf.at[pl.ds(8 * g, 8)], sems.at[2 + g]) for g in range(3)
+        pltpu.make_async_copy(off.at[pl.ds(EARLY + 8 * g, 8)], buf.at[pl.ds(8 * g, 8)], sems.at[2 + g])
+        for g in range(steps)
     ]
     for c in later:
         c.start()
     named.wait()
-    turn_x = (1 - lax.axis_index("gx") % 2) * HALO
-    turn_y = (1 - lax.axis_index("gy") % 2) * HALO
+    turn_x = (lax.axis_index("gx") % 2) * HALO
+    turn_y = (lax.axis_index("gy") % 2) * HALO
     number = cbuf[...]
     beyond = number - ROWS
     turned = ROWS + (beyond ^ jnp.where(beyond < 2 * HALO, turn_x, turn_y))
@@ -200,12 +203,12 @@
         hit = (lane == number[:, 2 * p : 2 * p + 1]) | (lane == number[:, 2 * p + 1 : 2 * p + 2] + 128.0)
         gather[ROWS * p : ROWS * p + ROWS, :] = hit.astype(F32).astype(BF16)
     middle.wait()
-    for n in range(0, half, 2):
-        pack_rows(near, dbuf, n, 0, wa)
-    for g in range(3):
+    for n in range(0, EARLY, 2):
+        pack_rows(near, n, dbuf, n, wa)
+    for g in range(steps):
         later[g].wait()
         for n in range(8 * g, 8 * g + 8, 2):
-            pack_rows(buf, dbuf, n, half, wb)
+            pack_rows(buf, n, dbuf, EARLY + n, wa if EARLY + n < ROWS // 2 else wb)
 
 
 def restrict_kernel(v, ze, h0, h1, h2, h3, wa, wb, gather, ptd, *rest):
@@ -238,16 +241,16 @@
     slot = idc - 24.0 * device
     upper = slot >= 11.5
     place = device * 16.0 + 4.0 + jnp.where(upper, slot - 12.0, slot)
-    total = jnp.zeros((128, 128), F32)
+    high, rest = [], []
     for b in range(8):
         src = x0[16 * b : 16 * b + 16].reshape(256, 128)
-        high = src.astype(BF16)
-        mid = (src - high.astype(F32)).astype(BF16)
-        rest = (src - high.astype(F32) - mid.astype(F32)).astype(BF16)
-        lane = lax.broadcasted_iota(jnp.int32, (128, 256), 1).astype(F32) + 256.0 * b
-        hit = (twice(place) == lane).astype(F32).astype(BF16)
-        got = jnp.dot(hit, jnp.concatenate([high, mid, rest], axis=1), preferred_element_type=F32)
-        total = total + (got[:, 0:128] + got[:, 128:256] + got[:, 256:384])
+        high.append(src.astype(BF16))
+        rest.append((src - high[-1].astype(F32)).astype(BF16))
+    lane = lax.broadcasted_iota(jnp.int32, (128, 128), 1).astype(F32)
+    hit = jnp.concatenate([(place - 128.0 * b == lane).astype(F32).astype(BF16) for b in range(16)], axis=1)
+    source = jnp.concatenate([jnp.concatenate(high, axis=0), jnp.concatenate(rest, axis=0)], axis=1)
+    total = jnp.dot(hit, source, preferred_element_type=F32)
+    total = total[:, 0:128] + total[:, 128:256]
     inverse = jnp.where(upper, swap(total), total)[:EXT]
     wide = []
     for c in range(CW):
@@ -296,16 +299,25 @@
     send_lists(ze[...], pick, (s0, s1, s2, s3))
 
 
-def last_kernel(shifts, ye, h0, h1, h2, h3, wa, wb, gather, v0, v1, v2, v3, v4, gram):
-    v4[...] = advance(3, shifts, v3, ye, h0, h1, h2, h3, (wa, wb), gather)
+def products(basis, pairs):
+    return [jnp.sum(basis[j] * basis[l], axis=0, keepdims=True) for j, l in pairs]
+
+
+def known_kernel(v0, v1, v2, v3, known):
+    basis = [v[...] for v in (v0, v1, v2, v3)]
+    known[...] = jnp.concatenate(products(basis, PAIRS[:10]) + [jnp.zeros((6, 128), F32)], axis=0)
+
+
+def last_kernel(slopes, ye, h0, h1, h2, h3, wa, wb, gather, v0, v1, v2, v3, known, v4, gram):
+    v4[...] = advance(3, slopes, v3, ye, h0, h1, h2, h3, (wa, wb), gather)
     basis = [v[...] for v in (v0, v1, v2, v3, v4)]
-    rows = []
-    for j, l in PAIRS:
-        rows.append(jnp.sum(basis[j] * basis[l], axis=0, keepdims=True))
-    rows.append(jnp.zeros((128 - len(rows), 128), F32))
-    rows = jnp.concatenate(rows, axis=0)
+    rows = [known[0:10, :]] + products(basis, PAIRS[10:]) + [jnp.zeros((113, 128), F32)]
     sums = lax.dot_general(
-        jnp.ones((8, 128), F32), rows, LAST, precision=lax.Precision.HIGHEST, preferred_element_type=F32
+        jnp.ones((8, 128), F32),
+        jnp.concatenate(rows, axis=0),
+        LAST,
+        precision=lax.Precision.HIGHEST,
+        preferred_element_type=F32,
     )
     gram[...] = sums[0:1]
 
@@ -369,11 +381,12 @@
 
 def exchange(sends):
     nx, ny = lax.axis_size("gx"), lax.axis_size("gy")
-    b = lax.ppermute(sends[1], "gx", swap_pairs(nx, 1))
-    d = lax.ppermute(sends[3], "gy", swap_pairs(ny, 1))
-    a = lax.ppermute(sends[0], "gx", swap_pairs(nx, 0))
-    c = lax.ppermute(sends[2], "gy", swap_pairs(ny, 0))
-    return a, b, c, d
+    return (
+        lax.ppermute(sends[0], "gx", swap_pairs(nx, 1)),
+        lax.ppermute(sends[1], "gx", swap_pairs(nx, 0)),
+        lax.ppermute(sends[2], "gy", swap_pairs(ny, 1)),
+        lax.ppermute(sends[3], "gy", swap_pairs(ny, 0)),
+    )
 
 
 def everywhere(x):
@@ -409,7 +422,7 @@
             shape(4, 128),
         ]
         + [shape(6, HALO, 128)] * 4
-        + [kept(ROWS // 2, KOFF, BS, BS)],
+        + [kept(EARLY, KOFF, BS, BS)],
         *[pltpu.with_memory_space_constraint(x, pltpu.HBM) for x in sources],
         matrices[0],
         specs=[HBM] * (len(sources) + 1),
@@ -426,10 +439,10 @@
         near,
         specs=[HBM] * 3 + [VM],
         scratch=[
-            pltpu.VMEM((ROWS // 2, KOFF, BS, BS), F32),
+            pltpu.VMEM((ROWS - EARLY, KOFF, BS, BS), F32),
             pltpu.VMEM((ROWS, BS, BS), F32),
             pltpu.VMEM((KOFF, ROWS), jnp.int32),
-            pltpu.SemaphoreType.DMA((5,)),
+            pltpu.SemaphoreType.DMA((2 + (ROWS - EARLY) // 8,)),
         ],
         flops=2_000_000_000,
         name="operator",
@@ -494,6 +507,7 @@
             )
             basis.append(v)
             around = exchange(sends)
+    (known,) = call(known_kernel, [shape(16, 128)], *basis, flops=500_000_000, name="known")
     v, gram = call(
         last_kernel,
         [shape(ROWS, 128), shape(1, 128)],
@@ -503,6 +517,7 @@
         *w_op,
         gather,
         *basis,
+        known,
         name="last",
     )
     basis.append(v)

time: 183 us -> 182 us (level)
  blocking collectives: 87.7 us -> 97.2 us
  waiting for transfers between devices: 22.4 us -> 16.3 us
  starting transfers between devices: 38.8 us -> 34.6 us
    all_to_all x5, blocking collectives: 87.7 us -> 97.2 us  [everywhere(): lax.all_to_all(y, ('gx', 'gy'), split_axis=0, concat_axis=0, tiled=True)]
    ppermute x32, waiting for transfers between devices: 22.4 us -> 16.3 us  [the longest x8 16.2 us: exchange(): lax.ppermute(sends[0], 'gx', swap_pairs(nx, 1))]
    ppermute x32, starting transfers between devices: 38.8 us -> 34.6 us  [the longest x8 19.9 us: exchange(): lax.ppermute(sends[0], 'gx', swap_pairs(nx, 1))]
    pallas_call x16 -> x17, Pallas kernels: 32.5 us -> 32.4 us  [call(): pl.pallas_call(kernel, out_shape=outs, in_specs=specs or [VM] * len(args)...]
  transfers between devices with their start and end apart: 32 -> 32, of which waited for: 13 -> 7; matrix products, arithmetic and copies ran while one was open for 0% -> 0% of each run, Pallas kernels for 3% -> 3%
where the time goes in v4:
time: 182 us
  blocking collectives  97.2 us (53%)
  starting transfers between devices  34.6 us (19%)
  Pallas kernels  32.4 us (18%)
  waiting for transfers between devices  16.3 us (9%)
    all_to_all x5, blocking collectives, everywhere(): lax.all_to_all(y, ('gx', 'gy'), split_axis=0, concat_axis=0, tiled=True)  97.2 us
    pallas_call x17, Pallas kernels, call(): pl.pallas_call(kernel, out_shape=outs, in_specs=specs or [VM] * len(args)...  32.4 us
    ppermute x8, starting transfers between devices, exchange(): lax.ppermute(sends[0], 'gx', swap_pairs(nx, 1))  19.9 us
    ppermute x8, waiting for transfers between devices, exchange(): lax.ppermute(sends[0], 'gx', swap_pairs(nx, 1))  16.2 us
    ppermute x8, starting transfers between devices, exchange(): lax.ppermute(sends[2], 'gy', swap_pairs(ny, 1))  11.1 us
  transfers between devices with their start and end apart: 32, of which 7 were waited for; matrix products, arithmetic and copies ran while one was open for 0% of the time, Pallas kernels for 3%

profile of v4, /device:TPU:1, one launch (start us, length us, event | category | flops | bytes accessed | tf_op | source)
XLA Modules:
  0.0 181.6 jit_solution(15844111523117243104)
XLA Ops:
  0.6 2.9 %first.1 = (f32[48,128]{1,0:T(8,128)S(1)}, bf16[128,3072]{1,0:T(8,128)(2,1)S(1)}, f32[8,48,128]{2,1,0:T(8,128)S(1)}, bf16[64,48]{1,0:T(8,128)(2,1)S(1)}, f32[48,...) custom-call(f32[48,64]{1,0:T(8,128)} %refs_0_.1, ...), custom_call_target="tpu_custom_call" | custom-call | flops 2000000 | bytes 100000 | tf_op jit(solution)/shard_map/first/pallas_call | solution.py:364
  3.5 6.9 %collective-permute-start = (f32[6,16,128]{2,1,0:T(8,128)S(1)}, f32[6,16,128]{2,1,0:T(8,128)S(1)}, u32[]{:S(2)}, u32[]{:S(2)}) collective-permute-start(f32[6,16,128]{2,1,0:T(8,128)S(1)} %get-tuple-element.76), channel_id=1, source_target_pairs={{0,120},{8,16},{16,8},{24,32},{32,24},{40,48},{48,40},{56,64},{64,... | collective-permute-start | bytes 147464 | tf_op jit(solution)/shard_map/ppermute | solution.py:385
  10.4 2.1 %collective-permute-start.2 = (f32[6,16,128]{2,1,0:T(8,128)S(1)}, f32[6,16,128]{2,1,0:T(8,128)S(1)}, u32[]{:S(2)}, u32[]{:S(2)}) collective-permute-start(f32[6,16,128]{2,1,0:T(8,128)S(1)} %get-tuple-element.78), channel_id=1, source_target_pairs={{0,7},{1,2},{2,1},{3,4},{4,3},{5,6},{6,5},{7,0},{8,15},{9,10},{10,... | collective-permute-start | bytes 147464 | tf_op jit(solution)/shard_map/ppermute | solution.py:387
  13.5 5.2 %operator.1 = (bf16[896,1536]{1,0:T(8,128)(2,1)S(1)}, bf16[896,1536]{1,0:T(8,128)(2,1)S(1)}, bf16[144,256]{1,0:T(8,128)(2,1)S(1)}) custom-call(f32[48,6,64,64]{3,2,1,0:T(8,128)} %off.1, f32[48,64,64]{2,1,0:T(8,128)} %diag.1, s32[6,48]{1,0:T(8,128)} %bitcast.31, f32[16,6,64,64]{3,2,1,0:T(8,128)S(1)} %get-tuple-element.80.near), custom_call_target="tpu_custom_call" | custom-call | flops 2000000000 | bytes 100000 | tf_op jit(solution)/shard_map/operator/pallas_call | solution.py:364
  20.2 23.9 %all_to_all.25.x0 = f32[128,16,128]{2,1,0:T(8,128)S(1)} all-to-all(f32[128,16,128]{2,1,0:T(8,128)S(1)} %broadcast_in_dim.12), channel_id=1, replica_groups=mesh['gx'=16,'gy'=8] {'gx','gy'}, dimensions={0} | all-to-all | bytes 2097152 | tf_op jit(solution)/shard_map/all_to_all | solution.py:395
  44.1 2.7 %coarse.1 = (bf16[8192,128]{1,0:T(8,128)(2,1)S(1)}, f32[8,112,128]{2,1,0:T(8,128)S(1)}, f32[64,8,128]{2,1,0:T(8,128)S(1)}) custom-call(f32[128,16,128]{2,1,0:T(8,128)S(1)} %all_to_all.25.x0, f32[48,128]{1,0:T(8,128)S(1)} %get-tuple-element.87.ids, f32[8,48,128]{2,1,0:T(8,128)S(1)} %get-tuple-element.84.ptd, f32[6,16,128]{2,1,0:T(8,128)S(1)} %collective-permute-done.g0, ...), custom_call_target="tpu_custom_call" | custom-call | flops 2000000 | bytes 100000 | tf_op jit(solution)/shard_map/coarse/pallas_call | solution.py:364
  46.8 2.3 %correct.4 = (f32[48,128]{1,0:T(8,128)S(1)}, f32[16,128]{1,0:T(8,128)S(1)}, f32[16,128]{1,0:T(8,128)S(1)}, f32[16,128]{1,0:T(8,128)S(1)}, f32[16,128]{1,0:T(8,128)S(1)}) custom-call(f32[64,8,128]{2,1,0:T(8,128)S(1)} %get-tuple-element.88.x, bf16[8192,128]{1,0:T(8,128)(2,1)S(1)} %get-tuple-element.89.mask, f32[8,112,128]{2,1,0:T(8,128)S(1)} %get-tuple-element.90.pte, ...), custom_call_target="tpu_custom_call" | custom-call | flops 2000000 | bytes 100000 | tf_op jit(solution)/shard_map/correct/pallas_call | solution.py:364
  51.5 3.5 %collective-permute-done.4.h0 = f32[16,128]{1,0:T(8,128)S(1)} collective-permute-done((f32[16,128]{1,0:T(8,128)S(1)}, f32[16,128]{1,0:T(8,128)S(1)}, u32[]{:S(2)}, u32[]{:S(2)}) %collective-permute-start.4) | collective-permute-done | bytes 8224 | tf_op jit(solution)/shard_map/ppermute | solution.py:385
  56.5 2.3 %collective-permute-start.8 = (f32[16,128]{1,0:T(8,128)S(1)}, f32[16,128]{1,0:T(8,128)S(1)}, u32[]{:S(2)}, u32[]{:S(2)}) collective-permute-start(f32[16,128]{1,0:T(8,128)S(1)} %get-tuple-element.102), channel_id=1, source_target_pairs={{0,120},{8,16},{16,8},{24,32},{32,24},{40,48},{48,40},{56,64},{64,... | collective-permute-start | bytes 24584 | tf_op jit(solution)/shard_map/ppermute | solution.py:385
  58.8 2.0 %collective-permute-start.10 = (f32[16,128]{1,0:T(8,128)S(1)}, f32[16,128]{1,0:T(8,128)S(1)}, u32[]{:S(2)}, u32[]{:S(2)}) collective-permute-start(f32[16,128]{1,0:T(8,128)S(1)} %get-tuple-element.104), channel_id=1, source_target_pairs={{0,7},{1,2},{2,1},{3,4},{4,3},{5,6},{6,5},{7,0},{8,15},{9,10},{10,... | collective-permute-start | bytes 24584 | tf_op jit(solution)/shard_map/ppermute | solution.py:387
  63.7 19.1 %all_to_all.26 = f32[128,4,128]{2,1,0:T(4,128)S(1)} all-to-all(f32[128,4,128]{2,1,0:T(4,128)S(1)} %broadcast_in_dim.13), channel_id=1, replica_groups=mesh['gx'=16,'gy'=8] {'gx','gy'}, dimensions={0} | all-to-all | bytes 524288 | tf_op jit(solution)/shard_map/all_to_all | solution.py:395
  82.8 2.3 %correct.5 = (f32[48,128]{1,0:T(8,128)S(1)}, f32[16,128]{1,0:T(8,128)S(1)}, f32[16,128]{1,0:T(8,128)S(1)}, f32[16,128]{1,0:T(8,128)S(1)}, f32[16,128]{1,0:T(8,128)S(1)}) custom-call(f32[64,8,128]{2,1,0:T(8,128)S(1)} %bitcast.24, bf16[8192,128]{1,0:T(8,128)(2,1)S(1)} %get-tuple-element.89.mask, f32[8,112,128]{2,1,0:T(8,128)S(1)} %get-tuple-element.90.pte, ...), custom_call_target="tpu_custom_call" | custom-call | flops 2000000 | bytes 100000 | tf_op jit(solution)/shard_map/correct/pallas_call | solution.py:364
  87.6 3.4 %collective-permute-done.12.h0 = f32[16,128]{1,0:T(8,128)S(1)} collective-permute-done((f32[16,128]{1,0:T(8,128)S(1)}, f32[16,128]{1,0:T(8,128)S(1)}, u32[]{:S(2)}, u32[]{:S(2)}) %collective-permute-start.12) | collective-permute-done | bytes 8224 | tf_op jit(solution)/shard_map/ppermute | solution.py:385
  92.5 2.3 %collective-permute-start.16 = (f32[16,128]{1,0:T(8,128)S(1)}, f32[16,128]{1,0:T(8,128)S(1)}, u32[]{:S(2)}, u32[]{:S(2)}) collective-permute-start(f32[16,128]{1,0:T(8,128)S(1)} %get-tuple-element.116), channel_id=1, source_target_pairs={{0,120},{8,16},{16,8},{24,32},{32,24},{40,48},{48,40},{56,64},{64,... | collective-permute-start | bytes 24584 | tf_op jit(solution)/shard_map/ppermute | solution.py:385
  94.8 1.8 %collective-permute-start.18 = (f32[16,128]{1,0:T(8,128)S(1)}, f32[16,128]{1,0:T(8,128)S(1)}, u32[]{:S(2)}, u32[]{:S(2)}) collective-permute-start(f32[16,128]{1,0:T(8,128)S(1)} %get-tuple-element.118), channel_id=1, source_target_pairs={{0,7},{1,2},{2,1},{3,4},{4,3},{5,6},{6,5},{7,0},{8,15},{9,10},{10,... | collective-permute-start | bytes 24584 | tf_op jit(solution)/shard_map/ppermute | solution.py:387
  99.7 18.9 %all_to_all.27 = f32[128,4,128]{2,1,0:T(4,128)S(1)} all-to-all(f32[128,4,128]{2,1,0:T(4,128)S(1)} %broadcast_in_dim.14), channel_id=1, replica_groups=mesh['gx'=16,'gy'=8] {'gx','gy'}, dimensions={0} | all-to-all | bytes 524288 | tf_op jit(solution)/shard_map/all_to_all | solution.py:395
  118.6 2.3 %correct.6 = (f32[48,128]{1,0:T(8,128)S(1)}, f32[16,128]{1,0:T(8,128)S(1)}, f32[16,128]{1,0:T(8,128)S(1)}, f32[16,128]{1,0:T(8,128)S(1)}, f32[16,128]{1,0:T(8,128)S(1)}) custom-call(f32[64,8,128]{2,1,0:T(8,128)S(1)} %bitcast.25, bf16[8192,128]{1,0:T(8,128)(2,1)S(1)} %get-tuple-element.89.mask, f32[8,112,128]{2,1,0:T(8,128)S(1)} %get-tuple-element.90.pte, ...), custom_call_target="tpu_custom_call" | custom-call | flops 2000000 | bytes 100000 | tf_op jit(solution)/shard_map/correct/pallas_call | solution.py:364
  123.4 3.4 %collective-permute-done.20.h0 = f32[16,128]{1,0:T(8,128)S(1)} collective-permute-done((f32[16,128]{1,0:T(8,128)S(1)}, f32[16,128]{1,0:T(8,128)S(1)}, u32[]{:S(2)}, u32[]{:S(2)}) %collective-permute-start.20) | collective-permute-done | bytes 8224 | tf_op jit(solution)/shard_map/ppermute | solution.py:385
  128.3 2.3 %collective-permute-start.24 = (f32[16,128]{1,0:T(8,128)S(1)}, f32[16,128]{1,0:T(8,128)S(1)}, u32[]{:S(2)}, u32[]{:S(2)}) collective-permute-start(f32[16,128]{1,0:T(8,128)S(1)} %get-tuple-element.130), channel_id=1, source_target_pairs={{0,120},{8,16},{16,8},{24,32},{32,24},{40,48},{48,40},{56,64},{64,... | collective-permute-start | bytes 24584 | tf_op jit(solution)/shard_map/ppermute | solution.py:385
  130.6 1.8 %collective-permute-start.26 = (f32[16,128]{1,0:T(8,128)S(1)}, f32[16,128]{1,0:T(8,128)S(1)}, u32[]{:S(2)}, u32[]{:S(2)}) collective-permute-start(f32[16,128]{1,0:T(8,128)S(1)} %get-tuple-element.132), channel_id=1, source_target_pairs={{0,7},{1,2},{2,1},{3,4},{4,3},{5,6},{6,5},{7,0},{8,15},{9,10},{10,... | collective-permute-start | bytes 24584 | tf_op jit(solution)/shard_map/ppermute | solution.py:387
  135.5 18.9 %all_to_all.28 = f32[128,4,128]{2,1,0:T(4,128)S(1)} all-to-all(f32[128,4,128]{2,1,0:T(4,128)S(1)} %broadcast_in_dim.15), channel_id=1, replica_groups=mesh['gx'=16,'gy'=8] {'gx','gy'}, dimensions={0} | all-to-all | bytes 524288 | tf_op jit(solution)/shard_map/all_to_all | solution.py:395
  154.4 2.3 %correct.7 = (f32[48,128]{1,0:T(8,128)S(1)}, f32[16,128]{1,0:T(8,128)S(1)}, f32[16,128]{1,0:T(8,128)S(1)}, f32[16,128]{1,0:T(8,128)S(1)}, f32[16,128]{1,0:T(8,128)S(1)}) custom-call(f32[64,8,128]{2,1,0:T(8,128)S(1)} %bitcast.23, bf16[8192,128]{1,0:T(8,128)(2,1)S(1)} %get-tuple-element.89.mask, f32[8,112,128]{2,1,0:T(8,128)S(1)} %get-tuple-element.90.pte, ...), custom_call_target="tpu_custom_call" | custom-call | flops 2000000 | bytes 100000 | tf_op jit(solution)/shard_map/correct/pallas_call | solution.py:364
  159.2 3.3 %collective-permute-done.28.h0 = f32[16,128]{1,0:T(8,128)S(1)} collective-permute-done((f32[16,128]{1,0:T(8,128)S(1)}, f32[16,128]{1,0:T(8,128)S(1)}, u32[]{:S(2)}, u32[]{:S(2)}) %collective-permute-start.28) | collective-permute-done | bytes 8224 | tf_op jit(solution)/shard_map/ppermute | solution.py:385
  163.9 16.4 %all_to_all.29 = f32[128,1,128]{2,1,0:T(1,128)S(1)} all-to-all(f32[128,1,128]{2,1,0:T(1,128)S(1)} %broadcast_in_dim.17), channel_id=1, replica_groups=mesh['gx'=16,'gy'=8] {'gx','gy'}, dimensions={0} | all-to-all | bytes 131072 | tf_op jit(solution)/shard_map/all_to_all | solution.py:395
  (71 shorter events, 28.4 us)
Async XLA Ops:
  3.5 15.2 %collective-permute-start = (f32[6,16,128]{2,1,0:T(8,128)S(1)}, f32[6,16,128]{2,1,0:T(8,128)S(1)}, u32[]{:S(2)}, u32[]{:S(2)}) collective-permute-start(f32[6,16,128]{2,1,0:T(8,128)S(1)} %get-tuple-element.76), channel_id=1, source_target_pairs={{0,120},{8,16},{16,8},{24,32},{32,24},{40,48},{48,40},{56,64},{64,... | collective-permute-start | bytes 147464 | tf_op jit(solution)/shard_map/ppermute | solution.py:385
  10.4 8.3 %collective-permute-start.1 = (f32[6,16,128]{2,1,0:T(8,128)S(1)}, f32[6,16,128]{2,1,0:T(8,128)S(1)}, u32[]{:S(2)}, u32[]{:S(2)}) collective-permute-start(f32[6,16,128]{2,1,0:T(8,128)S(1)} %get-tuple-element.77), channel_id=1, source_target_pairs={{0,8},{8,0},{16,24},{24,16},{32,40},{40,32},{48,56},{56,48},{64,72... | collective-permute-start | bytes 147464 | tf_op jit(solution)/shard_map/ppermute | solution.py:386
  10.4 8.4 %collective-permute-start.2 = (f32[6,16,128]{2,1,0:T(8,128)S(1)}, f32[6,16,128]{2,1,0:T(8,128)S(1)}, u32[]{:S(2)}, u32[]{:S(2)}) collective-permute-start(f32[6,16,128]{2,1,0:T(8,128)S(1)} %get-tuple-element.78), channel_id=1, source_target_pairs={{0,7},{1,2},{2,1},{3,4},{4,3},{5,6},{6,5},{7,0},{8,15},{9,10},{10,... | collective-permute-start | bytes 147464 | tf_op jit(solution)/shard_map/ppermute | solution.py:387
  12.5 6.2 %collective-permute-start.3 = (f32[6,16,128]{2,1,0:T(8,128)S(1)}, f32[6,16,128]{2,1,0:T(8,128)S(1)}, u32[]{:S(2)}, u32[]{:S(2)}) collective-permute-start(f32[6,16,128]{2,1,0:T(8,128)S(1)} %get-tuple-element.79), channel_id=1, source_target_pairs={{0,1},{1,0},{2,3},{3,2},{4,5},{5,4},{6,7},{7,6},{8,9},{9,8},{10,11... | collective-permute-start | bytes 147464 | tf_op jit(solution)/shard_map/ppermute | solution.py:388
  49.1 5.8 %collective-permute-start.4 = (f32[16,128]{1,0:T(8,128)S(1)}, f32[16,128]{1,0:T(8,128)S(1)}, u32[]{:S(2)}, u32[]{:S(2)}) collective-permute-start(f32[16,128]{1,0:T(8,128)S(1)} %get-tuple-element.96), channel_id=1, source_target_pairs={{0,120},{8,16},{16,8},{24,32},{32,24},{40,48},{48,40},{56,64},{64,... | collective-permute-start | bytes 24584 | tf_op jit(solution)/shard_map/ppermute | solution.py:385
  50.5 4.4 %collective-permute-start.5 = (f32[16,128]{1,0:T(8,128)S(1)}, f32[16,128]{1,0:T(8,128)S(1)}, u32[]{:S(2)}, u32[]{:S(2)}) collective-permute-start(f32[16,128]{1,0:T(8,128)S(1)} %get-tuple-element.97), channel_id=1, source_target_pairs={{0,8},{8,0},{16,24},{24,16},{32,40},{40,32},{48,56},{56,48},{64,72... | collective-permute-start | bytes 24584 | tf_op jit(solution)/shard_map/ppermute | solution.py:386
  50.5 4.4 %collective-permute-start.6 = (f32[16,128]{1,0:T(8,128)S(1)}, f32[16,128]{1,0:T(8,128)S(1)}, u32[]{:S(2)}, u32[]{:S(2)}) collective-permute-start(f32[16,128]{1,0:T(8,128)S(1)} %get-tuple-element.98), channel_id=1, source_target_pairs={{0,7},{1,2},{2,1},{3,4},{4,3},{5,6},{6,5},{7,0},{8,15},{9,10},{10,... | collective-permute-start | bytes 24584 | tf_op jit(solution)/shard_map/ppermute | solution.py:387
  51.1 3.9 %collective-permute-start.7 = (f32[16,128]{1,0:T(8,128)S(1)}, f32[16,128]{1,0:T(8,128)S(1)}, u32[]{:S(2)}, u32[]{:S(2)}) collective-permute-start(f32[16,128]{1,0:T(8,128)S(1)} %get-tuple-element.99), channel_id=1, source_target_pairs={{0,1},{1,0},{2,3},{3,2},{4,5},{5,4},{6,7},{7,6},{8,9},{9,8},{10,11... | collective-permute-start | bytes 24584 | tf_op jit(solution)/shard_map/ppermute | solution.py:388
  56.5 5.8 %collective-permute-start.8 = (f32[16,128]{1,0:T(8,128)S(1)}, f32[16,128]{1,0:T(8,128)S(1)}, u32[]{:S(2)}, u32[]{:S(2)}) collective-permute-start(f32[16,128]{1,0:T(8,128)S(1)} %get-tuple-element.102), channel_id=1, source_target_pairs={{0,120},{8,16},{16,8},{24,32},{32,24},{40,48},{48,40},{56,64},{64,... | collective-permute-start | bytes 24584 | tf_op jit(solution)/shard_map/ppermute | solution.py:385
  58.8 3.5 %collective-permute-start.9 = (f32[16,128]{1,0:T(8,128)S(1)}, f32[16,128]{1,0:T(8,128)S(1)}, u32[]{:S(2)}, u32[]{:S(2)}) collective-permute-start(f32[16,128]{1,0:T(8,128)S(1)} %get-tuple-element.103), channel_id=1, source_target_pairs={{0,8},{8,0},{16,24},{24,16},{32,40},{40,32},{48,56},{56,48},{64,72... | collective-permute-start | bytes 24584 | tf_op jit(solution)/shard_map/ppermute | solution.py:386
  58.8 3.5 %collective-permute-start.10 = (f32[16,128]{1,0:T(8,128)S(1)}, f32[16,128]{1,0:T(8,128)S(1)}, u32[]{:S(2)}, u32[]{:S(2)}) collective-permute-start(f32[16,128]{1,0:T(8,128)S(1)} %get-tuple-element.104), channel_id=1, source_target_pairs={{0,7},{1,2},{2,1},{3,4},{4,3},{5,6},{6,5},{7,0},{8,15},{9,10},{10,... | collective-permute-start | bytes 24584 | tf_op jit(solution)/shard_map/ppermute | solution.py:387
  85.1 5.8 %collective-permute-start.12 = (f32[16,128]{1,0:T(8,128)S(1)}, f32[16,128]{1,0:T(8,128)S(1)}, u32[]{:S(2)}, u32[]{:S(2)}) collective-permute-start(f32[16,128]{1,0:T(8,128)S(1)} %get-tuple-element.110), channel_id=1, source_target_pairs={{0,120},{8,16},{16,8},{24,32},{32,24},{40,48},{48,40},{56,64},{64,... | collective-permute-start | bytes 24584 | tf_op jit(solution)/shard_map/ppermute | solution.py:385
  86.7 4.3 %collective-permute-start.13 = (f32[16,128]{1,0:T(8,128)S(1)}, f32[16,128]{1,0:T(8,128)S(1)}, u32[]{:S(2)}, u32[]{:S(2)}) collective-permute-start(f32[16,128]{1,0:T(8,128)S(1)} %get-tuple-element.111), channel_id=1, source_target_pairs={{0,8},{8,0},{16,24},{24,16},{32,40},{40,32},{48,56},{56,48},{64,72... | collective-permute-start | bytes 24584 | tf_op jit(solution)/shard_map/ppermute | solution.py:386
  86.7 4.3 %collective-permute-start.14 = (f32[16,128]{1,0:T(8,128)S(1)}, f32[16,128]{1,0:T(8,128)S(1)}, u32[]{:S(2)}, u32[]{:S(2)}) collective-permute-start(f32[16,128]{1,0:T(8,128)S(1)} %get-tuple-element.112), channel_id=1, source_target_pairs={{0,7},{1,2},{2,1},{3,4},{4,3},{5,6},{6,5},{7,0},{8,15},{9,10},{10,... | collective-permute-start | bytes 24584 | tf_op jit(solution)/shard_map/ppermute | solution.py:387
  92.5 5.8 %collective-permute-start.16 = (f32[16,128]{1,0:T(8,128)S(1)}, f32[16,128]{1,0:T(8,128)S(1)}, u32[]{:S(2)}, u32[]{:S(2)}) collective-permute-start(f32[16,128]{1,0:T(8,128)S(1)} %get-tuple-element.116), channel_id=1, source_target_pairs={{0,120},{8,16},{16,8},{24,32},{32,24},{40,48},{48,40},{56,64},{64,... | collective-permute-start | bytes 24584 | tf_op jit(solution)/shard_map/ppermute | solution.py:385
  94.8 3.5 %collective-permute-start.17 = (f32[16,128]{1,0:T(8,128)S(1)}, f32[16,128]{1,0:T(8,128)S(1)}, u32[]{:S(2)}, u32[]{:S(2)}) collective-permute-start(f32[16,128]{1,0:T(8,128)S(1)} %get-tuple-element.117), channel_id=1, source_target_pairs={{0,8},{8,0},{16,24},{24,16},{32,40},{40,32},{48,56},{56,48},{64,72... | collective-permute-start | bytes 24584 | tf_op jit(solution)/shard_map/ppermute | solution.py:386
  94.8 3.5 %collective-permute-start.18 = (f32[16,128]{1,0:T(8,128)S(1)}, f32[16,128]{1,0:T(8,128)S(1)}, u32[]{:S(2)}, u32[]{:S(2)}) collective-permute-start(f32[16,128]{1,0:T(8,128)S(1)} %get-tuple-element.118), channel_id=1, source_target_pairs={{0,7},{1,2},{2,1},{3,4},{4,3},{5,6},{6,5},{7,0},{8,15},{9,10},{10,... | collective-permute-start | bytes 24584 | tf_op jit(solution)/shard_map/ppermute | solution.py:387
  120.9 5.8 %collective-permute-start.20 = (f32[16,128]{1,0:T(8,128)S(1)}, f32[16,128]{1,0:T(8,128)S(1)}, u32[]{:S(2)}, u32[]{:S(2)}) collective-permute-start(f32[16,128]{1,0:T(8,128)S(1)} %get-tuple-element.124), channel_id=1, source_target_pairs={{0,120},{8,16},{16,8},{24,32},{32,24},{40,48},{48,40},{56,64},{64,... | collective-permute-start | bytes 24584 | tf_op jit(solution)/shard_map/ppermute | solution.py:385
  122.5 4.3 %collective-permute-start.21 = (f32[16,128]{1,0:T(8,128)S(1)}, f32[16,128]{1,0:T(8,128)S(1)}, u32[]{:S(2)}, u32[]{:S(2)}) collective-permute-start(f32[16,128]{1,0:T(8,128)S(1)} %get-tuple-element.125), channel_id=1, source_target_pairs={{0,8},{8,0},{16,24},{24,16},{32,40},{40,32},{48,56},{56,48},{64,72... | collective-permute-start | bytes 24584 | tf_op jit(solution)/shard_map/ppermute | solution.py:386
  122.5 4.3 %collective-permute-start.22 = (f32[16,128]{1,0:T(8,128)S(1)}, f32[16,128]{1,0:T(8,128)S(1)}, u32[]{:S(2)}, u32[]{:S(2)}) collective-permute-start(f32[16,128]{1,0:T(8,128)S(1)} %get-tuple-element.126), channel_id=1, source_target_pairs={{0,7},{1,2},{2,1},{3,4},{4,3},{5,6},{6,5},{7,0},{8,15},{9,10},{10,... | collective-permute-start | bytes 24584 | tf_op jit(solution)/shard_map/ppermute | solution.py:387
  128.3 5.8 %collective-permute-start.24 = (f32[16,128]{1,0:T(8,128)S(1)}, f32[16,128]{1,0:T(8,128)S(1)}, u32[]{:S(2)}, u32[]{:S(2)}) collective-permute-start(f32[16,128]{1,0:T(8,128)S(1)} %get-tuple-element.130), channel_id=1, source_target_pairs={{0,120},{8,16},{16,8},{24,32},{32,24},{40,48},{48,40},{56,64},{64,... | collective-permute-start | bytes 24584 | tf_op jit(solution)/shard_map/ppermute | solution.py:385
  156.7 5.8 %collective-permute-start.28 = (f32[16,128]{1,0:T(8,128)S(1)}, f32[16,128]{1,0:T(8,128)S(1)}, u32[]{:S(2)}, u32[]{:S(2)}) collective-permute-start(f32[16,128]{1,0:T(8,128)S(1)} %get-tuple-element.138), channel_id=1, source_target_pairs={{0,120},{8,16},{16,8},{24,32},{32,24},{40,48},{48,40},{56,64},{64,... | collective-permute-start | bytes 24584 | tf_op jit(solution)/shard_map/ppermute | solution.py:385
  158.2 4.3 %collective-permute-start.29 = (f32[16,128]{1,0:T(8,128)S(1)}, f32[16,128]{1,0:T(8,128)S(1)}, u32[]{:S(2)}, u32[]{:S(2)}) collective-permute-start(f32[16,128]{1,0:T(8,128)S(1)} %get-tuple-element.139), channel_id=1, source_target_pairs={{0,8},{8,0},{16,24},{24,16},{32,40},{40,32},{48,56},{56,48},{64,72... | collective-permute-start | bytes 24584 | tf_op jit(solution)/shard_map/ppermute | solution.py:386
  158.2 4.3 %collective-permute-start.30 = (f32[16,128]{1,0:T(8,128)S(1)}, f32[16,128]{1,0:T(8,128)S(1)}, u32[]{:S(2)}, u32[]{:S(2)}) collective-permute-start(f32[16,128]{1,0:T(8,128)S(1)} %get-tuple-element.140), channel_id=1, source_target_pairs={{0,7},{1,2},{2,1},{3,4},{4,3},{5,6},{6,5},{7,0},{8,15},{9,10},{10,... | collective-permute-start | bytes 24584 | tf_op jit(solution)/shard_map/ppermute | solution.py:387
  (8 other events, 22.0 us)

commit v5 on v4

--- a/solution.py
+++ b/solution.py
@@ -16,6 +16,7 @@
 EXT = ROWS + 4 * HALO
 KOFF = 6
 EARLY = 16
+OWN = 6 * 128
 WIDTH = 7 * 128
 jacobi_weight = 2.0 / 3.0
 PAIRS = [(j, l) for l in range(5) for j in range(l + 1)]
@@ -48,12 +49,14 @@
     return jnp.where(low, packed, turned), jnp.where(low, turned, 0.0)
 
 
-def row_blocks(top, bottom, w_ref):
+def row_blocks(top, bottom, w_ref, first=0):
     out = []
     for g in range(ROWS // 8):
         lhs = jnp.concatenate([top[8 * g : 8 * g + 8], bottom[8 * g : 8 * g + 8]], axis=0).astype(BF16)
         ref, n = (w_ref[g // 3], g % 3) if isinstance(w_ref, tuple) else (w_ref, g)
-        r = jnp.dot(lhs, ref[:, 512 * n : 512 * n + 512], preferred_element_type=F32)
+        r = jnp.dot(
+            lhs, ref[first : first + top.shape[1], 512 * n : 512 * n + 512], preferred_element_type=F32
+        )
         s = r[:8] + r[8:]
         own = lax.broadcasted_iota(jnp.int32, s.shape, 0) == lax.broadcasted_iota(jnp.int32, s.shape, 1) // BS
         s = jnp.where(own, s, 0.0)
@@ -67,7 +70,12 @@
     return row_blocks(top, bottom, wj_ref)
 
 
-def operate(packed, w_ref, gather_ref):
+def operate_own(packed, w_ref):
+    top, bottom = lhs_parts(packed)
+    return row_blocks(top, bottom, w_ref, OWN)
+
+
+def operate(packed, w_ref, gather_ref, own=True):
     e = jnp.concatenate([packed, jnp.zeros((128 - EXT, 128), F32)], axis=0)
     s = swap(e)
     low = low_lanes(e)
@@ -82,11 +90,12 @@
     x = jnp.dot(gather_ref[...], rhs, preferred_element_type=F32)
     high = [x[ROWS * p : ROWS * p + ROWS, 0:128] for p in range(3)]
     rest = [x[ROWS * p : ROWS * p + ROWS, 128:256] for p in range(3)]
-    top, bottom = lhs_parts(packed[:ROWS])
     none = [jnp.zeros((ROWS, 128), F32)] * 3
-    return row_blocks(
-        jnp.concatenate(high + high + [top], axis=1), jnp.concatenate(rest + none + [bottom], axis=1), w_ref
-    )
+    top, bottom = high + high, rest + none
+    if own:
+        for x, part in zip((top, bottom), lhs_parts(packed[:ROWS])):
+            x.append(part)
+    return row_blocks(jnp.concatenate(top, axis=1), jnp.concatenate(bottom, axis=1), w_ref)
 
 
 def send_lists(packed, pick_ref, outs):
@@ -211,10 +220,18 @@
             pack_rows(buf, n, dbuf, EARLY + n, wa if EARLY + n < ROWS // 2 else wb)
 
 
-def restrict_kernel(v, ze, h0, h1, h2, h3, wa, wb, gather, ptd, *rest):
+def before_restrict(v, ze, wa, wb, base):
+    base[...] = v[...] - operate_own(ze[...], (wa, wb))
+
+
+def before_advance(k, slopes, v, ye, wa, wb, base):
+    base[...] = operate_own(ye[...], (wa, wb)) - slopes[k : k + 1, :] * v[...]
+
+
+def restrict_kernel(base, ze, h0, h1, h2, h3, wa, wb, gather, ptd, *rest):
     *extra, w, p = rest
     ext = jnp.concatenate([ze[...], h0[...], h1[...], h2[...], h3[...]], axis=0)
-    r = v[...] - operate(ext, (wa, wb), gather)
+    r = base[...] - operate(ext, (wa, wb), gather, own=False)
     w[...] = r
     ones = jnp.ones((16, 128), BF16)
     pad = jnp.zeros((16, 128), F32)
@@ -287,13 +304,13 @@
     send_lists(ye[...], pick, (s0, s1, s2, s3))
 
 
-def advance(k, shifts, v, ye, h0, h1, h2, h3, w_op, gather):
+def advance(base, ye, h0, h1, h2, h3, w_op, gather):
     ext = jnp.concatenate([ye[...], h0[...], h1[...], h2[...], h3[...]], axis=0)
-    return operate(ext, w_op, gather) - shifts[k : k + 1, :] * v[...]
-
-
-def advance_kernel(k, shifts, v, ye, h0, h1, h2, h3, wa, wb, gather, wj, pick, vn, z, ze, s0, s1, s2, s3):
-    vn[...] = advance(k, shifts, v, ye, h0, h1, h2, h3, (wa, wb), gather)
+    return operate(ext, w_op, gather, own=False) + base[...]
+
+
+def advance_kernel(base, ye, h0, h1, h2, h3, wa, wb, gather, wj, pick, vn, z, ze, s0, s1, s2, s3):
+    vn[...] = advance(base, ye, h0, h1, h2, h3, (wa, wb), gather)
     z[...] = smooth(vn[...], wj)
     ze[...] = pack(z[...])
     send_lists(ze[...], pick, (s0, s1, s2, s3))
@@ -308,8 +325,8 @@
     known[...] = jnp.concatenate(products(basis, PAIRS[:10]) + [jnp.zeros((6, 128), F32)], axis=0)
 
 
-def last_kernel(slopes, ye, h0, h1, h2, h3, wa, wb, gather, v0, v1, v2, v3, known, v4, gram):
-    v4[...] = advance(3, slopes, v3, ye, h0, h1, h2, h3, (wa, wb), gather)
+def last_kernel(base, ye, h0, h1, h2, h3, wa, wb, gather, v0, v1, v2, v3, known, v4, gram):
+    v4[...] = advance(base, ye, h0, h1, h2, h3, (wa, wb), gather)
     basis = [v[...] for v in (v0, v1, v2, v3, v4)]
     rows = [known[0:10, :]] + products(basis, PAIRS[10:]) + [jnp.zeros((113, 128), F32)]
     sums = lax.dot_general(
@@ -451,10 +468,11 @@
     basis = [v]
     mask = pte = None
     for k in range(4):
+        (base,) = call(before_restrict, [shape(ROWS, 128)], v, ze, *w_op, flops=500_000_000, name="before_restrict")
         w, p = call(
             restrict_kernel,
             [shape(ROWS, 128), shape(4 if k else 16, 128)],
-            v,
+            base,
             ze,
             *around,
             *w_op,
@@ -491,12 +509,21 @@
             name="correct",
         )
         around = exchange(sends)
+        (base,) = call(
+            functools.partial(before_advance, k),
+            [shape(ROWS, 128)],
+            slopes,
+            v,
+            ye,
+            *w_op,
+            flops=500_000_000,
+            name="before_advance",
+        )
         if k < 3:
             v, z, ze, *sends = call(
-                functools.partial(advance_kernel, k),
+                advance_kernel,
                 [shape(ROWS, 128)] * 3 + halo,
-                slopes,
-                v,
+                base,
                 ye,
                 *around,
                 *w_op,
@@ -511,7 +538,7 @@
     v, gram = call(
         last_kernel,
         [shape(ROWS, 128), shape(1, 128)],
-        slopes,
+        base,
         ye,
         *around,
         *w_op,

time: 182 us -> 192 us (1.055)
  blocking collectives: 97.2 us -> 78.2 us
  local copies, waits for them, and re-layouts: 0.37 us -> 12.6 us
  starting transfers between devices: 34.6 us -> 43.2 us
  waiting for transfers between devices: 16.3 us -> 20.9 us
  Pallas kernels: 32.4 us -> 35.1 us
    all_to_all x5 -> x4, blocking collectives: 97.2 us -> 78.2 us  [everywhere(): lax.all_to_all(y, ('gx', 'gy'), split_axis=0, concat_axis=0, tiled=True)]
    unnamed x0 -> x58, local copies, waits for them, and re-layouts: none -> 11.6 us
    all_to_all x0 -> x1, starting transfers between devices: none -> 8.65 us  [everywhere(): lax.all_to_all(y, ('gx', 'gy'), split_axis=0, concat_axis=0, tiled=True)]
    all_to_all x0 -> x1, waiting for transfers between devices: none -> 6.98 us  [everywhere(): lax.all_to_all(y, ('gx', 'gy'), split_axis=0, concat_axis=0, tiled=True)]
    pallas_call x17 -> x25, Pallas kernels: 32.4 us -> 35.1 us  [call(): pl.pallas_call(kernel, out_shape=outs, in_specs=specs or [VM] * len(args)...]
    ppermute x8, waiting for transfers between devices: 16.2 us -> 13.9 us  [exchange(): lax.ppermute(sends[0], 'gx', swap_pairs(nx, 1))]
  transfers between devices with their start and end apart: 32 -> 33, of which waited for: 7 -> 8; matrix products, arithmetic and copies ran while one was open for 0% -> 0% of each run, Pallas kernels for 3% -> 4%
where the time goes in v5:
time: 192 us; the launch traced here: 191 us
  blocking collectives  78.2 us (41%)
  starting transfers between devices  43.2 us (22%)
  Pallas kernels  35.1 us (18%)
  waiting for transfers between devices  20.9 us (11%)
  local copies, waits for them, and re-layouts  12.6 us (7%)
    all_to_all x4, blocking collectives, everywhere(): lax.all_to_all(y, ('gx', 'gy'), split_axis=0, concat_axis=0, tiled=True)  78.2 us
    pallas_call x25, Pallas kernels, call(): pl.pallas_call(kernel, out_shape=outs, in_specs=specs or [VM] * len(args)...  35.1 us
    ppermute x8, starting transfers between devices, exchange(): lax.ppermute(sends[0], 'gx', swap_pairs(nx, 1))  19.8 us
    ppermute x8, waiting for transfers between devices, exchange(): lax.ppermute(sends[0], 'gx', swap_pairs(nx, 1))  13.9 us
    unnamed x58, local copies, waits for them, and re-layouts  11.6 us
    ppermute x8, starting transfers between devices, exchange(): lax.ppermute(sends[2], 'gy', swap_pairs(ny, 1))  11.1 us
    all_to_all x1, starting transfers between devices, everywhere(): lax.all_to_all(y, ('gx', 'gy'), split_axis=0, concat_axis=0, tiled=True)  8.65 us
    all_to_all x1, waiting for transfers between devices, everywhere(): lax.all_to_all(y, ('gx', 'gy'), split_axis=0, concat_axis=0, tiled=True)  6.98 us
  transfers between devices with their start and end apart: 33, of which 8 were waited for; matrix products, arithmetic and copies ran while one was open for 0% of the time, Pallas kernels for 4%

profile of v5, /device:TPU:1, one launch (start us, length us, event | category | flops | bytes accessed | tf_op | source)
XLA Modules:
  0.0 191.1 jit_solution(15261227611201291315)
XLA Ops:
  0.6 2.9 %first.1 = (f32[48,128]{1,0:T(8,128)S(1)}, bf16[128,3072]{1,0:T(8,128)(2,1)S(1)}, f32[8,48,128]{2,1,0:T(8,128)S(1)}, bf16[64,48]{1,0:T(8,128)(2,1)S(1)}, f32[48,...) custom-call(f32[48,64]{1,0:T(8,128)} %refs_0_.1, ...), custom_call_target="tpu_custom_call" | custom-call | flops 2000000 | bytes 100000 | tf_op jit(solution)/shard_map/first/pallas_call | solution.py:381
  3.5 6.9 %collective-permute-start = (f32[6,16,128]{2,1,0:T(8,128)S(1)}, f32[6,16,128]{2,1,0:T(8,128)S(1)}, u32[]{:S(2)}, u32[]{:S(2)}) collective-permute-start(f32[6,16,128]{2,1,0:T(8,128)S(1)} %get-tuple-element.79), channel_id=1, source_target_pairs={{0,120},{8,16},{16,8},{24,32},{32,24},{40,48},{48,40},{56,64},{64,... | collective-permute-start | bytes 147464 | tf_op jit(solution)/shard_map/ppermute | solution.py:402
  10.4 2.1 %collective-permute-start.2 = (f32[6,16,128]{2,1,0:T(8,128)S(1)}, f32[6,16,128]{2,1,0:T(8,128)S(1)}, u32[]{:S(2)}, u32[]{:S(2)}) collective-permute-start(f32[6,16,128]{2,1,0:T(8,128)S(1)} %get-tuple-element.81), channel_id=1, source_target_pairs={{0,7},{1,2},{2,1},{3,4},{4,3},{5,6},{6,5},{7,0},{8,15},{9,10},{10,... | collective-permute-start | bytes 147464 | tf_op jit(solution)/shard_map/ppermute | solution.py:404
  13.5 5.2 %operator.1 = (bf16[896,1536]{1,0:T(8,128)(2,1)S(1)}, bf16[896,1536]{1,0:T(8,128)(2,1)S(1)}, bf16[144,256]{1,0:T(8,128)(2,1)S(1)}) custom-call(f32[48,6,64,64]{3,2,1,0:T(8,128)} %off.1, f32[48,64,64]{2,1,0:T(8,128)} %diag.1, s32[6,48]{1,0:T(8,128)} %bitcast.30, f32[16,6,64,64]{3,2,1,0:T(8,128)S(1)} %get-tuple-element.76.near), custom_call_target="tpu_custom_call" | custom-call | flops 2000000000 | bytes 100000 | tf_op jit(solution)/shard_map/operator/pallas_call | solution.py:381
  20.4 23.9 %all_to_all.25.x0 = f32[128,16,128]{2,1,0:T(8,128)S(1)} all-to-all(f32[128,16,128]{2,1,0:T(8,128)S(1)} %broadcast_in_dim.12), channel_id=1, replica_groups=mesh['gx'=16,'gy'=8] {'gx','gy'}, dimensions={0} | all-to-all | bytes 2097152 | tf_op jit(solution)/shard_map/all_to_all | solution.py:412
  44.3 2.7 %coarse.1 = (bf16[8192,128]{1,0:T(8,128)(2,1)S(1)}, f32[8,112,128]{2,1,0:T(8,128)S(1)}, f32[64,8,128]{2,1,0:T(8,128)S(1)}) custom-call(f32[128,16,128]{2,1,0:T(8,128)S(1)} %all_to_all.25.x0, f32[48,128]{1,0:T(8,128)S(1)} %get-tuple-element.87.ids, f32[8,48,128]{2,1,0:T(8,128)S(1)} %get-tuple-element.84.ptd, f32[6,16,128]{2,1,0:T(8,128)S(1)} %collective-permute-done.g0, ...), custom_call_target="tpu_custom_call" | custom-call | flops 2000000 | bytes 100000 | tf_op jit(solution)/shard_map/coarse/pallas_call | solution.py:381
  47.1 2.3 %correct.4 = (f32[48,128]{1,0:T(8,128)S(1)}, f32[16,128]{1,0:T(8,128)S(1)}, f32[16,128]{1,0:T(8,128)S(1)}, f32[16,128]{1,0:T(8,128)S(1)}, f32[16,128]{1,0:T(8,128)S(1)}) custom-call(f32[64,8,128]{2,1,0:T(8,128)S(1)} %get-tuple-element.88.x, bf16[8192,128]{1,0:T(8,128)(2,1)S(1)} %get-tuple-element.89.mask, f32[8,112,128]{2,1,0:T(8,128)S(1)} %get-tuple-element.90.pte, ...), custom_call_target="tpu_custom_call" | custom-call | flops 2000000 | bytes 100000 | tf_op jit(solution)/shard_map/correct/pallas_call | solution.py:381
  52.1 3.1 %collective-permute-done.4.h0 = f32[16,128]{1,0:T(8,128)S(1)} collective-permute-done((f32[16,128]{1,0:T(8,128)S(1)}, f32[16,128]{1,0:T(8,128)S(1)}, u32[]{:S(2)}, u32[]{:S(2)}) %collective-permute-start.4) | collective-permute-done | bytes 8224 | tf_op jit(solution)/shard_map/ppermute | solution.py:402
  56.6 2.3 %collective-permute-start.8 = (f32[16,128]{1,0:T(8,128)S(1)}, f32[16,128]{1,0:T(8,128)S(1)}, u32[]{:S(2)}, u32[]{:S(2)}) collective-permute-start(f32[16,128]{1,0:T(8,128)S(1)} %get-tuple-element.102), channel_id=1, source_target_pairs={{0,120},{8,16},{16,8},{24,32},{32,24},{40,48},{48,40},{56,64},{64,... | collective-permute-start | bytes 24584 | tf_op jit(solution)/shard_map/ppermute | solution.py:402
  59.0 2.0 %collective-permute-start.10 = (f32[16,128]{1,0:T(8,128)S(1)}, f32[16,128]{1,0:T(8,128)S(1)}, u32[]{:S(2)}, u32[]{:S(2)}) collective-permute-start(f32[16,128]{1,0:T(8,128)S(1)} %get-tuple-element.104), channel_id=1, source_target_pairs={{0,7},{1,2},{2,1},{3,4},{4,3},{5,6},{6,5},{7,0},{8,15},{9,10},{10,... | collective-permute-start | bytes 24584 | tf_op jit(solution)/shard_map/ppermute | solution.py:404
  63.7 19.1 %all_to_all.26 = f32[128,4,128]{2,1,0:T(4,128)S(1)} all-to-all(f32[128,4,128]{2,1,0:T(4,128)S(1)} %broadcast_in_dim.13), channel_id=1, replica_groups=mesh['gx'=16,'gy'=8] {'gx','gy'}, dimensions={0} | all-to-all | bytes 524288 | tf_op jit(solution)/shard_map/all_to_all | solution.py:412
  82.9 2.3 %correct.5 = (f32[48,128]{1,0:T(8,128)S(1)}, f32[16,128]{1,0:T(8,128)S(1)}, f32[16,128]{1,0:T(8,128)S(1)}, f32[16,128]{1,0:T(8,128)S(1)}, f32[16,128]{1,0:T(8,128)S(1)}) custom-call(f32[64,8,128]{2,1,0:T(8,128)S(1)} %bitcast.23, bf16[8192,128]{1,0:T(8,128)(2,1)S(1)} %get-tuple-element.89.mask, f32[8,112,128]{2,1,0:T(8,128)S(1)} %get-tuple-element.90.pte, ...), custom_call_target="tpu_custom_call" | custom-call | flops 2000000 | bytes 100000 | tf_op jit(solution)/shard_map/correct/pallas_call | solution.py:381
  88.0 3.0 %collective-permute-done.12.h0 = f32[16,128]{1,0:T(8,128)S(1)} collective-permute-done((f32[16,128]{1,0:T(8,128)S(1)}, f32[16,128]{1,0:T(8,128)S(1)}, u32[]{:S(2)}, u32[]{:S(2)}) %collective-permute-start.12) | collective-permute-done | bytes 8224 | tf_op jit(solution)/shard_map/ppermute | solution.py:402
  92.4 2.3 %collective-permute-start.16 = (f32[16,128]{1,0:T(8,128)S(1)}, f32[16,128]{1,0:T(8,128)S(1)}, u32[]{:S(2)}, u32[]{:S(2)}) collective-permute-start(f32[16,128]{1,0:T(8,128)S(1)} %get-tuple-element.116), channel_id=1, source_target_pairs={{0,120},{8,16},{16,8},{24,32},{32,24},{40,48},{48,40},{56,64},{64,... | collective-permute-start | bytes 24584 | tf_op jit(solution)/shard_map/ppermute | solution.py:402
  94.8 1.8 collective-permute-start.18
  99.5 18.9 %all_to_all.27 = f32[128,4,128]{2,1,0:T(4,128)S(1)} all-to-all(f32[128,4,128]{2,1,0:T(4,128)S(1)} %broadcast_in_dim.14), channel_id=1, replica_groups=mesh['gx'=16,'gy'=8] {'gx','gy'}, dimensions={0} | all-to-all | bytes 524288 | tf_op jit(solution)/shard_map/all_to_all | solution.py:412
  118.4 2.3 %correct.6 = (f32[48,128]{1,0:T(8,128)S(1)}, f32[16,128]{1,0:T(8,128)S(1)}, f32[16,128]{1,0:T(8,128)S(1)}, f32[16,128]{1,0:T(8,128)S(1)}, f32[16,128]{1,0:T(8,128)S(1)}) custom-call(f32[64,8,128]{2,1,0:T(8,128)S(1)} %bitcast.24, bf16[8192,128]{1,0:T(8,128)(2,1)S(1)} %get-tuple-element.89.mask, f32[8,112,128]{2,1,0:T(8,128)S(1)} %get-tuple-element.90.pte, ...), custom_call_target="tpu_custom_call" | custom-call | flops 2000000 | bytes 100000 | tf_op jit(solution)/shard_map/correct/pallas_call | solution.py:381
  123.6 3.0 %collective-permute-done.20.h0 = f32[16,128]{1,0:T(8,128)S(1)} collective-permute-done((f32[16,128]{1,0:T(8,128)S(1)}, f32[16,128]{1,0:T(8,128)S(1)}, u32[]{:S(2)}, u32[]{:S(2)}) %collective-permute-start.20) | collective-permute-done | bytes 8224 | tf_op jit(solution)/shard_map/ppermute | solution.py:402
  128.6 2.3 %collective-permute-start.24 = (f32[16,128]{1,0:T(8,128)S(1)}, f32[16,128]{1,0:T(8,128)S(1)}, u32[]{:S(2)}, u32[]{:S(2)}) collective-permute-start(f32[16,128]{1,0:T(8,128)S(1)} %get-tuple-element.130), channel_id=1, source_target_pairs={{0,120},{8,16},{16,8},{24,32},{32,24},{40,48},{48,40},{56,64},{64,... | collective-permute-start | bytes 24584 | tf_op jit(solution)/shard_map/ppermute | solution.py:402
  137.0 8.6 %all-to-all-start.3 = ((f32[128,4,128]{2,1,0:T(4,128)}), f32[128,4,128]{2,1,0:T(4,128)}, u32[]{:S(2)}, u32[]{:S(2)}) async-start(f32[128,4,128]{2,1,0:T(4,128)} %broadcast_in_dim.15), calls=%async_computation.3 | async-start | bytes 524288 | tf_op jit(solution)/shard_map/all_to_all | solution.py:412
  149.3 7.0 %all-to-all-done.3 = f32[128,4,128]{2,1,0:T(4,128)} async-done(((f32[128,4,128]{2,1,0:T(4,128)}), f32[128,4,128]{2,1,0:T(4,128)}, u32[]{:S(2)}, u32[]{:S(2)}) %all-to-all-start.3) | async-done | bytes 262176 | tf_op jit(solution)/shard_map/all_to_all | solution.py:412
  163.0 3.3 %correct.7 = (f32[48,128]{1,0:T(8,128)S(1)}, f32[16,128]{1,0:T(8,128)S(1)}, f32[16,128]{1,0:T(8,128)S(1)}, f32[16,128]{1,0:T(8,128)S(1)}, f32[16,128]{1,0:T(8,128)S(1)}) custom-call(f32[64,8,128]{2,1,0:T(8,128)} %bitcast.15.x, bf16[8192,128]{1,0:T(8,128)(2,1)S(1)} %copy-done.3, f32[8,112,128]{2,1,0:T(8,128)S(1)} %copy-done.8, f32[48,128]{1,0:T(8,128)S(1)} %copy-done.24, ...), custom_call_target="tpu_custom_call" | custom-call | flops 2000000 | bytes 100000 | tf_op jit(solution)/shard_map/correct/pallas_call | solution.py:381
  169.1 3.0 %collective-permute-done.28.h0 = f32[16,128]{1,0:T(8,128)S(1)} collective-permute-done((f32[16,128]{1,0:T(8,128)S(1)}, f32[16,128]{1,0:T(8,128)S(1)}, u32[]{:S(2)}, u32[]{:S(2)}) %collective-permute-start.28) | collective-permute-done | bytes 8224 | tf_op jit(solution)/shard_map/ppermute | solution.py:402
  173.4 16.3 %all_to_all.28 = f32[128,1,128]{2,1,0:T(1,128)S(1)} all-to-all(f32[128,1,128]{2,1,0:T(1,128)S(1)} %broadcast_in_dim.17), channel_id=1, replica_groups=mesh['gx'=16,'gy'=8] {'gx','gy'}, dimensions={0} | all-to-all | bytes 131072 | tf_op jit(solution)/shard_map/all_to_all | solution.py:412
  (138 shorter events, 43.2 us)
Async XLA Ops:
  3.5 15.5 %collective-permute-start = (f32[6,16,128]{2,1,0:T(8,128)S(1)}, f32[6,16,128]{2,1,0:T(8,128)S(1)}, u32[]{:S(2)}, u32[]{:S(2)}) collective-permute-start(f32[6,16,128]{2,1,0:T(8,128)S(1)} %get-tuple-element.79), channel_id=1, source_target_pairs={{0,120},{8,16},{16,8},{24,32},{32,24},{40,48},{48,40},{56,64},{64,... | collective-permute-start | bytes 147464 | tf_op jit(solution)/shard_map/ppermute | solution.py:402
  10.4 8.7 %collective-permute-start.1 = (f32[6,16,128]{2,1,0:T(8,128)S(1)}, f32[6,16,128]{2,1,0:T(8,128)S(1)}, u32[]{:S(2)}, u32[]{:S(2)}) collective-permute-start(f32[6,16,128]{2,1,0:T(8,128)S(1)} %get-tuple-element.80), channel_id=1, source_target_pairs={{0,8},{8,0},{16,24},{24,16},{32,40},{40,32},{48,56},{56,48},{64,72... | collective-permute-start | bytes 147464 | tf_op jit(solution)/shard_map/ppermute | solution.py:403
  10.4 8.7 %collective-permute-start.2 = (f32[6,16,128]{2,1,0:T(8,128)S(1)}, f32[6,16,128]{2,1,0:T(8,128)S(1)}, u32[]{:S(2)}, u32[]{:S(2)}) collective-permute-start(f32[6,16,128]{2,1,0:T(8,128)S(1)} %get-tuple-element.81), channel_id=1, source_target_pairs={{0,7},{1,2},{2,1},{3,4},{4,3},{5,6},{6,5},{7,0},{8,15},{9,10},{10,... | collective-permute-start | bytes 147464 | tf_op jit(solution)/shard_map/ppermute | solution.py:404
  12.5 6.6 %collective-permute-start.3 = (f32[6,16,128]{2,1,0:T(8,128)S(1)}, f32[6,16,128]{2,1,0:T(8,128)S(1)}, u32[]{:S(2)}, u32[]{:S(2)}) collective-permute-start(f32[6,16,128]{2,1,0:T(8,128)S(1)} %get-tuple-element.82), channel_id=1, source_target_pairs={{0,1},{1,0},{2,3},{3,2},{4,5},{5,4},{6,7},{7,6},{8,9},{9,8},{10,11... | collective-permute-start | bytes 147464 | tf_op jit(solution)/shard_map/ppermute | solution.py:405
  49.4 5.8 %collective-permute-start.4 = (f32[16,128]{1,0:T(8,128)S(1)}, f32[16,128]{1,0:T(8,128)S(1)}, u32[]{:S(2)}, u32[]{:S(2)}) collective-permute-start(f32[16,128]{1,0:T(8,128)S(1)} %get-tuple-element.96), channel_id=1, source_target_pairs={{0,120},{8,16},{16,8},{24,32},{32,24},{40,48},{48,40},{56,64},{64,... | collective-permute-start | bytes 24584 | tf_op jit(solution)/shard_map/ppermute | solution.py:402
  50.8 4.4 %collective-permute-start.5 = (f32[16,128]{1,0:T(8,128)S(1)}, f32[16,128]{1,0:T(8,128)S(1)}, u32[]{:S(2)}, u32[]{:S(2)}) collective-permute-start(f32[16,128]{1,0:T(8,128)S(1)} %get-tuple-element.97), channel_id=1, source_target_pairs={{0,8},{8,0},{16,24},{24,16},{32,40},{40,32},{48,56},{56,48},{64,72... | collective-permute-start | bytes 24584 | tf_op jit(solution)/shard_map/ppermute | solution.py:403
  50.8 4.4 %collective-permute-start.6 = (f32[16,128]{1,0:T(8,128)S(1)}, f32[16,128]{1,0:T(8,128)S(1)}, u32[]{:S(2)}, u32[]{:S(2)}) collective-permute-start(f32[16,128]{1,0:T(8,128)S(1)} %get-tuple-element.98), channel_id=1, source_target_pairs={{0,7},{1,2},{2,1},{3,4},{4,3},{5,6},{6,5},{7,0},{8,15},{9,10},{10,... | collective-permute-start | bytes 24584 | tf_op jit(solution)/shard_map/ppermute | solution.py:404
  51.3 3.9 %collective-permute-start.7 = (f32[16,128]{1,0:T(8,128)S(1)}, f32[16,128]{1,0:T(8,128)S(1)}, u32[]{:S(2)}, u32[]{:S(2)}) collective-permute-start(f32[16,128]{1,0:T(8,128)S(1)} %get-tuple-element.99), channel_id=1, source_target_pairs={{0,1},{1,0},{2,3},{3,2},{4,5},{5,4},{6,7},{7,6},{8,9},{9,8},{10,11... | collective-permute-start | bytes 24584 | tf_op jit(solution)/shard_map/ppermute | solution.py:405
  56.6 5.8 %collective-permute-start.8 = (f32[16,128]{1,0:T(8,128)S(1)}, f32[16,128]{1,0:T(8,128)S(1)}, u32[]{:S(2)}, u32[]{:S(2)}) collective-permute-start(f32[16,128]{1,0:T(8,128)S(1)} %get-tuple-element.102), channel_id=1, source_target_pairs={{0,120},{8,16},{16,8},{24,32},{32,24},{40,48},{48,40},{56,64},{64,... | collective-permute-start | bytes 24584 | tf_op jit(solution)/shard_map/ppermute | solution.py:402
  85.2 5.8 %collective-permute-start.12 = (f32[16,128]{1,0:T(8,128)S(1)}, f32[16,128]{1,0:T(8,128)S(1)}, u32[]{:S(2)}, u32[]{:S(2)}) collective-permute-start(f32[16,128]{1,0:T(8,128)S(1)} %get-tuple-element.110), channel_id=1, source_target_pairs={{0,120},{8,16},{16,8},{24,32},{32,24},{40,48},{48,40},{56,64},{64,... | collective-permute-start | bytes 24584 | tf_op jit(solution)/shard_map/ppermute | solution.py:402
  86.7 4.3 %collective-permute-start.13 = (f32[16,128]{1,0:T(8,128)S(1)}, f32[16,128]{1,0:T(8,128)S(1)}, u32[]{:S(2)}, u32[]{:S(2)}) collective-permute-start(f32[16,128]{1,0:T(8,128)S(1)} %get-tuple-element.111), channel_id=1, source_target_pairs={{0,8},{8,0},{16,24},{24,16},{32,40},{40,32},{48,56},{56,48},{64,72... | collective-permute-start | bytes 24584 | tf_op jit(solution)/shard_map/ppermute | solution.py:403
  86.7 4.3 %collective-permute-start.14 = (f32[16,128]{1,0:T(8,128)S(1)}, f32[16,128]{1,0:T(8,128)S(1)}, u32[]{:S(2)}, u32[]{:S(2)}) collective-permute-start(f32[16,128]{1,0:T(8,128)S(1)} %get-tuple-element.112), channel_id=1, source_target_pairs={{0,7},{1,2},{2,1},{3,4},{4,3},{5,6},{6,5},{7,0},{8,15},{9,10},{10,... | collective-permute-start | bytes 24584 | tf_op jit(solution)/shard_map/ppermute | solution.py:404
  92.4 5.8 %collective-permute-start.16 = (f32[16,128]{1,0:T(8,128)S(1)}, f32[16,128]{1,0:T(8,128)S(1)}, u32[]{:S(2)}, u32[]{:S(2)}) collective-permute-start(f32[16,128]{1,0:T(8,128)S(1)} %get-tuple-element.116), channel_id=1, source_target_pairs={{0,120},{8,16},{16,8},{24,32},{32,24},{40,48},{48,40},{56,64},{64,... | collective-permute-start | bytes 24584 | tf_op jit(solution)/shard_map/ppermute | solution.py:402
  94.8 3.5 %collective-permute-start.17 = (f32[16,128]{1,0:T(8,128)S(1)}, f32[16,128]{1,0:T(8,128)S(1)}, u32[]{:S(2)}, u32[]{:S(2)}) collective-permute-start(f32[16,128]{1,0:T(8,128)S(1)} %get-tuple-element.117), channel_id=1, source_target_pairs={{0,8},{8,0},{16,24},{24,16},{32,40},{40,32},{48,56},{56,48},{64,72... | collective-permute-start | bytes 24584 | tf_op jit(solution)/shard_map/ppermute | solution.py:403
  94.8 3.5 %collective-permute-start.18 = (f32[16,128]{1,0:T(8,128)S(1)}, f32[16,128]{1,0:T(8,128)S(1)}, u32[]{:S(2)}, u32[]{:S(2)}) collective-permute-start(f32[16,128]{1,0:T(8,128)S(1)} %get-tuple-element.118), channel_id=1, source_target_pairs={{0,7},{1,2},{2,1},{3,4},{4,3},{5,6},{6,5},{7,0},{8,15},{9,10},{10,... | collective-permute-start | bytes 24584 | tf_op jit(solution)/shard_map/ppermute | solution.py:404
  120.7 5.8 %collective-permute-start.20 = (f32[16,128]{1,0:T(8,128)S(1)}, f32[16,128]{1,0:T(8,128)S(1)}, u32[]{:S(2)}, u32[]{:S(2)}) collective-permute-start(f32[16,128]{1,0:T(8,128)S(1)} %get-tuple-element.124), channel_id=1, source_target_pairs={{0,120},{8,16},{16,8},{24,32},{32,24},{40,48},{48,40},{56,64},{64,... | collective-permute-start | bytes 24584 | tf_op jit(solution)/shard_map/ppermute | solution.py:402
  122.3 4.3 %collective-permute-start.21 = (f32[16,128]{1,0:T(8,128)S(1)}, f32[16,128]{1,0:T(8,128)S(1)}, u32[]{:S(2)}, u32[]{:S(2)}) collective-permute-start(f32[16,128]{1,0:T(8,128)S(1)} %get-tuple-element.125), channel_id=1, source_target_pairs={{0,8},{8,0},{16,24},{24,16},{32,40},{40,32},{48,56},{56,48},{64,72... | collective-permute-start | bytes 24584 | tf_op jit(solution)/shard_map/ppermute | solution.py:403
  122.3 4.3 %collective-permute-start.22 = (f32[16,128]{1,0:T(8,128)S(1)}, f32[16,128]{1,0:T(8,128)S(1)}, u32[]{:S(2)}, u32[]{:S(2)}) collective-permute-start(f32[16,128]{1,0:T(8,128)S(1)} %get-tuple-element.126), channel_id=1, source_target_pairs={{0,7},{1,2},{2,1},{3,4},{4,3},{5,6},{6,5},{7,0},{8,15},{9,10},{10,... | collective-permute-start | bytes 24584 | tf_op jit(solution)/shard_map/ppermute | solution.py:404
  128.6 5.8 %collective-permute-start.24 = (f32[16,128]{1,0:T(8,128)S(1)}, f32[16,128]{1,0:T(8,128)S(1)}, u32[]{:S(2)}, u32[]{:S(2)}) collective-permute-start(f32[16,128]{1,0:T(8,128)S(1)} %get-tuple-element.130), channel_id=1, source_target_pairs={{0,120},{8,16},{16,8},{24,32},{32,24},{40,48},{48,40},{56,64},{64,... | collective-permute-start | bytes 24584 | tf_op jit(solution)/shard_map/ppermute | solution.py:402
  130.9 3.5 %collective-permute-start.25 = (f32[16,128]{1,0:T(8,128)S(1)}, f32[16,128]{1,0:T(8,128)S(1)}, u32[]{:S(2)}, u32[]{:S(2)}) collective-permute-start(f32[16,128]{1,0:T(8,128)S(1)} %get-tuple-element.131), channel_id=1, source_target_pairs={{0,8},{8,0},{16,24},{24,16},{32,40},{40,32},{48,56},{56,48},{64,72... | collective-permute-start | bytes 24584 | tf_op jit(solution)/shard_map/ppermute | solution.py:403
  137.0 19.2 %all-to-all-start.3 = ((f32[128,4,128]{2,1,0:T(4,128)}), f32[128,4,128]{2,1,0:T(4,128)}, u32[]{:S(2)}, u32[]{:S(2)}) async-start(f32[128,4,128]{2,1,0:T(4,128)} %broadcast_in_dim.15), calls=%async_computation.3 | async-start | bytes 524288 | tf_op jit(solution)/shard_map/all_to_all | solution.py:412
  166.3 5.8 %collective-permute-start.28 = (f32[16,128]{1,0:T(8,128)S(1)}, f32[16,128]{1,0:T(8,128)S(1)}, u32[]{:S(2)}, u32[]{:S(2)}) collective-permute-start(f32[16,128]{1,0:T(8,128)S(1)} %get-tuple-element.138), channel_id=1, source_target_pairs={{0,120},{8,16},{16,8},{24,32},{32,24},{40,48},{48,40},{56,64},{64,... | collective-permute-start | bytes 24584 | tf_op jit(solution)/shard_map/ppermute | solution.py:402
  167.8 4.3 %collective-permute-start.29 = (f32[16,128]{1,0:T(8,128)S(1)}, f32[16,128]{1,0:T(8,128)S(1)}, u32[]{:S(2)}, u32[]{:S(2)}) collective-permute-start(f32[16,128]{1,0:T(8,128)S(1)} %get-tuple-element.139), channel_id=1, source_target_pairs={{0,8},{8,0},{16,24},{24,16},{32,40},{40,32},{48,56},{56,48},{64,72... | collective-permute-start | bytes 24584 | tf_op jit(solution)/shard_map/ppermute | solution.py:403
  167.8 4.3 %collective-permute-start.30 = (f32[16,128]{1,0:T(8,128)S(1)}, f32[16,128]{1,0:T(8,128)S(1)}, u32[]{:S(2)}, u32[]{:S(2)}) collective-permute-start(f32[16,128]{1,0:T(8,128)S(1)} %get-tuple-element.140), channel_id=1, source_target_pairs={{0,7},{1,2},{2,1},{3,4},{4,3},{5,6},{6,5},{7,0},{8,15},{9,10},{10,... | collective-permute-start | bytes 24584 | tf_op jit(solution)/shard_map/ppermute | solution.py:404
  (38 other events, 674.8 us)

commit v6 on v5

--- a/solution.py
+++ b/solution.py
@@ -320,8 +320,9 @@
     return [jnp.sum(basis[j] * basis[l], axis=0, keepdims=True) for j, l in pairs]
 
 
-def known_kernel(v0, v1, v2, v3, known):
-    basis = [v[...] for v in (v0, v1, v2, v3)]
+def before_last(slopes, v, ye, wa, wb, v0, v1, v2, base, known):
+    before_advance(3, slopes, v, ye, wa, wb, base)
+    basis = [x[...] for x in (v0, v1, v2, v)]
     known[...] = jnp.concatenate(products(basis, PAIRS[:10]) + [jnp.zeros((6, 128), F32)], axis=0)
 
 
@@ -509,13 +510,14 @@
             name="correct",
         )
         around = exchange(sends)
-        (base,) = call(
-            functools.partial(before_advance, k),
-            [shape(ROWS, 128)],
+        base, *known = call(
+            functools.partial(before_advance, k) if k < 3 else before_last,
+            [shape(ROWS, 128)] if k < 3 else [shape(ROWS, 128), shape(16, 128)],
             slopes,
             v,
             ye,
             *w_op,
+            *([] if k < 3 else basis[:3]),
             flops=500_000_000,
             name="before_advance",
         )
@@ -534,7 +536,6 @@
             )
             basis.append(v)
             around = exchange(sends)
-    (known,) = call(known_kernel, [shape(16, 128)], *basis, flops=500_000_000, name="known")
     v, gram = call(
         last_kernel,
         [shape(ROWS, 128), shape(1, 128)],
@@ -544,7 +545,7 @@
         *w_op,
         gather,
         *basis,
-        known,
+        *known,
         name="last",
     )
     basis.append(v)

time: 192 us -> 181 us (0.943)
  blocking collectives: 78.2 us -> 97.2 us
  local copies, waits for them, and re-layouts: 12.6 us -> 0.37 us
  starting transfers between devices: 43.2 us -> 34.6 us
  waiting for transfers between devices: 20.9 us -> 14 us
    all_to_all x4 -> x5, blocking collectives: 78.2 us -> 97.2 us  [everywhere(): lax.all_to_all(y, ('gx', 'gy'), split_axis=0, concat_axis=0, tiled=True)]
    unnamed x58 -> x0, local copies, waits for them, and re-layouts: 11.6 us -> none
    all_to_all x1 -> x0, starting transfers between devices: 8.65 us -> none  [everywhere(): lax.all_to_all(y, ('gx', 'gy'), split_axis=0, concat_axis=0, tiled=True)]
    all_to_all x1 -> x0, waiting for transfers between devices: 6.98 us -> none  [everywhere(): lax.all_to_all(y, ('gx', 'gy'), split_axis=0, concat_axis=0, tiled=True)]
    pallas_call x25 -> x24, Pallas kernels: 35.1 us -> 34.1 us  [call(): pl.pallas_call(kernel, out_shape=outs, in_specs=specs or [VM] * len(args)...]
  transfers between devices with their start and end apart: 33 -> 32, of which waited for: 8 -> 7; matrix products, arithmetic and copies ran while one was open for 0% -> 0% of each run, Pallas kernels for 4% -> 4%
where the time goes in v6:
time: 181 us
  blocking collectives  97.2 us (54%)
  starting transfers between devices  34.6 us (19%)
  Pallas kernels  34.1 us (19%)
  waiting for transfers between devices  14 us (8%)
    all_to_all x5, blocking collectives, everywhere(): lax.all_to_all(y, ('gx', 'gy'), split_axis=0, concat_axis=0, tiled=True)  97.2 us
    pallas_call x24, Pallas kernels, call(): pl.pallas_call(kernel, out_shape=outs, in_specs=specs or [VM] * len(args)...  34.1 us
    ppermute x8, starting transfers between devices, exchange(): lax.ppermute(sends[0], 'gx', swap_pairs(nx, 1))  19.9 us
    ppermute x8, waiting for transfers between devices, exchange(): lax.ppermute(sends[0], 'gx', swap_pairs(nx, 1))  13.9 us
    ppermute x8, starting transfers between devices, exchange(): lax.ppermute(sends[2], 'gy', swap_pairs(ny, 1))  11.1 us
  transfers between devices with their start and end apart: 32, of which 7 were waited for; matrix products, arithmetic and copies ran while one was open for 0% of the time, Pallas kernels for 4%

profile of v6, /device:TPU:1, one launch (start us, length us, event | category | flops | bytes accessed | tf_op | source)
XLA Modules:
  0.0 181.1 jit_solution(17005632010345028747)
XLA Ops:
  0.6 2.9 %first.1 = (f32[48,128]{1,0:T(8,128)S(1)}, bf16[128,3072]{1,0:T(8,128)(2,1)S(1)}, f32[8,48,128]{2,1,0:T(8,128)S(1)}, bf16[64,48]{1,0:T(8,128)(2,1)S(1)}, f32[48,...) custom-call(f32[48,64]{1,0:T(8,128)} %refs_0_.1, ...), custom_call_target="tpu_custom_call" | custom-call | flops 2000000 | bytes 100000 | tf_op jit(solution)/shard_map/first/pallas_call | solution.py:382
  3.5 6.9 %collective-permute-start = (f32[6,16,128]{2,1,0:T(8,128)S(1)}, f32[6,16,128]{2,1,0:T(8,128)S(1)}, u32[]{:S(2)}, u32[]{:S(2)}) collective-permute-start(f32[6,16,128]{2,1,0:T(8,128)S(1)} %get-tuple-element.81), channel_id=1, source_target_pairs={{0,120},{8,16},{16,8},{24,32},{32,24},{40,48},{48,40},{56,64},{64,... | collective-permute-start | bytes 147464 | tf_op jit(solution)/shard_map/ppermute | solution.py:403
  10.4 2.1 %collective-permute-start.2 = (f32[6,16,128]{2,1,0:T(8,128)S(1)}, f32[6,16,128]{2,1,0:T(8,128)S(1)}, u32[]{:S(2)}, u32[]{:S(2)}) collective-permute-start(f32[6,16,128]{2,1,0:T(8,128)S(1)} %get-tuple-element.83), channel_id=1, source_target_pairs={{0,7},{1,2},{2,1},{3,4},{4,3},{5,6},{6,5},{7,0},{8,15},{9,10},{10,... | collective-permute-start | bytes 147464 | tf_op jit(solution)/shard_map/ppermute | solution.py:405
  13.5 5.2 %operator.1 = (bf16[896,1536]{1,0:T(8,128)(2,1)S(1)}, bf16[896,1536]{1,0:T(8,128)(2,1)S(1)}, bf16[144,256]{1,0:T(8,128)(2,1)S(1)}) custom-call(f32[48,6,64,64]{3,2,1,0:T(8,128)} %off.1, f32[48,64,64]{2,1,0:T(8,128)} %diag.1, s32[6,48]{1,0:T(8,128)} %bitcast.31, f32[16,6,64,64]{3,2,1,0:T(8,128)S(1)} %get-tuple-element.78.near), custom_call_target="tpu_custom_call" | custom-call | flops 2000000000 | bytes 100000 | tf_op jit(solution)/shard_map/operator/pallas_call | solution.py:382
  20.4 23.9 %all_to_all.25.x0 = f32[128,16,128]{2,1,0:T(8,128)S(1)} all-to-all(f32[128,16,128]{2,1,0:T(8,128)S(1)} %broadcast_in_dim.12), channel_id=1, replica_groups=mesh['gx'=16,'gy'=8] {'gx','gy'}, dimensions={0} | all-to-all | bytes 2097152 | tf_op jit(solution)/shard_map/all_to_all | solution.py:413
  44.3 2.8 %coarse.1 = (bf16[8192,128]{1,0:T(8,128)(2,1)S(1)}, f32[8,112,128]{2,1,0:T(8,128)S(1)}, f32[64,8,128]{2,1,0:T(8,128)S(1)}) custom-call(f32[128,16,128]{2,1,0:T(8,128)S(1)} %all_to_all.25.x0, f32[48,128]{1,0:T(8,128)S(1)} %get-tuple-element.89.ids, f32[8,48,128]{2,1,0:T(8,128)S(1)} %get-tuple-element.86.ptd, f32[6,16,128]{2,1,0:T(8,128)S(1)} %collective-permute-done.g0, ...), custom_call_target="tpu_custom_call" | custom-call | flops 2000000 | bytes 100000 | tf_op jit(solution)/shard_map/coarse/pallas_call | solution.py:382
  47.0 2.3 %correct.4 = (f32[48,128]{1,0:T(8,128)S(1)}, f32[16,128]{1,0:T(8,128)S(1)}, f32[16,128]{1,0:T(8,128)S(1)}, f32[16,128]{1,0:T(8,128)S(1)}, f32[16,128]{1,0:T(8,128)S(1)}) custom-call(f32[64,8,128]{2,1,0:T(8,128)S(1)} %get-tuple-element.90.x, bf16[8192,128]{1,0:T(8,128)(2,1)S(1)} %get-tuple-element.91.mask, f32[8,112,128]{2,1,0:T(8,128)S(1)} %get-tuple-element.92.pte, ...), custom_call_target="tpu_custom_call" | custom-call | flops 2000000 | bytes 100000 | tf_op jit(solution)/shard_map/correct/pallas_call | solution.py:382
  52.1 3.1 %collective-permute-done.4.h0 = f32[16,128]{1,0:T(8,128)S(1)} collective-permute-done((f32[16,128]{1,0:T(8,128)S(1)}, f32[16,128]{1,0:T(8,128)S(1)}, u32[]{:S(2)}, u32[]{:S(2)}) %collective-permute-start.4) | collective-permute-done | bytes 8224 | tf_op jit(solution)/shard_map/ppermute | solution.py:403
  56.6 2.3 %collective-permute-start.8 = (f32[16,128]{1,0:T(8,128)S(1)}, f32[16,128]{1,0:T(8,128)S(1)}, u32[]{:S(2)}, u32[]{:S(2)}) collective-permute-start(f32[16,128]{1,0:T(8,128)S(1)} %get-tuple-element.104), channel_id=1, source_target_pairs={{0,120},{8,16},{16,8},{24,32},{32,24},{40,48},{48,40},{56,64},{64,... | collective-permute-start | bytes 24584 | tf_op jit(solution)/shard_map/ppermute | solution.py:403
  59.0 2.0 %collective-permute-start.10 = (f32[16,128]{1,0:T(8,128)S(1)}, f32[16,128]{1,0:T(8,128)S(1)}, u32[]{:S(2)}, u32[]{:S(2)}) collective-permute-start(f32[16,128]{1,0:T(8,128)S(1)} %get-tuple-element.106), channel_id=1, source_target_pairs={{0,7},{1,2},{2,1},{3,4},{4,3},{5,6},{6,5},{7,0},{8,15},{9,10},{10,... | collective-permute-start | bytes 24584 | tf_op jit(solution)/shard_map/ppermute | solution.py:405
  63.7 19.1 %all_to_all.26 = f32[128,4,128]{2,1,0:T(4,128)S(1)} all-to-all(f32[128,4,128]{2,1,0:T(4,128)S(1)} %broadcast_in_dim.13), channel_id=1, replica_groups=mesh['gx'=16,'gy'=8] {'gx','gy'}, dimensions={0} | all-to-all | bytes 524288 | tf_op jit(solution)/shard_map/all_to_all | solution.py:413
  82.9 2.3 %correct.5 = (f32[48,128]{1,0:T(8,128)S(1)}, f32[16,128]{1,0:T(8,128)S(1)}, f32[16,128]{1,0:T(8,128)S(1)}, f32[16,128]{1,0:T(8,128)S(1)}, f32[16,128]{1,0:T(8,128)S(1)}) custom-call(f32[64,8,128]{2,1,0:T(8,128)S(1)} %bitcast.24, bf16[8192,128]{1,0:T(8,128)(2,1)S(1)} %get-tuple-element.91.mask, f32[8,112,128]{2,1,0:T(8,128)S(1)} %get-tuple-element.92.pte, ...), custom_call_target="tpu_custom_call" | custom-call | flops 2000000 | bytes 100000 | tf_op jit(solution)/shard_map/correct/pallas_call | solution.py:382
  88.0 3.0 %collective-permute-done.12.h0 = f32[16,128]{1,0:T(8,128)S(1)} collective-permute-done((f32[16,128]{1,0:T(8,128)S(1)}, f32[16,128]{1,0:T(8,128)S(1)}, u32[]{:S(2)}, u32[]{:S(2)}) %collective-permute-start.12) | collective-permute-done | bytes 8224 | tf_op jit(solution)/shard_map/ppermute | solution.py:403
  92.4 2.3 %collective-permute-start.16 = (f32[16,128]{1,0:T(8,128)S(1)}, f32[16,128]{1,0:T(8,128)S(1)}, u32[]{:S(2)}, u32[]{:S(2)}) collective-permute-start(f32[16,128]{1,0:T(8,128)S(1)} %get-tuple-element.118), channel_id=1, source_target_pairs={{0,120},{8,16},{16,8},{24,32},{32,24},{40,48},{48,40},{56,64},{64,... | collective-permute-start | bytes 24584 | tf_op jit(solution)/shard_map/ppermute | solution.py:403
  94.8 1.8 %collective-permute-start.18 = (f32[16,128]{1,0:T(8,128)S(1)}, f32[16,128]{1,0:T(8,128)S(1)}, u32[]{:S(2)}, u32[]{:S(2)}) collective-permute-start(f32[16,128]{1,0:T(8,128)S(1)} %get-tuple-element.120), channel_id=1, source_target_pairs={{0,7},{1,2},{2,1},{3,4},{4,3},{5,6},{6,5},{7,0},{8,15},{9,10},{10,... | collective-permute-start | bytes 24584 | tf_op jit(solution)/shard_map/ppermute | solution.py:405
  99.5 18.9 %all_to_all.27 = f32[128,4,128]{2,1,0:T(4,128)S(1)} all-to-all(f32[128,4,128]{2,1,0:T(4,128)S(1)} %broadcast_in_dim.14), channel_id=1, replica_groups=mesh['gx'=16,'gy'=8] {'gx','gy'}, dimensions={0} | all-to-all | bytes 524288 | tf_op jit(solution)/shard_map/all_to_all | solution.py:413
  118.4 2.3 %correct.6 = (f32[48,128]{1,0:T(8,128)S(1)}, f32[16,128]{1,0:T(8,128)S(1)}, f32[16,128]{1,0:T(8,128)S(1)}, f32[16,128]{1,0:T(8,128)S(1)}, f32[16,128]{1,0:T(8,128)S(1)}) custom-call(f32[64,8,128]{2,1,0:T(8,128)S(1)} %bitcast.25, bf16[8192,128]{1,0:T(8,128)(2,1)S(1)} %get-tuple-element.91.mask, f32[8,112,128]{2,1,0:T(8,128)S(1)} %get-tuple-element.92.pte, ...), custom_call_target="tpu_custom_call" | custom-call | flops 2000000 | bytes 100000 | tf_op jit(solution)/shard_map/correct/pallas_call | solution.py:382
  123.5 3.0 %collective-permute-done.20.h0 = f32[16,128]{1,0:T(8,128)S(1)} collective-permute-done((f32[16,128]{1,0:T(8,128)S(1)}, f32[16,128]{1,0:T(8,128)S(1)}, u32[]{:S(2)}, u32[]{:S(2)}) %collective-permute-start.20) | collective-permute-done | bytes 8224 | tf_op jit(solution)/shard_map/ppermute | solution.py:403
  128.0 2.3 %collective-permute-start.24 = (f32[16,128]{1,0:T(8,128)S(1)}, f32[16,128]{1,0:T(8,128)S(1)}, u32[]{:S(2)}, u32[]{:S(2)}) collective-permute-start(f32[16,128]{1,0:T(8,128)S(1)} %get-tuple-element.132), channel_id=1, source_target_pairs={{0,120},{8,16},{16,8},{24,32},{32,24},{40,48},{48,40},{56,64},{64,... | collective-permute-start | bytes 24584 | tf_op jit(solution)/shard_map/ppermute | solution.py:403
  130.3 1.8 %collective-permute-start.26 = (f32[16,128]{1,0:T(8,128)S(1)}, f32[16,128]{1,0:T(8,128)S(1)}, u32[]{:S(2)}, u32[]{:S(2)}) collective-permute-start(f32[16,128]{1,0:T(8,128)S(1)} %get-tuple-element.134), channel_id=1, source_target_pairs={{0,7},{1,2},{2,1},{3,4},{4,3},{5,6},{6,5},{7,0},{8,15},{9,10},{10,... | collective-permute-start | bytes 24584 | tf_op jit(solution)/shard_map/ppermute | solution.py:405
  135.1 18.9 %all_to_all.28 = f32[128,4,128]{2,1,0:T(4,128)S(1)} all-to-all(f32[128,4,128]{2,1,0:T(4,128)S(1)} %broadcast_in_dim.15), channel_id=1, replica_groups=mesh['gx'=16,'gy'=8] {'gx','gy'}, dimensions={0} | all-to-all | bytes 524288 | tf_op jit(solution)/shard_map/all_to_all | solution.py:413
  154.0 2.3 %correct.7 = (f32[48,128]{1,0:T(8,128)S(1)}, f32[16,128]{1,0:T(8,128)S(1)}, f32[16,128]{1,0:T(8,128)S(1)}, f32[16,128]{1,0:T(8,128)S(1)}, f32[16,128]{1,0:T(8,128)S(1)}) custom-call(f32[64,8,128]{2,1,0:T(8,128)S(1)} %bitcast.23, bf16[8192,128]{1,0:T(8,128)(2,1)S(1)} %get-tuple-element.91.mask, f32[8,112,128]{2,1,0:T(8,128)S(1)} %get-tuple-element.92.pte, ...), custom_call_target="tpu_custom_call" | custom-call | flops 2000000 | bytes 100000 | tf_op jit(solution)/shard_map/correct/pallas_call | solution.py:382
  159.1 3.0 %collective-permute-done.28.h0 = f32[16,128]{1,0:T(8,128)S(1)} collective-permute-done((f32[16,128]{1,0:T(8,128)S(1)}, f32[16,128]{1,0:T(8,128)S(1)}, u32[]{:S(2)}, u32[]{:S(2)}) %collective-permute-start.28) | collective-permute-done | bytes 8224 | tf_op jit(solution)/shard_map/ppermute | solution.py:403
  163.3 16.4 %all_to_all.29 = f32[128,1,128]{2,1,0:T(1,128)S(1)} all-to-all(f32[128,1,128]{2,1,0:T(1,128)S(1)} %broadcast_in_dim.17), channel_id=1, replica_groups=mesh['gx'=16,'gy'=8] {'gx','gy'}, dimensions={0} | all-to-all | bytes 131072 | tf_op jit(solution)/shard_map/all_to_all | solution.py:413
  (78 shorter events, 29.1 us)
Async XLA Ops:
  3.5 15.5 %collective-permute-start = (f32[6,16,128]{2,1,0:T(8,128)S(1)}, f32[6,16,128]{2,1,0:T(8,128)S(1)}, u32[]{:S(2)}, u32[]{:S(2)}) collective-permute-start(f32[6,16,128]{2,1,0:T(8,128)S(1)} %get-tuple-element.81), channel_id=1, source_target_pairs={{0,120},{8,16},{16,8},{24,32},{32,24},{40,48},{48,40},{56,64},{64,... | collective-permute-start | bytes 147464 | tf_op jit(solution)/shard_map/ppermute | solution.py:403
  10.4 8.7 %collective-permute-start.1 = (f32[6,16,128]{2,1,0:T(8,128)S(1)}, f32[6,16,128]{2,1,0:T(8,128)S(1)}, u32[]{:S(2)}, u32[]{:S(2)}) collective-permute-start(f32[6,16,128]{2,1,0:T(8,128)S(1)} %get-tuple-element.82), channel_id=1, source_target_pairs={{0,8},{8,0},{16,24},{24,16},{32,40},{40,32},{48,56},{56,48},{64,72... | collective-permute-start | bytes 147464 | tf_op jit(solution)/shard_map/ppermute | solution.py:404
  10.4 8.7 %collective-permute-start.2 = (f32[6,16,128]{2,1,0:T(8,128)S(1)}, f32[6,16,128]{2,1,0:T(8,128)S(1)}, u32[]{:S(2)}, u32[]{:S(2)}) collective-permute-start(f32[6,16,128]{2,1,0:T(8,128)S(1)} %get-tuple-element.83), channel_id=1, source_target_pairs={{0,7},{1,2},{2,1},{3,4},{4,3},{5,6},{6,5},{7,0},{8,15},{9,10},{10,... | collective-permute-start | bytes 147464 | tf_op jit(solution)/shard_map/ppermute | solution.py:405
  12.5 6.6 %collective-permute-start.3 = (f32[6,16,128]{2,1,0:T(8,128)S(1)}, f32[6,16,128]{2,1,0:T(8,128)S(1)}, u32[]{:S(2)}, u32[]{:S(2)}) collective-permute-start(f32[6,16,128]{2,1,0:T(8,128)S(1)} %get-tuple-element.84), channel_id=1, source_target_pairs={{0,1},{1,0},{2,3},{3,2},{4,5},{5,4},{6,7},{7,6},{8,9},{9,8},{10,11... | collective-permute-start | bytes 147464 | tf_op jit(solution)/shard_map/ppermute | solution.py:406
  49.4 5.8 %collective-permute-start.4 = (f32[16,128]{1,0:T(8,128)S(1)}, f32[16,128]{1,0:T(8,128)S(1)}, u32[]{:S(2)}, u32[]{:S(2)}) collective-permute-start(f32[16,128]{1,0:T(8,128)S(1)} %get-tuple-element.98), channel_id=1, source_target_pairs={{0,120},{8,16},{16,8},{24,32},{32,24},{40,48},{48,40},{56,64},{64,... | collective-permute-start | bytes 24584 | tf_op jit(solution)/shard_map/ppermute | solution.py:403
  50.8 4.4 %collective-permute-start.5 = (f32[16,128]{1,0:T(8,128)S(1)}, f32[16,128]{1,0:T(8,128)S(1)}, u32[]{:S(2)}, u32[]{:S(2)}) collective-permute-start(f32[16,128]{1,0:T(8,128)S(1)} %get-tuple-element.99), channel_id=1, source_target_pairs={{0,8},{8,0},{16,24},{24,16},{32,40},{40,32},{48,56},{56,48},{64,72... | collective-permute-start | bytes 24584 | tf_op jit(solution)/shard_map/ppermute | solution.py:404
  50.8 4.4 %collective-permute-start.6 = (f32[16,128]{1,0:T(8,128)S(1)}, f32[16,128]{1,0:T(8,128)S(1)}, u32[]{:S(2)}, u32[]{:S(2)}) collective-permute-start(f32[16,128]{1,0:T(8,128)S(1)} %get-tuple-element.100), channel_id=1, source_target_pairs={{0,7},{1,2},{2,1},{3,4},{4,3},{5,6},{6,5},{7,0},{8,15},{9,10},{10,... | collective-permute-start | bytes 24584 | tf_op jit(solution)/shard_map/ppermute | solution.py:405
  51.3 3.9 %collective-permute-start.7 = (f32[16,128]{1,0:T(8,128)S(1)}, f32[16,128]{1,0:T(8,128)S(1)}, u32[]{:S(2)}, u32[]{:S(2)}) collective-permute-start(f32[16,128]{1,0:T(8,128)S(1)} %get-tuple-element.101), channel_id=1, source_target_pairs={{0,1},{1,0},{2,3},{3,2},{4,5},{5,4},{6,7},{7,6},{8,9},{9,8},{10,11... | collective-permute-start | bytes 24584 | tf_op jit(solution)/shard_map/ppermute | solution.py:406
  56.6 5.8 %collective-permute-start.8 = (f32[16,128]{1,0:T(8,128)S(1)}, f32[16,128]{1,0:T(8,128)S(1)}, u32[]{:S(2)}, u32[]{:S(2)}) collective-permute-start(f32[16,128]{1,0:T(8,128)S(1)} %get-tuple-element.104), channel_id=1, source_target_pairs={{0,120},{8,16},{16,8},{24,32},{32,24},{40,48},{48,40},{56,64},{64,... | collective-permute-start | bytes 24584 | tf_op jit(solution)/shard_map/ppermute | solution.py:403
  59.0 3.5 %collective-permute-start.9 = (f32[16,128]{1,0:T(8,128)S(1)}, f32[16,128]{1,0:T(8,128)S(1)}, u32[]{:S(2)}, u32[]{:S(2)}) collective-permute-start(f32[16,128]{1,0:T(8,128)S(1)} %get-tuple-element.105), channel_id=1, source_target_pairs={{0,8},{8,0},{16,24},{24,16},{32,40},{40,32},{48,56},{56,48},{64,72... | collective-permute-start | bytes 24584 | tf_op jit(solution)/shard_map/ppermute | solution.py:404
  59.0 3.5 %collective-permute-start.10 = (f32[16,128]{1,0:T(8,128)S(1)}, f32[16,128]{1,0:T(8,128)S(1)}, u32[]{:S(2)}, u32[]{:S(2)}) collective-permute-start(f32[16,128]{1,0:T(8,128)S(1)} %get-tuple-element.106), channel_id=1, source_target_pairs={{0,7},{1,2},{2,1},{3,4},{4,3},{5,6},{6,5},{7,0},{8,15},{9,10},{10,... | collective-permute-start | bytes 24584 | tf_op jit(solution)/shard_map/ppermute | solution.py:405
  85.2 5.8 %collective-permute-start.12 = (f32[16,128]{1,0:T(8,128)S(1)}, f32[16,128]{1,0:T(8,128)S(1)}, u32[]{:S(2)}, u32[]{:S(2)}) collective-permute-start(f32[16,128]{1,0:T(8,128)S(1)} %get-tuple-element.112), channel_id=1, source_target_pairs={{0,120},{8,16},{16,8},{24,32},{32,24},{40,48},{48,40},{56,64},{64,... | collective-permute-start | bytes 24584 | tf_op jit(solution)/shard_map/ppermute | solution.py:403
  86.7 4.3 %collective-permute-start.13 = (f32[16,128]{1,0:T(8,128)S(1)}, f32[16,128]{1,0:T(8,128)S(1)}, u32[]{:S(2)}, u32[]{:S(2)}) collective-permute-start(f32[16,128]{1,0:T(8,128)S(1)} %get-tuple-element.113), channel_id=1, source_target_pairs={{0,8},{8,0},{16,24},{24,16},{32,40},{40,32},{48,56},{56,48},{64,72... | collective-permute-start | bytes 24584 | tf_op jit(solution)/shard_map/ppermute | solution.py:404
  86.7 4.3 %collective-permute-start.14 = (f32[16,128]{1,0:T(8,128)S(1)}, f32[16,128]{1,0:T(8,128)S(1)}, u32[]{:S(2)}, u32[]{:S(2)}) collective-permute-start(f32[16,128]{1,0:T(8,128)S(1)} %get-tuple-element.114), channel_id=1, source_target_pairs={{0,7},{1,2},{2,1},{3,4},{4,3},{5,6},{6,5},{7,0},{8,15},{9,10},{10,... | collective-permute-start | bytes 24584 | tf_op jit(solution)/shard_map/ppermute | solution.py:405
  92.4 5.8 %collective-permute-start.16 = (f32[16,128]{1,0:T(8,128)S(1)}, f32[16,128]{1,0:T(8,128)S(1)}, u32[]{:S(2)}, u32[]{:S(2)}) collective-permute-start(f32[16,128]{1,0:T(8,128)S(1)} %get-tuple-element.118), channel_id=1, source_target_pairs={{0,120},{8,16},{16,8},{24,32},{32,24},{40,48},{48,40},{56,64},{64,... | collective-permute-start | bytes 24584 | tf_op jit(solution)/shard_map/ppermute | solution.py:403
  120.7 5.8 %collective-permute-start.20 = (f32[16,128]{1,0:T(8,128)S(1)}, f32[16,128]{1,0:T(8,128)S(1)}, u32[]{:S(2)}, u32[]{:S(2)}) collective-permute-start(f32[16,128]{1,0:T(8,128)S(1)} %get-tuple-element.126), channel_id=1, source_target_pairs={{0,120},{8,16},{16,8},{24,32},{32,24},{40,48},{48,40},{56,64},{64,... | collective-permute-start | bytes 24584 | tf_op jit(solution)/shard_map/ppermute | solution.py:403
  122.3 4.3 %collective-permute-start.21 = (f32[16,128]{1,0:T(8,128)S(1)}, f32[16,128]{1,0:T(8,128)S(1)}, u32[]{:S(2)}, u32[]{:S(2)}) collective-permute-start(f32[16,128]{1,0:T(8,128)S(1)} %get-tuple-element.127), channel_id=1, source_target_pairs={{0,8},{8,0},{16,24},{24,16},{32,40},{40,32},{48,56},{56,48},{64,72... | collective-permute-start | bytes 24584 | tf_op jit(solution)/shard_map/ppermute | solution.py:404
  122.3 4.3 %collective-permute-start.22 = (f32[16,128]{1,0:T(8,128)S(1)}, f32[16,128]{1,0:T(8,128)S(1)}, u32[]{:S(2)}, u32[]{:S(2)}) collective-permute-start(f32[16,128]{1,0:T(8,128)S(1)} %get-tuple-element.128), channel_id=1, source_target_pairs={{0,7},{1,2},{2,1},{3,4},{4,3},{5,6},{6,5},{7,0},{8,15},{9,10},{10,... | collective-permute-start | bytes 24584 | tf_op jit(solution)/shard_map/ppermute | solution.py:405
  128.0 5.8 %collective-permute-start.24 = (f32[16,128]{1,0:T(8,128)S(1)}, f32[16,128]{1,0:T(8,128)S(1)}, u32[]{:S(2)}, u32[]{:S(2)}) collective-permute-start(f32[16,128]{1,0:T(8,128)S(1)} %get-tuple-element.132), channel_id=1, source_target_pairs={{0,120},{8,16},{16,8},{24,32},{32,24},{40,48},{48,40},{56,64},{64,... | collective-permute-start | bytes 24584 | tf_op jit(solution)/shard_map/ppermute | solution.py:403
  130.3 3.5 %collective-permute-start.25 = (f32[16,128]{1,0:T(8,128)S(1)}, f32[16,128]{1,0:T(8,128)S(1)}, u32[]{:S(2)}, u32[]{:S(2)}) collective-permute-start(f32[16,128]{1,0:T(8,128)S(1)} %get-tuple-element.133), channel_id=1, source_target_pairs={{0,8},{8,0},{16,24},{24,16},{32,40},{40,32},{48,56},{56,48},{64,72... | collective-permute-start | bytes 24584 | tf_op jit(solution)/shard_map/ppermute | solution.py:404
  130.3 3.5 %collective-permute-start.26 = (f32[16,128]{1,0:T(8,128)S(1)}, f32[16,128]{1,0:T(8,128)S(1)}, u32[]{:S(2)}, u32[]{:S(2)}) collective-permute-start(f32[16,128]{1,0:T(8,128)S(1)} %get-tuple-element.134), channel_id=1, source_target_pairs={{0,7},{1,2},{2,1},{3,4},{4,3},{5,6},{6,5},{7,0},{8,15},{9,10},{10,... | collective-permute-start | bytes 24584 | tf_op jit(solution)/shard_map/ppermute | solution.py:405
  156.3 5.8 %collective-permute-start.28 = (f32[16,128]{1,0:T(8,128)S(1)}, f32[16,128]{1,0:T(8,128)S(1)}, u32[]{:S(2)}, u32[]{:S(2)}) collective-permute-start(f32[16,128]{1,0:T(8,128)S(1)} %get-tuple-element.141), channel_id=1, source_target_pairs={{0,120},{8,16},{16,8},{24,32},{32,24},{40,48},{48,40},{56,64},{64,... | collective-permute-start | bytes 24584 | tf_op jit(solution)/shard_map/ppermute | solution.py:403
  157.8 4.3 %collective-permute-start.29 = (f32[16,128]{1,0:T(8,128)S(1)}, f32[16,128]{1,0:T(8,128)S(1)}, u32[]{:S(2)}, u32[]{:S(2)}) collective-permute-start(f32[16,128]{1,0:T(8,128)S(1)} %get-tuple-element.142), channel_id=1, source_target_pairs={{0,8},{8,0},{16,24},{24,16},{32,40},{40,32},{48,56},{56,48},{64,72... | collective-permute-start | bytes 24584 | tf_op jit(solution)/shard_map/ppermute | solution.py:404
  157.8 4.3 %collective-permute-start.30 = (f32[16,128]{1,0:T(8,128)S(1)}, f32[16,128]{1,0:T(8,128)S(1)}, u32[]{:S(2)}, u32[]{:S(2)}) collective-permute-start(f32[16,128]{1,0:T(8,128)S(1)} %get-tuple-element.143), channel_id=1, source_target_pairs={{0,7},{1,2},{2,1},{3,4},{4,3},{5,6},{6,5},{7,0},{8,15},{9,10},{10,... | collective-permute-start | bytes 24584 | tf_op jit(solution)/shard_map/ppermute | solution.py:405
  (8 other events, 22.0 us)

commit v7 on v6

--- a/solution.py
+++ b/solution.py
@@ -243,24 +243,32 @@
         p[4:16, :] = extra[0][4:16, :]
 
 
-def coarse_kernel(x0, ids, ptd, g0, g1, g2, g3, mask, pte, xp):
+def coarse_kernel(same, other, ids, ptd, g0, g1, g2, g3, mask, pte, xp):
     idc = jnp.concatenate(
         [ids[...], g0[5], g1[5], g2[5], g3[5], jnp.full((128 - EXT, 128), -1.0, F32)], axis=0
     )
     wanted = idc.T[0:1]
-    given = [x0[:, r, :].T[ROWS:BS] for r in range(3)] + [jnp.full((BS - ROWS, 128), -1.0, F32)]
+    even = lax.axis_index("gy") % 2 == 0
+
+    def by_core(x, y):
+        return jnp.where(even, x, y), jnp.where(even, y, x)
+
+    given = [jnp.concatenate(by_core(same[:, r, :], other[:, r, :]), axis=0).T[ROWS:BS] for r in range(3)] + [jnp.full((BS - ROWS, 128), -1.0, F32)]
     given = jnp.concatenate(given + given, axis=0)
     for q in range(64):
-        line = jnp.concatenate([given[0:BS, 2 * q : 2 * q + 1], given[BS:128, 2 * q + 1 : 2 * q + 2]], axis=0)
+        line = jnp.concatenate([given[0:BS, q : q + 1], given[BS:128, BS + q : BS + q + 1]], axis=0)
         mask[128 * q : 128 * q + 128, :] = (line == wanted).astype(F32).astype(BF16)
-        xp[q] = jnp.concatenate([x0[2 * q, 0:4, :], x0[2 * q + 1, 0:4, :]], axis=0)
+        xp[q] = jnp.concatenate(by_core(same[q, 0:4, :], other[q, 0:4, :]), axis=0)
     device = jnp.floor((idc + 0.5) * (1.0 / 24.0))
     slot = idc - 24.0 * device
     upper = slot >= 11.5
-    place = device * 16.0 + 4.0 + jnp.where(upper, slot - 12.0, slot)
+    chip = jnp.floor(device * 0.5)
+    core = device - 2.0 * chip
+    core = jnp.where(even, core, 1.0 - core)
+    place = core * 1024.0 + chip * 16.0 + 4.0 + jnp.where(upper, slot - 12.0, slot)
     high, rest = [], []
     for b in range(8):
-        src = x0[16 * b : 16 * b + 16].reshape(256, 128)
+        src = (same if b < 4 else other)[16 * (b % 4) : 16 * (b % 4) + 16].reshape(256, 128)
         high.append(src.astype(BF16))
         rest.append((src - high[-1].astype(F32)).astype(BF16))
     lane = lax.broadcasted_iota(jnp.int32, (128, 128), 1).astype(F32)
@@ -411,6 +419,14 @@
     count = lax.axis_size("gx") * lax.axis_size("gy")
     y = jnp.broadcast_to(x[None], (count,) + x.shape)
     return lax.all_to_all(y, ("gx", "gy"), split_axis=0, concat_axis=0, tiled=True)
+
+
+def everywhere_by_core(x):
+    nx, ny = lax.axis_size("gx"), lax.axis_size("gy")
+    groups = [[p * ny + q for p in range(nx) for q in range(core, ny, 2)] for core in range(2)]
+    y = jnp.broadcast_to(x[None], (nx * ny // 2,) + x.shape)
+    same = lax.all_to_all(y, ("gx", "gy"), split_axis=0, concat_axis=0, tiled=True, axis_index_groups=groups)
+    return same, lax.ppermute(same, "gy", swap_pairs(ny, 0))
 
 
 def per_device(start, shifts, diag_blocks, off_blocks, jacobi_inv, prolong, coarse_inv, cols, send_rows, owner, agg_slot):
@@ -482,18 +498,18 @@
             *([] if k else [extra]),
             name="restrict",
         )
-        x = everywhere(p)
         if k == 0:
             mask, pte, x = call(
                 coarse_kernel,
                 [kept(64 * 128, 128, dtype=BF16), shape(CW, EXT, 128), shape(64, 8, 128)],
-                x,
+                *everywhere_by_core(p),
                 id_col,
                 ptd,
                 *got,
                 name="coarse",
             )
-        x = x.reshape(64, 8, 128)
+        else:
+            x = everywhere(p).reshape(64, 8, 128)
         ye, *sends = call(
             correct_kernel,
             [shape(ROWS, 128)] + halo,

time: 181 us -> 178 us (0.983)
  blocking collectives: 97.2 us -> 89.7 us
  starting transfers between devices: 34.6 us -> 36.6 us
  waiting for transfers between devices: 14 us -> 16 us
    all_to_all x5 -> x4, blocking collectives: 97.2 us -> 72.5 us  [everywhere(): lax.all_to_all(y, ('gx', 'gy'), split_axis=0, concat_axis=0, tiled=True)]
    all_to_all x0 -> x1, blocking collectives: none -> 17.2 us  [everywhere_by_core(): lax.all_to_all(y, ('gx', 'gy'), split_axis=0, concat_axis=0, tiled=True,...]
    ppermute x0 -> x1, starting transfers between devices: none -> 2.27 us  [everywhere_by_core(): return (same, lax.ppermute(same, 'gy', swap_pairs(ny, 0)))]
  transfers between devices with their start and end apart: 32 -> 33, of which waited for: 7 -> 8; matrix products, arithmetic and copies ran while one was open for 0% -> 0% of each run, Pallas kernels for 4% -> 4%
where the time goes in v7:
time: 178 us
  blocking collectives  89.7 us (50%)
  starting transfers between devices  36.6 us (21%)
  Pallas kernels  34.5 us (19%)
  waiting for transfers between devices  16 us (9%)
    all_to_all x4, blocking collectives, everywhere(): lax.all_to_all(y, ('gx', 'gy'), split_axis=0, concat_axis=0, tiled=True)  72.5 us
    pallas_call x24, Pallas kernels, call(): pl.pallas_call(kernel, out_shape=outs, in_specs=specs or [VM] * len(args)...  34.5 us
    ppermute x8, starting transfers between devices, exchange(): lax.ppermute(sends[0], 'gx', swap_pairs(nx, 1))  19 us
    all_to_all x1, blocking collectives, everywhere_by_core(): lax.all_to_all(y, ('gx', 'gy'), split_axis=0, concat_axis=0, tiled=True,...  17.2 us
    ppermute x8, waiting for transfers between devices, exchange(): lax.ppermute(sends[0], 'gx', swap_pairs(nx, 1))  14.4 us
    ppermute x8, starting transfers between devices, exchange(): lax.ppermute(sends[2], 'gy', swap_pairs(ny, 1))  11.1 us
    ppermute x8, starting transfers between devices, exchange(): lax.ppermute(sends[3], 'gy', swap_pairs(ny, 0))  4.16 us
  transfers between devices with their start and end apart: 33, of which 8 were waited for; matrix products, arithmetic and copies ran while one was open for 0% of the time, Pallas kernels for 4%

profile of v7, /device:TPU:1, one launch (start us, length us, event | category | flops | bytes accessed | tf_op | source)
XLA Modules:
  0.0 178.0 jit_solution(9251983245690917162)
XLA Ops:
  0.6 2.9 %first.1 = (f32[48,128]{1,0:T(8,128)S(1)}, bf16[128,3072]{1,0:T(8,128)(2,1)S(1)}, f32[8,48,128]{2,1,0:T(8,128)S(1)}, bf16[64,48]{1,0:T(8,128)(2,1)S(1)}, f32[48,...) custom-call(f32[48,64]{1,0:T(8,128)} %refs_0_.1, ...), custom_call_target="tpu_custom_call" | custom-call | flops 2000000 | bytes 100000 | tf_op jit(solution)/shard_map/first/pallas_call | solution.py:390
  3.5 6.9 %collective-permute-start = (f32[6,16,128]{2,1,0:T(8,128)S(1)}, f32[6,16,128]{2,1,0:T(8,128)S(1)}, u32[]{:S(2)}, u32[]{:S(2)}) collective-permute-start(f32[6,16,128]{2,1,0:T(8,128)S(1)} %get-tuple-element.81), channel_id=1, source_target_pairs={{0,120},{8,16},{16,8},{24,32},{32,24},{40,48},{48,40},{56,64},{64,... | collective-permute-start | bytes 147464 | tf_op jit(solution)/shard_map/ppermute | solution.py:411
  10.4 2.1 %collective-permute-start.2 = (f32[6,16,128]{2,1,0:T(8,128)S(1)}, f32[6,16,128]{2,1,0:T(8,128)S(1)}, u32[]{:S(2)}, u32[]{:S(2)}) collective-permute-start(f32[6,16,128]{2,1,0:T(8,128)S(1)} %get-tuple-element.83), channel_id=1, source_target_pairs={{0,7},{1,2},{2,1},{3,4},{4,3},{5,6},{6,5},{7,0},{8,15},{9,10},{10,... | collective-permute-start | bytes 147464 | tf_op jit(solution)/shard_map/ppermute | solution.py:413
  13.5 5.2 %operator.1 = (bf16[896,1536]{1,0:T(8,128)(2,1)S(1)}, bf16[896,1536]{1,0:T(8,128)(2,1)S(1)}, bf16[144,256]{1,0:T(8,128)(2,1)S(1)}) custom-call(f32[48,6,64,64]{3,2,1,0:T(8,128)} %off.1, f32[48,64,64]{2,1,0:T(8,128)} %diag.1, s32[6,48]{1,0:T(8,128)} %bitcast.31, f32[16,6,64,64]{3,2,1,0:T(8,128)S(1)} %get-tuple-element.78.near), custom_call_target="tpu_custom_call" | custom-call | flops 2000000000 | bytes 100000 | tf_op jit(solution)/shard_map/operator/pallas_call | solution.py:390
  20.4 17.2 %all_to_all.25.same = f32[64,16,128]{2,1,0:T(8,128)S(1)} all-to-all(f32[64,16,128]{2,1,0:T(8,128)S(1)} %broadcast_in_dim.12), channel_id=1, replica_groups={{0,2,4,6,8,10,12,14,16,18,20,22,24,26,28,30,32,34,36,38,40,42,44,46,48,..., dimensions={0} | all-to-all | bytes 1048576 | tf_op jit(solution)/shard_map/all_to_all | solution.py:428
  37.6 2.3 %collective-permute-start.4 = (f32[64,16,128]{2,1,0:T(8,128)S(1)}, f32[64,16,128]{2,1,0:T(8,128)S(1)}, u32[]{:S(2)}, u32[]{:S(2)}) collective-permute-start(f32[64,16,128]{2,1,0:T(8,128)S(1)} %all_to_all.25.same), channel_id=1, source_target_pairs={{0,1},{1,0},{2,3},{3,2},{4,5},{5,4},{6,7},{7,6},{8,9},{9,8},{10,11... | collective-permute-start | bytes 1572872 | tf_op jit(solution)/shard_map/ppermute | solution.py:429
  41.4 3.2 %coarse.1 = (bf16[8192,128]{1,0:T(8,128)(2,1)S(1)}, f32[8,112,128]{2,1,0:T(8,128)S(1)}, f32[64,8,128]{2,1,0:T(8,128)S(1)}) custom-call(f32[64,16,128]{2,1,0:T(8,128)S(1)} %all_to_all.25.same, f32[64,16,128]{2,1,0:T(8,128)S(1)} %collective-permute-done.4.other, f32[48,128]{1,0:T(8,128)S(1)} %get-tuple-element.89.ids, ...), custom_call_target="tpu_custom_call" | custom-call | flops 2000000 | bytes 100000 | tf_op jit(solution)/shard_map/coarse/pallas_call | solution.py:390
  44.6 2.3 %correct.4 = (f32[48,128]{1,0:T(8,128)S(1)}, f32[16,128]{1,0:T(8,128)S(1)}, f32[16,128]{1,0:T(8,128)S(1)}, f32[16,128]{1,0:T(8,128)S(1)}, f32[16,128]{1,0:T(8,128)S(1)}) custom-call(f32[64,8,128]{2,1,0:T(8,128)S(1)} %get-tuple-element.90.x, bf16[8192,128]{1,0:T(8,128)(2,1)S(1)} %get-tuple-element.91.mask, f32[8,112,128]{2,1,0:T(8,128)S(1)} %get-tuple-element.92.pte, ...), custom_call_target="tpu_custom_call" | custom-call | flops 2000000 | bytes 100000 | tf_op jit(solution)/shard_map/correct/pallas_call | solution.py:390
  49.7 3.0 %collective-permute-done.5.h0 = f32[16,128]{1,0:T(8,128)S(1)} collective-permute-done((f32[16,128]{1,0:T(8,128)S(1)}, f32[16,128]{1,0:T(8,128)S(1)}, u32[]{:S(2)}, u32[]{:S(2)}) %collective-permute-start.5) | collective-permute-done | bytes 8224 | tf_op jit(solution)/shard_map/ppermute | solution.py:411
  54.1 2.0 %collective-permute-start.9 = (f32[16,128]{1,0:T(8,128)S(1)}, f32[16,128]{1,0:T(8,128)S(1)}, u32[]{:S(2)}, u32[]{:S(2)}) collective-permute-start(f32[16,128]{1,0:T(8,128)S(1)} %get-tuple-element.104), channel_id=1, source_target_pairs={{0,120},{8,16},{16,8},{24,32},{32,24},{40,48},{48,40},{56,64},{64,... | collective-permute-start | bytes 24584 | tf_op jit(solution)/shard_map/ppermute | solution.py:411
  61.2 18.3 %all_to_all.26 = f32[128,4,128]{2,1,0:T(4,128)S(1)} all-to-all(f32[128,4,128]{2,1,0:T(4,128)S(1)} %broadcast_in_dim.13), channel_id=1, replica_groups=mesh['gx'=16,'gy'=8] {'gx','gy'}, dimensions={0} | all-to-all | bytes 524288 | tf_op jit(solution)/shard_map/all_to_all | solution.py:421
  79.6 2.3 %correct.5 = (f32[48,128]{1,0:T(8,128)S(1)}, f32[16,128]{1,0:T(8,128)S(1)}, f32[16,128]{1,0:T(8,128)S(1)}, f32[16,128]{1,0:T(8,128)S(1)}, f32[16,128]{1,0:T(8,128)S(1)}) custom-call(f32[64,8,128]{2,1,0:T(8,128)S(1)} %bitcast.24, bf16[8192,128]{1,0:T(8,128)(2,1)S(1)} %get-tuple-element.91.mask, f32[8,112,128]{2,1,0:T(8,128)S(1)} %get-tuple-element.92.pte, ...), custom_call_target="tpu_custom_call" | custom-call | flops 2000000 | bytes 100000 | tf_op jit(solution)/shard_map/correct/pallas_call | solution.py:390
  84.7 3.0 %collective-permute-done.13.h0 = f32[16,128]{1,0:T(8,128)S(1)} collective-permute-done((f32[16,128]{1,0:T(8,128)S(1)}, f32[16,128]{1,0:T(8,128)S(1)}, u32[]{:S(2)}, u32[]{:S(2)}) %collective-permute-start.13) | collective-permute-done | bytes 8224 | tf_op jit(solution)/shard_map/ppermute | solution.py:411
  89.2 2.5 %collective-permute-start.17 = (f32[16,128]{1,0:T(8,128)S(1)}, f32[16,128]{1,0:T(8,128)S(1)}, u32[]{:S(2)}, u32[]{:S(2)}) collective-permute-start(f32[16,128]{1,0:T(8,128)S(1)} %get-tuple-element.118), channel_id=1, source_target_pairs={{0,120},{8,16},{16,8},{24,32},{32,24},{40,48},{48,40},{56,64},{64,... | collective-permute-start | bytes 24584 | tf_op jit(solution)/shard_map/ppermute | solution.py:411
  91.7 1.8 %collective-permute-start.19 = (f32[16,128]{1,0:T(8,128)S(1)}, f32[16,128]{1,0:T(8,128)S(1)}, u32[]{:S(2)}, u32[]{:S(2)}) collective-permute-start(f32[16,128]{1,0:T(8,128)S(1)} %get-tuple-element.120), channel_id=1, source_target_pairs={{0,7},{1,2},{2,1},{3,4},{4,3},{5,6},{6,5},{7,0},{8,15},{9,10},{10,... | collective-permute-start | bytes 24584 | tf_op jit(solution)/shard_map/ppermute | solution.py:413
  96.4 18.9 %all_to_all.27 = f32[128,4,128]{2,1,0:T(4,128)S(1)} all-to-all(f32[128,4,128]{2,1,0:T(4,128)S(1)} %broadcast_in_dim.14), channel_id=1, replica_groups=mesh['gx'=16,'gy'=8] {'gx','gy'}, dimensions={0} | all-to-all | bytes 524288 | tf_op jit(solution)/shard_map/all_to_all | solution.py:421
  115.3 2.3 %correct.6 = (f32[48,128]{1,0:T(8,128)S(1)}, f32[16,128]{1,0:T(8,128)S(1)}, f32[16,128]{1,0:T(8,128)S(1)}, f32[16,128]{1,0:T(8,128)S(1)}, f32[16,128]{1,0:T(8,128)S(1)}) custom-call(f32[64,8,128]{2,1,0:T(8,128)S(1)} %bitcast.25, bf16[8192,128]{1,0:T(8,128)(2,1)S(1)} %get-tuple-element.91.mask, f32[8,112,128]{2,1,0:T(8,128)S(1)} %get-tuple-element.92.pte, ...), custom_call_target="tpu_custom_call" | custom-call | flops 2000000 | bytes 100000 | tf_op jit(solution)/shard_map/correct/pallas_call | solution.py:390
  120.4 3.0 %collective-permute-done.21.h0 = f32[16,128]{1,0:T(8,128)S(1)} collective-permute-done((f32[16,128]{1,0:T(8,128)S(1)}, f32[16,128]{1,0:T(8,128)S(1)}, u32[]{:S(2)}, u32[]{:S(2)}) %collective-permute-start.21) | collective-permute-done | bytes 8224 | tf_op jit(solution)/shard_map/ppermute | solution.py:411
  124.9 2.3 %collective-permute-start.25 = (f32[16,128]{1,0:T(8,128)S(1)}, f32[16,128]{1,0:T(8,128)S(1)}, u32[]{:S(2)}, u32[]{:S(2)}) collective-permute-start(f32[16,128]{1,0:T(8,128)S(1)} %get-tuple-element.132), channel_id=1, source_target_pairs={{0,120},{8,16},{16,8},{24,32},{32,24},{40,48},{48,40},{56,64},{64,... | collective-permute-start | bytes 24584 | tf_op jit(solution)/shard_map/ppermute | solution.py:411
  127.2 1.8 %collective-permute-start.27 = (f32[16,128]{1,0:T(8,128)S(1)}, f32[16,128]{1,0:T(8,128)S(1)}, u32[]{:S(2)}, u32[]{:S(2)}) collective-permute-start(f32[16,128]{1,0:T(8,128)S(1)} %get-tuple-element.134), channel_id=1, source_target_pairs={{0,7},{1,2},{2,1},{3,4},{4,3},{5,6},{6,5},{7,0},{8,15},{9,10},{10,... | collective-permute-start | bytes 24584 | tf_op jit(solution)/shard_map/ppermute | solution.py:413
  132.0 18.9 %all_to_all.28 = f32[128,4,128]{2,1,0:T(4,128)S(1)} all-to-all(f32[128,4,128]{2,1,0:T(4,128)S(1)} %broadcast_in_dim.15), channel_id=1, replica_groups=mesh['gx'=16,'gy'=8] {'gx','gy'}, dimensions={0} | all-to-all | bytes 524288 | tf_op jit(solution)/shard_map/all_to_all | solution.py:421
  150.9 2.3 %correct.7 = (f32[48,128]{1,0:T(8,128)S(1)}, f32[16,128]{1,0:T(8,128)S(1)}, f32[16,128]{1,0:T(8,128)S(1)}, f32[16,128]{1,0:T(8,128)S(1)}, f32[16,128]{1,0:T(8,128)S(1)}) custom-call(f32[64,8,128]{2,1,0:T(8,128)S(1)} %bitcast.23, bf16[8192,128]{1,0:T(8,128)(2,1)S(1)} %get-tuple-element.91.mask, f32[8,112,128]{2,1,0:T(8,128)S(1)} %get-tuple-element.92.pte, ...), custom_call_target="tpu_custom_call" | custom-call | flops 2000000 | bytes 100000 | tf_op jit(solution)/shard_map/correct/pallas_call | solution.py:390
  156.0 3.0 %collective-permute-done.29.h0 = f32[16,128]{1,0:T(8,128)S(1)} collective-permute-done((f32[16,128]{1,0:T(8,128)S(1)}, f32[16,128]{1,0:T(8,128)S(1)}, u32[]{:S(2)}, u32[]{:S(2)}) %collective-permute-start.29) | collective-permute-done | bytes 8224 | tf_op jit(solution)/shard_map/ppermute | solution.py:411
  160.3 16.4 %all_to_all.29 = f32[128,1,128]{2,1,0:T(1,128)S(1)} all-to-all(f32[128,1,128]{2,1,0:T(1,128)S(1)} %broadcast_in_dim.17), channel_id=1, replica_groups=mesh['gx'=16,'gy'=8] {'gx','gy'}, dimensions={0} | all-to-all | bytes 131072 | tf_op jit(solution)/shard_map/all_to_all | solution.py:421
  (80 shorter events, 33.1 us)
Async XLA Ops:
  3.5 15.5 %collective-permute-start = (f32[6,16,128]{2,1,0:T(8,128)S(1)}, f32[6,16,128]{2,1,0:T(8,128)S(1)}, u32[]{:S(2)}, u32[]{:S(2)}) collective-permute-start(f32[6,16,128]{2,1,0:T(8,128)S(1)} %get-tuple-element.81), channel_id=1, source_target_pairs={{0,120},{8,16},{16,8},{24,32},{32,24},{40,48},{48,40},{56,64},{64,... | collective-permute-start | bytes 147464 | tf_op jit(solution)/shard_map/ppermute | solution.py:411
  10.4 8.7 %collective-permute-start.1 = (f32[6,16,128]{2,1,0:T(8,128)S(1)}, f32[6,16,128]{2,1,0:T(8,128)S(1)}, u32[]{:S(2)}, u32[]{:S(2)}) collective-permute-start(f32[6,16,128]{2,1,0:T(8,128)S(1)} %get-tuple-element.82), channel_id=1, source_target_pairs={{0,8},{8,0},{16,24},{24,16},{32,40},{40,32},{48,56},{56,48},{64,72... | collective-permute-start | bytes 147464 | tf_op jit(solution)/shard_map/ppermute | solution.py:412
  10.4 8.7 %collective-permute-start.2 = (f32[6,16,128]{2,1,0:T(8,128)S(1)}, f32[6,16,128]{2,1,0:T(8,128)S(1)}, u32[]{:S(2)}, u32[]{:S(2)}) collective-permute-start(f32[6,16,128]{2,1,0:T(8,128)S(1)} %get-tuple-element.83), channel_id=1, source_target_pairs={{0,7},{1,2},{2,1},{3,4},{4,3},{5,6},{6,5},{7,0},{8,15},{9,10},{10,... | collective-permute-start | bytes 147464 | tf_op jit(solution)/shard_map/ppermute | solution.py:413
  12.5 6.6 %collective-permute-start.3 = (f32[6,16,128]{2,1,0:T(8,128)S(1)}, f32[6,16,128]{2,1,0:T(8,128)S(1)}, u32[]{:S(2)}, u32[]{:S(2)}) collective-permute-start(f32[6,16,128]{2,1,0:T(8,128)S(1)} %get-tuple-element.84), channel_id=1, source_target_pairs={{0,1},{1,0},{2,3},{3,2},{4,5},{5,4},{6,7},{7,6},{8,9},{9,8},{10,11... | collective-permute-start | bytes 147464 | tf_op jit(solution)/shard_map/ppermute | solution.py:414
  37.6 3.8 %collective-permute-start.4 = (f32[64,16,128]{2,1,0:T(8,128)S(1)}, f32[64,16,128]{2,1,0:T(8,128)S(1)}, u32[]{:S(2)}, u32[]{:S(2)}) collective-permute-start(f32[64,16,128]{2,1,0:T(8,128)S(1)} %all_to_all.25.same), channel_id=1, source_target_pairs={{0,1},{1,0},{2,3},{3,2},{4,5},{5,4},{6,7},{7,6},{8,9},{9,8},{10,11... | collective-permute-start | bytes 1572872 | tf_op jit(solution)/shard_map/ppermute | solution.py:429
  46.9 5.8 %collective-permute-start.5 = (f32[16,128]{1,0:T(8,128)S(1)}, f32[16,128]{1,0:T(8,128)S(1)}, u32[]{:S(2)}, u32[]{:S(2)}) collective-permute-start(f32[16,128]{1,0:T(8,128)S(1)} %get-tuple-element.98), channel_id=1, source_target_pairs={{0,120},{8,16},{16,8},{24,32},{32,24},{40,48},{48,40},{56,64},{64,... | collective-permute-start | bytes 24584 | tf_op jit(solution)/shard_map/ppermute | solution.py:411
  47.5 5.2 %collective-permute-start.6 = (f32[16,128]{1,0:T(8,128)S(1)}, f32[16,128]{1,0:T(8,128)S(1)}, u32[]{:S(2)}, u32[]{:S(2)}) collective-permute-start(f32[16,128]{1,0:T(8,128)S(1)} %get-tuple-element.99), channel_id=1, source_target_pairs={{0,8},{8,0},{16,24},{24,16},{32,40},{40,32},{48,56},{56,48},{64,72... | collective-permute-start | bytes 24584 | tf_op jit(solution)/shard_map/ppermute | solution.py:412
  47.5 5.2 %collective-permute-start.7 = (f32[16,128]{1,0:T(8,128)S(1)}, f32[16,128]{1,0:T(8,128)S(1)}, u32[]{:S(2)}, u32[]{:S(2)}) collective-permute-start(f32[16,128]{1,0:T(8,128)S(1)} %get-tuple-element.100), channel_id=1, source_target_pairs={{0,7},{1,2},{2,1},{3,4},{4,3},{5,6},{6,5},{7,0},{8,15},{9,10},{10,... | collective-permute-start | bytes 24584 | tf_op jit(solution)/shard_map/ppermute | solution.py:413
  48.3 4.4 %collective-permute-start.8 = (f32[16,128]{1,0:T(8,128)S(1)}, f32[16,128]{1,0:T(8,128)S(1)}, u32[]{:S(2)}, u32[]{:S(2)}) collective-permute-start(f32[16,128]{1,0:T(8,128)S(1)} %get-tuple-element.101), channel_id=1, source_target_pairs={{0,1},{1,0},{2,3},{3,2},{4,5},{5,4},{6,7},{7,6},{8,9},{9,8},{10,11... | collective-permute-start | bytes 24584 | tf_op jit(solution)/shard_map/ppermute | solution.py:414
  54.1 5.8 %collective-permute-start.9 = (f32[16,128]{1,0:T(8,128)S(1)}, f32[16,128]{1,0:T(8,128)S(1)}, u32[]{:S(2)}, u32[]{:S(2)}) collective-permute-start(f32[16,128]{1,0:T(8,128)S(1)} %get-tuple-element.104), channel_id=1, source_target_pairs={{0,120},{8,16},{16,8},{24,32},{32,24},{40,48},{48,40},{56,64},{64,... | collective-permute-start | bytes 24584 | tf_op jit(solution)/shard_map/ppermute | solution.py:411
  56.2 3.8 %collective-permute-start.10 = (f32[16,128]{1,0:T(8,128)S(1)}, f32[16,128]{1,0:T(8,128)S(1)}, u32[]{:S(2)}, u32[]{:S(2)}) collective-permute-start(f32[16,128]{1,0:T(8,128)S(1)} %get-tuple-element.105), channel_id=1, source_target_pairs={{0,8},{8,0},{16,24},{24,16},{32,40},{40,32},{48,56},{56,48},{64,72... | collective-permute-start | bytes 24584 | tf_op jit(solution)/shard_map/ppermute | solution.py:412
  56.2 3.8 %collective-permute-start.11 = (f32[16,128]{1,0:T(8,128)S(1)}, f32[16,128]{1,0:T(8,128)S(1)}, u32[]{:S(2)}, u32[]{:S(2)}) collective-permute-start(f32[16,128]{1,0:T(8,128)S(1)} %get-tuple-element.106), channel_id=1, source_target_pairs={{0,7},{1,2},{2,1},{3,4},{4,3},{5,6},{6,5},{7,0},{8,15},{9,10},{10,... | collective-permute-start | bytes 24584 | tf_op jit(solution)/shard_map/ppermute | solution.py:413
  81.9 5.8 %collective-permute-start.13 = (f32[16,128]{1,0:T(8,128)S(1)}, f32[16,128]{1,0:T(8,128)S(1)}, u32[]{:S(2)}, u32[]{:S(2)}) collective-permute-start(f32[16,128]{1,0:T(8,128)S(1)} %get-tuple-element.112), channel_id=1, source_target_pairs={{0,120},{8,16},{16,8},{24,32},{32,24},{40,48},{48,40},{56,64},{64,... | collective-permute-start | bytes 24584 | tf_op jit(solution)/shard_map/ppermute | solution.py:411
  83.4 4.3 %collective-permute-start.14 = (f32[16,128]{1,0:T(8,128)S(1)}, f32[16,128]{1,0:T(8,128)S(1)}, u32[]{:S(2)}, u32[]{:S(2)}) collective-permute-start(f32[16,128]{1,0:T(8,128)S(1)} %get-tuple-element.113), channel_id=1, source_target_pairs={{0,8},{8,0},{16,24},{24,16},{32,40},{40,32},{48,56},{56,48},{64,72... | collective-permute-start | bytes 24584 | tf_op jit(solution)/shard_map/ppermute | solution.py:412
  83.4 4.3 %collective-permute-start.15 = (f32[16,128]{1,0:T(8,128)S(1)}, f32[16,128]{1,0:T(8,128)S(1)}, u32[]{:S(2)}, u32[]{:S(2)}) collective-permute-start(f32[16,128]{1,0:T(8,128)S(1)} %get-tuple-element.114), channel_id=1, source_target_pairs={{0,7},{1,2},{2,1},{3,4},{4,3},{5,6},{6,5},{7,0},{8,15},{9,10},{10,... | collective-permute-start | bytes 24584 | tf_op jit(solution)/shard_map/ppermute | solution.py:413
  89.2 6.0 %collective-permute-start.17 = (f32[16,128]{1,0:T(8,128)S(1)}, f32[16,128]{1,0:T(8,128)S(1)}, u32[]{:S(2)}, u32[]{:S(2)}) collective-permute-start(f32[16,128]{1,0:T(8,128)S(1)} %get-tuple-element.118), channel_id=1, source_target_pairs={{0,120},{8,16},{16,8},{24,32},{32,24},{40,48},{48,40},{56,64},{64,... | collective-permute-start | bytes 24584 | tf_op jit(solution)/shard_map/ppermute | solution.py:411
  91.7 3.5 %collective-permute-start.18 = (f32[16,128]{1,0:T(8,128)S(1)}, f32[16,128]{1,0:T(8,128)S(1)}, u32[]{:S(2)}, u32[]{:S(2)}) collective-permute-start(f32[16,128]{1,0:T(8,128)S(1)} %get-tuple-element.119), channel_id=1, source_target_pairs={{0,8},{8,0},{16,24},{24,16},{32,40},{40,32},{48,56},{56,48},{64,72... | collective-permute-start | bytes 24584 | tf_op jit(solution)/shard_map/ppermute | solution.py:412
  117.6 5.8 %collective-permute-start.21 = (f32[16,128]{1,0:T(8,128)S(1)}, f32[16,128]{1,0:T(8,128)S(1)}, u32[]{:S(2)}, u32[]{:S(2)}) collective-permute-start(f32[16,128]{1,0:T(8,128)S(1)} %get-tuple-element.126), channel_id=1, source_target_pairs={{0,120},{8,16},{16,8},{24,32},{32,24},{40,48},{48,40},{56,64},{64,... | collective-permute-start | bytes 24584 | tf_op jit(solution)/shard_map/ppermute | solution.py:411
  119.2 4.3 %collective-permute-start.22 = (f32[16,128]{1,0:T(8,128)S(1)}, f32[16,128]{1,0:T(8,128)S(1)}, u32[]{:S(2)}, u32[]{:S(2)}) collective-permute-start(f32[16,128]{1,0:T(8,128)S(1)} %get-tuple-element.127), channel_id=1, source_target_pairs={{0,8},{8,0},{16,24},{24,16},{32,40},{40,32},{48,56},{56,48},{64,72... | collective-permute-start | bytes 24584 | tf_op jit(solution)/shard_map/ppermute | solution.py:412
  119.2 4.3 %collective-permute-start.23 = (f32[16,128]{1,0:T(8,128)S(1)}, f32[16,128]{1,0:T(8,128)S(1)}, u32[]{:S(2)}, u32[]{:S(2)}) collective-permute-start(f32[16,128]{1,0:T(8,128)S(1)} %get-tuple-element.128), channel_id=1, source_target_pairs={{0,7},{1,2},{2,1},{3,4},{4,3},{5,6},{6,5},{7,0},{8,15},{9,10},{10,... | collective-permute-start | bytes 24584 | tf_op jit(solution)/shard_map/ppermute | solution.py:413
  124.9 5.8 %collective-permute-start.25 = (f32[16,128]{1,0:T(8,128)S(1)}, f32[16,128]{1,0:T(8,128)S(1)}, u32[]{:S(2)}, u32[]{:S(2)}) collective-permute-start(f32[16,128]{1,0:T(8,128)S(1)} %get-tuple-element.132), channel_id=1, source_target_pairs={{0,120},{8,16},{16,8},{24,32},{32,24},{40,48},{48,40},{56,64},{64,... | collective-permute-start | bytes 24584 | tf_op jit(solution)/shard_map/ppermute | solution.py:411
  153.2 5.8 %collective-permute-start.29 = (f32[16,128]{1,0:T(8,128)S(1)}, f32[16,128]{1,0:T(8,128)S(1)}, u32[]{:S(2)}, u32[]{:S(2)}) collective-permute-start(f32[16,128]{1,0:T(8,128)S(1)} %get-tuple-element.141), channel_id=1, source_target_pairs={{0,120},{8,16},{16,8},{24,32},{32,24},{40,48},{48,40},{56,64},{64,... | collective-permute-start | bytes 24584 | tf_op jit(solution)/shard_map/ppermute | solution.py:411
  154.7 4.3 %collective-permute-start.30 = (f32[16,128]{1,0:T(8,128)S(1)}, f32[16,128]{1,0:T(8,128)S(1)}, u32[]{:S(2)}, u32[]{:S(2)}) collective-permute-start(f32[16,128]{1,0:T(8,128)S(1)} %get-tuple-element.142), channel_id=1, source_target_pairs={{0,8},{8,0},{16,24},{24,16},{32,40},{40,32},{48,56},{56,48},{64,72... | collective-permute-start | bytes 24584 | tf_op jit(solution)/shard_map/ppermute | solution.py:412
  154.7 4.3 %collective-permute-start.31 = (f32[16,128]{1,0:T(8,128)S(1)}, f32[16,128]{1,0:T(8,128)S(1)}, u32[]{:S(2)}, u32[]{:S(2)}) collective-permute-start(f32[16,128]{1,0:T(8,128)S(1)} %get-tuple-element.143), channel_id=1, source_target_pairs={{0,7},{1,2},{2,1},{3,4},{4,3},{5,6},{6,5},{7,0},{8,15},{9,10},{10,... | collective-permute-start | bytes 24584 | tf_op jit(solution)/shard_map/ppermute | solution.py:413
  (9 other events, 26.0 us)

commit v8 on v7

--- a/solution.py
+++ b/solution.py
@@ -15,7 +15,7 @@
 HALO = 16
 EXT = ROWS + 4 * HALO
 KOFF = 6
-EARLY = 16
+EARLY = 8
 OWN = 6 * 128
 WIDTH = 7 * 128
 jacobi_weight = 2.0 / 3.0
@@ -116,9 +116,9 @@
 
 
 def first_kernel(*refs):
-    sources, off, rest = refs[:8], refs[8], refs[9:]
-    v, wj, ptd, pick, z, ze, ids, extra, slopes, s0, s1, s2, s3, near = rest[:14]
-    here, sems, far = rest[14:22], rest[22], rest[23]
+    sources, off, rest = refs[:7], refs[7], refs[8:]
+    v, wj, ptd, pick, z, ze, ids, spared, slopes, s0, s1, s2, s3, near = rest[:14]
+    here, sems, far = rest[14:21], rest[21], rest[22]
     copies = [pltpu.make_async_copy(x, y, sems.at[n]) for n, (x, y) in enumerate(zip(sources, here))]
     for c in copies:
         c.start()
@@ -126,7 +126,7 @@
     ahead.start()
     for c in copies:
         c.wait()
-    start, jac, pt, inverse, listed, owner, slot, shifts = here
+    start, jac, pt, listed, owner, slot, shifts = here
     v[...] = twice(start[...])
     for n in range(ROWS // 2):
         wj[:, 128 * n : 128 * n + 128] = pair_rows(jac[128 * n : 128 * n + 128, :] * jacobi_weight)
@@ -155,15 +155,12 @@
     for s, out in enumerate((s0, s1, s2, s3)):
         for k, x in enumerate(parts):
             out[k] = x[HALO * s : HALO * s + HALO]
-    wide = jnp.concatenate([inverse[...], jnp.zeros((BS, 104), F32)], axis=1)
-    wide = jnp.concatenate([wide, jnp.zeros((BS, 128), F32)], axis=0).T[0:24]
-    extra[4:16, :] = wide[0:12] + swap(wide[12:24])
     number = jnp.concatenate([number, jnp.zeros((1, 128 - ROWS), F32)], axis=1)
     lane = lax.broadcasted_iota(jnp.int32, (1, 128), 1)
     spare = (lane >= ROWS) & (lane < BS)
     for r in range(3):
-        extra[r : r + 1, :] = jnp.where(spare, pltpu.roll(jnp.broadcast_to(number, (8, 128)), ROWS - 16 * r, 1)[0:1], 0.0)
-    extra[3:4, :] = jnp.zeros((1, 128), F32)
+        spared[r : r + 1, :] = jnp.where(spare, pltpu.roll(jnp.broadcast_to(number, (8, 128)), ROWS - 16 * r, 1)[0:1], 0.0)
+    spared[3:4, :] = jnp.zeros((1, 128), F32)
     for k in range(4):
         slopes[k : k + 1, :] = jnp.broadcast_to(shifts[:, k : k + 1], (1, 128))
     ahead.wait()
@@ -186,17 +183,19 @@
     w[768:896, at] = pair_rows(jnp.concatenate([dbuf[row], dbuf[row + 1]], axis=0))
 
 
-def operator_kernel(off, diag, cols, near, wa, wb, gather, buf, dbuf, cbuf, sems):
+def operator_kernel(off, diag, cols, inverse, near, wa, wb, gather, inv, buf, dbuf, cbuf, ibuf, sems, isem):
     steps = (ROWS - EARLY) // 8
     named = pltpu.make_async_copy(cols, cbuf, sems.at[0])
     named.start()
+    small = pltpu.make_async_copy(inverse, ibuf, isem)
+    small.start()
     middle = pltpu.make_async_copy(diag, dbuf, sems.at[1])
     middle.start()
     later = [
         pltpu.make_async_copy(off.at[pl.ds(EARLY + 8 * g, 8)], buf.at[pl.ds(8 * g, 8)], sems.at[2 + g])
         for g in range(steps)
     ]
-    for c in later:
+    for c in later[:3]:
         c.start()
     named.wait()
     turn_x = (lax.axis_index("gx") % 2) * HALO
@@ -211,11 +210,17 @@
     for p in range(3):
         hit = (lane == number[:, 2 * p : 2 * p + 1]) | (lane == number[:, 2 * p + 1 : 2 * p + 2] + 128.0)
         gather[ROWS * p : ROWS * p + ROWS, :] = hit.astype(F32).astype(BF16)
+    small.wait()
+    wide = jnp.concatenate([ibuf[...], jnp.zeros((BS, 104), F32)], axis=1)
+    wide = jnp.concatenate([wide, jnp.zeros((BS, 128), F32)], axis=0).T[0:24]
+    inv[...] = wide[0:12] + swap(wide[12:24])
     middle.wait()
     for n in range(0, EARLY, 2):
         pack_rows(near, n, dbuf, n, wa)
     for g in range(steps):
         later[g].wait()
+        if g + 3 < steps:
+            later[g + 3].start()
         for n in range(8 * g, 8 * g + 8, 2):
             pack_rows(buf, n, dbuf, EARLY + n, wa if EARLY + n < ROWS // 2 else wb)
 
@@ -240,7 +245,7 @@
         line = lax.dot_general(ones, x, LAST, preferred_element_type=F32)[0:1]
         p[k : k + 1, :] = line + extra[0][k : k + 1, :] if extra else line
     if extra:
-        p[4:16, :] = extra[0][4:16, :]
+        p[4:16, :] = extra[1][...]
 
 
 def coarse_kernel(same, other, ids, ptd, g0, g1, g2, g3, mask, pte, xp):
@@ -436,13 +441,12 @@
         start,
         jacobi_inv.reshape(ROWS * BS, BS),
         jnp.transpose(prolong, (0, 2, 1)),
-        jnp.transpose(coarse_inv, (1, 2, 0)).reshape(BS, 24),
         send_rows[0],
         owner.reshape(1, ROWS),
         agg_slot.reshape(1, ROWS),
         shifts.reshape(1, 4),
     ]
-    v, wj, ptd, pick, z, ze, id_col, extra, slopes, *sends, near = call(
+    v, wj, ptd, pick, z, ze, id_col, spared, slopes, *sends, near = call(
         first_kernel,
         [
             shape(ROWS, 128),
@@ -452,7 +456,7 @@
             shape(ROWS, 128),
             shape(ROWS, 128),
             shape(ROWS, 128),
-            shape(16, 128),
+            shape(4, 128),
             shape(4, 128),
         ]
         + [shape(6, HALO, 128)] * 4
@@ -466,17 +470,21 @@
     )
     got = exchange(sends)
     half = kept(WIDTH, ROWS * BS // 2, dtype=BF16)
-    *w_op, gather = call(
+    inverse = jnp.transpose(coarse_inv, (1, 2, 0)).reshape(BS, 24)
+    *w_op, gather, inv = call(
         operator_kernel,
-        [half, half, shape(3 * ROWS, 256, dtype=BF16)],
+        [half, half, shape(3 * ROWS, 256, dtype=BF16), shape(12, 128)],
         *matrices,
+        pltpu.with_memory_space_constraint(inverse, pltpu.HBM),
         near,
-        specs=[HBM] * 3 + [VM],
+        specs=[HBM] * 4 + [VM],
         scratch=[
             pltpu.VMEM((ROWS - EARLY, KOFF, BS, BS), F32),
             pltpu.VMEM((ROWS, BS, BS), F32),
             pltpu.VMEM((KOFF, ROWS), jnp.int32),
+            pltpu.VMEM((BS, 24), F32),
             pltpu.SemaphoreType.DMA((2 + (ROWS - EARLY) // 8,)),
+            pltpu.SemaphoreType.DMA,
         ],
         flops=2_000_000_000,
         name="operator",
@@ -495,7 +503,7 @@
             *w_op,
             gather,
             ptd,
-            *([] if k else [extra]),
+            *([] if k else [spared, inv]),
             name="restrict",
         )
         if k == 0:

time: 178 us -> 179 us (level)
  transfers between devices with their start and end apart: 33 -> 33, of which waited for: 8 -> 8; matrix products, arithmetic and copies ran while one was open for 0% -> 0% of each run, Pallas kernels for 4% -> 5%
where the time goes in v8:
time: 179 us
  blocking collectives  89.7 us (50%)
  starting transfers between devices  36.6 us (20%)
  Pallas kernels  35.6 us (20%)
  waiting for transfers between devices  16 us (9%)
    all_to_all x4, blocking collectives, everywhere(): lax.all_to_all(y, ('gx', 'gy'), split_axis=0, concat_axis=0, tiled=True)  72.5 us
    pallas_call x24, Pallas kernels, call(): pl.pallas_call(kernel, out_shape=outs, in_specs=specs or [VM] * len(args)...  35.6 us
    ppermute x8, starting transfers between devices, exchange(): lax.ppermute(sends[0], 'gx', swap_pairs(nx, 1))  19 us
    all_to_all x1, blocking collectives, everywhere_by_core(): lax.all_to_all(y, ('gx', 'gy'), split_axis=0, concat_axis=0, tiled=True,...  17.2 us
    ppermute x8, waiting for transfers between devices, exchange(): lax.ppermute(sends[0], 'gx', swap_pairs(nx, 1))  14.4 us
    ppermute x8, starting transfers between devices, exchange(): lax.ppermute(sends[2], 'gy', swap_pairs(ny, 1))  11.1 us
    ppermute x8, starting transfers between devices, exchange(): lax.ppermute(sends[3], 'gy', swap_pairs(ny, 0))  4.15 us
  transfers between devices with their start and end apart: 33, of which 8 were waited for; matrix products, arithmetic and copies ran while one was open for 0% of the time, Pallas kernels for 5%

profile of v8, /device:TPU:1, one launch (start us, length us, event | category | flops | bytes accessed | tf_op | source)
XLA Modules:
  0.0 179.0 jit_solution(842962612849353878)
XLA Ops:
  0.6 2.9 %first.1 = (f32[48,128]{1,0:T(8,128)S(1)}, bf16[128,3072]{1,0:T(8,128)(2,1)S(1)}, f32[8,48,128]{2,1,0:T(8,128)S(1)}, bf16[64,48]{1,0:T(8,128)(2,1)S(1)}, f32[48,...) custom-call(f32[48,64]{1,0:T(8,128)} %refs_0_.1, ...), custom_call_target="tpu_custom_call" | custom-call | flops 2000000 | bytes 100000 | tf_op jit(solution)/shard_map/first/pallas_call | solution.py:395
  3.6 6.9 %collective-permute-start = (f32[6,16,128]{2,1,0:T(8,128)S(1)}, f32[6,16,128]{2,1,0:T(8,128)S(1)}, u32[]{:S(2)}, u32[]{:S(2)}) collective-permute-start(f32[6,16,128]{2,1,0:T(8,128)S(1)} %get-tuple-element.82), channel_id=1, source_target_pairs={{0,120},{8,16},{16,8},{24,32},{32,24},{40,48},{48,40},{56,64},{64,... | collective-permute-start | bytes 147464 | tf_op jit(solution)/shard_map/ppermute | solution.py:416
  10.4 2.1 %collective-permute-start.2 = (f32[6,16,128]{2,1,0:T(8,128)S(1)}, f32[6,16,128]{2,1,0:T(8,128)S(1)}, u32[]{:S(2)}, u32[]{:S(2)}) collective-permute-start(f32[6,16,128]{2,1,0:T(8,128)S(1)} %get-tuple-element.84), channel_id=1, source_target_pairs={{0,7},{1,2},{2,1},{3,4},{4,3},{5,6},{6,5},{7,0},{8,15},{9,10},{10,... | collective-permute-start | bytes 147464 | tf_op jit(solution)/shard_map/ppermute | solution.py:418
  13.6 6.2 %operator.1 = (bf16[896,1536]{1,0:T(8,128)(2,1)S(1)}, bf16[896,1536]{1,0:T(8,128)(2,1)S(1)}, bf16[144,256]{1,0:T(8,128)(2,1)S(1)}, f32[12,128]{1,0:T(8,128)S(1)}) custom-call(f32[48,6,64,64]{3,2,1,0:T(8,128)} %off.1, f32[48,64,64]{2,1,0:T(8,128)} %diag.1, s32[6,48]{1,0:T(8,128)} %bitcast.31, f32[64,24]{1,0:T(8,128)} %bitcast.30, ...), custom_call_target="tpu_custom_call" | custom-call | flops 2000000000 | bytes 100000 | tf_op jit(solution)/shard_map/operator/pallas_call | solution.py:395
  21.4 17.2 %all_to_all.25.same = f32[64,16,128]{2,1,0:T(8,128)S(1)} all-to-all(f32[64,16,128]{2,1,0:T(8,128)S(1)} %broadcast_in_dim.12), channel_id=1, replica_groups={{0,2,4,6,8,10,12,14,16,18,20,22,24,26,28,30,32,34,36,38,40,42,44,46,48,..., dimensions={0} | all-to-all | bytes 1048576 | tf_op jit(solution)/shard_map/all_to_all | solution.py:433
  38.6 2.3 %collective-permute-start.4 = (f32[64,16,128]{2,1,0:T(8,128)S(1)}, f32[64,16,128]{2,1,0:T(8,128)S(1)}, u32[]{:S(2)}, u32[]{:S(2)}) collective-permute-start(f32[64,16,128]{2,1,0:T(8,128)S(1)} %all_to_all.25.same), channel_id=1, source_target_pairs={{0,1},{1,0},{2,3},{3,2},{4,5},{5,4},{6,7},{7,6},{8,9},{9,8},{10,11... | collective-permute-start | bytes 1572872 | tf_op jit(solution)/shard_map/ppermute | solution.py:434
  42.4 3.2 %coarse.1 = (bf16[8192,128]{1,0:T(8,128)(2,1)S(1)}, f32[8,112,128]{2,1,0:T(8,128)S(1)}, f32[64,8,128]{2,1,0:T(8,128)S(1)}) custom-call(f32[64,16,128]{2,1,0:T(8,128)S(1)} %all_to_all.25.same, f32[64,16,128]{2,1,0:T(8,128)S(1)} %collective-permute-done.4.other, f32[48,128]{1,0:T(8,128)S(1)} %get-tuple-element.91.ids, ...), custom_call_target="tpu_custom_call" | custom-call | flops 2000000 | bytes 100000 | tf_op jit(solution)/shard_map/coarse/pallas_call | solution.py:395
  45.6 2.3 %correct.4 = (f32[48,128]{1,0:T(8,128)S(1)}, f32[16,128]{1,0:T(8,128)S(1)}, f32[16,128]{1,0:T(8,128)S(1)}, f32[16,128]{1,0:T(8,128)S(1)}, f32[16,128]{1,0:T(8,128)S(1)}) custom-call(f32[64,8,128]{2,1,0:T(8,128)S(1)} %get-tuple-element.92.x, bf16[8192,128]{1,0:T(8,128)(2,1)S(1)} %get-tuple-element.93.mask, f32[8,112,128]{2,1,0:T(8,128)S(1)} %get-tuple-element.94.pte, ...), custom_call_target="tpu_custom_call" | custom-call | flops 2000000 | bytes 100000 | tf_op jit(solution)/shard_map/correct/pallas_call | solution.py:395
  50.8 3.0 %collective-permute-done.5.h0 = f32[16,128]{1,0:T(8,128)S(1)} collective-permute-done((f32[16,128]{1,0:T(8,128)S(1)}, f32[16,128]{1,0:T(8,128)S(1)}, u32[]{:S(2)}, u32[]{:S(2)}) %collective-permute-start.5) | collective-permute-done | bytes 8224 | tf_op jit(solution)/shard_map/ppermute | solution.py:416
  55.2 2.0 %collective-permute-start.9 = (f32[16,128]{1,0:T(8,128)S(1)}, f32[16,128]{1,0:T(8,128)S(1)}, u32[]{:S(2)}, u32[]{:S(2)}) collective-permute-start(f32[16,128]{1,0:T(8,128)S(1)} %get-tuple-element.106), channel_id=1, source_target_pairs={{0,120},{8,16},{16,8},{24,32},{32,24},{40,48},{48,40},{56,64},{64,... | collective-permute-start | bytes 24584 | tf_op jit(solution)/shard_map/ppermute | solution.py:416
  62.3 18.3 %all_to_all.26 = f32[128,4,128]{2,1,0:T(4,128)S(1)} all-to-all(f32[128,4,128]{2,1,0:T(4,128)S(1)} %broadcast_in_dim.13), channel_id=1, replica_groups=mesh['gx'=16,'gy'=8] {'gx','gy'}, dimensions={0} | all-to-all | bytes 524288 | tf_op jit(solution)/shard_map/all_to_all | solution.py:426
  80.6 2.3 %correct.5 = (f32[48,128]{1,0:T(8,128)S(1)}, f32[16,128]{1,0:T(8,128)S(1)}, f32[16,128]{1,0:T(8,128)S(1)}, f32[16,128]{1,0:T(8,128)S(1)}, f32[16,128]{1,0:T(8,128)S(1)}) custom-call(f32[64,8,128]{2,1,0:T(8,128)S(1)} %bitcast.24, bf16[8192,128]{1,0:T(8,128)(2,1)S(1)} %get-tuple-element.93.mask, f32[8,112,128]{2,1,0:T(8,128)S(1)} %get-tuple-element.94.pte, ...), custom_call_target="tpu_custom_call" | custom-call | flops 2000000 | bytes 100000 | tf_op jit(solution)/shard_map/correct/pallas_call | solution.py:395
  85.7 3.0 %collective-permute-done.13.h0 = f32[16,128]{1,0:T(8,128)S(1)} collective-permute-done((f32[16,128]{1,0:T(8,128)S(1)}, f32[16,128]{1,0:T(8,128)S(1)}, u32[]{:S(2)}, u32[]{:S(2)}) %collective-permute-start.13) | collective-permute-done | bytes 8224 | tf_op jit(solution)/shard_map/ppermute | solution.py:416
  90.2 2.5 %collective-permute-start.17 = (f32[16,128]{1,0:T(8,128)S(1)}, f32[16,128]{1,0:T(8,128)S(1)}, u32[]{:S(2)}, u32[]{:S(2)}) collective-permute-start(f32[16,128]{1,0:T(8,128)S(1)} %get-tuple-element.120), channel_id=1, source_target_pairs={{0,120},{8,16},{16,8},{24,32},{32,24},{40,48},{48,40},{56,64},{64,... | collective-permute-start | bytes 24584 | tf_op jit(solution)/shard_map/ppermute | solution.py:416
  92.7 1.8 %collective-permute-start.19 = (f32[16,128]{1,0:T(8,128)S(1)}, f32[16,128]{1,0:T(8,128)S(1)}, u32[]{:S(2)}, u32[]{:S(2)}) collective-permute-start(f32[16,128]{1,0:T(8,128)S(1)} %get-tuple-element.122), channel_id=1, source_target_pairs={{0,7},{1,2},{2,1},{3,4},{4,3},{5,6},{6,5},{7,0},{8,15},{9,10},{10,... | collective-permute-start | bytes 24584 | tf_op jit(solution)/shard_map/ppermute | solution.py:418
  97.5 18.9 %all_to_all.27 = f32[128,4,128]{2,1,0:T(4,128)S(1)} all-to-all(f32[128,4,128]{2,1,0:T(4,128)S(1)} %broadcast_in_dim.14), channel_id=1, replica_groups=mesh['gx'=16,'gy'=8] {'gx','gy'}, dimensions={0} | all-to-all | bytes 524288 | tf_op jit(solution)/shard_map/all_to_all | solution.py:426
  116.4 2.3 %correct.6 = (f32[48,128]{1,0:T(8,128)S(1)}, f32[16,128]{1,0:T(8,128)S(1)}, f32[16,128]{1,0:T(8,128)S(1)}, f32[16,128]{1,0:T(8,128)S(1)}, f32[16,128]{1,0:T(8,128)S(1)}) custom-call(f32[64,8,128]{2,1,0:T(8,128)S(1)} %bitcast.25, bf16[8192,128]{1,0:T(8,128)(2,1)S(1)} %get-tuple-element.93.mask, f32[8,112,128]{2,1,0:T(8,128)S(1)} %get-tuple-element.94.pte, ...), custom_call_target="tpu_custom_call" | custom-call | flops 2000000 | bytes 100000 | tf_op jit(solution)/shard_map/correct/pallas_call | solution.py:395
  121.5 3.0 %collective-permute-done.21.h0 = f32[16,128]{1,0:T(8,128)S(1)} collective-permute-done((f32[16,128]{1,0:T(8,128)S(1)}, f32[16,128]{1,0:T(8,128)S(1)}, u32[]{:S(2)}, u32[]{:S(2)}) %collective-permute-start.21) | collective-permute-done | bytes 8224 | tf_op jit(solution)/shard_map/ppermute | solution.py:416
  125.9 2.3 %collective-permute-start.25 = (f32[16,128]{1,0:T(8,128)S(1)}, f32[16,128]{1,0:T(8,128)S(1)}, u32[]{:S(2)}, u32[]{:S(2)}) collective-permute-start(f32[16,128]{1,0:T(8,128)S(1)} %get-tuple-element.134), channel_id=1, source_target_pairs={{0,120},{8,16},{16,8},{24,32},{32,24},{40,48},{48,40},{56,64},{64,... | collective-permute-start | bytes 24584 | tf_op jit(solution)/shard_map/ppermute | solution.py:416
  128.3 1.8 %collective-permute-start.27 = (f32[16,128]{1,0:T(8,128)S(1)}, f32[16,128]{1,0:T(8,128)S(1)}, u32[]{:S(2)}, u32[]{:S(2)}) collective-permute-start(f32[16,128]{1,0:T(8,128)S(1)} %get-tuple-element.136), channel_id=1, source_target_pairs={{0,7},{1,2},{2,1},{3,4},{4,3},{5,6},{6,5},{7,0},{8,15},{9,10},{10,... | collective-permute-start | bytes 24584 | tf_op jit(solution)/shard_map/ppermute | solution.py:418
  133.0 18.9 %all_to_all.28 = f32[128,4,128]{2,1,0:T(4,128)S(1)} all-to-all(f32[128,4,128]{2,1,0:T(4,128)S(1)} %broadcast_in_dim.15), channel_id=1, replica_groups=mesh['gx'=16,'gy'=8] {'gx','gy'}, dimensions={0} | all-to-all | bytes 524288 | tf_op jit(solution)/shard_map/all_to_all | solution.py:426
  151.9 2.3 %correct.7 = (f32[48,128]{1,0:T(8,128)S(1)}, f32[16,128]{1,0:T(8,128)S(1)}, f32[16,128]{1,0:T(8,128)S(1)}, f32[16,128]{1,0:T(8,128)S(1)}, f32[16,128]{1,0:T(8,128)S(1)}) custom-call(f32[64,8,128]{2,1,0:T(8,128)S(1)} %bitcast.23, bf16[8192,128]{1,0:T(8,128)(2,1)S(1)} %get-tuple-element.93.mask, f32[8,112,128]{2,1,0:T(8,128)S(1)} %get-tuple-element.94.pte, ...), custom_call_target="tpu_custom_call" | custom-call | flops 2000000 | bytes 100000 | tf_op jit(solution)/shard_map/correct/pallas_call | solution.py:395
  157.0 3.0 %collective-permute-done.29.h0 = f32[16,128]{1,0:T(8,128)S(1)} collective-permute-done((f32[16,128]{1,0:T(8,128)S(1)}, f32[16,128]{1,0:T(8,128)S(1)}, u32[]{:S(2)}, u32[]{:S(2)}) %collective-permute-start.29) | collective-permute-done | bytes 8224 | tf_op jit(solution)/shard_map/ppermute | solution.py:416
  161.3 16.4 %all_to_all.29 = f32[128,1,128]{2,1,0:T(1,128)S(1)} all-to-all(f32[128,1,128]{2,1,0:T(1,128)S(1)} %broadcast_in_dim.17), channel_id=1, replica_groups=mesh['gx'=16,'gy'=8] {'gx','gy'}, dimensions={0} | all-to-all | bytes 131072 | tf_op jit(solution)/shard_map/all_to_all | solution.py:426
  (80 shorter events, 33.1 us)
Async XLA Ops:
  3.6 16.5 %collective-permute-start = (f32[6,16,128]{2,1,0:T(8,128)S(1)}, f32[6,16,128]{2,1,0:T(8,128)S(1)}, u32[]{:S(2)}, u32[]{:S(2)}) collective-permute-start(f32[6,16,128]{2,1,0:T(8,128)S(1)} %get-tuple-element.82), channel_id=1, source_target_pairs={{0,120},{8,16},{16,8},{24,32},{32,24},{40,48},{48,40},{56,64},{64,... | collective-permute-start | bytes 147464 | tf_op jit(solution)/shard_map/ppermute | solution.py:416
  10.4 9.7 %collective-permute-start.1 = (f32[6,16,128]{2,1,0:T(8,128)S(1)}, f32[6,16,128]{2,1,0:T(8,128)S(1)}, u32[]{:S(2)}, u32[]{:S(2)}) collective-permute-start(f32[6,16,128]{2,1,0:T(8,128)S(1)} %get-tuple-element.83), channel_id=1, source_target_pairs={{0,8},{8,0},{16,24},{24,16},{32,40},{40,32},{48,56},{56,48},{64,72... | collective-permute-start | bytes 147464 | tf_op jit(solution)/shard_map/ppermute | solution.py:417
  10.4 9.7 %collective-permute-start.2 = (f32[6,16,128]{2,1,0:T(8,128)S(1)}, f32[6,16,128]{2,1,0:T(8,128)S(1)}, u32[]{:S(2)}, u32[]{:S(2)}) collective-permute-start(f32[6,16,128]{2,1,0:T(8,128)S(1)} %get-tuple-element.84), channel_id=1, source_target_pairs={{0,7},{1,2},{2,1},{3,4},{4,3},{5,6},{6,5},{7,0},{8,15},{9,10},{10,... | collective-permute-start | bytes 147464 | tf_op jit(solution)/shard_map/ppermute | solution.py:418
  12.6 7.6 %collective-permute-start.3 = (f32[6,16,128]{2,1,0:T(8,128)S(1)}, f32[6,16,128]{2,1,0:T(8,128)S(1)}, u32[]{:S(2)}, u32[]{:S(2)}) collective-permute-start(f32[6,16,128]{2,1,0:T(8,128)S(1)} %get-tuple-element.85), channel_id=1, source_target_pairs={{0,1},{1,0},{2,3},{3,2},{4,5},{5,4},{6,7},{7,6},{8,9},{9,8},{10,11... | collective-permute-start | bytes 147464 | tf_op jit(solution)/shard_map/ppermute | solution.py:419
  38.6 3.8 %collective-permute-start.4 = (f32[64,16,128]{2,1,0:T(8,128)S(1)}, f32[64,16,128]{2,1,0:T(8,128)S(1)}, u32[]{:S(2)}, u32[]{:S(2)}) collective-permute-start(f32[64,16,128]{2,1,0:T(8,128)S(1)} %all_to_all.25.same), channel_id=1, source_target_pairs={{0,1},{1,0},{2,3},{3,2},{4,5},{5,4},{6,7},{7,6},{8,9},{9,8},{10,11... | collective-permute-start | bytes 1572872 | tf_op jit(solution)/shard_map/ppermute | solution.py:434
  47.9 5.8 %collective-permute-start.5 = (f32[16,128]{1,0:T(8,128)S(1)}, f32[16,128]{1,0:T(8,128)S(1)}, u32[]{:S(2)}, u32[]{:S(2)}) collective-permute-start(f32[16,128]{1,0:T(8,128)S(1)} %get-tuple-element.100), channel_id=1, source_target_pairs={{0,120},{8,16},{16,8},{24,32},{32,24},{40,48},{48,40},{56,64},{64,... | collective-permute-start | bytes 24584 | tf_op jit(solution)/shard_map/ppermute | solution.py:416
  48.6 5.2 %collective-permute-start.6 = (f32[16,128]{1,0:T(8,128)S(1)}, f32[16,128]{1,0:T(8,128)S(1)}, u32[]{:S(2)}, u32[]{:S(2)}) collective-permute-start(f32[16,128]{1,0:T(8,128)S(1)} %get-tuple-element.101), channel_id=1, source_target_pairs={{0,8},{8,0},{16,24},{24,16},{32,40},{40,32},{48,56},{56,48},{64,72... | collective-permute-start | bytes 24584 | tf_op jit(solution)/shard_map/ppermute | solution.py:417
  48.6 5.2 %collective-permute-start.7 = (f32[16,128]{1,0:T(8,128)S(1)}, f32[16,128]{1,0:T(8,128)S(1)}, u32[]{:S(2)}, u32[]{:S(2)}) collective-permute-start(f32[16,128]{1,0:T(8,128)S(1)} %get-tuple-element.102), channel_id=1, source_target_pairs={{0,7},{1,2},{2,1},{3,4},{4,3},{5,6},{6,5},{7,0},{8,15},{9,10},{10,... | collective-permute-start | bytes 24584 | tf_op jit(solution)/shard_map/ppermute | solution.py:418
  49.3 4.5 %collective-permute-start.8 = (f32[16,128]{1,0:T(8,128)S(1)}, f32[16,128]{1,0:T(8,128)S(1)}, u32[]{:S(2)}, u32[]{:S(2)}) collective-permute-start(f32[16,128]{1,0:T(8,128)S(1)} %get-tuple-element.103), channel_id=1, source_target_pairs={{0,1},{1,0},{2,3},{3,2},{4,5},{5,4},{6,7},{7,6},{8,9},{9,8},{10,11... | collective-permute-start | bytes 24584 | tf_op jit(solution)/shard_map/ppermute | solution.py:419
  55.2 5.8 %collective-permute-start.9 = (f32[16,128]{1,0:T(8,128)S(1)}, f32[16,128]{1,0:T(8,128)S(1)}, u32[]{:S(2)}, u32[]{:S(2)}) collective-permute-start(f32[16,128]{1,0:T(8,128)S(1)} %get-tuple-element.106), channel_id=1, source_target_pairs={{0,120},{8,16},{16,8},{24,32},{32,24},{40,48},{48,40},{56,64},{64,... | collective-permute-start | bytes 24584 | tf_op jit(solution)/shard_map/ppermute | solution.py:416
  57.2 3.8 %collective-permute-start.10 = (f32[16,128]{1,0:T(8,128)S(1)}, f32[16,128]{1,0:T(8,128)S(1)}, u32[]{:S(2)}, u32[]{:S(2)}) collective-permute-start(f32[16,128]{1,0:T(8,128)S(1)} %get-tuple-element.107), channel_id=1, source_target_pairs={{0,8},{8,0},{16,24},{24,16},{32,40},{40,32},{48,56},{56,48},{64,72... | collective-permute-start | bytes 24584 | tf_op jit(solution)/shard_map/ppermute | solution.py:417
  57.2 3.8 %collective-permute-start.11 = (f32[16,128]{1,0:T(8,128)S(1)}, f32[16,128]{1,0:T(8,128)S(1)}, u32[]{:S(2)}, u32[]{:S(2)}) collective-permute-start(f32[16,128]{1,0:T(8,128)S(1)} %get-tuple-element.108), channel_id=1, source_target_pairs={{0,7},{1,2},{2,1},{3,4},{4,3},{5,6},{6,5},{7,0},{8,15},{9,10},{10,... | collective-permute-start | bytes 24584 | tf_op jit(solution)/shard_map/ppermute | solution.py:418
  82.9 5.8 %collective-permute-start.13 = (f32[16,128]{1,0:T(8,128)S(1)}, f32[16,128]{1,0:T(8,128)S(1)}, u32[]{:S(2)}, u32[]{:S(2)}) collective-permute-start(f32[16,128]{1,0:T(8,128)S(1)} %get-tuple-element.114), channel_id=1, source_target_pairs={{0,120},{8,16},{16,8},{24,32},{32,24},{40,48},{48,40},{56,64},{64,... | collective-permute-start | bytes 24584 | tf_op jit(solution)/shard_map/ppermute | solution.py:416
  84.5 4.3 %collective-permute-start.14 = (f32[16,128]{1,0:T(8,128)S(1)}, f32[16,128]{1,0:T(8,128)S(1)}, u32[]{:S(2)}, u32[]{:S(2)}) collective-permute-start(f32[16,128]{1,0:T(8,128)S(1)} %get-tuple-element.115), channel_id=1, source_target_pairs={{0,8},{8,0},{16,24},{24,16},{32,40},{40,32},{48,56},{56,48},{64,72... | collective-permute-start | bytes 24584 | tf_op jit(solution)/shard_map/ppermute | solution.py:417
  84.5 4.3 %collective-permute-start.15 = (f32[16,128]{1,0:T(8,128)S(1)}, f32[16,128]{1,0:T(8,128)S(1)}, u32[]{:S(2)}, u32[]{:S(2)}) collective-permute-start(f32[16,128]{1,0:T(8,128)S(1)} %get-tuple-element.116), channel_id=1, source_target_pairs={{0,7},{1,2},{2,1},{3,4},{4,3},{5,6},{6,5},{7,0},{8,15},{9,10},{10,... | collective-permute-start | bytes 24584 | tf_op jit(solution)/shard_map/ppermute | solution.py:418
  90.2 6.0 %collective-permute-start.17 = (f32[16,128]{1,0:T(8,128)S(1)}, f32[16,128]{1,0:T(8,128)S(1)}, u32[]{:S(2)}, u32[]{:S(2)}) collective-permute-start(f32[16,128]{1,0:T(8,128)S(1)} %get-tuple-element.120), channel_id=1, source_target_pairs={{0,120},{8,16},{16,8},{24,32},{32,24},{40,48},{48,40},{56,64},{64,... | collective-permute-start | bytes 24584 | tf_op jit(solution)/shard_map/ppermute | solution.py:416
  92.7 3.5 %collective-permute-start.18 = (f32[16,128]{1,0:T(8,128)S(1)}, f32[16,128]{1,0:T(8,128)S(1)}, u32[]{:S(2)}, u32[]{:S(2)}) collective-permute-start(f32[16,128]{1,0:T(8,128)S(1)} %get-tuple-element.121), channel_id=1, source_target_pairs={{0,8},{8,0},{16,24},{24,16},{32,40},{40,32},{48,56},{56,48},{64,72... | collective-permute-start | bytes 24584 | tf_op jit(solution)/shard_map/ppermute | solution.py:417
  118.7 5.8 %collective-permute-start.21 = (f32[16,128]{1,0:T(8,128)S(1)}, f32[16,128]{1,0:T(8,128)S(1)}, u32[]{:S(2)}, u32[]{:S(2)}) collective-permute-start(f32[16,128]{1,0:T(8,128)S(1)} %get-tuple-element.128), channel_id=1, source_target_pairs={{0,120},{8,16},{16,8},{24,32},{32,24},{40,48},{48,40},{56,64},{64,... | collective-permute-start | bytes 24584 | tf_op jit(solution)/shard_map/ppermute | solution.py:416
  120.2 4.3 %collective-permute-start.22 = (f32[16,128]{1,0:T(8,128)S(1)}, f32[16,128]{1,0:T(8,128)S(1)}, u32[]{:S(2)}, u32[]{:S(2)}) collective-permute-start(f32[16,128]{1,0:T(8,128)S(1)} %get-tuple-element.129), channel_id=1, source_target_pairs={{0,8},{8,0},{16,24},{24,16},{32,40},{40,32},{48,56},{56,48},{64,72... | collective-permute-start | bytes 24584 | tf_op jit(solution)/shard_map/ppermute | solution.py:417
  120.2 4.3 %collective-permute-start.23 = (f32[16,128]{1,0:T(8,128)S(1)}, f32[16,128]{1,0:T(8,128)S(1)}, u32[]{:S(2)}, u32[]{:S(2)}) collective-permute-start(f32[16,128]{1,0:T(8,128)S(1)} %get-tuple-element.130), channel_id=1, source_target_pairs={{0,7},{1,2},{2,1},{3,4},{4,3},{5,6},{6,5},{7,0},{8,15},{9,10},{10,... | collective-permute-start | bytes 24584 | tf_op jit(solution)/shard_map/ppermute | solution.py:418
  125.9 5.8 %collective-permute-start.25 = (f32[16,128]{1,0:T(8,128)S(1)}, f32[16,128]{1,0:T(8,128)S(1)}, u32[]{:S(2)}, u32[]{:S(2)}) collective-permute-start(f32[16,128]{1,0:T(8,128)S(1)} %get-tuple-element.134), channel_id=1, source_target_pairs={{0,120},{8,16},{16,8},{24,32},{32,24},{40,48},{48,40},{56,64},{64,... | collective-permute-start | bytes 24584 | tf_op jit(solution)/shard_map/ppermute | solution.py:416
  154.2 5.8 %collective-permute-start.29 = (f32[16,128]{1,0:T(8,128)S(1)}, f32[16,128]{1,0:T(8,128)S(1)}, u32[]{:S(2)}, u32[]{:S(2)}) collective-permute-start(f32[16,128]{1,0:T(8,128)S(1)} %get-tuple-element.143), channel_id=1, source_target_pairs={{0,120},{8,16},{16,8},{24,32},{32,24},{40,48},{48,40},{56,64},{64,... | collective-permute-start | bytes 24584 | tf_op jit(solution)/shard_map/ppermute | solution.py:416
  155.8 4.3 %collective-permute-start.30 = (f32[16,128]{1,0:T(8,128)S(1)}, f32[16,128]{1,0:T(8,128)S(1)}, u32[]{:S(2)}, u32[]{:S(2)}) collective-permute-start(f32[16,128]{1,0:T(8,128)S(1)} %get-tuple-element.144), channel_id=1, source_target_pairs={{0,8},{8,0},{16,24},{24,16},{32,40},{40,32},{48,56},{56,48},{64,72... | collective-permute-start | bytes 24584 | tf_op jit(solution)/shard_map/ppermute | solution.py:417
  155.8 4.3 %collective-permute-start.31 = (f32[16,128]{1,0:T(8,128)S(1)}, f32[16,128]{1,0:T(8,128)S(1)}, u32[]{:S(2)}, u32[]{:S(2)}) collective-permute-start(f32[16,128]{1,0:T(8,128)S(1)} %get-tuple-element.145), channel_id=1, source_target_pairs={{0,7},{1,2},{2,1},{3,4},{4,3},{5,6},{6,5},{7,0},{8,15},{9,10},{10,... | collective-permute-start | bytes 24584 | tf_op jit(solution)/shard_map/ppermute | solution.py:418
  (9 other events, 26.0 us)

commit v9 on v7

--- a/solution.py
+++ b/solution.py
@@ -150,8 +150,13 @@
         ptd[c] = twice(pt[:, c, :])
     low = lax.broadcasted_iota(jnp.int32, (ROWS, 128), 1) < BS
     parts = [jnp.where(low, ptd[r], ptd[r + 4]) for r in range(4)] + [ids[...]]
-    parts = [jnp.dot(chosen, x, precision=lax.Precision.HIGHEST, preferred_element_type=F32) for x in parts]
-    parts = [jnp.dot(pick[...], ze[...].astype(BF16), preferred_element_type=F32)] + parts
+    high = [x.astype(BF16) for x in parts]
+    rest = [(x - y.astype(F32)).astype(BF16) for x, y in zip(parts, high)]
+    picked = jnp.concatenate([ze[...].astype(BF16)] + high + rest, axis=1)
+    picked = jnp.dot(pick[...], picked, preferred_element_type=F32)
+    parts = [picked[:, 0:128]]
+    for k in range(1, 6):
+        parts.append(picked[:, 128 * k : 128 * k + 128] + picked[:, 128 * k + 640 : 128 * k + 768])
     for s, out in enumerate((s0, s1, s2, s3)):
         for k, x in enumerate(parts):
             out[k] = x[HALO * s : HALO * s + HALO]

time: 178 us -> 178 us (level)
  no operation moved by 1% of the time
where the time goes in v9:
time: 178 us
  blocking collectives  89.7 us (50%)
  starting transfers between devices  36.6 us (21%)
  Pallas kernels  34.7 us (19%)
  waiting for transfers between devices  16 us (9%)
    all_to_all x4, blocking collectives, everywhere(): lax.all_to_all(y, ('gx', 'gy'), split_axis=0, concat_axis=0, tiled=True)  72.5 us
    pallas_call x24, Pallas kernels, call(): pl.pallas_call(kernel, out_shape=outs, in_specs=specs or [VM] * len(args)...  34.7 us
    ppermute x8, starting transfers between devices, exchange(): lax.ppermute(sends[0], 'gx', swap_pairs(nx, 1))  19 us
    all_to_all x1, blocking collectives, everywhere_by_core(): lax.all_to_all(y, ('gx', 'gy'), split_axis=0, concat_axis=0, tiled=True,...  17.2 us
    ppermute x8, waiting for transfers between devices, exchange(): lax.ppermute(sends[0], 'gx', swap_pairs(nx, 1))  14.4 us
    ppermute x8, starting transfers between devices, exchange(): lax.ppermute(sends[2], 'gy', swap_pairs(ny, 1))  11.1 us
    ppermute x8, starting transfers between devices, exchange(): lax.ppermute(sends[3], 'gy', swap_pairs(ny, 0))  4.15 us
  transfers between devices with their start and end apart: 33, of which 8 were waited for; matrix products, arithmetic and copies ran while one was open for 0% of the time, Pallas kernels for 4%

profile of v9, /device:TPU:1, one launch (start us, length us, event | category | flops | bytes accessed | tf_op | source)
XLA Modules:
  0.0 178.2 jit_solution(2328456989098664437)
XLA Ops:
  0.6 3.0 %first.1 = (f32[48,128]{1,0:T(8,128)S(1)}, bf16[128,3072]{1,0:T(8,128)(2,1)S(1)}, f32[8,48,128]{2,1,0:T(8,128)S(1)}, bf16[64,48]{1,0:T(8,128)(2,1)S(1)}, f32[48,...) custom-call(f32[48,64]{1,0:T(8,128)} %refs_0_.1, ...), custom_call_target="tpu_custom_call" | custom-call | flops 2000000 | bytes 100000 | tf_op jit(solution)/shard_map/first/pallas_call | solution.py:395
  3.7 6.9 %collective-permute-start = (f32[6,16,128]{2,1,0:T(8,128)S(1)}, f32[6,16,128]{2,1,0:T(8,128)S(1)}, u32[]{:S(2)}, u32[]{:S(2)}) collective-permute-start(f32[6,16,128]{2,1,0:T(8,128)S(1)} %get-tuple-element.81), channel_id=1, source_target_pairs={{0,120},{8,16},{16,8},{24,32},{32,24},{40,48},{48,40},{56,64},{64,... | collective-permute-start | bytes 147464 | tf_op jit(solution)/shard_map/ppermute | solution.py:416
  10.5 2.1 %collective-permute-start.2 = (f32[6,16,128]{2,1,0:T(8,128)S(1)}, f32[6,16,128]{2,1,0:T(8,128)S(1)}, u32[]{:S(2)}, u32[]{:S(2)}) collective-permute-start(f32[6,16,128]{2,1,0:T(8,128)S(1)} %get-tuple-element.83), channel_id=1, source_target_pairs={{0,7},{1,2},{2,1},{3,4},{4,3},{5,6},{6,5},{7,0},{8,15},{9,10},{10,... | collective-permute-start | bytes 147464 | tf_op jit(solution)/shard_map/ppermute | solution.py:418
  13.7 5.2 %operator.1 = (bf16[896,1536]{1,0:T(8,128)(2,1)S(1)}, bf16[896,1536]{1,0:T(8,128)(2,1)S(1)}, bf16[144,256]{1,0:T(8,128)(2,1)S(1)}) custom-call(f32[48,6,64,64]{3,2,1,0:T(8,128)} %off.1, f32[48,64,64]{2,1,0:T(8,128)} %diag.1, s32[6,48]{1,0:T(8,128)} %bitcast.31, f32[16,6,64,64]{3,2,1,0:T(8,128)S(1)} %get-tuple-element.78.near), custom_call_target="tpu_custom_call" | custom-call | flops 2000000000 | bytes 100000 | tf_op jit(solution)/shard_map/operator/pallas_call | solution.py:395
  20.5 17.2 %all_to_all.25.same = f32[64,16,128]{2,1,0:T(8,128)S(1)} all-to-all(f32[64,16,128]{2,1,0:T(8,128)S(1)} %broadcast_in_dim.12), channel_id=1, replica_groups={{0,2,4,6,8,10,12,14,16,18,20,22,24,26,28,30,32,34,36,38,40,42,44,46,48,..., dimensions={0} | all-to-all | bytes 1048576 | tf_op jit(solution)/shard_map/all_to_all | solution.py:433
  37.7 2.3 %collective-permute-start.4 = (f32[64,16,128]{2,1,0:T(8,128)S(1)}, f32[64,16,128]{2,1,0:T(8,128)S(1)}, u32[]{:S(2)}, u32[]{:S(2)}) collective-permute-start(f32[64,16,128]{2,1,0:T(8,128)S(1)} %all_to_all.25.same), channel_id=1, source_target_pairs={{0,1},{1,0},{2,3},{3,2},{4,5},{5,4},{6,7},{7,6},{8,9},{9,8},{10,11... | collective-permute-start | bytes 1572872 | tf_op jit(solution)/shard_map/ppermute | solution.py:434
  41.5 3.2 %coarse.1 = (bf16[8192,128]{1,0:T(8,128)(2,1)S(1)}, f32[8,112,128]{2,1,0:T(8,128)S(1)}, f32[64,8,128]{2,1,0:T(8,128)S(1)}) custom-call(f32[64,16,128]{2,1,0:T(8,128)S(1)} %all_to_all.25.same, f32[64,16,128]{2,1,0:T(8,128)S(1)} %collective-permute-done.4.other, f32[48,128]{1,0:T(8,128)S(1)} %get-tuple-element.89.ids, ...), custom_call_target="tpu_custom_call" | custom-call | flops 2000000 | bytes 100000 | tf_op jit(solution)/shard_map/coarse/pallas_call | solution.py:395
  44.7 2.3 %correct.4 = (f32[48,128]{1,0:T(8,128)S(1)}, f32[16,128]{1,0:T(8,128)S(1)}, f32[16,128]{1,0:T(8,128)S(1)}, f32[16,128]{1,0:T(8,128)S(1)}, f32[16,128]{1,0:T(8,128)S(1)}) custom-call(f32[64,8,128]{2,1,0:T(8,128)S(1)} %get-tuple-element.90.x, bf16[8192,128]{1,0:T(8,128)(2,1)S(1)} %get-tuple-element.91.mask, f32[8,112,128]{2,1,0:T(8,128)S(1)} %get-tuple-element.92.pte, ...), custom_call_target="tpu_custom_call" | custom-call | flops 2000000 | bytes 100000 | tf_op jit(solution)/shard_map/correct/pallas_call | solution.py:395
  49.9 3.0 %collective-permute-done.5.h0 = f32[16,128]{1,0:T(8,128)S(1)} collective-permute-done((f32[16,128]{1,0:T(8,128)S(1)}, f32[16,128]{1,0:T(8,128)S(1)}, u32[]{:S(2)}, u32[]{:S(2)}) %collective-permute-start.5) | collective-permute-done | bytes 8224 | tf_op jit(solution)/shard_map/ppermute | solution.py:416
  54.3 2.0 %collective-permute-start.9 = (f32[16,128]{1,0:T(8,128)S(1)}, f32[16,128]{1,0:T(8,128)S(1)}, u32[]{:S(2)}, u32[]{:S(2)}) collective-permute-start(f32[16,128]{1,0:T(8,128)S(1)} %get-tuple-element.104), channel_id=1, source_target_pairs={{0,120},{8,16},{16,8},{24,32},{32,24},{40,48},{48,40},{56,64},{64,... | collective-permute-start | bytes 24584 | tf_op jit(solution)/shard_map/ppermute | solution.py:416
  61.4 18.4 %all_to_all.26 = f32[128,4,128]{2,1,0:T(4,128)S(1)} all-to-all(f32[128,4,128]{2,1,0:T(4,128)S(1)} %broadcast_in_dim.13), channel_id=1, replica_groups=mesh['gx'=16,'gy'=8] {'gx','gy'}, dimensions={0} | all-to-all | bytes 524288 | tf_op jit(solution)/shard_map/all_to_all | solution.py:426
  79.7 2.3 %correct.5 = (f32[48,128]{1,0:T(8,128)S(1)}, f32[16,128]{1,0:T(8,128)S(1)}, f32[16,128]{1,0:T(8,128)S(1)}, f32[16,128]{1,0:T(8,128)S(1)}, f32[16,128]{1,0:T(8,128)S(1)}) custom-call(f32[64,8,128]{2,1,0:T(8,128)S(1)} %bitcast.24, bf16[8192,128]{1,0:T(8,128)(2,1)S(1)} %get-tuple-element.91.mask, f32[8,112,128]{2,1,0:T(8,128)S(1)} %get-tuple-element.92.pte, ...), custom_call_target="tpu_custom_call" | custom-call | flops 2000000 | bytes 100000 | tf_op jit(solution)/shard_map/correct/pallas_call | solution.py:395
  84.8 3.0 %collective-permute-done.13.h0 = f32[16,128]{1,0:T(8,128)S(1)} collective-permute-done((f32[16,128]{1,0:T(8,128)S(1)}, f32[16,128]{1,0:T(8,128)S(1)}, u32[]{:S(2)}, u32[]{:S(2)}) %collective-permute-start.13) | collective-permute-done | bytes 8224 | tf_op jit(solution)/shard_map/ppermute | solution.py:416
  89.3 2.5 %collective-permute-start.17 = (f32[16,128]{1,0:T(8,128)S(1)}, f32[16,128]{1,0:T(8,128)S(1)}, u32[]{:S(2)}, u32[]{:S(2)}) collective-permute-start(f32[16,128]{1,0:T(8,128)S(1)} %get-tuple-element.118), channel_id=1, source_target_pairs={{0,120},{8,16},{16,8},{24,32},{32,24},{40,48},{48,40},{56,64},{64,... | collective-permute-start | bytes 24584 | tf_op jit(solution)/shard_map/ppermute | solution.py:416
  91.8 1.8 %collective-permute-start.19 = (f32[16,128]{1,0:T(8,128)S(1)}, f32[16,128]{1,0:T(8,128)S(1)}, u32[]{:S(2)}, u32[]{:S(2)}) collective-permute-start(f32[16,128]{1,0:T(8,128)S(1)} %get-tuple-element.120), channel_id=1, source_target_pairs={{0,7},{1,2},{2,1},{3,4},{4,3},{5,6},{6,5},{7,0},{8,15},{9,10},{10,... | collective-permute-start | bytes 24584 | tf_op jit(solution)/shard_map/ppermute | solution.py:418
  96.6 18.9 %all_to_all.27 = f32[128,4,128]{2,1,0:T(4,128)S(1)} all-to-all(f32[128,4,128]{2,1,0:T(4,128)S(1)} %broadcast_in_dim.14), channel_id=1, replica_groups=mesh['gx'=16,'gy'=8] {'gx','gy'}, dimensions={0} | all-to-all | bytes 524288 | tf_op jit(solution)/shard_map/all_to_all | solution.py:426
  115.5 2.3 %correct.6 = (f32[48,128]{1,0:T(8,128)S(1)}, f32[16,128]{1,0:T(8,128)S(1)}, f32[16,128]{1,0:T(8,128)S(1)}, f32[16,128]{1,0:T(8,128)S(1)}, f32[16,128]{1,0:T(8,128)S(1)}) custom-call(f32[64,8,128]{2,1,0:T(8,128)S(1)} %bitcast.25, bf16[8192,128]{1,0:T(8,128)(2,1)S(1)} %get-tuple-element.91.mask, f32[8,112,128]{2,1,0:T(8,128)S(1)} %get-tuple-element.92.pte, ...), custom_call_target="tpu_custom_call" | custom-call | flops 2000000 | bytes 100000 | tf_op jit(solution)/shard_map/correct/pallas_call | solution.py:395
  120.6 3.0 %collective-permute-done.21.h0 = f32[16,128]{1,0:T(8,128)S(1)} collective-permute-done((f32[16,128]{1,0:T(8,128)S(1)}, f32[16,128]{1,0:T(8,128)S(1)}, u32[]{:S(2)}, u32[]{:S(2)}) %collective-permute-start.21) | collective-permute-done | bytes 8224 | tf_op jit(solution)/shard_map/ppermute | solution.py:416
  125.0 2.3 %collective-permute-start.25 = (f32[16,128]{1,0:T(8,128)S(1)}, f32[16,128]{1,0:T(8,128)S(1)}, u32[]{:S(2)}, u32[]{:S(2)}) collective-permute-start(f32[16,128]{1,0:T(8,128)S(1)} %get-tuple-element.132), channel_id=1, source_target_pairs={{0,120},{8,16},{16,8},{24,32},{32,24},{40,48},{48,40},{56,64},{64,... | collective-permute-start | bytes 24584 | tf_op jit(solution)/shard_map/ppermute | solution.py:416
  127.4 1.8 %collective-permute-start.27 = (f32[16,128]{1,0:T(8,128)S(1)}, f32[16,128]{1,0:T(8,128)S(1)}, u32[]{:S(2)}, u32[]{:S(2)}) collective-permute-start(f32[16,128]{1,0:T(8,128)S(1)} %get-tuple-element.134), channel_id=1, source_target_pairs={{0,7},{1,2},{2,1},{3,4},{4,3},{5,6},{6,5},{7,0},{8,15},{9,10},{10,... | collective-permute-start | bytes 24584 | tf_op jit(solution)/shard_map/ppermute | solution.py:418
  132.1 18.9 %all_to_all.28 = f32[128,4,128]{2,1,0:T(4,128)S(1)} all-to-all(f32[128,4,128]{2,1,0:T(4,128)S(1)} %broadcast_in_dim.15), channel_id=1, replica_groups=mesh['gx'=16,'gy'=8] {'gx','gy'}, dimensions={0} | all-to-all | bytes 524288 | tf_op jit(solution)/shard_map/all_to_all | solution.py:426
  151.0 2.3 %correct.7 = (f32[48,128]{1,0:T(8,128)S(1)}, f32[16,128]{1,0:T(8,128)S(1)}, f32[16,128]{1,0:T(8,128)S(1)}, f32[16,128]{1,0:T(8,128)S(1)}, f32[16,128]{1,0:T(8,128)S(1)}) custom-call(f32[64,8,128]{2,1,0:T(8,128)S(1)} %bitcast.23, bf16[8192,128]{1,0:T(8,128)(2,1)S(1)} %get-tuple-element.91.mask, f32[8,112,128]{2,1,0:T(8,128)S(1)} %get-tuple-element.92.pte, ...), custom_call_target="tpu_custom_call" | custom-call | flops 2000000 | bytes 100000 | tf_op jit(solution)/shard_map/correct/pallas_call | solution.py:395
  156.2 3.0 %collective-permute-done.29.h0 = f32[16,128]{1,0:T(8,128)S(1)} collective-permute-done((f32[16,128]{1,0:T(8,128)S(1)}, f32[16,128]{1,0:T(8,128)S(1)}, u32[]{:S(2)}, u32[]{:S(2)}) %collective-permute-start.29) | collective-permute-done | bytes 8224 | tf_op jit(solution)/shard_map/ppermute | solution.py:416
  160.4 16.4 %all_to_all.29 = f32[128,1,128]{2,1,0:T(1,128)S(1)} all-to-all(f32[128,1,128]{2,1,0:T(1,128)S(1)} %broadcast_in_dim.17), channel_id=1, replica_groups=mesh['gx'=16,'gy'=8] {'gx','gy'}, dimensions={0} | all-to-all | bytes 131072 | tf_op jit(solution)/shard_map/all_to_all | solution.py:426
  (80 shorter events, 33.1 us)
Async XLA Ops:
  3.7 15.5 %collective-permute-start = (f32[6,16,128]{2,1,0:T(8,128)S(1)}, f32[6,16,128]{2,1,0:T(8,128)S(1)}, u32[]{:S(2)}, u32[]{:S(2)}) collective-permute-start(f32[6,16,128]{2,1,0:T(8,128)S(1)} %get-tuple-element.81), channel_id=1, source_target_pairs={{0,120},{8,16},{16,8},{24,32},{32,24},{40,48},{48,40},{56,64},{64,... | collective-permute-start | bytes 147464 | tf_op jit(solution)/shard_map/ppermute | solution.py:416
  10.5 8.7 %collective-permute-start.1 = (f32[6,16,128]{2,1,0:T(8,128)S(1)}, f32[6,16,128]{2,1,0:T(8,128)S(1)}, u32[]{:S(2)}, u32[]{:S(2)}) collective-permute-start(f32[6,16,128]{2,1,0:T(8,128)S(1)} %get-tuple-element.82), channel_id=1, source_target_pairs={{0,8},{8,0},{16,24},{24,16},{32,40},{40,32},{48,56},{56,48},{64,72... | collective-permute-start | bytes 147464 | tf_op jit(solution)/shard_map/ppermute | solution.py:417
  10.5 8.7 %collective-permute-start.2 = (f32[6,16,128]{2,1,0:T(8,128)S(1)}, f32[6,16,128]{2,1,0:T(8,128)S(1)}, u32[]{:S(2)}, u32[]{:S(2)}) collective-permute-start(f32[6,16,128]{2,1,0:T(8,128)S(1)} %get-tuple-element.83), channel_id=1, source_target_pairs={{0,7},{1,2},{2,1},{3,4},{4,3},{5,6},{6,5},{7,0},{8,15},{9,10},{10,... | collective-permute-start | bytes 147464 | tf_op jit(solution)/shard_map/ppermute | solution.py:418
  12.7 6.6 %collective-permute-start.3 = (f32[6,16,128]{2,1,0:T(8,128)S(1)}, f32[6,16,128]{2,1,0:T(8,128)S(1)}, u32[]{:S(2)}, u32[]{:S(2)}) collective-permute-start(f32[6,16,128]{2,1,0:T(8,128)S(1)} %get-tuple-element.84), channel_id=1, source_target_pairs={{0,1},{1,0},{2,3},{3,2},{4,5},{5,4},{6,7},{7,6},{8,9},{9,8},{10,11... | collective-permute-start | bytes 147464 | tf_op jit(solution)/shard_map/ppermute | solution.py:419
  37.7 3.8 %collective-permute-start.4 = (f32[64,16,128]{2,1,0:T(8,128)S(1)}, f32[64,16,128]{2,1,0:T(8,128)S(1)}, u32[]{:S(2)}, u32[]{:S(2)}) collective-permute-start(f32[64,16,128]{2,1,0:T(8,128)S(1)} %all_to_all.25.same), channel_id=1, source_target_pairs={{0,1},{1,0},{2,3},{3,2},{4,5},{5,4},{6,7},{7,6},{8,9},{9,8},{10,11... | collective-permute-start | bytes 1572872 | tf_op jit(solution)/shard_map/ppermute | solution.py:434
  47.0 5.8 %collective-permute-start.5 = (f32[16,128]{1,0:T(8,128)S(1)}, f32[16,128]{1,0:T(8,128)S(1)}, u32[]{:S(2)}, u32[]{:S(2)}) collective-permute-start(f32[16,128]{1,0:T(8,128)S(1)} %get-tuple-element.98), channel_id=1, source_target_pairs={{0,120},{8,16},{16,8},{24,32},{32,24},{40,48},{48,40},{56,64},{64,... | collective-permute-start | bytes 24584 | tf_op jit(solution)/shard_map/ppermute | solution.py:416
  47.7 5.2 %collective-permute-start.6 = (f32[16,128]{1,0:T(8,128)S(1)}, f32[16,128]{1,0:T(8,128)S(1)}, u32[]{:S(2)}, u32[]{:S(2)}) collective-permute-start(f32[16,128]{1,0:T(8,128)S(1)} %get-tuple-element.99), channel_id=1, source_target_pairs={{0,8},{8,0},{16,24},{24,16},{32,40},{40,32},{48,56},{56,48},{64,72... | collective-permute-start | bytes 24584 | tf_op jit(solution)/shard_map/ppermute | solution.py:417
  47.7 5.2 %collective-permute-start.7 = (f32[16,128]{1,0:T(8,128)S(1)}, f32[16,128]{1,0:T(8,128)S(1)}, u32[]{:S(2)}, u32[]{:S(2)}) collective-permute-start(f32[16,128]{1,0:T(8,128)S(1)} %get-tuple-element.100), channel_id=1, source_target_pairs={{0,7},{1,2},{2,1},{3,4},{4,3},{5,6},{6,5},{7,0},{8,15},{9,10},{10,... | collective-permute-start | bytes 24584 | tf_op jit(solution)/shard_map/ppermute | solution.py:418
  48.4 4.4 %collective-permute-start.8 = (f32[16,128]{1,0:T(8,128)S(1)}, f32[16,128]{1,0:T(8,128)S(1)}, u32[]{:S(2)}, u32[]{:S(2)}) collective-permute-start(f32[16,128]{1,0:T(8,128)S(1)} %get-tuple-element.101), channel_id=1, source_target_pairs={{0,1},{1,0},{2,3},{3,2},{4,5},{5,4},{6,7},{7,6},{8,9},{9,8},{10,11... | collective-permute-start | bytes 24584 | tf_op jit(solution)/shard_map/ppermute | solution.py:419
  54.3 5.8 %collective-permute-start.9 = (f32[16,128]{1,0:T(8,128)S(1)}, f32[16,128]{1,0:T(8,128)S(1)}, u32[]{:S(2)}, u32[]{:S(2)}) collective-permute-start(f32[16,128]{1,0:T(8,128)S(1)} %get-tuple-element.104), channel_id=1, source_target_pairs={{0,120},{8,16},{16,8},{24,32},{32,24},{40,48},{48,40},{56,64},{64,... | collective-permute-start | bytes 24584 | tf_op jit(solution)/shard_map/ppermute | solution.py:416
  56.3 3.8 %collective-permute-start.10 = (f32[16,128]{1,0:T(8,128)S(1)}, f32[16,128]{1,0:T(8,128)S(1)}, u32[]{:S(2)}, u32[]{:S(2)}) collective-permute-start(f32[16,128]{1,0:T(8,128)S(1)} %get-tuple-element.105), channel_id=1, source_target_pairs={{0,8},{8,0},{16,24},{24,16},{32,40},{40,32},{48,56},{56,48},{64,72... | collective-permute-start | bytes 24584 | tf_op jit(solution)/shard_map/ppermute | solution.py:417
  56.3 3.8 %collective-permute-start.11 = (f32[16,128]{1,0:T(8,128)S(1)}, f32[16,128]{1,0:T(8,128)S(1)}, u32[]{:S(2)}, u32[]{:S(2)}) collective-permute-start(f32[16,128]{1,0:T(8,128)S(1)} %get-tuple-element.106), channel_id=1, source_target_pairs={{0,7},{1,2},{2,1},{3,4},{4,3},{5,6},{6,5},{7,0},{8,15},{9,10},{10,... | collective-permute-start | bytes 24584 | tf_op jit(solution)/shard_map/ppermute | solution.py:418
  82.0 5.8 %collective-permute-start.13 = (f32[16,128]{1,0:T(8,128)S(1)}, f32[16,128]{1,0:T(8,128)S(1)}, u32[]{:S(2)}, u32[]{:S(2)}) collective-permute-start(f32[16,128]{1,0:T(8,128)S(1)} %get-tuple-element.112), channel_id=1, source_target_pairs={{0,120},{8,16},{16,8},{24,32},{32,24},{40,48},{48,40},{56,64},{64,... | collective-permute-start | bytes 24584 | tf_op jit(solution)/shard_map/ppermute | solution.py:416
  83.6 4.3 %collective-permute-start.14 = (f32[16,128]{1,0:T(8,128)S(1)}, f32[16,128]{1,0:T(8,128)S(1)}, u32[]{:S(2)}, u32[]{:S(2)}) collective-permute-start(f32[16,128]{1,0:T(8,128)S(1)} %get-tuple-element.113), channel_id=1, source_target_pairs={{0,8},{8,0},{16,24},{24,16},{32,40},{40,32},{48,56},{56,48},{64,72... | collective-permute-start | bytes 24584 | tf_op jit(solution)/shard_map/ppermute | solution.py:417
  83.6 4.3 %collective-permute-start.15 = (f32[16,128]{1,0:T(8,128)S(1)}, f32[16,128]{1,0:T(8,128)S(1)}, u32[]{:S(2)}, u32[]{:S(2)}) collective-permute-start(f32[16,128]{1,0:T(8,128)S(1)} %get-tuple-element.114), channel_id=1, source_target_pairs={{0,7},{1,2},{2,1},{3,4},{4,3},{5,6},{6,5},{7,0},{8,15},{9,10},{10,... | collective-permute-start | bytes 24584 | tf_op jit(solution)/shard_map/ppermute | solution.py:418
  89.3 6.0 %collective-permute-start.17 = (f32[16,128]{1,0:T(8,128)S(1)}, f32[16,128]{1,0:T(8,128)S(1)}, u32[]{:S(2)}, u32[]{:S(2)}) collective-permute-start(f32[16,128]{1,0:T(8,128)S(1)} %get-tuple-element.118), channel_id=1, source_target_pairs={{0,120},{8,16},{16,8},{24,32},{32,24},{40,48},{48,40},{56,64},{64,... | collective-permute-start | bytes 24584 | tf_op jit(solution)/shard_map/ppermute | solution.py:416
  117.8 5.8 %collective-permute-start.21 = (f32[16,128]{1,0:T(8,128)S(1)}, f32[16,128]{1,0:T(8,128)S(1)}, u32[]{:S(2)}, u32[]{:S(2)}) collective-permute-start(f32[16,128]{1,0:T(8,128)S(1)} %get-tuple-element.126), channel_id=1, source_target_pairs={{0,120},{8,16},{16,8},{24,32},{32,24},{40,48},{48,40},{56,64},{64,... | collective-permute-start | bytes 24584 | tf_op jit(solution)/shard_map/ppermute | solution.py:416
  119.3 4.3 %collective-permute-start.22 = (f32[16,128]{1,0:T(8,128)S(1)}, f32[16,128]{1,0:T(8,128)S(1)}, u32[]{:S(2)}, u32[]{:S(2)}) collective-permute-start(f32[16,128]{1,0:T(8,128)S(1)} %get-tuple-element.127), channel_id=1, source_target_pairs={{0,8},{8,0},{16,24},{24,16},{32,40},{40,32},{48,56},{56,48},{64,72... | collective-permute-start | bytes 24584 | tf_op jit(solution)/shard_map/ppermute | solution.py:417
  119.3 4.3 %collective-permute-start.23 = (f32[16,128]{1,0:T(8,128)S(1)}, f32[16,128]{1,0:T(8,128)S(1)}, u32[]{:S(2)}, u32[]{:S(2)}) collective-permute-start(f32[16,128]{1,0:T(8,128)S(1)} %get-tuple-element.128), channel_id=1, source_target_pairs={{0,7},{1,2},{2,1},{3,4},{4,3},{5,6},{6,5},{7,0},{8,15},{9,10},{10,... | collective-permute-start | bytes 24584 | tf_op jit(solution)/shard_map/ppermute | solution.py:418
  125.0 5.8 %collective-permute-start.25 = (f32[16,128]{1,0:T(8,128)S(1)}, f32[16,128]{1,0:T(8,128)S(1)}, u32[]{:S(2)}, u32[]{:S(2)}) collective-permute-start(f32[16,128]{1,0:T(8,128)S(1)} %get-tuple-element.132), channel_id=1, source_target_pairs={{0,120},{8,16},{16,8},{24,32},{32,24},{40,48},{48,40},{56,64},{64,... | collective-permute-start | bytes 24584 | tf_op jit(solution)/shard_map/ppermute | solution.py:416
  127.4 3.5 %collective-permute-start.26 = (f32[16,128]{1,0:T(8,128)S(1)}, f32[16,128]{1,0:T(8,128)S(1)}, u32[]{:S(2)}, u32[]{:S(2)}) collective-permute-start(f32[16,128]{1,0:T(8,128)S(1)} %get-tuple-element.133), channel_id=1, source_target_pairs={{0,8},{8,0},{16,24},{24,16},{32,40},{40,32},{48,56},{56,48},{64,72... | collective-permute-start | bytes 24584 | tf_op jit(solution)/shard_map/ppermute | solution.py:417
  153.3 5.8 %collective-permute-start.29 = (f32[16,128]{1,0:T(8,128)S(1)}, f32[16,128]{1,0:T(8,128)S(1)}, u32[]{:S(2)}, u32[]{:S(2)}) collective-permute-start(f32[16,128]{1,0:T(8,128)S(1)} %get-tuple-element.141), channel_id=1, source_target_pairs={{0,120},{8,16},{16,8},{24,32},{32,24},{40,48},{48,40},{56,64},{64,... | collective-permute-start | bytes 24584 | tf_op jit(solution)/shard_map/ppermute | solution.py:416
  154.9 4.3 %collective-permute-start.30 = (f32[16,128]{1,0:T(8,128)S(1)}, f32[16,128]{1,0:T(8,128)S(1)}, u32[]{:S(2)}, u32[]{:S(2)}) collective-permute-start(f32[16,128]{1,0:T(8,128)S(1)} %get-tuple-element.142), channel_id=1, source_target_pairs={{0,8},{8,0},{16,24},{24,16},{32,40},{40,32},{48,56},{56,48},{64,72... | collective-permute-start | bytes 24584 | tf_op jit(solution)/shard_map/ppermute | solution.py:417
  154.9 4.3 %collective-permute-start.31 = (f32[16,128]{1,0:T(8,128)S(1)}, f32[16,128]{1,0:T(8,128)S(1)}, u32[]{:S(2)}, u32[]{:S(2)}) collective-permute-start(f32[16,128]{1,0:T(8,128)S(1)} %get-tuple-element.143), channel_id=1, source_target_pairs={{0,7},{1,2},{2,1},{3,4},{4,3},{5,6},{6,5},{7,0},{8,15},{9,10},{10,... | collective-permute-start | bytes 24584 | tf_op jit(solution)/shard_map/ppermute | solution.py:418
  (9 other events, 26.0 us)

commit v10 on v9

--- a/solution.py
+++ b/solution.py
@@ -263,7 +263,13 @@
     for q in range(64):
         line = jnp.concatenate([given[0:BS, q : q + 1], given[BS:128, BS + q : BS + q + 1]], axis=0)
         mask[128 * q : 128 * q + 128, :] = (line == wanted).astype(F32).astype(BF16)
-        xp[q] = jnp.concatenate(by_core(same[q, 0:4, :], other[q, 0:4, :]), axis=0)
+
+    def in_order(x, y):
+        for q in range(64):
+            xp[q] = jnp.concatenate([x[q, 0:4, :], y[q, 0:4, :]], axis=0)
+
+    pl.when(even)(lambda: in_order(same, other))
+    pl.when(jnp.logical_not(even))(lambda: in_order(other, same))
     device = jnp.floor((idc + 0.5) * (1.0 / 24.0))
     slot = idc - 24.0 * device
     upper = slot >= 11.5
@@ -378,7 +384,7 @@
         t = v[...]
         for k in range(i):
             t = t - lower[(i, k)] * solved[k]
-        t = t / lower[(i, i)]
+        t = t * (1.0 / lower[(i, i)])
         solved.append(t)
         q_out[i] = t[:, 0:BS]
 

time: 178 us -> 178 us (level)
  no operation moved by 1% of the time
where the time goes in v10:
time: 178 us
  blocking collectives  89.7 us (50%)
  starting transfers between devices  36.4 us (20%)
  Pallas kernels  34.7 us (19%)
  waiting for transfers between devices  16 us (9%)
    all_to_all x4, blocking collectives, everywhere(): lax.all_to_all(y, ('gx', 'gy'), split_axis=0, concat_axis=0, tiled=True)  72.5 us
    pallas_call x24, Pallas kernels, call(): pl.pallas_call(kernel, out_shape=outs, in_specs=specs or [VM] * len(args)...  34.7 us
    ppermute x8, starting transfers between devices, exchange(): lax.ppermute(sends[0], 'gx', swap_pairs(nx, 1))  18.8 us
    all_to_all x1, blocking collectives, everywhere_by_core(): lax.all_to_all(y, ('gx', 'gy'), split_axis=0, concat_axis=0, tiled=True,...  17.2 us
    ppermute x8, waiting for transfers between devices, exchange(): lax.ppermute(sends[0], 'gx', swap_pairs(nx, 1))  14.4 us
    ppermute x8, starting transfers between devices, exchange(): lax.ppermute(sends[2], 'gy', swap_pairs(ny, 1))  11.1 us
    ppermute x8, starting transfers between devices, exchange(): lax.ppermute(sends[3], 'gy', swap_pairs(ny, 0))  4.17 us
  transfers between devices with their start and end apart: 33, of which 8 were waited for; matrix products, arithmetic and copies ran while one was open for 0% of the time, Pallas kernels for 4%

profile of v10, /device:TPU:1, one launch (start us, length us, event | category | flops | bytes accessed | tf_op | source)
XLA Modules:
  0.0 178.0 jit_solution(5607808211344315536)
XLA Ops:
  0.6 3.0 %first.1 = (f32[48,128]{1,0:T(8,128)S(1)}, bf16[128,3072]{1,0:T(8,128)(2,1)S(1)}, f32[8,48,128]{2,1,0:T(8,128)S(1)}, bf16[64,48]{1,0:T(8,128)(2,1)S(1)}, f32[48,...) custom-call(f32[48,64]{1,0:T(8,128)} %refs_0_.1, ...), custom_call_target="tpu_custom_call" | custom-call | flops 2000000 | bytes 100000 | tf_op jit(solution)/shard_map/first/pallas_call | solution.py:401
  3.7 6.9 %collective-permute-start = (f32[6,16,128]{2,1,0:T(8,128)S(1)}, f32[6,16,128]{2,1,0:T(8,128)S(1)}, u32[]{:S(2)}, u32[]{:S(2)}) collective-permute-start(f32[6,16,128]{2,1,0:T(8,128)S(1)} %get-tuple-element.81), channel_id=1, source_target_pairs={{0,120},{8,16},{16,8},{24,32},{32,24},{40,48},{48,40},{56,64},{64,... | collective-permute-start | bytes 147464 | tf_op jit(solution)/shard_map/ppermute | solution.py:422
  10.5 2.1 %collective-permute-start.2 = (f32[6,16,128]{2,1,0:T(8,128)S(1)}, f32[6,16,128]{2,1,0:T(8,128)S(1)}, u32[]{:S(2)}, u32[]{:S(2)}) collective-permute-start(f32[6,16,128]{2,1,0:T(8,128)S(1)} %get-tuple-element.83), channel_id=1, source_target_pairs={{0,7},{1,2},{2,1},{3,4},{4,3},{5,6},{6,5},{7,0},{8,15},{9,10},{10,... | collective-permute-start | bytes 147464 | tf_op jit(solution)/shard_map/ppermute | solution.py:424
  13.7 5.2 %operator.1 = (bf16[896,1536]{1,0:T(8,128)(2,1)S(1)}, bf16[896,1536]{1,0:T(8,128)(2,1)S(1)}, bf16[144,256]{1,0:T(8,128)(2,1)S(1)}) custom-call(f32[48,6,64,64]{3,2,1,0:T(8,128)} %off.1, f32[48,64,64]{2,1,0:T(8,128)} %diag.1, s32[6,48]{1,0:T(8,128)} %bitcast.31, f32[16,6,64,64]{3,2,1,0:T(8,128)S(1)} %get-tuple-element.78.near), custom_call_target="tpu_custom_call" | custom-call | flops 2000000000 | bytes 100000 | tf_op jit(solution)/shard_map/operator/pallas_call | solution.py:401
  20.5 17.2 %all_to_all.25.same = f32[64,16,128]{2,1,0:T(8,128)S(1)} all-to-all(f32[64,16,128]{2,1,0:T(8,128)S(1)} %broadcast_in_dim.12), channel_id=1, replica_groups={{0,2,4,6,8,10,12,14,16,18,20,22,24,26,28,30,32,34,36,38,40,42,44,46,48,..., dimensions={0} | all-to-all | bytes 1048576 | tf_op jit(solution)/shard_map/all_to_all | solution.py:439
  37.7 2.3 %collective-permute-start.4 = (f32[64,16,128]{2,1,0:T(8,128)S(1)}, f32[64,16,128]{2,1,0:T(8,128)S(1)}, u32[]{:S(2)}, u32[]{:S(2)}) collective-permute-start(f32[64,16,128]{2,1,0:T(8,128)S(1)} %all_to_all.25.same), channel_id=1, source_target_pairs={{0,1},{1,0},{2,3},{3,2},{4,5},{5,4},{6,7},{7,6},{8,9},{9,8},{10,11... | collective-permute-start | bytes 1572872 | tf_op jit(solution)/shard_map/ppermute | solution.py:440
  41.5 3.2 %coarse.1 = (bf16[8192,128]{1,0:T(8,128)(2,1)S(1)}, f32[8,112,128]{2,1,0:T(8,128)S(1)}, f32[64,8,128]{2,1,0:T(8,128)S(1)}) custom-call(f32[64,16,128]{2,1,0:T(8,128)S(1)} %all_to_all.25.same, f32[64,16,128]{2,1,0:T(8,128)S(1)} %collective-permute-done.4.other, f32[48,128]{1,0:T(8,128)S(1)} %get-tuple-element.89.ids, ...), custom_call_target="tpu_custom_call" | custom-call | flops 2000000 | bytes 100000 | tf_op jit(solution)/shard_map/coarse/pallas_call | solution.py:401
  44.7 2.3 %correct.4 = (f32[48,128]{1,0:T(8,128)S(1)}, f32[16,128]{1,0:T(8,128)S(1)}, f32[16,128]{1,0:T(8,128)S(1)}, f32[16,128]{1,0:T(8,128)S(1)}, f32[16,128]{1,0:T(8,128)S(1)}) custom-call(f32[64,8,128]{2,1,0:T(8,128)S(1)} %get-tuple-element.90.x, bf16[8192,128]{1,0:T(8,128)(2,1)S(1)} %get-tuple-element.91.mask, f32[8,112,128]{2,1,0:T(8,128)S(1)} %get-tuple-element.92.pte, ...), custom_call_target="tpu_custom_call" | custom-call | flops 2000000 | bytes 100000 | tf_op jit(solution)/shard_map/correct/pallas_call | solution.py:401
  49.9 3.0 %collective-permute-done.5.h0 = f32[16,128]{1,0:T(8,128)S(1)} collective-permute-done((f32[16,128]{1,0:T(8,128)S(1)}, f32[16,128]{1,0:T(8,128)S(1)}, u32[]{:S(2)}, u32[]{:S(2)}) %collective-permute-start.5) | collective-permute-done | bytes 8224 | tf_op jit(solution)/shard_map/ppermute | solution.py:422
  54.3 2.0 %collective-permute-start.9 = (f32[16,128]{1,0:T(8,128)S(1)}, f32[16,128]{1,0:T(8,128)S(1)}, u32[]{:S(2)}, u32[]{:S(2)}) collective-permute-start(f32[16,128]{1,0:T(8,128)S(1)} %get-tuple-element.104), channel_id=1, source_target_pairs={{0,120},{8,16},{16,8},{24,32},{32,24},{40,48},{48,40},{56,64},{64,... | collective-permute-start | bytes 24584 | tf_op jit(solution)/shard_map/ppermute | solution.py:422
  61.4 18.3 %all_to_all.26 = f32[128,4,128]{2,1,0:T(4,128)S(1)} all-to-all(f32[128,4,128]{2,1,0:T(4,128)S(1)} %broadcast_in_dim.13), channel_id=1, replica_groups=mesh['gx'=16,'gy'=8] {'gx','gy'}, dimensions={0} | all-to-all | bytes 524288 | tf_op jit(solution)/shard_map/all_to_all | solution.py:432
  79.7 2.3 %correct.5 = (f32[48,128]{1,0:T(8,128)S(1)}, f32[16,128]{1,0:T(8,128)S(1)}, f32[16,128]{1,0:T(8,128)S(1)}, f32[16,128]{1,0:T(8,128)S(1)}, f32[16,128]{1,0:T(8,128)S(1)}) custom-call(f32[64,8,128]{2,1,0:T(8,128)S(1)} %bitcast.24, bf16[8192,128]{1,0:T(8,128)(2,1)S(1)} %get-tuple-element.91.mask, f32[8,112,128]{2,1,0:T(8,128)S(1)} %get-tuple-element.92.pte, ...), custom_call_target="tpu_custom_call" | custom-call | flops 2000000 | bytes 100000 | tf_op jit(solution)/shard_map/correct/pallas_call | solution.py:401
  84.8 3.0 %collective-permute-done.13.h0 = f32[16,128]{1,0:T(8,128)S(1)} collective-permute-done((f32[16,128]{1,0:T(8,128)S(1)}, f32[16,128]{1,0:T(8,128)S(1)}, u32[]{:S(2)}, u32[]{:S(2)}) %collective-permute-start.13) | collective-permute-done | bytes 8224 | tf_op jit(solution)/shard_map/ppermute | solution.py:422
  89.3 2.3 %collective-permute-start.17 = (f32[16,128]{1,0:T(8,128)S(1)}, f32[16,128]{1,0:T(8,128)S(1)}, u32[]{:S(2)}, u32[]{:S(2)}) collective-permute-start(f32[16,128]{1,0:T(8,128)S(1)} %get-tuple-element.118), channel_id=1, source_target_pairs={{0,120},{8,16},{16,8},{24,32},{32,24},{40,48},{48,40},{56,64},{64,... | collective-permute-start | bytes 24584 | tf_op jit(solution)/shard_map/ppermute | solution.py:422
  91.6 1.8 %collective-permute-start.19 = (f32[16,128]{1,0:T(8,128)S(1)}, f32[16,128]{1,0:T(8,128)S(1)}, u32[]{:S(2)}, u32[]{:S(2)}) collective-permute-start(f32[16,128]{1,0:T(8,128)S(1)} %get-tuple-element.120), channel_id=1, source_target_pairs={{0,7},{1,2},{2,1},{3,4},{4,3},{5,6},{6,5},{7,0},{8,15},{9,10},{10,... | collective-permute-start | bytes 24584 | tf_op jit(solution)/shard_map/ppermute | solution.py:424
  96.4 18.9 %all_to_all.27 = f32[128,4,128]{2,1,0:T(4,128)S(1)} all-to-all(f32[128,4,128]{2,1,0:T(4,128)S(1)} %broadcast_in_dim.14), channel_id=1, replica_groups=mesh['gx'=16,'gy'=8] {'gx','gy'}, dimensions={0} | all-to-all | bytes 524288 | tf_op jit(solution)/shard_map/all_to_all | solution.py:432
  115.3 2.3 %correct.6 = (f32[48,128]{1,0:T(8,128)S(1)}, f32[16,128]{1,0:T(8,128)S(1)}, f32[16,128]{1,0:T(8,128)S(1)}, f32[16,128]{1,0:T(8,128)S(1)}, f32[16,128]{1,0:T(8,128)S(1)}) custom-call(f32[64,8,128]{2,1,0:T(8,128)S(1)} %bitcast.25, bf16[8192,128]{1,0:T(8,128)(2,1)S(1)} %get-tuple-element.91.mask, f32[8,112,128]{2,1,0:T(8,128)S(1)} %get-tuple-element.92.pte, ...), custom_call_target="tpu_custom_call" | custom-call | flops 2000000 | bytes 100000 | tf_op jit(solution)/shard_map/correct/pallas_call | solution.py:401
  120.4 3.0 %collective-permute-done.21.h0 = f32[16,128]{1,0:T(8,128)S(1)} collective-permute-done((f32[16,128]{1,0:T(8,128)S(1)}, f32[16,128]{1,0:T(8,128)S(1)}, u32[]{:S(2)}, u32[]{:S(2)}) %collective-permute-start.21) | collective-permute-done | bytes 8224 | tf_op jit(solution)/shard_map/ppermute | solution.py:422
  124.8 2.3 %collective-permute-start.25 = (f32[16,128]{1,0:T(8,128)S(1)}, f32[16,128]{1,0:T(8,128)S(1)}, u32[]{:S(2)}, u32[]{:S(2)}) collective-permute-start(f32[16,128]{1,0:T(8,128)S(1)} %get-tuple-element.132), channel_id=1, source_target_pairs={{0,120},{8,16},{16,8},{24,32},{32,24},{40,48},{48,40},{56,64},{64,... | collective-permute-start | bytes 24584 | tf_op jit(solution)/shard_map/ppermute | solution.py:422
  127.2 1.8 %collective-permute-start.27 = (f32[16,128]{1,0:T(8,128)S(1)}, f32[16,128]{1,0:T(8,128)S(1)}, u32[]{:S(2)}, u32[]{:S(2)}) collective-permute-start(f32[16,128]{1,0:T(8,128)S(1)} %get-tuple-element.134), channel_id=1, source_target_pairs={{0,7},{1,2},{2,1},{3,4},{4,3},{5,6},{6,5},{7,0},{8,15},{9,10},{10,... | collective-permute-start | bytes 24584 | tf_op jit(solution)/shard_map/ppermute | solution.py:424
  131.9 18.9 %all_to_all.28 = f32[128,4,128]{2,1,0:T(4,128)S(1)} all-to-all(f32[128,4,128]{2,1,0:T(4,128)S(1)} %broadcast_in_dim.15), channel_id=1, replica_groups=mesh['gx'=16,'gy'=8] {'gx','gy'}, dimensions={0} | all-to-all | bytes 524288 | tf_op jit(solution)/shard_map/all_to_all | solution.py:432
  150.8 2.3 %correct.7 = (f32[48,128]{1,0:T(8,128)S(1)}, f32[16,128]{1,0:T(8,128)S(1)}, f32[16,128]{1,0:T(8,128)S(1)}, f32[16,128]{1,0:T(8,128)S(1)}, f32[16,128]{1,0:T(8,128)S(1)}) custom-call(f32[64,8,128]{2,1,0:T(8,128)S(1)} %bitcast.23, bf16[8192,128]{1,0:T(8,128)(2,1)S(1)} %get-tuple-element.91.mask, f32[8,112,128]{2,1,0:T(8,128)S(1)} %get-tuple-element.92.pte, ...), custom_call_target="tpu_custom_call" | custom-call | flops 2000000 | bytes 100000 | tf_op jit(solution)/shard_map/correct/pallas_call | solution.py:401
  156.0 3.0 %collective-permute-done.29.h0 = f32[16,128]{1,0:T(8,128)S(1)} collective-permute-done((f32[16,128]{1,0:T(8,128)S(1)}, f32[16,128]{1,0:T(8,128)S(1)}, u32[]{:S(2)}, u32[]{:S(2)}) %collective-permute-start.29) | collective-permute-done | bytes 8224 | tf_op jit(solution)/shard_map/ppermute | solution.py:422
  160.2 16.4 %all_to_all.29 = f32[128,1,128]{2,1,0:T(1,128)S(1)} all-to-all(f32[128,1,128]{2,1,0:T(1,128)S(1)} %broadcast_in_dim.17), channel_id=1, replica_groups=mesh['gx'=16,'gy'=8] {'gx','gy'}, dimensions={0} | all-to-all | bytes 131072 | tf_op jit(solution)/shard_map/all_to_all | solution.py:432
  (80 shorter events, 33.1 us)
Async XLA Ops:
  3.7 15.5 %collective-permute-start = (f32[6,16,128]{2,1,0:T(8,128)S(1)}, f32[6,16,128]{2,1,0:T(8,128)S(1)}, u32[]{:S(2)}, u32[]{:S(2)}) collective-permute-start(f32[6,16,128]{2,1,0:T(8,128)S(1)} %get-tuple-element.81), channel_id=1, source_target_pairs={{0,120},{8,16},{16,8},{24,32},{32,24},{40,48},{48,40},{56,64},{64,... | collective-permute-start | bytes 147464 | tf_op jit(solution)/shard_map/ppermute | solution.py:422
  10.5 8.7 %collective-permute-start.1 = (f32[6,16,128]{2,1,0:T(8,128)S(1)}, f32[6,16,128]{2,1,0:T(8,128)S(1)}, u32[]{:S(2)}, u32[]{:S(2)}) collective-permute-start(f32[6,16,128]{2,1,0:T(8,128)S(1)} %get-tuple-element.82), channel_id=1, source_target_pairs={{0,8},{8,0},{16,24},{24,16},{32,40},{40,32},{48,56},{56,48},{64,72... | collective-permute-start | bytes 147464 | tf_op jit(solution)/shard_map/ppermute | solution.py:423
  10.5 8.7 %collective-permute-start.2 = (f32[6,16,128]{2,1,0:T(8,128)S(1)}, f32[6,16,128]{2,1,0:T(8,128)S(1)}, u32[]{:S(2)}, u32[]{:S(2)}) collective-permute-start(f32[6,16,128]{2,1,0:T(8,128)S(1)} %get-tuple-element.83), channel_id=1, source_target_pairs={{0,7},{1,2},{2,1},{3,4},{4,3},{5,6},{6,5},{7,0},{8,15},{9,10},{10,... | collective-permute-start | bytes 147464 | tf_op jit(solution)/shard_map/ppermute | solution.py:424
  12.7 6.6 %collective-permute-start.3 = (f32[6,16,128]{2,1,0:T(8,128)S(1)}, f32[6,16,128]{2,1,0:T(8,128)S(1)}, u32[]{:S(2)}, u32[]{:S(2)}) collective-permute-start(f32[6,16,128]{2,1,0:T(8,128)S(1)} %get-tuple-element.84), channel_id=1, source_target_pairs={{0,1},{1,0},{2,3},{3,2},{4,5},{5,4},{6,7},{7,6},{8,9},{9,8},{10,11... | collective-permute-start | bytes 147464 | tf_op jit(solution)/shard_map/ppermute | solution.py:425
  37.7 3.8 %collective-permute-start.4 = (f32[64,16,128]{2,1,0:T(8,128)S(1)}, f32[64,16,128]{2,1,0:T(8,128)S(1)}, u32[]{:S(2)}, u32[]{:S(2)}) collective-permute-start(f32[64,16,128]{2,1,0:T(8,128)S(1)} %all_to_all.25.same), channel_id=1, source_target_pairs={{0,1},{1,0},{2,3},{3,2},{4,5},{5,4},{6,7},{7,6},{8,9},{9,8},{10,11... | collective-permute-start | bytes 1572872 | tf_op jit(solution)/shard_map/ppermute | solution.py:440
  47.0 5.8 %collective-permute-start.5 = (f32[16,128]{1,0:T(8,128)S(1)}, f32[16,128]{1,0:T(8,128)S(1)}, u32[]{:S(2)}, u32[]{:S(2)}) collective-permute-start(f32[16,128]{1,0:T(8,128)S(1)} %get-tuple-element.98), channel_id=1, source_target_pairs={{0,120},{8,16},{16,8},{24,32},{32,24},{40,48},{48,40},{56,64},{64,... | collective-permute-start | bytes 24584 | tf_op jit(solution)/shard_map/ppermute | solution.py:422
  47.7 5.2 %collective-permute-start.6 = (f32[16,128]{1,0:T(8,128)S(1)}, f32[16,128]{1,0:T(8,128)S(1)}, u32[]{:S(2)}, u32[]{:S(2)}) collective-permute-start(f32[16,128]{1,0:T(8,128)S(1)} %get-tuple-element.99), channel_id=1, source_target_pairs={{0,8},{8,0},{16,24},{24,16},{32,40},{40,32},{48,56},{56,48},{64,72... | collective-permute-start | bytes 24584 | tf_op jit(solution)/shard_map/ppermute | solution.py:423
  47.7 5.2 %collective-permute-start.7 = (f32[16,128]{1,0:T(8,128)S(1)}, f32[16,128]{1,0:T(8,128)S(1)}, u32[]{:S(2)}, u32[]{:S(2)}) collective-permute-start(f32[16,128]{1,0:T(8,128)S(1)} %get-tuple-element.100), channel_id=1, source_target_pairs={{0,7},{1,2},{2,1},{3,4},{4,3},{5,6},{6,5},{7,0},{8,15},{9,10},{10,... | collective-permute-start | bytes 24584 | tf_op jit(solution)/shard_map/ppermute | solution.py:424
  48.4 4.5 %collective-permute-start.8 = (f32[16,128]{1,0:T(8,128)S(1)}, f32[16,128]{1,0:T(8,128)S(1)}, u32[]{:S(2)}, u32[]{:S(2)}) collective-permute-start(f32[16,128]{1,0:T(8,128)S(1)} %get-tuple-element.101), channel_id=1, source_target_pairs={{0,1},{1,0},{2,3},{3,2},{4,5},{5,4},{6,7},{7,6},{8,9},{9,8},{10,11... | collective-permute-start | bytes 24584 | tf_op jit(solution)/shard_map/ppermute | solution.py:425
  54.3 5.8 %collective-permute-start.9 = (f32[16,128]{1,0:T(8,128)S(1)}, f32[16,128]{1,0:T(8,128)S(1)}, u32[]{:S(2)}, u32[]{:S(2)}) collective-permute-start(f32[16,128]{1,0:T(8,128)S(1)} %get-tuple-element.104), channel_id=1, source_target_pairs={{0,120},{8,16},{16,8},{24,32},{32,24},{40,48},{48,40},{56,64},{64,... | collective-permute-start | bytes 24584 | tf_op jit(solution)/shard_map/ppermute | solution.py:422
  56.3 3.8 %collective-permute-start.10 = (f32[16,128]{1,0:T(8,128)S(1)}, f32[16,128]{1,0:T(8,128)S(1)}, u32[]{:S(2)}, u32[]{:S(2)}) collective-permute-start(f32[16,128]{1,0:T(8,128)S(1)} %get-tuple-element.105), channel_id=1, source_target_pairs={{0,8},{8,0},{16,24},{24,16},{32,40},{40,32},{48,56},{56,48},{64,72... | collective-permute-start | bytes 24584 | tf_op jit(solution)/shard_map/ppermute | solution.py:423
  56.3 3.8 %collective-permute-start.11 = (f32[16,128]{1,0:T(8,128)S(1)}, f32[16,128]{1,0:T(8,128)S(1)}, u32[]{:S(2)}, u32[]{:S(2)}) collective-permute-start(f32[16,128]{1,0:T(8,128)S(1)} %get-tuple-element.106), channel_id=1, source_target_pairs={{0,7},{1,2},{2,1},{3,4},{4,3},{5,6},{6,5},{7,0},{8,15},{9,10},{10,... | collective-permute-start | bytes 24584 | tf_op jit(solution)/shard_map/ppermute | solution.py:424
  82.0 5.8 %collective-permute-start.13 = (f32[16,128]{1,0:T(8,128)S(1)}, f32[16,128]{1,0:T(8,128)S(1)}, u32[]{:S(2)}, u32[]{:S(2)}) collective-permute-start(f32[16,128]{1,0:T(8,128)S(1)} %get-tuple-element.112), channel_id=1, source_target_pairs={{0,120},{8,16},{16,8},{24,32},{32,24},{40,48},{48,40},{56,64},{64,... | collective-permute-start | bytes 24584 | tf_op jit(solution)/shard_map/ppermute | solution.py:422
  83.6 4.3 %collective-permute-start.14 = (f32[16,128]{1,0:T(8,128)S(1)}, f32[16,128]{1,0:T(8,128)S(1)}, u32[]{:S(2)}, u32[]{:S(2)}) collective-permute-start(f32[16,128]{1,0:T(8,128)S(1)} %get-tuple-element.113), channel_id=1, source_target_pairs={{0,8},{8,0},{16,24},{24,16},{32,40},{40,32},{48,56},{56,48},{64,72... | collective-permute-start | bytes 24584 | tf_op jit(solution)/shard_map/ppermute | solution.py:423
  83.6 4.3 %collective-permute-start.15 = (f32[16,128]{1,0:T(8,128)S(1)}, f32[16,128]{1,0:T(8,128)S(1)}, u32[]{:S(2)}, u32[]{:S(2)}) collective-permute-start(f32[16,128]{1,0:T(8,128)S(1)} %get-tuple-element.114), channel_id=1, source_target_pairs={{0,7},{1,2},{2,1},{3,4},{4,3},{5,6},{6,5},{7,0},{8,15},{9,10},{10,... | collective-permute-start | bytes 24584 | tf_op jit(solution)/shard_map/ppermute | solution.py:424
  89.3 5.8 %collective-permute-start.17 = (f32[16,128]{1,0:T(8,128)S(1)}, f32[16,128]{1,0:T(8,128)S(1)}, u32[]{:S(2)}, u32[]{:S(2)}) collective-permute-start(f32[16,128]{1,0:T(8,128)S(1)} %get-tuple-element.118), channel_id=1, source_target_pairs={{0,120},{8,16},{16,8},{24,32},{32,24},{40,48},{48,40},{56,64},{64,... | collective-permute-start | bytes 24584 | tf_op jit(solution)/shard_map/ppermute | solution.py:422
  91.6 3.5 %collective-permute-start.19 = (f32[16,128]{1,0:T(8,128)S(1)}, f32[16,128]{1,0:T(8,128)S(1)}, u32[]{:S(2)}, u32[]{:S(2)}) collective-permute-start(f32[16,128]{1,0:T(8,128)S(1)} %get-tuple-element.120), channel_id=1, source_target_pairs={{0,7},{1,2},{2,1},{3,4},{4,3},{5,6},{6,5},{7,0},{8,15},{9,10},{10,... | collective-permute-start | bytes 24584 | tf_op jit(solution)/shard_map/ppermute | solution.py:424
  117.6 5.8 %collective-permute-start.21 = (f32[16,128]{1,0:T(8,128)S(1)}, f32[16,128]{1,0:T(8,128)S(1)}, u32[]{:S(2)}, u32[]{:S(2)}) collective-permute-start(f32[16,128]{1,0:T(8,128)S(1)} %get-tuple-element.126), channel_id=1, source_target_pairs={{0,120},{8,16},{16,8},{24,32},{32,24},{40,48},{48,40},{56,64},{64,... | collective-permute-start | bytes 24584 | tf_op jit(solution)/shard_map/ppermute | solution.py:422
  119.1 4.3 %collective-permute-start.22 = (f32[16,128]{1,0:T(8,128)S(1)}, f32[16,128]{1,0:T(8,128)S(1)}, u32[]{:S(2)}, u32[]{:S(2)}) collective-permute-start(f32[16,128]{1,0:T(8,128)S(1)} %get-tuple-element.127), channel_id=1, source_target_pairs={{0,8},{8,0},{16,24},{24,16},{32,40},{40,32},{48,56},{56,48},{64,72... | collective-permute-start | bytes 24584 | tf_op jit(solution)/shard_map/ppermute | solution.py:423
  119.1 4.3 %collective-permute-start.23 = (f32[16,128]{1,0:T(8,128)S(1)}, f32[16,128]{1,0:T(8,128)S(1)}, u32[]{:S(2)}, u32[]{:S(2)}) collective-permute-start(f32[16,128]{1,0:T(8,128)S(1)} %get-tuple-element.128), channel_id=1, source_target_pairs={{0,7},{1,2},{2,1},{3,4},{4,3},{5,6},{6,5},{7,0},{8,15},{9,10},{10,... | collective-permute-start | bytes 24584 | tf_op jit(solution)/shard_map/ppermute | solution.py:424
  124.8 5.8 %collective-permute-start.25 = (f32[16,128]{1,0:T(8,128)S(1)}, f32[16,128]{1,0:T(8,128)S(1)}, u32[]{:S(2)}, u32[]{:S(2)}) collective-permute-start(f32[16,128]{1,0:T(8,128)S(1)} %get-tuple-element.132), channel_id=1, source_target_pairs={{0,120},{8,16},{16,8},{24,32},{32,24},{40,48},{48,40},{56,64},{64,... | collective-permute-start | bytes 24584 | tf_op jit(solution)/shard_map/ppermute | solution.py:422
  153.2 5.8 %collective-permute-start.29 = (f32[16,128]{1,0:T(8,128)S(1)}, f32[16,128]{1,0:T(8,128)S(1)}, u32[]{:S(2)}, u32[]{:S(2)}) collective-permute-start(f32[16,128]{1,0:T(8,128)S(1)} %get-tuple-element.141), channel_id=1, source_target_pairs={{0,120},{8,16},{16,8},{24,32},{32,24},{40,48},{48,40},{56,64},{64,... | collective-permute-start | bytes 24584 | tf_op jit(solution)/shard_map/ppermute | solution.py:422
  154.7 4.3 %collective-permute-start.30 = (f32[16,128]{1,0:T(8,128)S(1)}, f32[16,128]{1,0:T(8,128)S(1)}, u32[]{:S(2)}, u32[]{:S(2)}) collective-permute-start(f32[16,128]{1,0:T(8,128)S(1)} %get-tuple-element.142), channel_id=1, source_target_pairs={{0,8},{8,0},{16,24},{24,16},{32,40},{40,32},{48,56},{56,48},{64,72... | collective-permute-start | bytes 24584 | tf_op jit(solution)/shard_map/ppermute | solution.py:423
  154.7 4.3 %collective-permute-start.31 = (f32[16,128]{1,0:T(8,128)S(1)}, f32[16,128]{1,0:T(8,128)S(1)}, u32[]{:S(2)}, u32[]{:S(2)}) collective-permute-start(f32[16,128]{1,0:T(8,128)S(1)} %get-tuple-element.143), channel_id=1, source_target_pairs={{0,7},{1,2},{2,1},{3,4},{4,3},{5,6},{6,5},{7,0},{8,15},{9,10},{10,... | collective-permute-start | bytes 24584 | tf_op jit(solution)/shard_map/ppermute | solution.py:424
  (9 other events, 26.0 us)
